TPU v7x, 32 devices: a whole 2x2x4 slice. The times are simulated.
32 devices in a mesh: lon: 8 (over z, x), lat: 4 (over y, core).
Axes of the slice: x: 2, y: 2, z: 4, core: 2. Of those that a mesh axis runs over, the one named last changes fastest.
Arguments:
- warmth_deviation: float32 [10, 256, 1024], P(None, 'lat', 'lon'), may hold values from -6 to 6
- saltiness_deviation: float32 [10, 256, 1024], P(None, 'lat', 'lon'), may hold values from -6 to 6
- easterly_speed: float32 [10, 256, 1024], P(None, 'lat', 'lon'), may hold values from -6 to 6
- poleward_speed: float32 [10, 256, 1024], P(None, 'lat', 'lon'), may hold values from -6 to 6
- stratum_spans: float32 [10], replicated, may hold values from 0.5 to 2
- water_indicator: int32 [256, 1024], P('lat', 'lon'), may hold values 0 or 1
- opposite_counterpart: int32 [1024], P('lon'), may hold values from 0 to 1023, as said below
- elevation_weights: float32 [256, 1024], P('lat', 'lon'), may hold values from 0.2 to 2
- elevation_anomaly: float32 [256, 1024], P('lat', 'lon'), may hold values from -3 to 17
Outputs:
- new_temperature: float32 [10, 256, 1024], P(None, 'lat', 'lon')
- new_salinity: float32 [10, 256, 1024], P(None, 'lat', 'lon')
- new_zonal: float32 [10, 256, 1024], P(None, 'lat', 'lon')
- new_meridional: float32 [10, 256, 1024], P(None, 'lat', 'lon')
- new_surface: float32 [256, 1024], P('lat', 'lon')
Inputs may be any that keep to these rules, and one draw needn't show every extreme that they name: opposite_counterpart[x] = (h - 1 - x) mod 1024 for a hinge column h chosen by the draw, so opposite_counterpart[opposite_counterpart[x]] = x.
All inputs are finite; a program needn't handle non-finite values. No bound on the sum of `water_indicator` on one device may be relied on, other than what follows from the above.
Results may differ from a plain program's by a relative error of at most 0.0001.
Values sent between devices are 32-bit elements; how exact they have to be, the bound alone decides.
No kernel may reach another device: no remote copies, remote signals or barrier semaphores. Data moves between devices by JAX's collectives and lax.ppermute only.
A program may use at most 64 MiB of HBM per device.

v0:
```python
import functools

import jax
import jax.numpy as jnp
from jax import lax
from jax.experimental import pallas as pl
from jax.experimental.pallas import tpu as pltpu
from jax.sharding import PartitionSpec as P

TIME_STEP = 0.1
MIXING = 0.1

DEEP = 5
FIELDS = 6
VMEM_LIMIT = 32 * 1024 * 1024


def density(heat, salt):
    return heat * (-1.0 - 0.15 * heat - 0.2 * salt) + 0.8 * salt


def iota(shape, axis):
    return lax.broadcasted_iota(jnp.int32, shape, axis)


def packet_rows(levels):
    return -(-(4 * levels + FIELDS * DEEP) // 8) * 8


def pack_kernel(meta, spans, heat, salt, zonal, merid, water, weights, anomaly, fields, first, second, columns):
    levels, rows, cols = heat.shape
    span = [spans[k] for k in range(levels)]
    below = [None] * levels
    total = 0.0
    for k in reversed(range(levels)):
        below[k] = span[k] * (0.5 * span[k] + total)
        total = total + span[k]
    press = jnp.zeros((rows, cols), jnp.float32)
    east = jnp.zeros((rows, cols), jnp.float32)
    north = jnp.zeros((rows, cols), jnp.float32)
    for k in range(levels):
        press = press + below[k] * density(heat[k], salt[k])
        east = east + span[k] * zonal[k]
        north = north + span[k] * merid[k]
    fields[0] = press
    fields[1] = east
    fields[2] = north
    fields[3] = water[...].astype(jnp.float32)
    fields[4] = weights[...]
    fields[5] = anomaly[...]
    odd = meta[0]
    for packet, at_top in ((first, odd == 0), (second, odd == 1)):
        for j in range(DEEP):
            row = jnp.where(at_top, rows - 1 - j, j)
            if j < 2:
                for place, source in ((0, heat), (2 * levels, salt)):
                    for k in range(levels):
                        at = place + j * levels + k
                        packet[at : at + 1, :] = source[k, pl.ds(row, 1), :]
            for f in range(FIELDS):
                at = 4 * levels + FIELDS * j + f
                packet[at : at + 1, :] = fields[f, pl.ds(row, 1), :]
        used = 4 * levels + FIELDS * DEEP
        if used < packet.shape[0]:
            packet[used:, :] = jnp.zeros((packet.shape[0] - used, cols), jnp.float32)
    group = iota((rows, cols), 1) // 4
    edge = jnp.zeros((rows, cols), jnp.float32)
    for q in range(2 * levels):
        layer = heat[q] if q < levels else salt[q - levels]
        edge = jnp.where(group == q, pltpu.roll(layer, (4 * q + 2) % cols, 1), edge)
    columns[...] = edge


def turn_kernel(meta, fields, first, second, third, columns, ext, north_rows, south_rows, to_east, to_west):
    high, cols = first.shape
    rows = fields.shape[1]
    tall = ext.shape[1]
    levels = north_rows.shape[0] // 4
    odd, offset, top = meta[0], meta[1], meta[2]
    lane = iota((high, cols), 1)
    place = iota((high, cols), 0) - 4 * levels
    kind = lax.rem(jnp.maximum(place, 0), FIELDS)
    flips = (place >= 0) & ((kind == 1) | (kind == 2))
    from_first = first[...]
    from_second = second[...]
    facing = jnp.where(lane < offset, third[...], from_second)
    source = offset - 1 - lane
    source = jnp.where(source < 0, source + cols, source)
    facing = jnp.take_along_axis(facing, source, axis=1)
    facing = jnp.where(flips, -facing, facing)
    beyond = jnp.where(top == 1, facing, from_second)
    north = jnp.where(odd == 1, beyond, from_first)
    south = jnp.where(odd == 1, from_first, from_second)
    north_rows[...] = north[: 4 * levels]
    south_rows[...] = south[: 4 * levels]
    for f in range(FIELDS):
        ext[f, :rows, :] = fields[f]
        ext[f, rows + DEEP : tall - DEEP, :] = jnp.zeros((tall - rows - 2 * DEEP, cols), jnp.float32)
        for j in range(DEEP):
            at = 4 * levels + FIELDS * j + f
            ext[f, rows + j : rows + j + 1, :] = north[at : at + 1]
            ext[f, tall - 1 - j : tall - j, :] = south[at : at + 1]
    used = 8 * levels
    lane = iota((tall, cols), 1)
    base = jnp.concatenate([columns[...], jnp.zeros((tall - rows, cols), jnp.float32)], axis=0)
    east, west = base, base
    for f in range(FIELDS):
        here = (lane >= used + DEEP * f) & (lane < used + DEEP * (f + 1))
        layer = ext[f]
        east = jnp.where(here, pltpu.roll(layer, (used + DEEP * f + DEEP) % cols, 1), east)
        west = jnp.where(here, pltpu.roll(layer, used + DEEP * f, 1), west)
    to_east[...] = east
    to_west[...] = west


def krylov_kernel(used, ext, from_west, from_east, base, moments):
    tall, cols = ext.shape[1], ext.shape[2]
    rows = base.shape[1]
    lane = iota((tall, cols), 1)
    west = from_west[...]
    east = from_east[...]
    first = lane == 0
    last = lane == cols - 1

    def load(f):
        a = pltpu.roll(west, (2 * cols - DEEP - used - DEEP * f) % cols, 1)
        b = pltpu.roll(east, (2 * cols - used - DEEP * f) % cols, 1)
        side = jnp.where(lane >= cols - DEEP, a, jnp.where(lane < DEEP, b, 0.0))
        return ext[f], side

    def plus_x(pair):
        a, b = (pltpu.roll(part, cols - 1, 1) for part in pair)
        return jnp.where(last, b, a), jnp.where(last, a, b)

    def minus_x(pair):
        a, b = (pltpu.roll(part, 1, 1) for part in pair)
        return jnp.where(first, b, a), jnp.where(first, a, b)

    def plus_y(pair):
        return tuple(pltpu.roll(part, tall - 1, 0) for part in pair)

    def minus_y(pair):
        return tuple(pltpu.roll(part, 1, 0) for part in pair)

    def each(function, *pairs):
        return tuple(function(*parts) for parts in zip(*pairs))

    def neighbours(pair):
        return each(
            lambda a, b, c, d: (a + b) + (c + d), plus_x(pair), minus_x(pair), plus_y(pair), minus_y(pair)
        )

    press, zonal, merid, wet, weights, anomaly = (load(f) for f in range(FIELDS))
    half = 0.5 * TIME_STEP
    flow = lambda w, speed, a, b: w * (speed - half * (a - b))
    east_flow = each(flow, wet, zonal, plus_x(press), minus_x(press))
    north_flow = each(flow, wet, merid, plus_y(press), minus_y(press))
    right = each(
        lambda w, g, n, a, b, c, d: w * (g * n - 0.5 * (a - b + c - d)),
        wet,
        weights,
        anomaly,
        plus_x(east_flow),
        minus_x(east_flow),
        plus_y(north_flow),
        minus_y(north_flow),
    )
    diagonal = each(lambda g: 4.0 + g, weights)
    inverse = each(lambda m: 1.0 / m, diagonal)
    scale = each(lambda w, i: w * i, wet, inverse)
    zero = each(lambda r, i: r * i, right, inverse)
    one = each(lambda a, n: a * n, scale, neighbours(zero))
    two = each(lambda a, n: a * n, scale, neighbours(one))
    last_sum = neighbours(two)[0][:rows]
    right, middle = right[0][:rows], diagonal[0][:rows]
    zero, one, two = zero[0][:rows], one[0][:rows], two[0][:rows]
    base[0] = zero
    base[1] = one
    base[2] = two
    weighted = middle * one
    products = (
        right * zero,
        right * one,
        weighted * one,
        weighted * two,
        middle * two * two,
        last_sum * two,
    )
    for k, product in enumerate(products):
        moments[k : k + 1, :] = jnp.sum(product, axis=0, keepdims=True)
    moments[len(products) :, :] = jnp.zeros((moments.shape[0] - len(products), cols), jnp.float32)


def step_kernel(
    spans, heat, salt, zonal, merid, water, north_rows, south_rows, from_west, from_east,
    new_heat, new_salt, new_zonal, new_merid,
):
    levels, rows, cols = heat.shape
    wet = water[...].astype(jnp.float32)
    lane = iota((rows, cols), 1)
    row = iota((rows, cols), 0)
    sides = jnp.where((lane & 3) < 2, from_west[:rows, :], from_east[:rows, :])

    def around(cells, q, k, place):
        side = pltpu.roll(sides, (2 * cols - (4 * q + 2)) % cols, 1)

        def shift_x(by):
            a = pltpu.roll(cells, by % cols, 1)
            b = pltpu.roll(side, by % cols, 1)
            own = lane >= by if by > 0 else lane < cols + by
            return jnp.where(own, a, b)

        n0 = north_rows[place + k : place + k + 1, :]
        n1 = north_rows[place + levels + k : place + levels + k + 1, :]
        s0 = south_rows[place + k : place + k + 1, :]
        s1 = south_rows[place + levels + k : place + levels + k + 1, :]
        north_one = jnp.where(row == rows - 1, n0, pltpu.roll(cells, rows - 1, 0))
        north_two = jnp.where(row == rows - 1, n1, jnp.where(row == rows - 2, n0, pltpu.roll(cells, rows - 2, 0)))
        south_one = jnp.where(row == 0, s0, pltpu.roll(cells, 1, 0))
        south_two = jnp.where(row == 0, s1, jnp.where(row == 1, s0, pltpu.roll(cells, 2, 0)))
        return (shift_x(-1), shift_x(1), shift_x(-2), shift_x(2), north_one, south_one, north_two, south_two)

    def advance(cells, parts, speed_x, speed_y):
        e1, w1, e2, w2, n1, s1, n2, s2 = parts
        grad_east = 8.0 * (e1 - w1) - (e2 - w2)
        grad_north = 8.0 * (n1 - s1) - (n2 - s2)
        laplace = (e1 + w1) + (n1 + s1) - 4.0 * cells
        tendency = (-TIME_STEP / 12.0) * (speed_x * grad_east + speed_y * grad_north) + MIXING * laplace
        return cells + wet * tendency

    half = 0.5 * TIME_STEP
    above_x = jnp.zeros((rows, cols), jnp.float32)
    above_y = jnp.zeros((rows, cols), jnp.float32)
    for k in range(levels):
        t, s, u, v = heat[k], salt[k], zonal[k], merid[k]
        around_t = around(t, k, k, 0)
        around_s = around(s, levels + k, k, 2 * levels)
        new_heat[k] = advance(t, around_t, u, v)
        new_salt[k] = advance(s, around_s, u, v)
        layer_x = spans[k] * (density(around_t[0], around_s[0]) - density(around_t[1], around_s[1]))
        layer_y = spans[k] * (density(around_t[4], around_s[4]) - density(around_t[5], around_s[5]))
        new_zonal[k] = wet * (u - half * (above_x + 0.5 * layer_x))
        new_merid[k] = wet * (v - half * (above_y + 0.5 * layer_y))
        above_x = above_x + layer_x
        above_y = above_y + layer_y


def surface_kernel(shares, base, surface):
    sums = jnp.sum(jnp.sum(shares[...], axis=0), axis=1, keepdims=True)
    nu = [sums[k : k + 1, :] for k in range(6)]

    def ratio(a, b):
        good = b > 0.0
        return jnp.where(good, a / jnp.where(good, b, 1.0), 0.0)

    def form(p, h):
        total = 0.0
        for i, a in enumerate(p):
            for j in range(i, len(p)):
                term = a * p[j] * h[i + j]
                total = total + (term if i == j else 2.0 * term)
        return total

    gap = [nu[k] - nu[k + 1] for k in range(5)]
    rz = nu[0]
    alpha = ratio(rz, gap[0])
    one = jnp.ones_like(rz)
    y = [one - alpha, alpha]
    x = [alpha, 0.0, 0.0]
    new = form(y, nu)
    beta = ratio(new, rz)
    rz = new
    p = [y[0] + beta, y[1]]
    alpha = ratio(rz, form(p, gap))
    x = [x[0] + alpha * p[0], alpha * p[1], 0.0]
    y = [y[0] - alpha * p[0], y[1] - alpha * (p[1] - p[0]), alpha * p[1]]
    new = form(y, nu)
    beta = ratio(new, rz)
    rz = new
    p = [y[0] + beta * p[0], y[1] + beta * p[1], y[2]]
    alpha = ratio(rz, form(p, gap))
    x = [x[0] + alpha * p[0], x[1] + alpha * p[1], alpha * p[2]]
    surface[...] = x[0] * base[0] + x[1] * base[1] + x[2] * base[2]


def call(kernel, outs, smem, flops, moved, **named):
    specs = lambda count: [pl.BlockSpec(memory_space=pltpu.VMEM)] * count

    def run(*args):
        return pl.pallas_call(
            kernel,
            out_shape=[jax.ShapeDtypeStruct(shape, jnp.float32) for shape in outs],
            in_specs=[pl.BlockSpec(memory_space=pltpu.SMEM)] * smem + specs(len(args) - smem),
            out_specs=specs(len(outs)),
            cost_estimate=pl.CostEstimate(flops=flops, bytes_accessed=moved, transcendentals=0),
            compiler_params=pltpu.CompilerParams(vmem_limit_bytes=VMEM_LIMIT),
            **named,
        )(*args)

    return run


def body(
    warmth_deviation,
    saltiness_deviation,
    easterly_speed,
    poleward_speed,
    stratum_spans,
    water_indicator,
    opposite_counterpart,
    elevation_weights,
    elevation_anomaly,
):
    lons, lats = lax.axis_size("lon"), lax.axis_size("lat")
    lon, lat = lax.axis_index("lon"), lax.axis_index("lat")
    levels, rows, cols = warmth_deviation.shape
    high = packet_rows(levels)
    tall = rows + 16
    width = cols * lons
    flat = lambda i, j: (i % lons) * lats + j

    hinge = lax.rem(opposite_counterpart[0] + 1 + cols * lon, width)
    block = hinge // cols
    meta = jnp.stack([lax.rem(lat, 2), lax.rem(hinge, cols), (lat == lats - 1).astype(jnp.int32)]).astype(jnp.int32)

    state = (warmth_deviation, saltiness_deviation, easterly_speed, poleward_speed)
    cells = levels * rows * cols
    fields, first, second, columns = call(
        pack_kernel,
        [(FIELDS, rows, cols), (high, cols), (high, cols), (rows, cols)],
        2,
        12 * cells,
        16 * cells,
        name="level_sums",
    )(meta, stratum_spans, *state, water_indicator, elevation_weights, elevation_anomaly)

    pairs_first = [(flat(i, j), flat(i, j ^ 1)) for i in range(lons) for j in range(lats)]
    pairs_inner = [
        (flat(i, a), flat(i, b))
        for i in range(lons)
        for j in range(1, lats - 1, 2)
        for a, b in ((j, j + 1), (j + 1, j))
    ]
    axes = ("lon", "lat")
    got_first = lax.ppermute(first, axes, pairs_first)

    def facing(shift, packet):
        near = [(flat(shift - 1 - i, lats - 1), flat(i, lats - 1)) for i in range(lons)]
        far = [(flat(shift - i, lats - 1), flat(i, lats - 1)) for i in range(lons)]
        return lax.ppermute(packet, axes, pairs_inner + near), lax.ppermute(packet, axes, far)

    got_second, got_third = lax.switch(block, [functools.partial(facing, s) for s in range(lons)], second)

    ext, north_rows, south_rows, to_east, to_west = call(
        turn_kernel,
        [(FIELDS, tall, cols), (4 * levels, cols), (4 * levels, cols), (tall, cols), (tall, cols)],
        1,
        FIELDS * tall * cols,
        4 * 4 * FIELDS * tall * cols,
        name="row_halos",
    )(meta, fields, got_first, got_second, got_third, columns)

    from_west = lax.ppermute(to_east, "lon", [(i, (i + 1) % lons) for i in range(lons)])
    from_east = lax.ppermute(to_west, "lon", [((i + 1) % lons, i) for i in range(lons)])

    base, moments = call(
        functools.partial(krylov_kernel, 8 * levels),
        [(3, rows, cols), (8, cols)],
        0,
        200 * tall * cols,
        4 * 12 * tall * cols,
        name="krylov",
    )(ext, from_west, from_east)

    new_heat, new_salt, new_zonal, new_merid = call(
        step_kernel,
        [(levels, rows, cols)] * 4,
        1,
        120 * cells,
        32 * cells,
        name="levels_step",
    )(stratum_spans, *state, water_indicator, north_rows, south_rows, from_west, from_east)

    count = lons * lats
    shares = lax.all_to_all(jnp.broadcast_to(moments, (count,) + moments.shape), axes, 0, 0)
    (surface,) = call(
        surface_kernel, [(rows, cols)], 0, 6 * rows * cols, 16 * rows * cols, name="surface"
    )(shares, base)
    return (new_heat, new_salt, new_zonal, new_merid, surface)


def solution(mesh):
    for axis in mesh.shape.values():
        assert axis > 1 and axis & (axis - 1) == 0
    levels = P(None, "lat", "lon")
    flat = P("lat", "lon")
    return jax.shard_map(
        body,
        mesh=mesh,
        in_specs=(levels, levels, levels, levels, P(), flat, P("lon"), flat, flat),
        out_specs=(levels, levels, levels, levels, flat),
        check_vma=False,
    )
```

profile of v0, /device:TPU:0, one launch (start us, length us, event | category | flops | bytes accessed | tf_op | source)
XLA Modules:
  0.0 42.8 jit_solution(3011091942689390651)
XLA Ops:
  0.6 0.0 copy-start.12
  0.7 0.6 %copy-done.12 = s32[128]{0:T(128)S(1)} copy-done((s32[128]{0:T(128)S(1)}, s32[128]{0:T(128)}, u32[]{:S(2)}) %copy-start.12) | copy-done | bytes 536
  1.4 0.1 pad_add_fusion.meta
  1.4 0.6 %copy-done.11 = f32[10]{0:T(128)S(1)} copy-done((f32[10]{0:T(128)S(1)}, f32[10]{0:T(128)}, u32[]{:S(2)}) %copy-start.11) | copy-done | bytes 64
  2.0 1.0 %copy-done = f32[10,64,128]{2,1,0:T(8,128)S(1)} copy-done((f32[10,64,128]{2,1,0:T(8,128)S(1)}, f32[10,64,128]{2,1,0:T(8,128)}, u32[]{:S(2)}) %copy-start) | copy-done | bytes 327704
  3.0 1.0 %copy-done.2 = f32[10,64,128]{2,1,0:T(8,128)S(1)} copy-done((f32[10,64,128]{2,1,0:T(8,128)S(1)}, f32[10,64,128]{2,1,0:T(8,128)}, u32[]{:S(2)}) %copy-start.2) | copy-done | bytes 327704
  4.0 1.0 %copy-done.4 = f32[10,64,128]{2,1,0:T(8,128)S(1)} copy-done((f32[10,64,128]{2,1,0:T(8,128)S(1)}, f32[10,64,128]{2,1,0:T(8,128)}, u32[]{:S(2)}) %copy-start.4) | copy-done | bytes 327704
  4.9 1.0 %copy-done.6 = f32[10,64,128]{2,1,0:T(8,128)S(1)} copy-done((f32[10,64,128]{2,1,0:T(8,128)S(1)}, f32[10,64,128]{2,1,0:T(8,128)}, u32[]{:S(2)}) %copy-start.6) | copy-done | bytes 327704
  5.9 0.8 %copy-done.10 = f32[64,128]{1,0:T(8,128)S(1)} copy-done((f32[64,128]{1,0:T(8,128)S(1)}, f32[64,128]{1,0:T(8,128)}, u32[]{:S(2)}) %copy-start.10) | copy-done | bytes 32792
  6.7 0.9 %level_sums.1 = (f32[6,64,128]{2,1,0:T(8,128)S(1)}, f32[72,128]{1,0:T(8,128)S(1)}, f32[72,128]{1,0:T(8,128)S(1)}, f32[64,128]{1,0:T(8,128)S(1)}) custom-call(s32[3]{0:T(128)S(1)} %pad_add_fusion.meta, f32[10]{0:T(128)S(1)} %copy-done.11, f32[10,64,128]{2,1,0:T(8,128)S(1)} %copy-done, f32[10,64,128]{2,1,0:T(8,128)S(1)} %copy-done.2, ...), custom_call_target="tpu_custom_call" | custom-call | flops 983040 | bytes 1310720 | tf_op jit(solution)/shard_map/level_sums/pallas_call | solution.py:290
  7.6 0.5 %collective-permute-start.16 = (f32[72,128]{1,0:T(8,128)S(1)}, f32[72,128]{1,0:T(8,128)S(1)}, u32[]{:S(2)}, u32[]{:S(2)}) collective-permute-start(f32[72,128]{1,0:T(8,128)S(1)} %get-tuple-element.31), channel_id=1, source_target_pairs={{0,1},{1,0},{2,3},{3,2},{4,5},{5,4},{6,7},{7,6},{8,9},{9,8},{10,11... | collective-permute-start | bytes 110600 | tf_op jit(solution)/shard_map/ppermute | solution.py:345
  8.1 2.5 %conditional.1 = (f32[72,128]{1,0:T(8,128)}, f32[72,128]{1,0:T(8,128)}) conditional(s32[]{:T(128)} %clamp.3, f32[72,128]{1,0:T(8,128)S(1)} %get-tuple-element.32, f32[72,128]{1,0:T(8,128)S(1)} %get-tuple-element.32, f32[72,128]{1,0:T(8,128)S(1)} %get-tuple-element.32, f32[72,128]{1,0:T(8,128)S(1)} %get-tuple-element.32, ...), branch_computations={%region_0.1_spmd, %region_1.2_spmd, %region_2.3_spmd, %region_3.4_... | conditional | bytes 295008 | solution.py:352
  8.1 1.3 %collective-permute-start.11 = (f32[72,128]{1,0:T(8,128)S(1)}, f32[72,128]{1,0:T(8,128)}, u32[]{:S(2)}, u32[]{:S(2)}) collective-permute-start(f32[72,128]{1,0:T(8,128)S(1)} %param.5), channel_id=1, source_target_pairs={{23,3},{19,7},{15,11},{11,15},{7,19},{3,23},{31,27},{27,31}} | collective-permute-start | bytes 110600 | tf_op jit(solution)/shard_map/cond/branch_5_fun/ppermute | solution.py:350
  9.4 1.3 %collective-permute-start.10 = (f32[72,128]{1,0:T(8,128)S(1)}, f32[72,128]{1,0:T(8,128)}, u32[]{:S(2)}, u32[]{:S(2)}) collective-permute-start(f32[72,128]{1,0:T(8,128)S(1)} %param.5), channel_id=1, source_target_pairs={{1,2},{2,1},{5,6},{6,5},{9,10},{10,9},{13,14},{14,13},{17,18},{18,... | collective-permute-start | bytes 110600 | tf_op jit(solution)/shard_map/cond/branch_5_fun/ppermute | solution.py:350
  10.6 0.0 collective-permute-done.11
  10.6 0.0 collective-permute-done.10
  10.7 0.0 collective-permute-done.16.first
  10.7 0.0 copy-start.5
  10.7 1.1 %row_halos.1 = (f32[6,80,128]{2,1,0:T(8,128)S(1)}, f32[40,128]{1,0:T(8,128)S(1)}, f32[40,128]{1,0:T(8,128)S(1)}, f32[80,128]{1,0:T(8,128)S(1)}, f32[80,128]{1,0:T(8,128)S(1)}) custom-call(s32[3]{0:T(128)S(1)} %pad_add_fusion.meta, f32[6,64,128]{2,1,0:T(8,128)S(1)} %get-tuple-element.30.fields, f32[72,128]{1,0:T(8,128)S(1)} %collective-permute-done.16.first, ...), custom_call_target="tpu_custom_call" | custom-call | flops 61440 | bytes 983040 | tf_op jit(solution)/shard_map/row_halos/pallas_call | solution.py:290
  11.7 2.6 %collective-permute-start.17 = (f32[80,128]{1,0:T(8,128)S(1)}, f32[80,128]{1,0:T(8,128)S(1)}, u32[]{:S(2)}, u32[]{:S(2)}) collective-permute-start(f32[80,128]{1,0:T(8,128)S(1)} %get-tuple-element.38), channel_id=1, source_target_pairs={{0,4},{4,8},{8,12},{12,16},{16,20},{20,24},{24,28},{28,0},{1,5},{5... | collective-permute-start | bytes 122888 | tf_op jit(solution)/shard_map/ppermute | solution.py:363
  14.4 3.1 %collective-permute-start.18 = (f32[80,128]{1,0:T(8,128)S(1)}, f32[80,128]{1,0:T(8,128)S(1)}, u32[]{:S(2)}, u32[]{:S(2)}) collective-permute-start(f32[80,128]{1,0:T(8,128)S(1)} %get-tuple-element.39), channel_id=1, source_target_pairs={{4,0},{8,4},{12,8},{16,12},{20,16},{24,20},{28,24},{0,28},{5,1},{9... | collective-permute-start | bytes 122888 | tf_op jit(solution)/shard_map/ppermute | solution.py:364
  17.5 1.9 %collective-permute-done.17.from_west = f32[80,128]{1,0:T(8,128)S(1)} collective-permute-done((f32[80,128]{1,0:T(8,128)S(1)}, f32[80,128]{1,0:T(8,128)S(1)}, u32[]{:S(2)}, u32[]{:S(2)}) %collective-permute-start.17) | collective-permute-done | bytes 40992 | tf_op jit(solution)/shard_map/ppermute | solution.py:363
  19.4 0.0 collective-permute-done.18.from_east
  19.4 0.6 %krylov.1 = (f32[3,64,128]{2,1,0:T(8,128)S(1)}, f32[8,128]{1,0:T(8,128)S(1)}) custom-call(f32[6,80,128]{2,1,0:T(8,128)S(1)} %get-tuple-element.44.ext, f32[80,128]{1,0:T(8,128)S(1)} %collective-permute-done.17.from_west, f32[80,128]{1,0:T(8,128)S(1)} %collective-permute-done.18.from_east), custom_call_target="tpu_custom_call" | custom-call | flops 2048000 | bytes 491520 | tf_op jit(solution)/shard_map/krylov/pallas_call | solution.py:290
  19.9 0.7 %broadcast_in_dim.3 = f32[32,8,128]{2,1,0:T(8,128)} broadcast(f32[8,128]{1,0:T(8,128)S(1)} %get-tuple-element.45), dimensions={1,2} | broadcast | bytes 135168 | tf_op jit(solution)/shard_map/broadcast_in_dim | solution.py:385
  20.6 13.1 %all-to-all-start = ((f32[32,8,128]{2,1,0:T(8,128)}), f32[32,8,128]{2,1,0:T(8,128)S(1)}, u32[]{:S(2)}, u32[]{:S(2)}) async-start(f32[32,8,128]{2,1,0:T(8,128)} %broadcast_in_dim.3), calls=%async_computation | async-start | bytes 262144 | tf_op jit(solution)/shard_map/all_to_all | solution.py:385
  33.7 0.0 copy-done.7
  33.8 0.0 copy-done.5
  33.8 0.0 copy-done.1
  33.8 4.1 %levels_step.1 = (f32[10,64,128]{2,1,0:T(8,128)}, f32[10,64,128]{2,1,0:T(8,128)}, f32[10,64,128]{2,1,0:T(8,128)}, f32[10,64,128]{2,1,0:T(8,128)}) custom-call(f32[10]{0:T(128)S(1)} %copy-done.11, f32[10,64,128]{2,1,0:T(8,128)S(1)} %copy-done.1, f32[10,64,128]{2,1,0:T(8,128)S(1)} %copy-done.3, f32[10,64,128]{2,1,0:T(8,128)S(1)} %copy-done.5, ...), custom_call_target="tpu_custom_call" | custom-call | flops 9830400 | bytes 2621440 | tf_op jit(solution)/shard_map/levels_step/pallas_call | solution.py:290
  37.9 4.1 %all-to-all-done.shares = f32[32,8,128]{2,1,0:T(8,128)S(1)} async-done(((f32[32,8,128]{2,1,0:T(8,128)}), f32[32,8,128]{2,1,0:T(8,128)S(1)}, u32[]{:S(2)}, u32[]{:S(2)}) %all-to-all-start) | async-done | bytes 131104 | tf_op jit(solution)/shard_map/all_to_all | solution.py:385
  42.0 0.8 %surface.1 = f32[64,128]{1,0:T(8,128)} custom-call(f32[32,8,128]{2,1,0:T(8,128)S(1)} %all-to-all-done.shares, f32[3,64,128]{2,1,0:T(8,128)S(1)} %get-tuple-element.46.base), custom_call_target="tpu_custom_call" | custom-call | flops 49152 | bytes 131072 | tf_op jit(solution)/shard_map/surface/pallas_call | solution.py:290
  (14 shorter events, 0.0 us)
Async XLA Ops:
  0.6 0.7 %copy-start.12 = (s32[128]{0:T(128)S(1)}, s32[128]{0:T(128)}, u32[]{:S(2)}) copy-start(s32[128]{0:T(128)} %param.23) | copy-start | bytes 1540
  0.6 0.8 %copy-start.9 = (f32[64,128]{1,0:T(8,128)S(1)}, f32[64,128]{1,0:T(8,128)}, u32[]{:S(2)}) copy-start(f32[64,128]{1,0:T(8,128)} %weights.1) | copy-start | bytes 98308
  0.7 0.8 %copy-start.8 = (s32[64,128]{1,0:T(8,128)S(1)}, s32[64,128]{1,0:T(8,128)}, u32[]{:S(2)}) copy-start(s32[64,128]{1,0:T(8,128)} %water.3) | copy-start | bytes 98308
  1.4 0.7 %copy-start.11 = (f32[10]{0:T(128)S(1)}, f32[10]{0:T(128)}, u32[]{:S(2)}) copy-start(f32[10]{0:T(128)} %spans.3) | copy-start | bytes 124
  2.0 1.0 %copy-start = (f32[10,64,128]{2,1,0:T(8,128)S(1)}, f32[10,64,128]{2,1,0:T(8,128)}, u32[]{:S(2)}) copy-start(f32[10,64,128]{2,1,0:T(8,128)} %heat.3) | copy-start | bytes 983044
  3.0 1.0 %copy-start.2 = (f32[10,64,128]{2,1,0:T(8,128)S(1)}, f32[10,64,128]{2,1,0:T(8,128)}, u32[]{:S(2)}) copy-start(f32[10,64,128]{2,1,0:T(8,128)} %salt.3) | copy-start | bytes 983044
  4.0 1.0 %copy-start.4 = (f32[10,64,128]{2,1,0:T(8,128)S(1)}, f32[10,64,128]{2,1,0:T(8,128)}, u32[]{:S(2)}) copy-start(f32[10,64,128]{2,1,0:T(8,128)} %zonal.3) | copy-start | bytes 983044
  4.9 1.0 %copy-start.6 = (f32[10,64,128]{2,1,0:T(8,128)S(1)}, f32[10,64,128]{2,1,0:T(8,128)}, u32[]{:S(2)}) copy-start(f32[10,64,128]{2,1,0:T(8,128)} %merid.3) | copy-start | bytes 983044
  5.9 0.8 %copy-start.10 = (f32[64,128]{1,0:T(8,128)S(1)}, f32[64,128]{1,0:T(8,128)}, u32[]{:S(2)}) copy-start(f32[64,128]{1,0:T(8,128)} %anomaly.1) | copy-start | bytes 98308
  6.7 27.1 %copy-start.7 = (f32[10,64,128]{2,1,0:T(8,128)S(1)}, f32[10,64,128]{2,1,0:T(8,128)}, u32[]{:S(2)}) copy-start(f32[10,64,128]{2,1,0:T(8,128)} %merid.3) | copy-start | bytes 983044
  7.6 3.1 %collective-permute-start.16 = (f32[72,128]{1,0:T(8,128)S(1)}, f32[72,128]{1,0:T(8,128)S(1)}, u32[]{:S(2)}, u32[]{:S(2)}) collective-permute-start(f32[72,128]{1,0:T(8,128)S(1)} %get-tuple-element.31), channel_id=1, source_target_pairs={{0,1},{1,0},{2,3},{3,2},{4,5},{5,4},{6,7},{7,6},{8,9},{9,8},{10,11... | collective-permute-start | bytes 110600 | tf_op jit(solution)/shard_map/ppermute | solution.py:345
  8.1 2.5 %collective-permute-start.11 = (f32[72,128]{1,0:T(8,128)S(1)}, f32[72,128]{1,0:T(8,128)}, u32[]{:S(2)}, u32[]{:S(2)}) collective-permute-start(f32[72,128]{1,0:T(8,128)S(1)} %param.5), channel_id=1, source_target_pairs={{23,3},{19,7},{15,11},{11,15},{7,19},{3,23},{31,27},{27,31}} | collective-permute-start | bytes 110600 | tf_op jit(solution)/shard_map/cond/branch_5_fun/ppermute | solution.py:350
  9.4 1.3 %collective-permute-start.10 = (f32[72,128]{1,0:T(8,128)S(1)}, f32[72,128]{1,0:T(8,128)}, u32[]{:S(2)}, u32[]{:S(2)}) collective-permute-start(f32[72,128]{1,0:T(8,128)S(1)} %param.5), channel_id=1, source_target_pairs={{1,2},{2,1},{5,6},{6,5},{9,10},{10,9},{13,14},{14,13},{17,18},{18,... | collective-permute-start | bytes 110600 | tf_op jit(solution)/shard_map/cond/branch_5_fun/ppermute | solution.py:350
  10.7 23.1 %copy-start.5 = (f32[10,64,128]{2,1,0:T(8,128)S(1)}, f32[10,64,128]{2,1,0:T(8,128)}, u32[]{:S(2)}) copy-start(f32[10,64,128]{2,1,0:T(8,128)} %zonal.3) | copy-start | bytes 983044
  11.7 7.6 %collective-permute-start.17 = (f32[80,128]{1,0:T(8,128)S(1)}, f32[80,128]{1,0:T(8,128)S(1)}, u32[]{:S(2)}, u32[]{:S(2)}) collective-permute-start(f32[80,128]{1,0:T(8,128)S(1)} %get-tuple-element.38), channel_id=1, source_target_pairs={{0,4},{4,8},{8,12},{12,16},{16,20},{20,24},{24,28},{28,0},{1,5},{5... | collective-permute-start | bytes 122888 | tf_op jit(solution)/shard_map/ppermute | solution.py:363
  14.4 5.0 %collective-permute-start.18 = (f32[80,128]{1,0:T(8,128)S(1)}, f32[80,128]{1,0:T(8,128)S(1)}, u32[]{:S(2)}, u32[]{:S(2)}) collective-permute-start(f32[80,128]{1,0:T(8,128)S(1)} %get-tuple-element.39), channel_id=1, source_target_pairs={{4,0},{8,4},{12,8},{16,12},{20,16},{24,20},{28,24},{0,28},{5,1},{9... | collective-permute-start | bytes 122888 | tf_op jit(solution)/shard_map/ppermute | solution.py:364
  19.4 14.4 %copy-start.1 = (f32[10,64,128]{2,1,0:T(8,128)S(1)}, f32[10,64,128]{2,1,0:T(8,128)}, u32[]{:S(2)}) copy-start(f32[10,64,128]{2,1,0:T(8,128)} %heat.3) | copy-start | bytes 983044
  19.4 14.4 %copy-start.3 = (f32[10,64,128]{2,1,0:T(8,128)S(1)}, f32[10,64,128]{2,1,0:T(8,128)}, u32[]{:S(2)}) copy-start(f32[10,64,128]{2,1,0:T(8,128)} %salt.3) | copy-start | bytes 983044
  20.6 21.4 %all-to-all-start = ((f32[32,8,128]{2,1,0:T(8,128)}), f32[32,8,128]{2,1,0:T(8,128)S(1)}, u32[]{:S(2)}, u32[]{:S(2)}) async-start(f32[32,8,128]{2,1,0:T(8,128)} %broadcast_in_dim.3), calls=%async_computation | async-start | bytes 262144 | tf_op jit(solution)/shard_map/all_to_all | solution.py:385
where the time goes:
time: 42.2 us; the launch traced here: 42.8 us
  starting transfers between devices  21.9 us (52%)
  Pallas kernels  7.48 us (18%)
  local copies, waits for them, and re-layouts  6.53 us (15%)
  waiting for transfers between devices  6.01 us (14%)
  between operations  0.81 us (2%)
    all_to_all x1, starting transfers between devices, body(): lax.all_to_all(jnp.broadcast_to(moments, (count,) + moments.shape), axes,...  13.1 us
    pallas_call x5, Pallas kernels, run(): pl.pallas_call(kernel, out_shape=[jax.ShapeDtypeStruct(shape, jnp.float32...  7.48 us
    unnamed x26, local copies, waits for them, and re-layouts  5.87 us
    all_to_all x1, waiting for transfers between devices, body(): lax.all_to_all(jnp.broadcast_to(moments, (count,) + moments.shape), axes,...  4.08 us
    ppermute x1, starting transfers between devices, body(): lax.ppermute(to_west, 'lon', [((i + 1) % lons, i) for i in range(lons)])  3.1 us
    ppermute x1, starting transfers between devices, body(): lax.ppermute(to_east, 'lon', [(i, (i + 1) % lons) for i in range(lons)])  2.61 us
    ppermute x1, waiting for transfers between devices, body(): lax.ppermute(to_east, 'lon', [(i, (i + 1) % lons) for i in range(lons)])  1.92 us
    ppermute x1, starting transfers between devices, facing(): lax.ppermute(packet, axes, far)  1.26 us
  transfers between devices with their start and end apart: 6, of which 2 were waited for; matrix products, arithmetic and copies ran while one was open for 0% of the time, Pallas kernels for 10%

commit v1 on v0

--- a/solution.py
+++ b/solution.py
@@ -13,6 +13,7 @@
 DEEP = 5
 FIELDS = 6
 VMEM_LIMIT = 32 * 1024 * 1024
+LOAD_FLOPS = 10**10
 
 
 def density(heat, salt):
@@ -27,7 +28,14 @@
     return -(-(4 * levels + FIELDS * DEEP) // 8) * 8
 
 
-def pack_kernel(meta, spans, heat, salt, zonal, merid, water, weights, anomaly, fields, first, second, columns):
+def place_kernel(meta, placed):
+    for i in range(4):
+        placed[i] = meta[i]
+
+
+def pack_kernel(
+    meta, spans, facing_of, heat, salt, zonal, merid, water, weights, anomaly, sums, first, second, columns
+):
     levels, rows, cols = heat.shape
     span = [spans[k] for k in range(levels)]
     below = [None] * levels
@@ -35,48 +43,49 @@
     for k in reversed(range(levels)):
         below[k] = span[k] * (0.5 * span[k] + total)
         total = total + span[k]
+    odd = meta[0]
+    packets = ((first, odd == 0), (second, odd == 1))
+    near_row = [[jnp.where(at_top, rows - 1 - j, j) for j in range(DEEP)] for _, at_top in packets]
+    group = iota((rows, cols), 1) // 4
     press = jnp.zeros((rows, cols), jnp.float32)
     east = jnp.zeros((rows, cols), jnp.float32)
     north = jnp.zeros((rows, cols), jnp.float32)
+    edge = jnp.zeros((rows, cols), jnp.float32)
     for k in range(levels):
         press = press + below[k] * density(heat[k], salt[k])
         east = east + span[k] * zonal[k]
         north = north + span[k] * merid[k]
-    fields[0] = press
-    fields[1] = east
-    fields[2] = north
-    fields[3] = water[...].astype(jnp.float32)
-    fields[4] = weights[...]
-    fields[5] = anomaly[...]
-    odd = meta[0]
-    for packet, at_top in ((first, odd == 0), (second, odd == 1)):
+        for q, source in ((k, heat), (levels + k, salt)):
+            edge = jnp.where(group == q, pltpu.roll(source[k], (4 * q + 2) % cols, 1), edge)
+            for (packet, _), near in zip(packets, near_row):
+                for j in range(2):
+                    at = q + j * levels if q < levels else q + (j + 1) * levels
+                    packet[at : at + 1, :] = source[k, pl.ds(near[j], 1), :]
+    columns[...] = edge
+    sums[0] = press
+    sums[1] = east
+    sums[2] = north
+    fields = (sums.at[0], sums.at[1], sums.at[2], water, weights, anomaly)
+    for (packet, _), near in zip(packets, near_row):
         for j in range(DEEP):
-            row = jnp.where(at_top, rows - 1 - j, j)
-            if j < 2:
-                for place, source in ((0, heat), (2 * levels, salt)):
-                    for k in range(levels):
-                        at = place + j * levels + k
-                        packet[at : at + 1, :] = source[k, pl.ds(row, 1), :]
-            for f in range(FIELDS):
+            for f, field in enumerate(fields):
                 at = 4 * levels + FIELDS * j + f
-                packet[at : at + 1, :] = fields[f, pl.ds(row, 1), :]
+                packet[at : at + 1, :] = field[pl.ds(near[j], 1), :].astype(jnp.float32)
         used = 4 * levels + FIELDS * DEEP
         if used < packet.shape[0]:
             packet[used:, :] = jnp.zeros((packet.shape[0] - used, cols), jnp.float32)
-    group = iota((rows, cols), 1) // 4
-    edge = jnp.zeros((rows, cols), jnp.float32)
-    for q in range(2 * levels):
-        layer = heat[q] if q < levels else salt[q - levels]
-        edge = jnp.where(group == q, pltpu.roll(layer, (4 * q + 2) % cols, 1), edge)
-    columns[...] = edge
-
-
-def turn_kernel(meta, fields, first, second, third, columns, ext, north_rows, south_rows, to_east, to_west):
+
+
+def turn_kernel(
+    meta, facing_of, sums, water, weights, anomaly, first, second, third, columns,
+    ext, north_rows, south_rows, to_near, to_far,
+):
     high, cols = first.shape
-    rows = fields.shape[1]
+    rows = sums.shape[1]
     tall = ext.shape[1]
     levels = north_rows.shape[0] // 4
-    odd, offset, top = meta[0], meta[1], meta[2]
+    odd, top, lon_odd, lon = meta[0], meta[1], meta[2], meta[3]
+    offset = lax.rem(facing_of[0] + 1 + cols * lon, cols)
     lane = iota((high, cols), 1)
     place = iota((high, cols), 0) - 4 * levels
     kind = lax.rem(jnp.maximum(place, 0), FIELDS)
@@ -93,8 +102,9 @@
     south = jnp.where(odd == 1, from_first, from_second)
     north_rows[...] = north[: 4 * levels]
     south_rows[...] = south[: 4 * levels]
+    fields = (sums.at[0], sums.at[1], sums.at[2], water, weights, anomaly)
     for f in range(FIELDS):
-        ext[f, :rows, :] = fields[f]
+        ext[f, :rows, :] = fields[f][...].astype(jnp.float32)
         ext[f, rows + DEEP : tall - DEEP, :] = jnp.zeros((tall - rows - 2 * DEEP, cols), jnp.float32)
         for j in range(DEEP):
             at = 4 * levels + FIELDS * j + f
@@ -109,16 +119,16 @@
         layer = ext[f]
         east = jnp.where(here, pltpu.roll(layer, (used + DEEP * f + DEEP) % cols, 1), east)
         west = jnp.where(here, pltpu.roll(layer, used + DEEP * f, 1), west)
-    to_east[...] = east
-    to_west[...] = west
-
-
-def krylov_kernel(used, ext, from_west, from_east, base, moments):
+    to_near[...] = jnp.where(lon_odd == 1, west, east)
+    to_far[...] = jnp.where(lon_odd == 1, east, west)
+
+
+def krylov_kernel(used, meta, ext, from_near, from_far, base, moments):
     tall, cols = ext.shape[1], ext.shape[2]
     rows = base.shape[1]
     lane = iota((tall, cols), 1)
-    west = from_west[...]
-    east = from_east[...]
+    west = jnp.where(meta[2] == 1, from_near[...], from_far[...])
+    east = jnp.where(meta[2] == 1, from_far[...], from_near[...])
     first = lane == 0
     last = lane == cols - 1
 
@@ -186,20 +196,26 @@
         middle * two * two,
         last_sum * two,
     )
+    which = iota((8, cols), 0)
+    sums = jnp.zeros((8, cols), jnp.float32)
     for k, product in enumerate(products):
-        moments[k : k + 1, :] = jnp.sum(product, axis=0, keepdims=True)
-    moments[len(products) :, :] = jnp.zeros((moments.shape[0] - len(products), cols), jnp.float32)
+        sums = jnp.where(which == k, jnp.sum(product, axis=0, keepdims=True), sums)
+    sums = jnp.sum(sums, axis=1, keepdims=True)
+    sums = jnp.sum(jnp.where(which == iota((8, cols), 1), sums, 0.0), axis=0, keepdims=True)
+    moments[...] = jnp.broadcast_to(sums, moments.shape)
 
 
 def step_kernel(
-    spans, heat, salt, zonal, merid, water, north_rows, south_rows, from_west, from_east,
-    new_heat, new_salt, new_zonal, new_merid,
+    meta, spans, heat, salt, zonal, merid, water, north_rows, south_rows, from_near, from_far,
+    heat_out, salt_out, zonal_out, merid_out,
+    new_heat, new_salt, new_zonal, new_merid, sems,
 ):
     levels, rows, cols = heat.shape
     wet = water[...].astype(jnp.float32)
     lane = iota((rows, cols), 1)
     row = iota((rows, cols), 0)
-    sides = jnp.where((lane & 3) < 2, from_west[:rows, :], from_east[:rows, :])
+    near = ((lane & 3) < 2) == (meta[2] == 1)
+    sides = jnp.where(near, from_near[:rows, :], from_far[:rows, :])
 
     def around(cells, q, k, place):
         side = pltpu.roll(sides, (2 * cols - (4 * q + 2)) % cols, 1)
@@ -228,6 +244,9 @@
         tendency = (-TIME_STEP / 12.0) * (speed_x * grad_east + speed_y * grad_north) + MIXING * laplace
         return cells + wet * tendency
 
+    stores = ((new_heat, heat_out), (new_salt, salt_out), (new_zonal, zonal_out), (new_merid, merid_out))
+    size = levels // sems.shape[1]
+    copies = []
     half = 0.5 * TIME_STEP
     above_x = jnp.zeros((rows, cols), jnp.float32)
     above_y = jnp.zeros((rows, cols), jnp.float32)
@@ -243,11 +262,19 @@
         new_merid[k] = wet * (v - half * (above_y + 0.5 * layer_y))
         above_x = above_x + layer_x
         above_y = above_y + layer_y
+        if (k + 1) % size == 0:
+            piece = pl.ds(k + 1 - size, size)
+            for i, (near_ref, far_ref) in enumerate(stores):
+                copies.append(pltpu.make_async_copy(near_ref.at[piece], far_ref.at[piece], sems.at[i, k // size]))
+                copies[-1].start()
+    for copy in copies:
+        copy.wait()
 
 
 def surface_kernel(shares, base, surface):
-    sums = jnp.sum(jnp.sum(shares[...], axis=0), axis=1, keepdims=True)
-    nu = [sums[k : k + 1, :] for k in range(6)]
+    sums = jnp.sum(shares[...], axis=0, keepdims=True)
+    lane = iota(sums.shape, 1)
+    nu = [jnp.sum(jnp.where(lane == k, sums, 0.0), axis=1, keepdims=True) for k in range(6)]
 
     def ratio(a, b):
         good = b > 0.0
@@ -283,21 +310,18 @@
     surface[...] = x[0] * base[0] + x[1] * base[1] + x[2] * base[2]
 
 
-def call(kernel, outs, smem, flops, moved, **named):
-    specs = lambda count: [pl.BlockSpec(memory_space=pltpu.VMEM)] * count
-
-    def run(*args):
-        return pl.pallas_call(
-            kernel,
-            out_shape=[jax.ShapeDtypeStruct(shape, jnp.float32) for shape in outs],
-            in_specs=[pl.BlockSpec(memory_space=pltpu.SMEM)] * smem + specs(len(args) - smem),
-            out_specs=specs(len(outs)),
-            cost_estimate=pl.CostEstimate(flops=flops, bytes_accessed=moved, transcendentals=0),
-            compiler_params=pltpu.CompilerParams(vmem_limit_bytes=VMEM_LIMIT),
-            **named,
-        )(*args)
-
-    return run
+def call(kernel, outs, ins, flops, moved, name, out_space=pltpu.VMEM, scratch=(), types=jnp.float32):
+    space = {"s": pltpu.SMEM, "v": pltpu.VMEM, "h": pltpu.HBM}
+    return pl.pallas_call(
+        kernel,
+        out_shape=[jax.ShapeDtypeStruct(shape, types) for shape in outs],
+        in_specs=[pl.BlockSpec(memory_space=space[letter]) for letter in ins],
+        out_specs=[pl.BlockSpec(memory_space=out_space)] * len(outs),
+        scratch_shapes=list(scratch),
+        cost_estimate=pl.CostEstimate(flops=flops, bytes_accessed=moved, transcendentals=0),
+        compiler_params=pltpu.CompilerParams(vmem_limit_bytes=VMEM_LIMIT),
+        name=name,
+    )
 
 
 def body(
@@ -321,18 +345,25 @@
 
     hinge = lax.rem(opposite_counterpart[0] + 1 + cols * lon, width)
     block = hinge // cols
-    meta = jnp.stack([lax.rem(lat, 2), lax.rem(hinge, cols), (lat == lats - 1).astype(jnp.int32)]).astype(jnp.int32)
+    meta = jnp.stack([lax.rem(lat, 2), (lat == lats - 1).astype(jnp.int32), lax.rem(lon, 2), lon]).astype(jnp.int32)
+
+    (meta,) = call(place_kernel, [(4,)], "s", LOAD_FLOPS, 16, "place", out_space=pltpu.SMEM, types=jnp.int32)(meta)
 
     state = (warmth_deviation, saltiness_deviation, easterly_speed, poleward_speed)
     cells = levels * rows * cols
-    fields, first, second, columns = call(
+    chunks = 5 if levels % 5 == 0 else 1
+    level_buffers = [pltpu.VMEM((levels, rows, cols), jnp.float32)] * 4
+    sums, first, second, columns = call(
         pack_kernel,
-        [(FIELDS, rows, cols), (high, cols), (high, cols), (rows, cols)],
-        2,
+        [(3, rows, cols), (high, cols), (high, cols), (rows, cols)],
+        "sssvvvvvvv",
         12 * cells,
         16 * cells,
-        name="level_sums",
-    )(meta, stratum_spans, *state, water_indicator, elevation_weights, elevation_anomaly)
+        "level_sums",
+    )(
+        meta, stratum_spans, opposite_counterpart, *state,
+        water_indicator, elevation_weights, elevation_anomaly,
+    )
 
     pairs_first = [(flat(i, j), flat(i, j ^ 1)) for i in range(lons) for j in range(lats)]
     pairs_inner = [
@@ -351,41 +382,44 @@
 
     got_second, got_third = lax.switch(block, [functools.partial(facing, s) for s in range(lons)], second)
 
-    ext, north_rows, south_rows, to_east, to_west = call(
+    ext, north_rows, south_rows, to_near, to_far = call(
         turn_kernel,
         [(FIELDS, tall, cols), (4 * levels, cols), (4 * levels, cols), (tall, cols), (tall, cols)],
-        1,
+        "ssvvvvvvvv",
         FIELDS * tall * cols,
         4 * 4 * FIELDS * tall * cols,
-        name="row_halos",
-    )(meta, fields, got_first, got_second, got_third, columns)
-
-    from_west = lax.ppermute(to_east, "lon", [(i, (i + 1) % lons) for i in range(lons)])
-    from_east = lax.ppermute(to_west, "lon", [((i + 1) % lons, i) for i in range(lons)])
-
+        "row_halos",
+    )(
+        meta, opposite_counterpart, sums, water_indicator, elevation_weights, elevation_anomaly,
+        got_first, got_second, got_third, columns,
+    )
+
+    from_near = lax.ppermute(to_near, "lon", [(i, i ^ 1) for i in range(lons)])
+    from_far = lax.ppermute(to_far, "lon", [(i, (i + 1 if i % 2 else i - 1) % lons) for i in range(lons)])
+
+    count = lons * lats
     base, moments = call(
         functools.partial(krylov_kernel, 8 * levels),
-        [(3, rows, cols), (8, cols)],
-        0,
+        [(3, rows, cols), (count, cols)],
+        "svvv",
         200 * tall * cols,
         4 * 12 * tall * cols,
-        name="krylov",
-    )(ext, from_west, from_east)
+        "krylov",
+    )(meta, ext, from_near, from_far)
 
     new_heat, new_salt, new_zonal, new_merid = call(
         step_kernel,
         [(levels, rows, cols)] * 4,
-        1,
+        "ssvvvvvvvvv",
         120 * cells,
         32 * cells,
-        name="levels_step",
-    )(stratum_spans, *state, water_indicator, north_rows, south_rows, from_west, from_east)
-
-    count = lons * lats
-    shares = lax.all_to_all(jnp.broadcast_to(moments, (count,) + moments.shape), axes, 0, 0)
-    (surface,) = call(
-        surface_kernel, [(rows, cols)], 0, 6 * rows * cols, 16 * rows * cols, name="surface"
-    )(shares, base)
+        "levels_step",
+        out_space=pltpu.HBM,
+        scratch=[*level_buffers, pltpu.SemaphoreType.DMA((4, chunks))],
+    )(meta, stratum_spans, *state, water_indicator, north_rows, south_rows, from_near, from_far)
+
+    shares = lax.all_to_all(moments, axes, 0, 0, tiled=True)
+    (surface,) = call(surface_kernel, [(rows, cols)], "vv", 6 * rows * cols, 16 * rows * cols, "surface")(shares, base)
     return (new_heat, new_salt, new_zonal, new_merid, surface)
 
 

time: 42.2 us -> 35.7 us (0.85); the launches traced: 42.8 us -> 35.2 us
  local copies, waits for them, and re-layouts: 6.53 us -> 0.07 us
  starting transfers between devices: 21.9 us -> 18.5 us
  Pallas kernels: 7.48 us -> 9.58 us
    unnamed x26 -> x18, local copies, waits for them, and re-layouts: 5.87 us -> 0.07 us
    all_to_all x1, starting transfers between devices: 13.1 us -> 9.26 us  [body(): shares = lax.all_to_all(moments, axes, 0, 0, tiled=True)]
    pallas_call x5 -> x6, Pallas kernels: 7.48 us -> 9.58 us  [the longest x1 4 us: body(): call(step_kernel, [(levels, rows, cols)] * 4, 'ssvvvvvvvvv', 120 * cells,...]
    ppermute x2, waiting for transfers between devices: 1.92 us -> 3.13 us  [the longest x1 3.12 us: body(): lax.ppermute(to_far, 'lon', [(i, (i + 1 if i % 2 else i - 1) % lons) for...]
    all_to_all x1, waiting for transfers between devices: 4.08 us -> 3.06 us  [body(): shares = lax.all_to_all(moments, axes, 0, 0, tiled=True)]
    broadcast_in_dim x1 -> x0, local copies, waits for them, and re-layouts: 0.66 us -> none  [body(): jnp.broadcast_to(moments, (count,) + moments.shape)]
  transfers between devices with their start and end apart: 6 -> 6, of which waited for: 2 -> 2; matrix products, arithmetic and copies ran while one was open for 0% -> 0% of each run, Pallas kernels for 10% -> 11%
where the time goes in v1:
time: 35.7 us; the launch traced here: 35.2 us
  starting transfers between devices  18.5 us (52%)
  Pallas kernels  9.58 us (27%)
  waiting for transfers between devices  6.2 us (17%)
  between operations  0.85 us (2%)
    all_to_all x1, starting transfers between devices, body(): shares = lax.all_to_all(moments, axes, 0, 0, tiled=True)  9.26 us
    pallas_call x1, Pallas kernels, body(): call(step_kernel, [(levels, rows, cols)] * 4, 'ssvvvvvvvvv', 120 * cells,...  4 us
    ppermute x1, starting transfers between devices, body(): lax.ppermute(to_far, 'lon', [(i, (i + 1 if i % 2 else i - 1) % lons) for...  3.57 us
    ppermute x1, waiting for transfers between devices, body(): lax.ppermute(to_far, 'lon', [(i, (i + 1 if i % 2 else i - 1) % lons) for...  3.12 us
    all_to_all x1, waiting for transfers between devices, body(): shares = lax.all_to_all(moments, axes, 0, 0, tiled=True)  3.06 us
    ppermute x1, starting transfers between devices, body(): from_near = lax.ppermute(to_near, 'lon', [(i, i ^ 1) for i in range(lons)])  2.56 us
    pallas_call x1, Pallas kernels, body(): call(functools.partial(krylov_kernel, 8 * levels), [(3, rows, cols), (cou...  1.76 us
    ppermute x1, starting transfers between devices, facing(): lax.ppermute(packet, axes, far)  1.27 us
  transfers between devices with their start and end apart: 6, of which 2 were waited for; matrix products, arithmetic and copies ran while one was open for 0% of the time, Pallas kernels for 11%

profile of v1, /device:TPU:0, one launch (start us, length us, event | category | flops | bytes accessed | tf_op | source)
XLA Modules:
  0.0 35.2 jit_solution(1165319766156924174)
XLA Ops:
  0.6 0.1 pad_add_fusion.meta
  0.7 0.0 copy-start.4
  0.7 0.0 copy-start.5
  0.8 0.0 copy-start.6
  0.8 0.0 copy-start.7
  0.8 0.0 copy-start.8
  0.8 1.1 %place.1.meta = s32[4]{0:T(128)S(1)} custom-call(s32[4]{0:T(128)S(1)} %pad_add_fusion.meta), custom_call_target="tpu_custom_call" | custom-call | flops 10000000000 | bytes 16 | tf_op jit(solution)/shard_map/place/pallas_call | solution.py:350
  1.9 0.0 copy-done
  1.9 0.0 copy-done.1
  2.0 0.0 copy-done.2
  2.0 0.0 copy-done.3
  2.0 0.0 copy-done.4
  2.0 0.0 copy-done.5
  2.0 0.0 copy-done.6
  2.0 0.9 %level_sums.1 = (f32[3,64,128]{2,1,0:T(8,128)S(1)}, f32[72,128]{1,0:T(8,128)S(1)}, f32[72,128]{1,0:T(8,128)S(1)}, f32[64,128]{1,0:T(8,128)S(1)}) custom-call(s32[4]{0:T(128)S(1)} %place.1.meta, f32[10]{0:T(128)S(1)} %copy-done.7, s32[128]{0:T(128)S(1)} %copy-done.8, f32[10,64,128]{2,1,0:T(8,128)S(1)} %copy-done, f32[10,64,128]{2,1,0:T(8,128)S(1)} %copy-done.1, ...), custom_call_target="tpu_custom_call" | custom-call | flops 983040 | bytes 1310720 | tf_op jit(solution)/shard_map/level_sums/pallas_call | solution.py:356
  2.9 0.5 %collective-permute-start.16 = (f32[72,128]{1,0:T(8,128)S(1)}, f32[72,128]{1,0:T(8,128)S(1)}, u32[]{:S(2)}, u32[]{:S(2)}) collective-permute-start(f32[72,128]{1,0:T(8,128)S(1)} %get-tuple-element.31), channel_id=1, source_target_pairs={{0,1},{1,0},{2,3},{3,2},{4,5},{5,4},{6,7},{7,6},{8,9},{9,8},{10,11... | collective-permute-start | bytes 110600 | tf_op jit(solution)/shard_map/ppermute | solution.py:376
  3.5 2.6 %conditional.1 = (f32[72,128]{1,0:T(8,128)}, f32[72,128]{1,0:T(8,128)}) conditional(s32[]{:T(128)} %clamp.3, f32[72,128]{1,0:T(8,128)S(1)} %get-tuple-element.32, f32[72,128]{1,0:T(8,128)S(1)} %get-tuple-element.32, f32[72,128]{1,0:T(8,128)S(1)} %get-tuple-element.32, f32[72,128]{1,0:T(8,128)S(1)} %get-tuple-element.32, ...), branch_computations={%region_0.1_spmd, %region_1.2_spmd, %region_2.3_spmd, %region_3.4_... | conditional | bytes 295008 | solution.py:383
  3.5 1.3 %collective-permute-start.13 = (f32[72,128]{1,0:T(8,128)S(1)}, f32[72,128]{1,0:T(8,128)}, u32[]{:S(2)}, u32[]{:S(2)}) collective-permute-start(f32[72,128]{1,0:T(8,128)S(1)} %param.6), channel_id=1, source_target_pairs={{27,3},{23,7},{19,11},{15,15},{11,19},{7,23},{3,27},{31,31}} | collective-permute-start | bytes 110600 | tf_op jit(solution)/shard_map/cond/branch_6_fun/ppermute | solution.py:381
  4.8 1.3 %collective-permute-start.12 = (f32[72,128]{1,0:T(8,128)S(1)}, f32[72,128]{1,0:T(8,128)}, u32[]{:S(2)}, u32[]{:S(2)}) collective-permute-start(f32[72,128]{1,0:T(8,128)S(1)} %param.6), channel_id=1, source_target_pairs={{1,2},{2,1},{5,6},{6,5},{9,10},{10,9},{13,14},{14,13},{17,18},{18,... | collective-permute-start | bytes 110600 | tf_op jit(solution)/shard_map/cond/branch_6_fun/ppermute | solution.py:381
  6.1 0.0 collective-permute-done.13
  6.1 0.0 collective-permute-done.12
  6.1 0.0 collective-permute-done.16.first
  6.1 1.0 %row_halos.1 = (f32[6,80,128]{2,1,0:T(8,128)S(1)}, f32[40,128]{1,0:T(8,128)S(1)}, f32[40,128]{1,0:T(8,128)S(1)}, f32[80,128]{1,0:T(8,128)S(1)}, f32[80,128]{1,0:T(8,128)S(1)}) custom-call(s32[4]{0:T(128)S(1)} %place.1.meta, s32[128]{0:T(128)S(1)} %copy-done.8, f32[3,64,128]{2,1,0:T(8,128)S(1)} %get-tuple-element.30.sums, s32[64,128]{1,0:T(8,128)S(1)} %copy-done.4, ...), custom_call_target="tpu_custom_call" | custom-call | flops 61440 | bytes 983040 | tf_op jit(solution)/shard_map/row_halos/pallas_call | solution.py:385
  7.1 2.6 %collective-permute-start.17 = (f32[80,128]{1,0:T(8,128)S(1)}, f32[80,128]{1,0:T(8,128)S(1)}, u32[]{:S(2)}, u32[]{:S(2)}) collective-permute-start(f32[80,128]{1,0:T(8,128)S(1)} %get-tuple-element.38), channel_id=1, source_target_pairs={{0,4},{4,0},{8,12},{12,8},{16,20},{20,16},{24,28},{28,24},{1,5},{5... | collective-permute-start | bytes 122888 | tf_op jit(solution)/shard_map/ppermute | solution.py:397
  9.7 3.6 %collective-permute-start.18 = (f32[80,128]{1,0:T(8,128)S(1)}, f32[80,128]{1,0:T(8,128)S(1)}, u32[]{:S(2)}, u32[]{:S(2)}) collective-permute-start(f32[80,128]{1,0:T(8,128)S(1)} %get-tuple-element.39), channel_id=1, source_target_pairs={{0,28},{4,8},{8,4},{12,16},{16,12},{20,24},{24,20},{28,0},{1,29},{... | collective-permute-start | bytes 122888 | tf_op jit(solution)/shard_map/ppermute | solution.py:398
  13.2 0.0 collective-permute-done.17.from_near
  13.2 3.1 %collective-permute-done.18.from_far = f32[80,128]{1,0:T(8,128)S(1)} collective-permute-done((f32[80,128]{1,0:T(8,128)S(1)}, f32[80,128]{1,0:T(8,128)S(1)}, u32[]{:S(2)}, u32[]{:S(2)}) %collective-permute-start.18) | collective-permute-done | bytes 40992 | tf_op jit(solution)/shard_map/ppermute | solution.py:398
  16.4 1.8 %krylov.1 = (f32[3,64,128]{2,1,0:T(8,128)S(1)}, f32[32,128]{1,0:T(8,128)}) custom-call(s32[4]{0:T(128)S(1)} %place.1.meta, f32[6,80,128]{2,1,0:T(8,128)S(1)} %get-tuple-element.44.ext, f32[80,128]{1,0:T(8,128)S(1)} %collective-permute-done.17.from_near, f32[80,128]{1,0:T(8,128)S(1)} %collective-permute-done.18.from_far), custom_call_target="tpu_custom_call" | custom-call | flops 2048000 | bytes 491520 | tf_op jit(solution)/shard_map/krylov/pallas_call | solution.py:401
  18.1 9.3 %all-to-all-start = ((f32[32,1,128]{2,1,0:T(1,128)}), f32[32,1,128]{2,1,0:T(1,128)S(1)}, u32[]{:S(2)}, u32[]{:S(2)}) async-start(f32[32,1,128]{2,1,0:T(1,128)} %bitcast.6), calls=%async_computation | async-start | bytes 32768 | tf_op jit(solution)/shard_map/all_to_all | solution.py:421
  27.4 4.0 %levels_step.1 = (f32[10,64,128]{2,1,0:T(8,128)}, f32[10,64,128]{2,1,0:T(8,128)}, f32[10,64,128]{2,1,0:T(8,128)}, f32[10,64,128]{2,1,0:T(8,128)}) custom-call(s32[4]{0:T(128)S(1)} %place.1.meta, f32[10]{0:T(128)S(1)} %copy-done.7, f32[10,64,128]{2,1,0:T(8,128)S(1)} %copy-done, f32[10,64,128]{2,1,0:T(8,128)S(1)} %copy-done.1, f32[10,64,128]{2,1,0:T(8,128)S(1)} %copy-done.2, ...), custom_call_target="tpu_custom_call" | custom-call | flops 9830400 | bytes 2621440 | tf_op jit(solution)/shard_map/levels_step/pallas_call | solution.py:410
  31.4 3.1 %all-to-all-done = f32[32,1,128]{2,1,0:T(1,128)S(1)} async-done(((f32[32,1,128]{2,1,0:T(1,128)}), f32[32,1,128]{2,1,0:T(1,128)S(1)}, u32[]{:S(2)}, u32[]{:S(2)}) %all-to-all-start) | async-done | bytes 16416 | tf_op jit(solution)/shard_map/all_to_all | solution.py:421
  34.5 0.8 %surface.1 = f32[64,128]{1,0:T(8,128)} custom-call(f32[32,128]{1,0:T(8,128)S(1)} %bitcast.10, f32[3,64,128]{2,1,0:T(8,128)S(1)} %get-tuple-element.46.base), custom_call_target="tpu_custom_call" | custom-call | flops 49152 | bytes 131072 | tf_op jit(solution)/shard_map/surface/pallas_call | solution.py:422
  (6 shorter events, 0.0 us)
Async XLA Ops:
  0.7 1.2 %copy-start = (f32[10,64,128]{2,1,0:T(8,128)S(1)}, f32[10,64,128]{2,1,0:T(8,128)}, u32[]{:S(2)}) copy-start(f32[10,64,128]{2,1,0:T(8,128)} %heat.3) | copy-start | bytes 983044
  0.7 1.2 %copy-start.1 = (f32[10,64,128]{2,1,0:T(8,128)S(1)}, f32[10,64,128]{2,1,0:T(8,128)}, u32[]{:S(2)}) copy-start(f32[10,64,128]{2,1,0:T(8,128)} %salt.3) | copy-start | bytes 983044
  0.7 1.2 %copy-start.2 = (f32[10,64,128]{2,1,0:T(8,128)S(1)}, f32[10,64,128]{2,1,0:T(8,128)}, u32[]{:S(2)}) copy-start(f32[10,64,128]{2,1,0:T(8,128)} %zonal.3) | copy-start | bytes 983044
  0.7 1.3 %copy-start.3 = (f32[10,64,128]{2,1,0:T(8,128)S(1)}, f32[10,64,128]{2,1,0:T(8,128)}, u32[]{:S(2)}) copy-start(f32[10,64,128]{2,1,0:T(8,128)} %merid.3) | copy-start | bytes 983044
  0.7 1.3 %copy-start.4 = (s32[64,128]{1,0:T(8,128)S(1)}, s32[64,128]{1,0:T(8,128)}, u32[]{:S(2)}) copy-start(s32[64,128]{1,0:T(8,128)} %water.5) | copy-start | bytes 98308
  0.7 1.3 %copy-start.5 = (f32[64,128]{1,0:T(8,128)S(1)}, f32[64,128]{1,0:T(8,128)}, u32[]{:S(2)}) copy-start(f32[64,128]{1,0:T(8,128)} %weights.3) | copy-start | bytes 98308
  0.8 1.2 %copy-start.6 = (f32[64,128]{1,0:T(8,128)S(1)}, f32[64,128]{1,0:T(8,128)}, u32[]{:S(2)}) copy-start(f32[64,128]{1,0:T(8,128)} %anomaly.3) | copy-start | bytes 98308
  0.8 1.2 %copy-start.7 = (f32[10]{0:T(128)S(1)}, f32[10]{0:T(128)}, u32[]{:S(2)}) copy-start(f32[10]{0:T(128)} %spans.3) | copy-start | bytes 124
  0.8 1.2 %copy-start.8 = (s32[128]{0:T(128)S(1)}, s32[128]{0:T(128)}, u32[]{:S(2)}) copy-start(s32[128]{0:T(128)} %facing_of.3) | copy-start | bytes 1540
  2.9 3.2 %collective-permute-start.16 = (f32[72,128]{1,0:T(8,128)S(1)}, f32[72,128]{1,0:T(8,128)S(1)}, u32[]{:S(2)}, u32[]{:S(2)}) collective-permute-start(f32[72,128]{1,0:T(8,128)S(1)} %get-tuple-element.31), channel_id=1, source_target_pairs={{0,1},{1,0},{2,3},{3,2},{4,5},{5,4},{6,7},{7,6},{8,9},{9,8},{10,11... | collective-permute-start | bytes 110600 | tf_op jit(solution)/shard_map/ppermute | solution.py:376
  3.5 2.5 %collective-permute-start.13 = (f32[72,128]{1,0:T(8,128)S(1)}, f32[72,128]{1,0:T(8,128)}, u32[]{:S(2)}, u32[]{:S(2)}) collective-permute-start(f32[72,128]{1,0:T(8,128)S(1)} %param.6), channel_id=1, source_target_pairs={{27,3},{23,7},{19,11},{15,15},{11,19},{7,23},{3,27},{31,31}} | collective-permute-start | bytes 110600 | tf_op jit(solution)/shard_map/cond/branch_6_fun/ppermute | solution.py:381
  4.8 1.3 %collective-permute-start.12 = (f32[72,128]{1,0:T(8,128)S(1)}, f32[72,128]{1,0:T(8,128)}, u32[]{:S(2)}, u32[]{:S(2)}) collective-permute-start(f32[72,128]{1,0:T(8,128)S(1)} %param.6), channel_id=1, source_target_pairs={{1,2},{2,1},{5,6},{6,5},{9,10},{10,9},{13,14},{14,13},{17,18},{18,... | collective-permute-start | bytes 110600 | tf_op jit(solution)/shard_map/cond/branch_6_fun/ppermute | solution.py:381
  7.1 6.1 %collective-permute-start.17 = (f32[80,128]{1,0:T(8,128)S(1)}, f32[80,128]{1,0:T(8,128)S(1)}, u32[]{:S(2)}, u32[]{:S(2)}) collective-permute-start(f32[80,128]{1,0:T(8,128)S(1)} %get-tuple-element.38), channel_id=1, source_target_pairs={{0,4},{4,0},{8,12},{12,8},{16,20},{20,16},{24,28},{28,24},{1,5},{5... | collective-permute-start | bytes 122888 | tf_op jit(solution)/shard_map/ppermute | solution.py:397
  9.7 6.7 %collective-permute-start.18 = (f32[80,128]{1,0:T(8,128)S(1)}, f32[80,128]{1,0:T(8,128)S(1)}, u32[]{:S(2)}, u32[]{:S(2)}) collective-permute-start(f32[80,128]{1,0:T(8,128)S(1)} %get-tuple-element.39), channel_id=1, source_target_pairs={{0,28},{4,8},{8,4},{12,16},{16,12},{20,24},{24,20},{28,0},{1,29},{... | collective-permute-start | bytes 122888 | tf_op jit(solution)/shard_map/ppermute | solution.py:398
  18.1 16.3 %all-to-all-start = ((f32[32,1,128]{2,1,0:T(1,128)}), f32[32,1,128]{2,1,0:T(1,128)S(1)}, u32[]{:S(2)}, u32[]{:S(2)}) async-start(f32[32,1,128]{2,1,0:T(1,128)} %bitcast.6), calls=%async_computation | async-start | bytes 32768 | tf_op jit(solution)/shard_map/all_to_all | solution.py:421

commit v2 on v1

v2 whole, which is shorter than its diff:
```python
import functools

import jax
import jax.numpy as jnp
from jax import lax
from jax.experimental import pallas as pl
from jax.experimental.pallas import tpu as pltpu
from jax.sharding import PartitionSpec as P

TIME_STEP = 0.1
MIXING = 0.1

DEEP = 5
SIDE = (5, 4, 3, 4, 3, 3)
FIELDS = len(SIDE)
START = tuple(sum(SIDE[:f]) for f in range(FIELDS))
FLIPPED = (1, 2)
VMEM_LIMIT = 32 * 1024 * 1024
LOAD_FLOPS = 10**10


def density(heat, salt):
    return heat * (-1.0 - 0.15 * heat - 0.2 * salt) + 0.8 * salt


def iota(shape, axis):
    return lax.broadcasted_iota(jnp.int32, shape, axis)


def packet_rows(levels):
    return -(-(4 * levels + FIELDS * DEEP) // 8) * 8


def flags(meta):
    return meta[0:1, :] == 1, meta[1:2, :] == 1, meta[2:3, :] == 1


def place_kernel(meta, placed):
    for i in range(3):
        placed[i : i + 1, :] = jnp.broadcast_to(meta[0:1, i : i + 1], (1, placed.shape[1]))
    placed[3:, :] = jnp.zeros((placed.shape[0] - 3, placed.shape[1]), jnp.int32)


def pack_kernel(
    meta, spans, facing, heat, salt, zonal, merid, water, weights, anomaly,
    sums, first, second, east_columns, west_columns,
    top, bottom, back,
):
    levels, rows, cols = heat.shape
    span = [spans[0:1, k : k + 1] for k in range(levels)]
    below = [None] * levels
    total = jnp.zeros((1, 1), jnp.float32)
    for k in reversed(range(levels)):
        below[k] = span[k] * (0.5 * span[k] + total)
        total = total + span[k]
    pair = iota((rows, cols), 1) // 2
    zero = jnp.zeros((rows, cols), jnp.float32)
    press, east, north, east_edge, west_edge = zero, zero, zero, zero, zero
    for k in range(levels):
        press = press + below[k] * density(heat[k], salt[k])
        east = east + span[k] * zonal[k]
        north = north + span[k] * merid[k]
        for q, source in ((k, heat), (levels + k, salt)):
            cells = source[k]
            here = pair == q
            east_edge = jnp.where(here, pltpu.roll(cells, (2 * q + 2) % cols, 1), east_edge)
            west_edge = jnp.where(here, pltpu.roll(cells, 2 * q, 1), west_edge)
            top[2 * q : 2 * q + 2, :] = source[k, rows - 2 :, :]
            bottom[2 * q : 2 * q + 2, :] = source[k, :2, :]
            for i in range(2):
                back[2 * q + i : 2 * q + i + 1, :] = source[k, rows - 1 - i : rows - i, :]
    east_columns[...] = east_edge
    west_columns[...] = west_edge
    sums[0] = press
    sums[1] = east
    sums[2] = north
    fields = (sums.at[0], sums.at[1], sums.at[2], water, weights, anomaly)
    for f, field in enumerate(fields):
        at = 4 * levels + DEEP * f
        top[at : at + DEEP, :] = field[rows - DEEP :, :].astype(jnp.float32)
        bottom[at : at + DEEP, :] = field[:DEEP, :].astype(jnp.float32)
        for j in range(DEEP):
            back[at + j : at + j + 1, :] = field[rows - 1 - j : rows - j, :].astype(jnp.float32)
    used = 4 * levels + DEEP * FIELDS
    high = first.shape[0]
    if used < high:
        for packet in (top, bottom, back):
            packet[used:, :] = jnp.zeros((high - used, cols), jnp.float32)
    odd, last, _ = flags(meta)
    first[...] = jnp.where(odd, bottom[...], top[...])
    second[...] = jnp.where(last, back[...], jnp.where(odd, top[...], bottom[...]))


def turn_kernel(
    meta, sums, water, weights, anomaly, first, second, east_columns, west_columns,
    ext, to_near, to_far,
):
    rows, cols = sums.shape[1], sums.shape[2]
    tall = ext.shape[1]
    high = first.shape[0]
    deep = high - to_near.shape[0] + tall
    odd, _, lon_odd = flags(meta)
    from_first = first[...]
    from_second = second[...]
    north = jnp.where(odd, from_second, from_first)
    south = jnp.where(odd, from_first, from_second)
    fields = (sums.at[0], sums.at[1], sums.at[2], water, weights, anomaly)
    for f in range(FIELDS):
        at = deep + DEEP * f
        ext[f, :rows, :] = fields[f][...].astype(jnp.float32)
        ext[f, rows : rows + DEEP, :] = north[at : at + DEEP]
        ext[f, rows + DEEP : tall - DEEP, :] = jnp.zeros((tall - rows - 2 * DEEP, cols), jnp.float32)
        ext[f, tall - DEEP :, :] = south[at : at + DEEP]
    lane = iota((tall, cols), 1)
    spare = jnp.zeros((tall - rows, cols), jnp.float32)
    passed = from_second[:deep]
    fill = jnp.zeros((tall - deep, cols), jnp.float32)
    half = lane >= cols // 2
    east = jnp.where(half, jnp.concatenate([pltpu.roll(passed, cols // 2, 1), fill], axis=0),
                     jnp.concatenate([east_columns[...], spare], axis=0))
    west = jnp.where(half, jnp.concatenate([passed, fill], axis=0),
                     jnp.concatenate([west_columns[...], spare], axis=0))
    for f in range(FIELDS):
        at = deep + START[f]
        here = (lane >= at) & (lane < at + SIDE[f])
        layer = ext[f]
        east = jnp.where(here, pltpu.roll(layer, (at + SIDE[f]) % cols, 1), east)
        west = jnp.where(here, pltpu.roll(layer, at, 1), west)
    to_near[:tall, :] = jnp.where(lon_odd, west, east)
    to_far[:tall, :] = jnp.where(lon_odd, east, west)
    to_near[tall:, :] = from_second[deep:]
    to_far[tall:, :] = from_second[deep:]


def fold_shift(facing):
    cols = facing.shape[1]
    offset = (facing[0:1, 0:1] + 1) & (cols - 1)
    return jnp.where(offset >= cols // 2, offset - cols, offset)


def fold(shift, west, own, east, beside):
    rows, cols = own.shape
    lane = iota((rows, cols), 1)
    source = cols - 1 - lane
    if beside:
        place = (source + shift) & (cols - 1)
        low = jnp.where(place - cols < shift, west, own)
        merged = jnp.where(place >= cols // 2, low, jnp.where(place >= shift, east, own))
    else:
        merged = jnp.where(source >= cols - shift, west, jnp.where(source < -shift, east, own))
    return jnp.take_along_axis(merged, cols - 1 - ((lane - shift) & (cols - 1)), axis=1)


def krylov_kernel(used, meta, facing, ext, second, from_near, from_far, base, moments, folded):
    tall, cols = ext.shape[1], ext.shape[2]
    rows = base.shape[1]
    size = from_near.shape[0] - tall
    _, top, lon_odd = flags(meta)
    west = jnp.where(lon_odd, from_near[...], from_far[...])
    east = jnp.where(lon_odd, from_far[...], from_near[...])
    shift = fold_shift(facing)
    row = iota((size, cols), 0)
    flips = (row >= DEEP * FLIPPED[0]) & (row < DEEP * (FLIPPED[-1] + 1))
    for side in range(2):
        cells = fold(shift, west[tall:], second[used:, :], east[tall:], side == 1)
        folded[side, :size, :] = jnp.where(flips, -cells, cells)
    folded[:, size:, :] = jnp.zeros((2, folded.shape[1] - size, cols), jnp.float32)
    lane = iota((tall, cols), 1)
    first = lane == 0
    last = lane == cols - 1
    kept = iota((8, cols), 0) < DEEP

    def load(f):
        at = used + START[f]
        a = pltpu.roll(west[:tall], (2 * cols - SIDE[f] - at) % cols, 1)
        b = pltpu.roll(east[:tall], (cols - at) % cols, 1)
        beside = jnp.where(lane >= cols - SIDE[f], a, jnp.where(lane < SIDE[f], b, 0.0))

        def put(cells, side):
            new = folded[side, DEEP * f : DEEP * f + 8, :]
            new = jnp.where(kept, jnp.where(top, new, cells[rows : rows + 8]), 0.0)
            return jnp.concatenate([cells[:rows], new, cells[rows + 8 :]], axis=0)

        return put(ext[f], 0), put(beside, 1)

    def plus_x(pair):
        a, b = (pltpu.roll(part, cols - 1, 1) for part in pair)
        return jnp.where(last, b, a), jnp.where(last, a, b)

    def minus_x(pair):
        a, b = (pltpu.roll(part, 1, 1) for part in pair)
        return jnp.where(first, b, a), jnp.where(first, a, b)

    def plus_y(pair):
        return tuple(pltpu.roll(part, tall - 1, 0) for part in pair)

    def minus_y(pair):
        return tuple(pltpu.roll(part, 1, 0) for part in pair)

    def each(function, *pairs):
        return tuple(function(*parts) for parts in zip(*pairs))

    def neighbours(pair):
        return each(
            lambda a, b, c, d: (a + b) + (c + d), plus_x(pair), minus_x(pair), plus_y(pair), minus_y(pair)
        )

    press, zonal, merid, wet, weights, anomaly = (load(f) for f in range(FIELDS))
    half = 0.5 * TIME_STEP
    flow = lambda w, speed, a, b: w * (speed - half * (a - b))
    east_flow = each(flow, wet, zonal, plus_x(press), minus_x(press))
    north_flow = each(flow, wet, merid, plus_y(press), minus_y(press))
    right = each(
        lambda w, g, n, a, b, c, d: w * (g * n - 0.5 * (a - b + c - d)),
        wet,
        weights,
        anomaly,
        plus_x(east_flow),
        minus_x(east_flow),
        plus_y(north_flow),
        minus_y(north_flow),
    )
    diagonal = each(lambda g: 4.0 + g, weights)
    inverse = each(lambda m: 1.0 / m, diagonal)
    scale = each(lambda w, i: w * i, wet, inverse)
    zero = each(lambda r, i: r * i, right, inverse)
    one = each(lambda a, n: a * n, scale, neighbours(zero))
    two = each(lambda a, n: a * n, scale, neighbours(one))
    last_sum = neighbours(two)[0][:rows]
    right, middle = right[0][:rows], diagonal[0][:rows]
    zero, one, two = zero[0][:rows], one[0][:rows], two[0][:rows]
    base[0] = zero
    base[1] = one
    base[2] = two
    weighted = middle * one
    products = (
        right * zero,
        right * one,
        weighted * one,
        weighted * two,
        middle * two * two,
        last_sum * two,
    )
    which = iota((8, cols), 0)
    sums = jnp.zeros((8, cols), jnp.float32)
    for k, product in enumerate(products):
        sums = jnp.where(which == k, jnp.sum(product, axis=0, keepdims=True), sums)
    sums = jnp.sum(sums, axis=1, keepdims=True)
    sums = jnp.sum(jnp.where(which == iota((8, cols), 1), sums, 0.0), axis=0, keepdims=True)
    moments[...] = jnp.broadcast_to(sums, moments.shape)


def step_kernel(
    meta, spans, facing, heat, salt, zonal, merid, water, first, second, from_near, from_far,
    heat_out, salt_out, zonal_out, merid_out,
    new_heat, new_salt, new_zonal, new_merid, north_rows, south_rows, sems,
):
    levels, rows, cols = heat.shape
    deep = 4 * levels
    odd, top, lon_odd = flags(meta)
    wet = water[...].astype(jnp.float32)
    lane = iota((rows, cols), 1)
    row = iota((rows, cols), 0)
    east = jnp.where(lon_odd, from_far[:rows, :], from_near[:rows, :])
    west = jnp.where(lon_odd, from_near[:rows, :], from_far[:rows, :])
    from_second = second[:deep, :]
    across = fold(fold_shift(facing), pltpu.roll(west[:deep], cols // 2, 1), from_second, east[:deep], False)
    north_rows[...] = jnp.where(odd, jnp.where(top, across, from_second), first[:deep, :])
    south_rows[...] = jnp.where(odd, first[:deep, :], from_second)

    def around(cells, q):
        a = pltpu.roll(east, (cols - 2 * q) % cols, 1)
        b = pltpu.roll(west, (2 * cols - 2 - 2 * q) % cols, 1)
        side = jnp.where(lane < 2, a, b)

        def shift_x(by):
            a = pltpu.roll(cells, by % cols, 1)
            b = pltpu.roll(side, by % cols, 1)
            own = lane >= by if by > 0 else lane < cols + by
            return jnp.where(own, a, b)

        n0 = north_rows[2 * q : 2 * q + 1, :]
        n1 = north_rows[2 * q + 1 : 2 * q + 2, :]
        s0 = south_rows[2 * q + 1 : 2 * q + 2, :]
        s1 = south_rows[2 * q : 2 * q + 1, :]
        north_one = jnp.where(row == rows - 1, n0, pltpu.roll(cells, rows - 1, 0))
        north_two = jnp.where(row == rows - 1, n1, jnp.where(row == rows - 2, n0, pltpu.roll(cells, rows - 2, 0)))
        south_one = jnp.where(row == 0, s0, pltpu.roll(cells, 1, 0))
        south_two = jnp.where(row == 0, s1, jnp.where(row == 1, s0, pltpu.roll(cells, 2, 0)))
        return (shift_x(-1), shift_x(1), shift_x(-2), shift_x(2), north_one, south_one, north_two, south_two)

    def advance(cells, parts, speed_x, speed_y):
        e1, w1, e2, w2, n1, s1, n2, s2 = parts
        grad_east = 8.0 * (e1 - w1) - (e2 - w2)
        grad_north = 8.0 * (n1 - s1) - (n2 - s2)
        laplace = (e1 + w1) + (n1 + s1) - 4.0 * cells
        tendency = (-TIME_STEP / 12.0) * (speed_x * grad_east + speed_y * grad_north) + MIXING * laplace
        return cells + wet * tendency

    stores = ((new_heat, heat_out), (new_salt, salt_out), (new_zonal, zonal_out), (new_merid, merid_out))
    size = levels // sems.shape[1]
    copies = []
    half = 0.5 * TIME_STEP
    above_x = jnp.zeros((rows, cols), jnp.float32)
    above_y = jnp.zeros((rows, cols), jnp.float32)
    for k in range(levels):
        t, s, u, v = heat[k], salt[k], zonal[k], merid[k]
        around_t = around(t, k)
        around_s = around(s, levels + k)
        new_heat[k] = advance(t, around_t, u, v)
        new_salt[k] = advance(s, around_s, u, v)
        span = spans[0:1, k : k + 1]
        layer_x = span * (density(around_t[0], around_s[0]) - density(around_t[1], around_s[1]))
        layer_y = span * (density(around_t[4], around_s[4]) - density(around_t[5], around_s[5]))
        new_zonal[k] = wet * (u - half * (above_x + 0.5 * layer_x))
        new_merid[k] = wet * (v - half * (above_y + 0.5 * layer_y))
        above_x = above_x + layer_x
        above_y = above_y + layer_y
        if (k + 1) % size == 0:
            piece = pl.ds(k + 1 - size, size)
            for i, (near_ref, far_ref) in enumerate(stores):
                copies.append(pltpu.make_async_copy(near_ref.at[piece], far_ref.at[piece], sems.at[i, k // size]))
                copies[-1].start()
    for copy in copies:
        copy.wait()


def surface_kernel(shares, base, surface):
    sums = jnp.sum(shares[...], axis=0, keepdims=True)
    lane = iota(sums.shape, 1)
    nu = [jnp.sum(jnp.where(lane == k, sums, 0.0), axis=1, keepdims=True) for k in range(6)]

    def ratio(a, b):
        good = b > 0.0
        return jnp.where(good, a / jnp.where(good, b, 1.0), 0.0)

    def form(p, h):
        total = 0.0
        for i, a in enumerate(p):
            for j in range(i, len(p)):
                term = a * p[j] * h[i + j]
                total = total + (term if i == j else 2.0 * term)
        return total

    gap = [nu[k] - nu[k + 1] for k in range(5)]
    rz = nu[0]
    alpha = ratio(rz, gap[0])
    one = jnp.ones_like(rz)
    y = [one - alpha, alpha]
    x = [alpha, 0.0, 0.0]
    new = form(y, nu)
    beta = ratio(new, rz)
    rz = new
    p = [y[0] + beta, y[1]]
    alpha = ratio(rz, form(p, gap))
    x = [x[0] + alpha * p[0], alpha * p[1], 0.0]
    y = [y[0] - alpha * p[0], y[1] - alpha * (p[1] - p[0]), alpha * p[1]]
    new = form(y, nu)
    beta = ratio(new, rz)
    rz = new
    p = [y[0] + beta * p[0], y[1] + beta * p[1], y[2]]
    alpha = ratio(rz, form(p, gap))
    x = [x[0] + alpha * p[0], x[1] + alpha * p[1], alpha * p[2]]
    surface[...] = x[0] * base[0] + x[1] * base[1] + x[2] * base[2]


def call(kernel, outs, flops, moved, name, out_space=pltpu.VMEM, scratch=(), types=jnp.float32):
    def run(*args):
        return pl.pallas_call(
            kernel,
            out_shape=[jax.ShapeDtypeStruct(shape, types) for shape in outs],
            in_specs=[pl.BlockSpec(memory_space=pltpu.VMEM)] * len(args),
            out_specs=[pl.BlockSpec(memory_space=out_space)] * len(outs),
            scratch_shapes=list(scratch),
            cost_estimate=pl.CostEstimate(flops=flops, bytes_accessed=moved, transcendentals=0),
            compiler_params=pltpu.CompilerParams(vmem_limit_bytes=VMEM_LIMIT),
            name=name,
        )(*args)

    return run


def body(
    warmth_deviation,
    saltiness_deviation,
    easterly_speed,
    poleward_speed,
    stratum_spans,
    water_indicator,
    opposite_counterpart,
    elevation_weights,
    elevation_anomaly,
):
    lons, lats = lax.axis_size("lon"), lax.axis_size("lat")
    lon, lat = lax.axis_index("lon"), lax.axis_index("lat")
    levels, rows, cols = warmth_deviation.shape
    assert cols & (cols - 1) == 0 and 4 * levels + sum(SIDE) <= cols // 2
    high = packet_rows(levels)
    tall = rows + 16
    long = tall + high - 4 * levels
    width = cols * lons
    flat = lambda i, j: (i % lons) * lats + j

    place = (lax.rem(lat, 2), (lat == lats - 1).astype(jnp.int32), lax.rem(lon, 2))
    meta = jnp.stack(place).astype(jnp.int32).reshape(1, 3)
    (meta,) = call(place_kernel, [(8, cols)], LOAD_FLOPS, 16, "place", types=jnp.int32)(meta)

    spans = stratum_spans.reshape(1, levels)
    facing = opposite_counterpart.reshape(1, cols)
    state = (warmth_deviation, saltiness_deviation, easterly_speed, poleward_speed)
    flat_state = (water_indicator, elevation_weights, elevation_anomaly)
    cells = levels * rows * cols
    sums, first, second, east_columns, west_columns = call(
        pack_kernel,
        [(3, rows, cols), (high, cols), (high, cols), (rows, cols), (rows, cols)],
        12 * cells,
        16 * cells,
        "level_sums",
        scratch=[pltpu.VMEM((high, cols), jnp.float32)] * 3,
    )(meta, spans, facing, *state, *flat_state)

    axes = ("lon", "lat")
    pairs_first = [(flat(i, j), flat(i, j ^ 1)) for i in range(lons) for j in range(lats)]
    pairs_inner = [
        (flat(i, a), flat(i, b))
        for i in range(lons)
        for j in range(1, lats - 1, 2)
        for a, b in ((j, j + 1), (j + 1, j))
    ]

    counterpart, first = lax.optimization_barrier((opposite_counterpart, first))
    hinge = lax.rem(counterpart[0] + 1 + cols * lon, width)
    block = lax.rem((hinge + cols // 2) // cols, lons)

    def exchange(shift, first, second):
        pairs_fold = [(flat(shift - 1 - i, lats - 1), flat(i, lats - 1)) for i in range(lons)]
        second = lax.ppermute(second, axes, pairs_inner + pairs_fold)
        return lax.ppermute(first, axes, pairs_first), second

    first, second = lax.switch(block, [functools.partial(exchange, s) for s in range(lons)], first, second)

    ext, to_near, to_far = call(
        turn_kernel,
        [(FIELDS, tall, cols), (long, cols), (long, cols)],
        FIELDS * tall * cols,
        4 * 4 * FIELDS * tall * cols,
        "row_halos",
    )(meta, sums, *flat_state, first, second, east_columns, west_columns)

    from_far = lax.ppermute(to_far, "lon", [(i, (i + 1 if i % 2 else i - 1) % lons) for i in range(lons)])
    from_near = lax.ppermute(to_near, "lon", [(i, i ^ 1) for i in range(lons)])

    count = lons * lats
    base, moments = call(
        functools.partial(krylov_kernel, 4 * levels),
        [(3, rows, cols), (count, cols)],
        200 * tall * cols,
        4 * 12 * tall * cols,
        "krylov",
        scratch=[pltpu.VMEM((2, high - 4 * levels + 8, cols), jnp.float32)],
    )(meta, facing, ext, second, from_near, from_far)

    chunks = 5 if levels % 5 == 0 else 1
    new_heat, new_salt, new_zonal, new_merid = call(
        step_kernel,
        [(levels, rows, cols)] * 4,
        120 * cells,
        32 * cells,
        "levels_step",
        out_space=pltpu.HBM,
        scratch=[
            *[pltpu.VMEM((levels, rows, cols), jnp.float32)] * 4,
            *[pltpu.VMEM((4 * levels, cols), jnp.float32)] * 2,
            pltpu.SemaphoreType.DMA((4, chunks)),
        ],
    )(meta, spans, facing, *state, water_indicator, first, second, from_near, from_far)

    shares = lax.all_to_all(moments, axes, 0, 0, tiled=True)
    (surface,) = call(surface_kernel, [(rows, cols)], 6 * rows * cols, 16 * rows * cols, "surface")(shares, base)
    return (new_heat, new_salt, new_zonal, new_merid, surface)


def solution(mesh):
    for axis in mesh.shape.values():
        assert axis > 1 and axis & (axis - 1) == 0
    levels = P(None, "lat", "lon")
    flat = P("lat", "lon")
    return jax.shard_map(
        body,
        mesh=mesh,
        in_specs=(levels, levels, levels, levels, P(), flat, P("lon"), flat, flat),
        out_specs=(levels, levels, levels, levels, flat),
        check_vma=False,
    )
```

time: 35.7 us -> 34.2 us (0.958)
  starting transfers between devices: 18.5 us -> 16.9 us
  local copies, waits for them, and re-layouts: 0.07 us -> 1.18 us
  Pallas kernels: 9.58 us -> 8.92 us
  waiting for transfers between devices: 6.2 us -> 5.83 us
    ppermute x3 -> x2, starting transfers between devices: 3.05 us -> 1.77 us  [the longest x1 1.26 us: exchange(): second = lax.ppermute(second, axes, pairs_inner + pairs_fold)]
    unnamed x18, local copies, waits for them, and re-layouts: 0.07 us -> 1.18 us
    pallas_call x6, Pallas kernels: 9.58 us -> 8.92 us  [run(): pl.pallas_call(kernel, out_shape=[jax.ShapeDtypeStruct(shape, types) for...]
    all_to_all x1, waiting for transfers between devices: 3.06 us -> 2.53 us  [body(): shares = lax.all_to_all(moments, axes, 0, 0, tiled=True)]
  transfers between devices with their start and end apart: 6 -> 5, of which waited for: 2 -> 2; matrix products, arithmetic and copies ran while one was open for 0% -> 0% of each run, Pallas kernels for 11% -> 13%
where the time goes in v2:
time: 34.2 us; the launch traced here: 33.8 us
  starting transfers between devices  16.9 us (49%)
  Pallas kernels  8.92 us (26%)
  waiting for transfers between devices  5.83 us (17%)
  local copies, waits for them, and re-layouts  1.18 us (3%)
  between operations  0.8 us (2%)
    all_to_all x1, starting transfers between devices, body(): shares = lax.all_to_all(moments, axes, 0, 0, tiled=True)  8.94 us
    pallas_call x6, Pallas kernels, run(): pl.pallas_call(kernel, out_shape=[jax.ShapeDtypeStruct(shape, types) for...  8.92 us
    ppermute x1, starting transfers between devices, body(): lax.ppermute(to_far, 'lon', [(i, (i + 1 if i % 2 else i - 1) % lons) for...  3.57 us
    ppermute x1, waiting for transfers between devices, body(): lax.ppermute(to_far, 'lon', [(i, (i + 1 if i % 2 else i - 1) % lons) for...  3.3 us
    ppermute x1, starting transfers between devices, body(): from_near = lax.ppermute(to_near, 'lon', [(i, i ^ 1) for i in range(lons)])  2.64 us
    all_to_all x1, waiting for transfers between devices, body(): shares = lax.all_to_all(moments, axes, 0, 0, tiled=True)  2.53 us
    ppermute x1, starting transfers between devices, exchange(): second = lax.ppermute(second, axes, pairs_inner + pairs_fold)  1.26 us
    unnamed x18, local copies, waits for them, and re-layouts  1.18 us
  transfers between devices with their start and end apart: 5, of which 2 were waited for; matrix products, arithmetic and copies ran while one was open for 0% of the time, Pallas kernels for 13%

profile of v2, /device:TPU:0, one launch (start us, length us, event | category | flops | bytes accessed | tf_op | source)
XLA Modules:
  0.0 33.8 jit_solution(15574733782709050599)
XLA Ops:
  0.6 0.1 add_bitcast_fusion.meta
  0.7 0.0 copy-start
  0.7 0.0 copy-start.2
  0.7 0.0 copy-start.4
  0.7 0.0 copy-start.5
  0.8 0.0 copy-start.6
  0.8 0.1 place.1.meta
  0.8 0.8 %copy-done = f32[10,64,128]{2,1,0:T(8,128)S(1)} copy-done((f32[10,64,128]{2,1,0:T(8,128)S(1)}, f32[10,64,128]{2,1,0:T(8,128)}, u32[]{:S(2)}) %copy-start) | copy-done | bytes 327704
  1.7 0.1 copy-done.1
  1.8 0.1 copy-done.2
  1.9 0.1 copy-done.3
  2.0 0.0 copy-done.4
  2.0 0.0 copy-done.5
  2.0 0.0 copy-done.6
  2.0 0.0 copy-done.7
  2.0 0.0 copy-done.8
  2.0 0.5 %level_sums.1 = (f32[3,64,128]{2,1,0:T(8,128)S(1)}, f32[72,128]{1,0:T(8,128)S(1)}, f32[72,128]{1,0:T(8,128)S(1)}, f32[64,128]{1,0:T(8,128)S(1)}, f32[64,128]{1,0:T(8,128)S(1)}) custom-call(s32[8,128]{1,0:T(8,128)S(1)} %place.1.meta, f32[1,10]{1,0:T(1,128)S(1)} %bitcast.18, s32[1,128]{1,0:T(1,128)S(1)} %bitcast.14, f32[10,64,128]{2,1,0:T(8,128)S(1)} %copy-done, ...), custom_call_target="tpu_custom_call" | custom-call | flops 983040 | bytes 1310720 | tf_op jit(solution)/shard_map/level_sums/pallas_call | solution.py:369
  2.6 1.8 %conditional.1 = (f32[72,128]{1,0:T(8,128)}, f32[72,128]{1,0:T(8,128)}) conditional(s32[]{:T(128)} %clamp.3, (f32[72,128]{1,0:T(8,128)S(1)}, f32[72,128]{1,0:T(8,128)S(1)}) %tuple.42, (f32[72,128]{1,0:T(8,128)S(1)}, f32[72,128]{1,0:T(8,128)S(1)}) %tuple.42, (f32[72,128]{1,0:T(8,128)S(1)}, ...), branch_computations={%region_0.1_spmd, %region_1.2_spmd, %region_2.3_spmd, %region_3.4_... | conditional | bytes 295008 | solution.py:440
  2.7 0.5 %collective-permute-start.12 = (f32[72,128]{1,0:T(8,128)S(1)}, f32[72,128]{1,0:T(8,128)}, u32[]{:S(2)}, u32[]{:S(2)}) collective-permute-start(f32[72,128]{1,0:T(8,128)S(1)} %get-tuple-element.44), channel_id=1, source_target_pairs={{0,1},{1,0},{2,3},{3,2},{4,5},{5,4},{6,7},{7,6},{8,9},{9,8},{10,11... | collective-permute-start | bytes 110600 | tf_op jit(solution)/shard_map/cond/branch_6_fun/ppermute | solution.py:438
  3.2 1.3 %collective-permute-start.13 = (f32[72,128]{1,0:T(8,128)S(1)}, f32[72,128]{1,0:T(8,128)}, u32[]{:S(2)}, u32[]{:S(2)}) collective-permute-start(f32[72,128]{1,0:T(8,128)S(1)} %get-tuple-element.45), channel_id=1, source_target_pairs={{1,2},{2,1},{5,6},{6,5},{9,10},{10,9},{13,14},{14,13},{17,18},{18,... | collective-permute-start | bytes 110600 | tf_op jit(solution)/shard_map/cond/branch_6_fun/ppermute | solution.py:437
  4.4 0.0 collective-permute-done.12
  4.4 0.0 collective-permute-done.13
  4.4 1.0 %row_halos.1 = (f32[6,80,128]{2,1,0:T(8,128)S(1)}, f32[112,128]{1,0:T(8,128)S(1)}, f32[112,128]{1,0:T(8,128)S(1)}) custom-call(s32[8,128]{1,0:T(8,128)S(1)} %place.1.meta, f32[3,64,128]{2,1,0:T(8,128)S(1)} %get-tuple-element.77.sums, s32[64,128]{1,0:T(8,128)S(1)} %copy-done.4, f32[64,128]{1,0:T(8,128)S(1)} %copy-done.5, f32[64,128]{1,0:T(8,128)S(1)} %copy-done.6, ...), custom_call_target="tpu_custom_call" | custom-call | flops 61440 | bytes 983040 | tf_op jit(solution)/shard_map/row_halos/pallas_call | solution.py:369
  5.4 2.6 %collective-permute-start.16 = (f32[112,128]{1,0:T(8,128)S(1)}, f32[112,128]{1,0:T(8,128)S(1)}, u32[]{:S(2)}, u32[]{:S(2)}) collective-permute-start(f32[112,128]{1,0:T(8,128)S(1)} %get-tuple-element.80), channel_id=1, source_target_pairs={{0,4},{4,0},{8,12},{12,8},{16,20},{20,16},{24,28},{28,24},{1,5},{5... | collective-permute-start | bytes 172040 | tf_op jit(solution)/shard_map/ppermute | solution.py:451
  8.1 3.6 %collective-permute-start.17 = (f32[112,128]{1,0:T(8,128)S(1)}, f32[112,128]{1,0:T(8,128)S(1)}, u32[]{:S(2)}, u32[]{:S(2)}) collective-permute-start(f32[112,128]{1,0:T(8,128)S(1)} %get-tuple-element.81), channel_id=1, source_target_pairs={{0,28},{4,8},{8,4},{12,16},{16,12},{20,24},{24,20},{28,0},{1,29},{... | collective-permute-start | bytes 172040 | tf_op jit(solution)/shard_map/ppermute | solution.py:450
  11.6 0.0 collective-permute-done.16.from_near
  11.6 3.3 %collective-permute-done.17.from_far = f32[112,128]{1,0:T(8,128)S(1)} collective-permute-done((f32[112,128]{1,0:T(8,128)S(1)}, f32[112,128]{1,0:T(8,128)S(1)}, u32[]{:S(2)}, u32[]{:S(2)}) %collective-permute-start.17) | collective-permute-done | bytes 57376 | tf_op jit(solution)/shard_map/ppermute | solution.py:450
  14.9 2.0 %krylov.1 = (f32[3,64,128]{2,1,0:T(8,128)S(1)}, f32[32,128]{1,0:T(8,128)}) custom-call(s32[8,128]{1,0:T(8,128)S(1)} %place.1.meta, s32[1,128]{1,0:T(1,128)S(1)} %bitcast.16, f32[6,80,128]{2,1,0:T(8,128)S(1)} %get-tuple-element.86.ext, f32[72,128]{1,0:T(8,128)} %get-tuple-element.76.second, f32[112,128]{1,0:T(8,128)S(1)} %collective-permute-done.16.from_near, ...), custom_call_target="tpu_custom_call" | custom-call | flops 2048000 | bytes 491520 | tf_op jit(solution)/shard_map/krylov/pallas_call | solution.py:369
  17.0 8.9 %all-to-all-start = ((f32[32,1,128]{2,1,0:T(1,128)}), f32[32,1,128]{2,1,0:T(1,128)S(1)}, u32[]{:S(2)}, u32[]{:S(2)}) async-start(f32[32,1,128]{2,1,0:T(1,128)} %bitcast.8), calls=%async_computation | async-start | bytes 32768 | tf_op jit(solution)/shard_map/all_to_all | solution.py:478
  25.9 4.5 %levels_step.1 = (f32[10,64,128]{2,1,0:T(8,128)}, f32[10,64,128]{2,1,0:T(8,128)}, f32[10,64,128]{2,1,0:T(8,128)}, f32[10,64,128]{2,1,0:T(8,128)}) custom-call(s32[8,128]{1,0:T(8,128)S(1)} %place.1.meta, f32[1,10]{1,0:T(1,128)S(1)} %bitcast.19, s32[1,128]{1,0:T(1,128)S(1)} %bitcast.17, f32[10,64,128]{2,1,0:T(8,128)S(1)} %copy-done, ...), custom_call_target="tpu_custom_call" | custom-call | flops 9830400 | bytes 2621440 | tf_op jit(solution)/shard_map/levels_step/pallas_call | solution.py:369
  30.5 2.5 %all-to-all-done = f32[32,1,128]{2,1,0:T(1,128)S(1)} async-done(((f32[32,1,128]{2,1,0:T(1,128)}), f32[32,1,128]{2,1,0:T(1,128)S(1)}, u32[]{:S(2)}, u32[]{:S(2)}) %all-to-all-start) | async-done | bytes 16416 | tf_op jit(solution)/shard_map/all_to_all | solution.py:478
  33.0 0.8 %surface.1 = f32[64,128]{1,0:T(8,128)} custom-call(f32[32,128]{1,0:T(8,128)S(1)} %bitcast.13, f32[3,64,128]{2,1,0:T(8,128)S(1)} %get-tuple-element.88.base), custom_call_target="tpu_custom_call" | custom-call | flops 49152 | bytes 131072 | tf_op jit(solution)/shard_map/surface/pallas_call | solution.py:369
  (4 shorter events, 0.0 us)
Async XLA Ops:
  0.7 1.0 %copy-start = (f32[10,64,128]{2,1,0:T(8,128)S(1)}, f32[10,64,128]{2,1,0:T(8,128)}, u32[]{:S(2)}) copy-start(f32[10,64,128]{2,1,0:T(8,128)} %heat.3) | copy-start | bytes 983044
  0.7 1.1 %copy-start.1 = (f32[10,64,128]{2,1,0:T(8,128)S(1)}, f32[10,64,128]{2,1,0:T(8,128)}, u32[]{:S(2)}) copy-start(f32[10,64,128]{2,1,0:T(8,128)} %salt.3) | copy-start | bytes 983044
  0.7 1.2 %copy-start.2 = (f32[10,64,128]{2,1,0:T(8,128)S(1)}, f32[10,64,128]{2,1,0:T(8,128)}, u32[]{:S(2)}) copy-start(f32[10,64,128]{2,1,0:T(8,128)} %zonal.3) | copy-start | bytes 983044
  0.7 1.3 %copy-start.3 = (f32[10,64,128]{2,1,0:T(8,128)S(1)}, f32[10,64,128]{2,1,0:T(8,128)}, u32[]{:S(2)}) copy-start(f32[10,64,128]{2,1,0:T(8,128)} %merid.3) | copy-start | bytes 983044
  0.7 1.3 %copy-start.4 = (s32[64,128]{1,0:T(8,128)S(1)}, s32[64,128]{1,0:T(8,128)}, u32[]{:S(2)}) copy-start(s32[64,128]{1,0:T(8,128)} %water.5) | copy-start | bytes 98308
  0.7 1.3 %copy-start.5 = (f32[64,128]{1,0:T(8,128)S(1)}, f32[64,128]{1,0:T(8,128)}, u32[]{:S(2)}) copy-start(f32[64,128]{1,0:T(8,128)} %weights.3) | copy-start | bytes 98308
  0.8 1.2 %copy-start.6 = (f32[64,128]{1,0:T(8,128)S(1)}, f32[64,128]{1,0:T(8,128)}, u32[]{:S(2)}) copy-start(f32[64,128]{1,0:T(8,128)} %anomaly.3) | copy-start | bytes 98308
  0.8 1.2 %copy-start.7 = (s32[128]{0:T(128)S(1)}, s32[128]{0:T(128)}, u32[]{:S(2)}) copy-start(s32[128]{0:T(128)} %param.23) | copy-start | bytes 1540
  0.8 1.2 %copy-start.8 = (f32[10]{0:T(128)S(1)}, f32[10]{0:T(128)}, u32[]{:S(2)}) copy-start(f32[10]{0:T(128)} %param.21) | copy-start | bytes 124
  2.7 1.8 %collective-permute-start.12 = (f32[72,128]{1,0:T(8,128)S(1)}, f32[72,128]{1,0:T(8,128)}, u32[]{:S(2)}, u32[]{:S(2)}) collective-permute-start(f32[72,128]{1,0:T(8,128)S(1)} %get-tuple-element.44), channel_id=1, source_target_pairs={{0,1},{1,0},{2,3},{3,2},{4,5},{5,4},{6,7},{7,6},{8,9},{9,8},{10,11... | collective-permute-start | bytes 110600 | tf_op jit(solution)/shard_map/cond/branch_6_fun/ppermute | solution.py:438
  3.2 1.3 %collective-permute-start.13 = (f32[72,128]{1,0:T(8,128)S(1)}, f32[72,128]{1,0:T(8,128)}, u32[]{:S(2)}, u32[]{:S(2)}) collective-permute-start(f32[72,128]{1,0:T(8,128)S(1)} %get-tuple-element.45), channel_id=1, source_target_pairs={{1,2},{2,1},{5,6},{6,5},{9,10},{10,9},{13,14},{14,13},{17,18},{18,... | collective-permute-start | bytes 110600 | tf_op jit(solution)/shard_map/cond/branch_6_fun/ppermute | solution.py:437
  5.4 6.2 %collective-permute-start.16 = (f32[112,128]{1,0:T(8,128)S(1)}, f32[112,128]{1,0:T(8,128)S(1)}, u32[]{:S(2)}, u32[]{:S(2)}) collective-permute-start(f32[112,128]{1,0:T(8,128)S(1)} %get-tuple-element.80), channel_id=1, source_target_pairs={{0,4},{4,0},{8,12},{12,8},{16,20},{20,16},{24,28},{28,24},{1,5},{5... | collective-permute-start | bytes 172040 | tf_op jit(solution)/shard_map/ppermute | solution.py:451
  8.1 6.9 %collective-permute-start.17 = (f32[112,128]{1,0:T(8,128)S(1)}, f32[112,128]{1,0:T(8,128)S(1)}, u32[]{:S(2)}, u32[]{:S(2)}) collective-permute-start(f32[112,128]{1,0:T(8,128)S(1)} %get-tuple-element.81), channel_id=1, source_target_pairs={{0,28},{4,8},{8,4},{12,16},{16,12},{20,24},{24,20},{28,0},{1,29},{... | collective-permute-start | bytes 172040 | tf_op jit(solution)/shard_map/ppermute | solution.py:450
  17.0 16.0 %all-to-all-start = ((f32[32,1,128]{2,1,0:T(1,128)}), f32[32,1,128]{2,1,0:T(1,128)S(1)}, u32[]{:S(2)}, u32[]{:S(2)}) async-start(f32[32,1,128]{2,1,0:T(1,128)} %bitcast.8), calls=%async_computation | async-start | bytes 32768 | tf_op jit(solution)/shard_map/all_to_all | solution.py:478

commit v3 on v2

--- a/solution.py
+++ b/solution.py
@@ -10,9 +10,10 @@
 TIME_STEP = 0.1
 MIXING = 0.1
 
-DEEP = 5
+DEEP = (5, 3, 4, 4, 3, 3)
 SIDE = (5, 4, 3, 4, 3, 3)
 FIELDS = len(SIDE)
+ROW = tuple(sum(DEEP[:f]) for f in range(FIELDS + 1))
 START = tuple(sum(SIDE[:f]) for f in range(FIELDS))
 FLIPPED = (1, 2)
 VMEM_LIMIT = 32 * 1024 * 1024
@@ -28,7 +29,7 @@
 
 
 def packet_rows(levels):
-    return -(-(4 * levels + FIELDS * DEEP) // 8) * 8
+    return -(-(4 * levels + ROW[-1]) // 8) * 8
 
 
 def flags(meta):
@@ -76,12 +77,13 @@
     sums[2] = north
     fields = (sums.at[0], sums.at[1], sums.at[2], water, weights, anomaly)
     for f, field in enumerate(fields):
-        at = 4 * levels + DEEP * f
-        top[at : at + DEEP, :] = field[rows - DEEP :, :].astype(jnp.float32)
-        bottom[at : at + DEEP, :] = field[:DEEP, :].astype(jnp.float32)
-        for j in range(DEEP):
+        at = 4 * levels + ROW[f]
+        deep = DEEP[f]
+        top[at : at + deep, :] = field[rows - deep :, :].astype(jnp.float32)
+        bottom[at : at + deep, :] = field[:deep, :].astype(jnp.float32)
+        for j in range(deep):
             back[at + j : at + j + 1, :] = field[rows - 1 - j : rows - j, :].astype(jnp.float32)
-    used = 4 * levels + DEEP * FIELDS
+    used = 4 * levels + ROW[-1]
     high = first.shape[0]
     if used < high:
         for packet in (top, bottom, back):
@@ -92,13 +94,12 @@
 
 
 def turn_kernel(
-    meta, sums, water, weights, anomaly, first, second, east_columns, west_columns,
-    ext, to_near, to_far,
+    meta, sums, water, weights, anomaly, second, first, east_columns, west_columns,
+    ext, to_far, to_near, facing_rows, north_rows, south_rows,
 ):
     rows, cols = sums.shape[1], sums.shape[2]
     tall = ext.shape[1]
-    high = first.shape[0]
-    deep = high - to_near.shape[0] + tall
+    deep = north_rows.shape[0]
     odd, _, lon_odd = flags(meta)
     from_first = first[...]
     from_second = second[...]
@@ -106,11 +107,12 @@
     south = jnp.where(odd, from_first, from_second)
     fields = (sums.at[0], sums.at[1], sums.at[2], water, weights, anomaly)
     for f in range(FIELDS):
-        at = deep + DEEP * f
+        at = deep + ROW[f]
+        size = DEEP[f]
         ext[f, :rows, :] = fields[f][...].astype(jnp.float32)
-        ext[f, rows : rows + DEEP, :] = north[at : at + DEEP]
-        ext[f, rows + DEEP : tall - DEEP, :] = jnp.zeros((tall - rows - 2 * DEEP, cols), jnp.float32)
-        ext[f, tall - DEEP :, :] = south[at : at + DEEP]
+        ext[f, rows : rows + size, :] = north[at : at + size]
+        ext[f, rows + size : tall - size, :] = jnp.zeros((tall - rows - 2 * size, cols), jnp.float32)
+        ext[f, tall - size :, :] = south[at : at + size]
     lane = iota((tall, cols), 1)
     spare = jnp.zeros((tall - rows, cols), jnp.float32)
     passed = from_second[:deep]
@@ -130,6 +132,9 @@
     to_far[:tall, :] = jnp.where(lon_odd, east, west)
     to_near[tall:, :] = from_second[deep:]
     to_far[tall:, :] = from_second[deep:]
+    facing_rows[...] = from_second[deep:]
+    north_rows[...] = north[:deep]
+    south_rows[...] = south[:deep]
 
 
 def fold_shift(facing):
@@ -151,7 +156,7 @@
     return jnp.take_along_axis(merged, cols - 1 - ((lane - shift) & (cols - 1)), axis=1)
 
 
-def krylov_kernel(used, meta, facing, ext, second, from_near, from_far, base, moments, folded):
+def krylov_kernel(used, meta, facing, ext, facing_rows, from_far, from_near, base, moments, folded):
     tall, cols = ext.shape[1], ext.shape[2]
     rows = base.shape[1]
     size = from_near.shape[0] - tall
@@ -160,15 +165,15 @@
     east = jnp.where(lon_odd, from_far[...], from_near[...])
     shift = fold_shift(facing)
     row = iota((size, cols), 0)
-    flips = (row >= DEEP * FLIPPED[0]) & (row < DEEP * (FLIPPED[-1] + 1))
+    flips = (row >= ROW[FLIPPED[0]]) & (row < ROW[FLIPPED[-1] + 1])
     for side in range(2):
-        cells = fold(shift, west[tall:], second[used:, :], east[tall:], side == 1)
+        cells = fold(shift, west[tall:], facing_rows[...], east[tall:], side == 1)
         folded[side, :size, :] = jnp.where(flips, -cells, cells)
     folded[:, size:, :] = jnp.zeros((2, folded.shape[1] - size, cols), jnp.float32)
     lane = iota((tall, cols), 1)
     first = lane == 0
     last = lane == cols - 1
-    kept = iota((8, cols), 0) < DEEP
+    eighth = iota((8, cols), 0)
 
     def load(f):
         at = used + START[f]
@@ -177,8 +182,8 @@
         beside = jnp.where(lane >= cols - SIDE[f], a, jnp.where(lane < SIDE[f], b, 0.0))
 
         def put(cells, side):
-            new = folded[side, DEEP * f : DEEP * f + 8, :]
-            new = jnp.where(kept, jnp.where(top, new, cells[rows : rows + 8]), 0.0)
+            new = folded[side, ROW[f] : ROW[f] + 8, :]
+            new = jnp.where(eighth < DEEP[f], jnp.where(top, new, cells[rows : rows + 8]), 0.0)
             return jnp.concatenate([cells[:rows], new, cells[rows + 8 :]], axis=0)
 
         return put(ext[f], 0), put(beside, 1)
@@ -251,22 +256,21 @@
 
 
 def step_kernel(
-    meta, spans, facing, heat, salt, zonal, merid, water, first, second, from_near, from_far,
+    meta, spans, facing, heat, salt, zonal, merid, water, north_came, south_rows, from_far, from_near,
     heat_out, salt_out, zonal_out, merid_out,
-    new_heat, new_salt, new_zonal, new_merid, north_rows, south_rows, sems,
+    new_heat, new_salt, new_zonal, new_merid, north_rows, sems,
 ):
     levels, rows, cols = heat.shape
     deep = 4 * levels
-    odd, top, lon_odd = flags(meta)
+    _, top, lon_odd = flags(meta)
     wet = water[...].astype(jnp.float32)
     lane = iota((rows, cols), 1)
     row = iota((rows, cols), 0)
     east = jnp.where(lon_odd, from_far[:rows, :], from_near[:rows, :])
     west = jnp.where(lon_odd, from_near[:rows, :], from_far[:rows, :])
-    from_second = second[:deep, :]
-    across = fold(fold_shift(facing), pltpu.roll(west[:deep], cols // 2, 1), from_second, east[:deep], False)
-    north_rows[...] = jnp.where(odd, jnp.where(top, across, from_second), first[:deep, :])
-    south_rows[...] = jnp.where(odd, first[:deep, :], from_second)
+    came = north_came[...]
+    across = fold(fold_shift(facing), pltpu.roll(west[:deep], cols // 2, 1), came, east[:deep], False)
+    north_rows[...] = jnp.where(top, across, came)
 
     def around(cells, q):
         a = pltpu.roll(east, (cols - 2 * q) % cols, 1)
@@ -435,17 +439,18 @@
     def exchange(shift, first, second):
         pairs_fold = [(flat(shift - 1 - i, lats - 1), flat(i, lats - 1)) for i in range(lons)]
         second = lax.ppermute(second, axes, pairs_inner + pairs_fold)
-        return lax.ppermute(first, axes, pairs_first), second
-
-    first, second = lax.switch(block, [functools.partial(exchange, s) for s in range(lons)], first, second)
-
-    ext, to_near, to_far = call(
+        return second, lax.ppermute(first, axes, pairs_first)
+
+    second, first = lax.switch(block, [functools.partial(exchange, s) for s in range(lons)], first, second)
+
+    deep = 4 * levels
+    ext, to_far, to_near, facing_rows, north_rows, south_rows = call(
         turn_kernel,
-        [(FIELDS, tall, cols), (long, cols), (long, cols)],
+        [(FIELDS, tall, cols), (long, cols), (long, cols), (high - deep, cols), (deep, cols), (deep, cols)],
         FIELDS * tall * cols,
         4 * 4 * FIELDS * tall * cols,
         "row_halos",
-    )(meta, sums, *flat_state, first, second, east_columns, west_columns)
+    )(meta, sums, *flat_state, second, first, east_columns, west_columns)
 
     from_far = lax.ppermute(to_far, "lon", [(i, (i + 1 if i % 2 else i - 1) % lons) for i in range(lons)])
     from_near = lax.ppermute(to_near, "lon", [(i, i ^ 1) for i in range(lons)])
@@ -457,8 +462,8 @@
         200 * tall * cols,
         4 * 12 * tall * cols,
         "krylov",
-        scratch=[pltpu.VMEM((2, high - 4 * levels + 8, cols), jnp.float32)],
-    )(meta, facing, ext, second, from_near, from_far)
+        scratch=[pltpu.VMEM((2, high - deep + 8, cols), jnp.float32)],
+    )(meta, facing, ext, facing_rows, from_far, from_near)
 
     chunks = 5 if levels % 5 == 0 else 1
     new_heat, new_salt, new_zonal, new_merid = call(
@@ -470,10 +475,10 @@
         out_space=pltpu.HBM,
         scratch=[
             *[pltpu.VMEM((levels, rows, cols), jnp.float32)] * 4,
-            *[pltpu.VMEM((4 * levels, cols), jnp.float32)] * 2,
+            pltpu.VMEM((deep, cols), jnp.float32),
             pltpu.SemaphoreType.DMA((4, chunks)),
         ],
-    )(meta, spans, facing, *state, water_indicator, first, second, from_near, from_far)
+    )(meta, spans, facing, *state, water_indicator, north_rows, south_rows, from_far, from_near)
 
     shares = lax.all_to_all(moments, axes, 0, 0, tiled=True)
     (surface,) = call(surface_kernel, [(rows, cols)], 6 * rows * cols, 16 * rows * cols, "surface")(shares, base)

time: 34.2 us -> 32.5 us (0.950)
  waiting for transfers between devices: 5.83 us -> 8.44 us
  starting transfers between devices: 16.9 us -> 14.4 us
  Pallas kernels: 8.92 us -> 7.36 us
    all_to_all x1, starting transfers between devices: 8.94 us -> 4.74 us  [body(): shares = lax.all_to_all(moments, axes, 0, 0, tiled=True)]
    ppermute x1, starting transfers between devices: 0.52 us -> 3.79 us  [exchange(): return (second, lax.ppermute(first, axes, pairs_first))]
    ppermute x1, starting transfers between devices: 2.64 us -> 0.01 us  [body(): from_near = lax.ppermute(to_near, 'lon', [(i, i ^ 1) for i in range(lons)])]
    pallas_call x6, Pallas kernels: 8.92 us -> 7.36 us  [run(): pl.pallas_call(kernel, out_shape=[jax.ShapeDtypeStruct(shape, types) for...]
    ppermute x1, waiting for transfers between devices: 0.01 us -> 1.52 us  [body(): from_near = lax.ppermute(to_near, 'lon', [(i, i ^ 1) for i in range(lons)])]
    ppermute x1, starting transfers between devices: 3.57 us -> 4.59 us  [body(): lax.ppermute(to_far, 'lon', [(i, (i + 1 if i % 2 else i - 1) % lons) for...]
    ppermute x1, waiting for transfers between devices: 0.01 us -> 0.99 us  [exchange(): return (second, lax.ppermute(first, axes, pairs_first))]
    all_to_all x1, waiting for transfers between devices: 2.53 us -> 3.31 us  [body(): shares = lax.all_to_all(moments, axes, 0, 0, tiled=True)]
  transfers between devices with their start and end apart: 5 -> 5, of which waited for: 2 -> 4; matrix products, arithmetic and copies ran while one was open for 0% -> 0% of each run, Pallas kernels for 13% -> 12%
where the time goes in v3:
time: 32.5 us; the launch traced here: 32.3 us
  starting transfers between devices  14.4 us (44%)
  waiting for transfers between devices  8.44 us (26%)
  Pallas kernels  7.36 us (23%)
  local copies, waits for them, and re-layouts  1.18 us (4%)
  between operations  0.8 us (2%)
    pallas_call x6, Pallas kernels, run(): pl.pallas_call(kernel, out_shape=[jax.ShapeDtypeStruct(shape, types) for...  7.36 us
    all_to_all x1, starting transfers between devices, body(): shares = lax.all_to_all(moments, axes, 0, 0, tiled=True)  4.74 us
    ppermute x1, starting transfers between devices, body(): lax.ppermute(to_far, 'lon', [(i, (i + 1 if i % 2 else i - 1) % lons) for...  4.59 us
    ppermute x1, starting transfers between devices, exchange(): return (second, lax.ppermute(first, axes, pairs_first))  3.79 us
    all_to_all x1, waiting for transfers between devices, body(): shares = lax.all_to_all(moments, axes, 0, 0, tiled=True)  3.31 us
    ppermute x1, waiting for transfers between devices, body(): lax.ppermute(to_far, 'lon', [(i, (i + 1 if i % 2 else i - 1) % lons) for...  2.63 us
    ppermute x1, waiting for transfers between devices, body(): from_near = lax.ppermute(to_near, 'lon', [(i, i ^ 1) for i in range(lons)])  1.52 us
    ppermute x1, starting transfers between devices, exchange(): second = lax.ppermute(second, axes, pairs_inner + pairs_fold)  1.28 us
  transfers between devices with their start and end apart: 5, of which 4 were waited for; matrix products, arithmetic and copies ran while one was open for 0% of the time, Pallas kernels for 12%

profile of v3, /device:TPU:0, one launch (start us, length us, event | category | flops | bytes accessed | tf_op | source)
XLA Modules:
  0.0 32.3 jit_solution(11359128981135669231)
XLA Ops:
  0.6 0.1 add_bitcast_fusion.meta
  0.7 0.0 copy-start
  0.7 0.0 copy-start.1
  0.7 0.0 copy-start.4
  0.7 0.0 copy-start.5
  0.8 0.0 copy-start.6
  0.8 0.1 place.1.meta
  0.8 0.8 %copy-done = f32[10,64,128]{2,1,0:T(8,128)S(1)} copy-done((f32[10,64,128]{2,1,0:T(8,128)S(1)}, f32[10,64,128]{2,1,0:T(8,128)}, u32[]{:S(2)}) %copy-start) | copy-done | bytes 327704
  1.7 0.1 copy-done.1
  1.8 0.1 copy-done.2
  1.9 0.1 copy-done.3
  2.0 0.0 copy-done.4
  2.0 0.0 copy-done.5
  2.0 0.0 copy-done.6
  2.0 0.0 copy-done.7
  2.0 0.0 copy-done.8
  2.0 0.5 %level_sums.1 = (f32[3,64,128]{2,1,0:T(8,128)S(1)}, f32[64,128]{1,0:T(8,128)S(1)}, f32[64,128]{1,0:T(8,128)S(1)}, f32[64,128]{1,0:T(8,128)S(1)}, f32[64,128]{1,0:T(8,128)S(1)}) custom-call(s32[8,128]{1,0:T(8,128)S(1)} %place.1.meta, f32[1,10]{1,0:T(1,128)S(1)} %bitcast.18, s32[1,128]{1,0:T(1,128)S(1)} %bitcast.14, f32[10,64,128]{2,1,0:T(8,128)S(1)} %copy-done, ...), custom_call_target="tpu_custom_call" | custom-call | flops 983040 | bytes 1310720 | tf_op jit(solution)/shard_map/level_sums/pallas_call | solution.py:373
  2.6 6.1 %conditional.1 = (f32[64,128]{1,0:T(8,128)}, f32[64,128]{1,0:T(8,128)}) conditional(s32[]{:T(128)} %clamp.3, (f32[64,128]{1,0:T(8,128)S(1)}, f32[64,128]{1,0:T(8,128)S(1)}) %tuple.42, (f32[64,128]{1,0:T(8,128)S(1)}, f32[64,128]{1,0:T(8,128)S(1)}) %tuple.42, (f32[64,128]{1,0:T(8,128)S(1)}, ...), branch_computations={%region_0.1_spmd, %region_1.2_spmd, %region_2.3_spmd, %region_3.4_... | conditional | bytes 262240 | solution.py:444
  2.6 1.3 %collective-permute-start.8 = (f32[64,128]{1,0:T(8,128)S(1)}, f32[64,128]{1,0:T(8,128)}, u32[]{:S(2)}, u32[]{:S(2)}) collective-permute-start(f32[64,128]{1,0:T(8,128)S(1)} %get-tuple-element.40), channel_id=1, source_target_pairs={{1,2},{2,1},{5,6},{6,5},{9,10},{10,9},{13,14},{14,13},{17,18},{18,... | collective-permute-start | bytes 98312 | tf_op jit(solution)/shard_map/cond/branch_4_fun/ppermute | solution.py:441
  3.9 3.8 %collective-permute-start.9 = (f32[64,128]{1,0:T(8,128)S(1)}, f32[64,128]{1,0:T(8,128)}, u32[]{:S(2)}, u32[]{:S(2)}) collective-permute-start(f32[64,128]{1,0:T(8,128)S(1)} %get-tuple-element.41), channel_id=1, source_target_pairs={{0,1},{1,0},{2,3},{3,2},{4,5},{5,4},{6,7},{7,6},{8,9},{9,8},{10,11... | collective-permute-start | bytes 98312 | tf_op jit(solution)/shard_map/cond/branch_4_fun/ppermute | solution.py:442
  7.7 0.0 collective-permute-done.8
  7.7 1.0 %collective-permute-done.9 = f32[64,128]{1,0:T(8,128)} collective-permute-done((f32[64,128]{1,0:T(8,128)S(1)}, f32[64,128]{1,0:T(8,128)}, u32[]{:S(2)}, u32[]{:S(2)}) %collective-permute-start.9) | collective-permute-done | bytes 32800 | tf_op jit(solution)/shard_map/cond/branch_4_fun/ppermute | solution.py:442
  8.7 1.0 %row_halos.1 = (f32[6,80,128]{2,1,0:T(8,128)S(1)}, f32[104,128]{1,0:T(8,128)S(1)}, f32[104,128]{1,0:T(8,128)S(1)}, f32[24,128]{1,0:T(8,128)S(1)}, f32[40,128]{1,0:T(8,128)S(1)}, /*index=5*/f32[40,128]{1,0:T(8,128)S(1)}) custom-call(s32[8,128]{1,0:T(8,128)S(1)} %place.1.meta, f32[3,64,128]{2,1,0:T(8,128)S(1)} %get-tuple-element.74.sums, ...), custom_call_target="tpu_custom_call" | custom-call | flops 61440 | bytes 983040 | tf_op jit(solution)/shard_map/row_halos/pallas_call | solution.py:373
  9.7 4.6 %collective-permute-start.16 = (f32[104,128]{1,0:T(8,128)S(1)}, f32[104,128]{1,0:T(8,128)S(1)}, u32[]{:S(2)}, u32[]{:S(2)}) collective-permute-start(f32[104,128]{1,0:T(8,128)S(1)} %get-tuple-element.85), channel_id=1, source_target_pairs={{0,28},{4,8},{8,4},{12,16},{16,12},{20,24},{24,20},{28,0},{1,29},{... | collective-permute-start | bytes 159752 | tf_op jit(solution)/shard_map/ppermute | solution.py:455
  14.3 0.0 collective-permute-start.17
  14.3 2.6 %collective-permute-done.16.from_far = f32[104,128]{1,0:T(8,128)S(1)} collective-permute-done((f32[104,128]{1,0:T(8,128)S(1)}, f32[104,128]{1,0:T(8,128)S(1)}, u32[]{:S(2)}, u32[]{:S(2)}) %collective-permute-start.16) | collective-permute-done | bytes 53280 | tf_op jit(solution)/shard_map/ppermute | solution.py:455
  16.9 1.5 %collective-permute-done.17.from_near = f32[104,128]{1,0:T(8,128)S(1)} collective-permute-done((f32[104,128]{1,0:T(8,128)S(1)}, f32[104,128]{1,0:T(8,128)S(1)}, u32[]{:S(2)}, u32[]{:S(2)}) %collective-permute-start.17) | collective-permute-done | bytes 53280 | tf_op jit(solution)/shard_map/ppermute | solution.py:456
  18.4 1.3 %krylov.1 = (f32[3,64,128]{2,1,0:T(8,128)S(1)}, f32[32,128]{1,0:T(8,128)}) custom-call(s32[8,128]{1,0:T(8,128)S(1)} %place.1.meta, s32[1,128]{1,0:T(1,128)S(1)} %bitcast.16, f32[6,80,128]{2,1,0:T(8,128)S(1)} %get-tuple-element.91.ext, f32[24,128]{1,0:T(8,128)S(1)} %get-tuple-element.92.facing_rows, f32[104,128]{1,0:T(8,128)S(1)} %collective-permute-done.16.from_far, ...), custom_call_target="tpu_custom_call" | custom-call | flops 2048000 | bytes 491520 | tf_op jit(solution)/shard_map/krylov/pallas_call | solution.py:373
  19.7 4.7 %all-to-all-start = ((f32[32,1,128]{2,1,0:T(1,128)}), f32[32,1,128]{2,1,0:T(1,128)S(1)}, u32[]{:S(2)}, u32[]{:S(2)}) async-start(f32[32,1,128]{2,1,0:T(1,128)} %bitcast.8), calls=%async_computation | async-start | bytes 32768 | tf_op jit(solution)/shard_map/all_to_all | solution.py:483
  24.4 3.8 %levels_step.1 = (f32[10,64,128]{2,1,0:T(8,128)}, f32[10,64,128]{2,1,0:T(8,128)}, f32[10,64,128]{2,1,0:T(8,128)}, f32[10,64,128]{2,1,0:T(8,128)}) custom-call(s32[8,128]{1,0:T(8,128)S(1)} %place.1.meta, f32[1,10]{1,0:T(1,128)S(1)} %bitcast.19, s32[1,128]{1,0:T(1,128)S(1)} %bitcast.17, f32[10,64,128]{2,1,0:T(8,128)S(1)} %copy-done, ...), custom_call_target="tpu_custom_call" | custom-call | flops 9830400 | bytes 2621440 | tf_op jit(solution)/shard_map/levels_step/pallas_call | solution.py:373
  28.2 3.3 %all-to-all-done = f32[32,1,128]{2,1,0:T(1,128)S(1)} async-done(((f32[32,1,128]{2,1,0:T(1,128)}), f32[32,1,128]{2,1,0:T(1,128)S(1)}, u32[]{:S(2)}, u32[]{:S(2)}) %all-to-all-start) | async-done | bytes 16416 | tf_op jit(solution)/shard_map/all_to_all | solution.py:483
  31.5 0.8 %surface.1 = f32[64,128]{1,0:T(8,128)} custom-call(f32[32,128]{1,0:T(8,128)S(1)} %bitcast.13, f32[3,64,128]{2,1,0:T(8,128)S(1)} %get-tuple-element.94.base), custom_call_target="tpu_custom_call" | custom-call | flops 49152 | bytes 131072 | tf_op jit(solution)/shard_map/surface/pallas_call | solution.py:373
  (4 shorter events, 0.0 us)
Async XLA Ops:
  0.7 1.0 %copy-start = (f32[10,64,128]{2,1,0:T(8,128)S(1)}, f32[10,64,128]{2,1,0:T(8,128)}, u32[]{:S(2)}) copy-start(f32[10,64,128]{2,1,0:T(8,128)} %heat.3) | copy-start | bytes 983044
  0.7 1.1 %copy-start.1 = (f32[10,64,128]{2,1,0:T(8,128)S(1)}, f32[10,64,128]{2,1,0:T(8,128)}, u32[]{:S(2)}) copy-start(f32[10,64,128]{2,1,0:T(8,128)} %salt.3) | copy-start | bytes 983044
  0.7 1.2 %copy-start.2 = (f32[10,64,128]{2,1,0:T(8,128)S(1)}, f32[10,64,128]{2,1,0:T(8,128)}, u32[]{:S(2)}) copy-start(f32[10,64,128]{2,1,0:T(8,128)} %zonal.3) | copy-start | bytes 983044
  0.7 1.3 %copy-start.3 = (f32[10,64,128]{2,1,0:T(8,128)S(1)}, f32[10,64,128]{2,1,0:T(8,128)}, u32[]{:S(2)}) copy-start(f32[10,64,128]{2,1,0:T(8,128)} %merid.3) | copy-start | bytes 983044
  0.7 1.3 %copy-start.4 = (s32[64,128]{1,0:T(8,128)S(1)}, s32[64,128]{1,0:T(8,128)}, u32[]{:S(2)}) copy-start(s32[64,128]{1,0:T(8,128)} %water.5) | copy-start | bytes 98308
  0.7 1.3 %copy-start.5 = (f32[64,128]{1,0:T(8,128)S(1)}, f32[64,128]{1,0:T(8,128)}, u32[]{:S(2)}) copy-start(f32[64,128]{1,0:T(8,128)} %weights.3) | copy-start | bytes 98308
  0.8 1.2 %copy-start.6 = (f32[64,128]{1,0:T(8,128)S(1)}, f32[64,128]{1,0:T(8,128)}, u32[]{:S(2)}) copy-start(f32[64,128]{1,0:T(8,128)} %anomaly.3) | copy-start | bytes 98308
  0.8 1.2 %copy-start.7 = (s32[128]{0:T(128)S(1)}, s32[128]{0:T(128)}, u32[]{:S(2)}) copy-start(s32[128]{0:T(128)} %param.23) | copy-start | bytes 1540
  0.8 1.2 %copy-start.8 = (f32[10]{0:T(128)S(1)}, f32[10]{0:T(128)}, u32[]{:S(2)}) copy-start(f32[10]{0:T(128)} %param.21) | copy-start | bytes 124
  2.6 5.1 %collective-permute-start.8 = (f32[64,128]{1,0:T(8,128)S(1)}, f32[64,128]{1,0:T(8,128)}, u32[]{:S(2)}, u32[]{:S(2)}) collective-permute-start(f32[64,128]{1,0:T(8,128)S(1)} %get-tuple-element.40), channel_id=1, source_target_pairs={{1,2},{2,1},{5,6},{6,5},{9,10},{10,9},{13,14},{14,13},{17,18},{18,... | collective-permute-start | bytes 98312 | tf_op jit(solution)/shard_map/cond/branch_4_fun/ppermute | solution.py:441
  3.9 4.8 %collective-permute-start.9 = (f32[64,128]{1,0:T(8,128)S(1)}, f32[64,128]{1,0:T(8,128)}, u32[]{:S(2)}, u32[]{:S(2)}) collective-permute-start(f32[64,128]{1,0:T(8,128)S(1)} %get-tuple-element.41), channel_id=1, source_target_pairs={{0,1},{1,0},{2,3},{3,2},{4,5},{5,4},{6,7},{7,6},{8,9},{9,8},{10,11... | collective-permute-start | bytes 98312 | tf_op jit(solution)/shard_map/cond/branch_4_fun/ppermute | solution.py:442
  9.7 7.2 %collective-permute-start.16 = (f32[104,128]{1,0:T(8,128)S(1)}, f32[104,128]{1,0:T(8,128)S(1)}, u32[]{:S(2)}, u32[]{:S(2)}) collective-permute-start(f32[104,128]{1,0:T(8,128)S(1)} %get-tuple-element.85), channel_id=1, source_target_pairs={{0,28},{4,8},{8,4},{12,16},{16,12},{20,24},{24,20},{28,0},{1,29},{... | collective-permute-start | bytes 159752 | tf_op jit(solution)/shard_map/ppermute | solution.py:455
  14.3 4.1 %collective-permute-start.17 = (f32[104,128]{1,0:T(8,128)S(1)}, f32[104,128]{1,0:T(8,128)S(1)}, u32[]{:S(2)}, u32[]{:S(2)}) collective-permute-start(f32[104,128]{1,0:T(8,128)S(1)} %get-tuple-element.86), channel_id=1, source_target_pairs={{0,4},{4,0},{8,12},{12,8},{16,20},{20,16},{24,28},{28,24},{1,5},{5... | collective-permute-start | bytes 159752 | tf_op jit(solution)/shard_map/ppermute | solution.py:456
  19.7 11.8 %all-to-all-start = ((f32[32,1,128]{2,1,0:T(1,128)}), f32[32,1,128]{2,1,0:T(1,128)S(1)}, u32[]{:S(2)}, u32[]{:S(2)}) async-start(f32[32,1,128]{2,1,0:T(1,128)} %bitcast.8), calls=%async_computation | async-start | bytes 32768 | tf_op jit(solution)/shard_map/all_to_all | solution.py:483

commit v4 on v3

--- a/solution.py
+++ b/solution.py
@@ -14,7 +14,8 @@
 SIDE = (5, 4, 3, 4, 3, 3)
 FIELDS = len(SIDE)
 ROW = tuple(sum(DEEP[:f]) for f in range(FIELDS + 1))
-START = tuple(sum(SIDE[:f]) for f in range(FIELDS))
+START = tuple(sum(SIDE[:f]) for f in range(FIELDS + 1))
+RELAY = 56
 FLIPPED = (1, 2)
 VMEM_LIMIT = 32 * 1024 * 1024
 LOAD_FLOPS = 10**10
@@ -95,7 +96,7 @@
 
 def turn_kernel(
     meta, sums, water, weights, anomaly, second, first, east_columns, west_columns,
-    ext, to_far, to_near, facing_rows, north_rows, south_rows,
+    ext, to_far, to_near, state_far, state_near, facing_rows, north_rows, south_rows,
 ):
     rows, cols = sums.shape[1], sums.shape[2]
     tall = ext.shape[1]
@@ -113,25 +114,29 @@
         ext[f, rows : rows + size, :] = north[at : at + size]
         ext[f, rows + size : tall - size, :] = jnp.zeros((tall - rows - 2 * size, cols), jnp.float32)
         ext[f, tall - size :, :] = south[at : at + size]
-    lane = iota((tall, cols), 1)
-    spare = jnp.zeros((tall - rows, cols), jnp.float32)
+    middle = tall // 2
+    passed = from_second[deep:]
+    spare = jnp.zeros((middle - passed.shape[0], cols), jnp.float32)
+    lane = iota((middle, cols), 1)
+    relay = lane >= RELAY
+    east = jnp.where(relay, jnp.concatenate([pltpu.roll(passed, RELAY, 1), spare], axis=0), 0.0)
+    west = jnp.where(relay, jnp.concatenate([passed, spare], axis=0), 0.0)
+    for f in range(FIELDS):
+        for part in range(2):
+            at = START[f] + part * START[-1]
+            here = (lane >= at) & (lane < at + SIDE[f])
+            layer = ext[f, part * middle : (part + 1) * middle, :]
+            east = jnp.where(here, pltpu.roll(layer, (at + SIDE[f]) % cols, 1), east)
+            west = jnp.where(here, pltpu.roll(layer, at, 1), west)
+    to_far[...] = jnp.where(lon_odd, east, west)
+    to_near[...] = jnp.where(lon_odd, west, east)
     passed = from_second[:deep]
-    fill = jnp.zeros((tall - deep, cols), jnp.float32)
-    half = lane >= cols // 2
-    east = jnp.where(half, jnp.concatenate([pltpu.roll(passed, cols // 2, 1), fill], axis=0),
-                     jnp.concatenate([east_columns[...], spare], axis=0))
-    west = jnp.where(half, jnp.concatenate([passed, fill], axis=0),
-                     jnp.concatenate([west_columns[...], spare], axis=0))
-    for f in range(FIELDS):
-        at = deep + START[f]
-        here = (lane >= at) & (lane < at + SIDE[f])
-        layer = ext[f]
-        east = jnp.where(here, pltpu.roll(layer, (at + SIDE[f]) % cols, 1), east)
-        west = jnp.where(here, pltpu.roll(layer, at, 1), west)
-    to_near[:tall, :] = jnp.where(lon_odd, west, east)
-    to_far[:tall, :] = jnp.where(lon_odd, east, west)
-    to_near[tall:, :] = from_second[deep:]
-    to_far[tall:, :] = from_second[deep:]
+    spare = jnp.zeros((rows - deep, cols), jnp.float32)
+    half = iota((rows, cols), 1) >= cols // 2
+    east = jnp.where(half, jnp.concatenate([pltpu.roll(passed, cols // 2, 1), spare], axis=0), east_columns[...])
+    west = jnp.where(half, jnp.concatenate([passed, spare], axis=0), west_columns[...])
+    state_far[...] = jnp.where(lon_odd, east, west)
+    state_near[...] = jnp.where(lon_odd, west, east)
     facing_rows[...] = from_second[deep:]
     north_rows[...] = north[:deep]
     south_rows[...] = south[:deep]
@@ -156,10 +161,11 @@
     return jnp.take_along_axis(merged, cols - 1 - ((lane - shift) & (cols - 1)), axis=1)
 
 
-def krylov_kernel(used, meta, facing, ext, facing_rows, from_far, from_near, base, moments, folded):
+def krylov_kernel(meta, facing, ext, facing_rows, from_far, from_near, base, moments, folded):
     tall, cols = ext.shape[1], ext.shape[2]
     rows = base.shape[1]
-    size = from_near.shape[0] - tall
+    size = facing_rows.shape[0]
+    middle = tall // 2
     _, top, lon_odd = flags(meta)
     west = jnp.where(lon_odd, from_near[...], from_far[...])
     east = jnp.where(lon_odd, from_far[...], from_near[...])
@@ -167,7 +173,7 @@
     row = iota((size, cols), 0)
     flips = (row >= ROW[FLIPPED[0]]) & (row < ROW[FLIPPED[-1] + 1])
     for side in range(2):
-        cells = fold(shift, west[tall:], facing_rows[...], east[tall:], side == 1)
+        cells = fold(shift, pltpu.roll(west[:size], cols - RELAY, 1), facing_rows[...], east[:size], side == 1)
         folded[side, :size, :] = jnp.where(flips, -cells, cells)
     folded[:, size:, :] = jnp.zeros((2, folded.shape[1] - size, cols), jnp.float32)
     lane = iota((tall, cols), 1)
@@ -176,9 +182,9 @@
     eighth = iota((8, cols), 0)
 
     def load(f):
-        at = used + START[f]
-        a = pltpu.roll(west[:tall], (2 * cols - SIDE[f] - at) % cols, 1)
-        b = pltpu.roll(east[:tall], (cols - at) % cols, 1)
+        both = [START[f], START[f] + START[-1]]
+        a = jnp.concatenate([pltpu.roll(west, (2 * cols - SIDE[f] - at) % cols, 1) for at in both], axis=0)
+        b = jnp.concatenate([pltpu.roll(east, (cols - at) % cols, 1) for at in both], axis=0)
         beside = jnp.where(lane >= cols - SIDE[f], a, jnp.where(lane < SIDE[f], b, 0.0))
 
         def put(cells, side):
@@ -266,8 +272,8 @@
     wet = water[...].astype(jnp.float32)
     lane = iota((rows, cols), 1)
     row = iota((rows, cols), 0)
-    east = jnp.where(lon_odd, from_far[:rows, :], from_near[:rows, :])
-    west = jnp.where(lon_odd, from_near[:rows, :], from_far[:rows, :])
+    east = jnp.where(lon_odd, from_far[...], from_near[...])
+    west = jnp.where(lon_odd, from_near[...], from_far[...])
     came = north_came[...]
     across = fold(fold_shift(facing), pltpu.roll(west[:deep], cols // 2, 1), came, east[:deep], False)
     north_rows[...] = jnp.where(top, across, came)
@@ -398,10 +404,9 @@
     lons, lats = lax.axis_size("lon"), lax.axis_size("lat")
     lon, lat = lax.axis_index("lon"), lax.axis_index("lat")
     levels, rows, cols = warmth_deviation.shape
-    assert cols & (cols - 1) == 0 and 4 * levels + sum(SIDE) <= cols // 2
+    assert cols & (cols - 1) == 0 and 4 * levels <= cols // 2 and 2 * START[-1] <= RELAY and cols == 128
     high = packet_rows(levels)
     tall = rows + 16
-    long = tall + high - 4 * levels
     width = cols * lons
     flat = lambda i, j: (i % lons) * lats + j
 
@@ -444,20 +449,28 @@
     second, first = lax.switch(block, [functools.partial(exchange, s) for s in range(lons)], first, second)
 
     deep = 4 * levels
-    ext, to_far, to_near, facing_rows, north_rows, south_rows = call(
+    ext, to_far, to_near, state_far, state_near, facing_rows, north_rows, south_rows = call(
         turn_kernel,
-        [(FIELDS, tall, cols), (long, cols), (long, cols), (high - deep, cols), (deep, cols), (deep, cols)],
+        [
+            (FIELDS, tall, cols),
+            *[(tall // 2, cols)] * 2,
+            *[(rows, cols)] * 2,
+            (high - deep, cols),
+            *[(deep, cols)] * 2,
+        ],
         FIELDS * tall * cols,
         4 * 4 * FIELDS * tall * cols,
         "row_halos",
     )(meta, sums, *flat_state, second, first, east_columns, west_columns)
 
-    from_far = lax.ppermute(to_far, "lon", [(i, (i + 1 if i % 2 else i - 1) % lons) for i in range(lons)])
-    from_near = lax.ppermute(to_near, "lon", [(i, i ^ 1) for i in range(lons)])
+    near = lambda cells: lax.ppermute(cells, "lon", [(i, i ^ 1) for i in range(lons)])
+    far = lambda cells: lax.ppermute(cells, "lon", [(i, (i + 1 if i % 2 else i - 1) % lons) for i in range(lons)])
+    from_far, from_near = far(to_far), near(to_near)
+    state_far, state_near = far(state_far), near(state_near)
 
     count = lons * lats
     base, moments = call(
-        functools.partial(krylov_kernel, 4 * levels),
+        krylov_kernel,
         [(3, rows, cols), (count, cols)],
         200 * tall * cols,
         4 * 12 * tall * cols,
@@ -478,7 +491,7 @@
             pltpu.VMEM((deep, cols), jnp.float32),
             pltpu.SemaphoreType.DMA((4, chunks)),
         ],
-    )(meta, spans, facing, *state, water_indicator, north_rows, south_rows, from_far, from_near)
+    )(meta, spans, facing, *state, water_indicator, north_rows, south_rows, state_far, state_near)
 
     shares = lax.all_to_all(moments, axes, 0, 0, tiled=True)
     (surface,) = call(surface_kernel, [(rows, cols)], 6 * rows * cols, 16 * rows * cols, "surface")(shares, base)

time: 32.5 us -> 32.3 us (level)
  waiting for transfers between devices: 8.44 us -> 6.04 us
  starting transfers between devices: 14.4 us -> 16.5 us
    ppermute x2 -> x4, waiting for transfers between devices: 4.14 us -> 1.76 us  [the longest x2 1.75 us: body(): lax.ppermute(cells, 'lon', [(i, i ^ 1) for i in range(lons)])]
    ppermute x2 -> x4, starting transfers between devices: 4.6 us -> 6.64 us  [the longest x2 6.52 us: body(): lax.ppermute(cells, 'lon', [(i, (i + 1 if i % 2 else i - 1) % lons) for i...]
  transfers between devices with their start and end apart: 5 -> 7, of which waited for: 4 -> 3; matrix products, arithmetic and copies ran while one was open for 0% -> 0% of each run, Pallas kernels for 12% -> 16%
where the time goes in v4:
time: 32.3 us; the launch traced here: 32 us
  starting transfers between devices  16.5 us (51%)
  Pallas kernels  7.35 us (23%)
  waiting for transfers between devices  6.04 us (19%)
  local copies, waits for them, and re-layouts  1.18 us (4%)
  between operations  0.82 us (3%)
    pallas_call x6, Pallas kernels, run(): pl.pallas_call(kernel, out_shape=[jax.ShapeDtypeStruct(shape, types) for...  7.35 us
    ppermute x2, starting transfers between devices, body(): lax.ppermute(cells, 'lon', [(i, (i + 1 if i % 2 else i - 1) % lons) for i...  6.52 us
    all_to_all x1, starting transfers between devices, body(): shares = lax.all_to_all(moments, axes, 0, 0, tiled=True)  4.85 us
    ppermute x1, starting transfers between devices, exchange(): return (second, lax.ppermute(first, axes, pairs_first))  3.78 us
    all_to_all x1, waiting for transfers between devices, body(): shares = lax.all_to_all(moments, axes, 0, 0, tiled=True)  3.29 us
    ppermute x2, waiting for transfers between devices, body(): lax.ppermute(cells, 'lon', [(i, i ^ 1) for i in range(lons)])  1.75 us
    ppermute x1, starting transfers between devices, exchange(): second = lax.ppermute(second, axes, pairs_inner + pairs_fold)  1.28 us
    unnamed x18, local copies, waits for them, and re-layouts  1.18 us
  transfers between devices with their start and end apart: 7, of which 3 were waited for; matrix products, arithmetic and copies ran while one was open for 0% of the time, Pallas kernels for 16%

profile of v4, /device:TPU:0, one launch (start us, length us, event | category | flops | bytes accessed | tf_op | source)
XLA Modules:
  0.0 32.0 jit_solution(3548832064587948447)
XLA Ops:
  0.6 0.1 add_bitcast_fusion.meta
  0.7 0.0 copy-start.4
  0.7 0.0 copy-start.5
  0.8 0.0 copy-start.6
  0.8 0.1 place.1.meta
  0.8 0.8 %copy-done = f32[10,64,128]{2,1,0:T(8,128)S(1)} copy-done((f32[10,64,128]{2,1,0:T(8,128)S(1)}, f32[10,64,128]{2,1,0:T(8,128)}, u32[]{:S(2)}) %copy-start) | copy-done | bytes 327704
  1.7 0.1 copy-done.1
  1.8 0.1 copy-done.2
  1.9 0.1 copy-done.3
  2.0 0.0 copy-done.4
  2.0 0.0 copy-done.5
  2.0 0.0 copy-done.6
  2.0 0.5 %level_sums.1 = (f32[3,64,128]{2,1,0:T(8,128)S(1)}, f32[64,128]{1,0:T(8,128)S(1)}, f32[64,128]{1,0:T(8,128)S(1)}, f32[64,128]{1,0:T(8,128)S(1)}, f32[64,128]{1,0:T(8,128)S(1)}) custom-call(s32[8,128]{1,0:T(8,128)S(1)} %place.1.meta, f32[1,10]{1,0:T(1,128)S(1)} %bitcast.18, s32[1,128]{1,0:T(1,128)S(1)} %bitcast.14, f32[10,64,128]{2,1,0:T(8,128)S(1)} %copy-done, ...), custom_call_target="tpu_custom_call" | custom-call | flops 983040 | bytes 1310720 | tf_op jit(solution)/shard_map/level_sums/pallas_call | solution.py:379
  2.6 6.1 %conditional.1 = (f32[64,128]{1,0:T(8,128)}, f32[64,128]{1,0:T(8,128)}) conditional(s32[]{:T(128)} %clamp.3, (f32[64,128]{1,0:T(8,128)S(1)}, f32[64,128]{1,0:T(8,128)S(1)}) %tuple.42, (f32[64,128]{1,0:T(8,128)S(1)}, f32[64,128]{1,0:T(8,128)S(1)}) %tuple.42, (f32[64,128]{1,0:T(8,128)S(1)}, ...), branch_computations={%region_0.1_spmd, %region_1.2_spmd, %region_2.3_spmd, %region_3.4_... | conditional | bytes 262240 | solution.py:449
  2.7 1.3 %collective-permute-start.12 = (f32[64,128]{1,0:T(8,128)S(1)}, f32[64,128]{1,0:T(8,128)}, u32[]{:S(2)}, u32[]{:S(2)}) collective-permute-start(f32[64,128]{1,0:T(8,128)S(1)} %get-tuple-element.44), channel_id=1, source_target_pairs={{1,2},{2,1},{5,6},{6,5},{9,10},{10,9},{13,14},{14,13},{17,18},{18,... | collective-permute-start | bytes 98312 | tf_op jit(solution)/shard_map/cond/branch_6_fun/ppermute | solution.py:446
  3.9 3.8 %collective-permute-start.13 = (f32[64,128]{1,0:T(8,128)S(1)}, f32[64,128]{1,0:T(8,128)}, u32[]{:S(2)}, u32[]{:S(2)}) collective-permute-start(f32[64,128]{1,0:T(8,128)S(1)} %get-tuple-element.45), channel_id=1, source_target_pairs={{0,1},{1,0},{2,3},{3,2},{4,5},{5,4},{6,7},{7,6},{8,9},{9,8},{10,11... | collective-permute-start | bytes 98312 | tf_op jit(solution)/shard_map/cond/branch_6_fun/ppermute | solution.py:447
  7.7 0.0 collective-permute-done.12
  7.7 1.0 %collective-permute-done.13 = f32[64,128]{1,0:T(8,128)} collective-permute-done((f32[64,128]{1,0:T(8,128)S(1)}, f32[64,128]{1,0:T(8,128)}, u32[]{:S(2)}, u32[]{:S(2)}) %collective-permute-start.13) | collective-permute-done | bytes 32800 | tf_op jit(solution)/shard_map/cond/branch_6_fun/ppermute | solution.py:447
  8.7 1.0 %row_halos.1 = (f32[6,80,128]{2,1,0:T(8,128)S(1)}, f32[40,128]{1,0:T(8,128)S(1)}, f32[40,128]{1,0:T(8,128)S(1)}, f32[64,128]{1,0:T(8,128)S(1)}, f32[64,128]{1,0:...) custom-call(s32[8,128]{1,0:T(8,128)S(1)} %place.1.meta, ...), custom_call_target="tpu_custom_call" | custom-call | flops 61440 | bytes 983040 | tf_op jit(solution)/shard_map/row_halos/pallas_call | solution.py:379
  9.7 4.6 %collective-permute-start.18 = (f32[40,128]{1,0:T(8,128)S(1)}, f32[40,128]{1,0:T(8,128)S(1)}, u32[]{:S(2)}, u32[]{:S(2)}) collective-permute-start(f32[40,128]{1,0:T(8,128)S(1)} %get-tuple-element.95), channel_id=1, source_target_pairs={{0,28},{4,8},{8,4},{12,16},{16,12},{20,24},{24,20},{28,0},{1,29},{... | collective-permute-start | bytes 61448 | tf_op jit(solution)/shard_map/ppermute | solution.py:467
  14.3 0.0 collective-permute-start.19
  14.3 1.9 %collective-permute-start.16 = (f32[64,128]{1,0:T(8,128)S(1)}, f32[64,128]{1,0:T(8,128)S(1)}, u32[]{:S(2)}, u32[]{:S(2)}) collective-permute-start(f32[64,128]{1,0:T(8,128)S(1)} %get-tuple-element.87), channel_id=1, source_target_pairs={{0,28},{4,8},{8,4},{12,16},{16,12},{20,24},{24,20},{28,0},{1,29},{... | collective-permute-start | bytes 98312 | tf_op jit(solution)/shard_map/ppermute | solution.py:467
  16.2 0.1 collective-permute-start.17
  16.3 0.0 collective-permute-done.18.from_far
  16.3 1.7 %collective-permute-done.19.from_near = f32[40,128]{1,0:T(8,128)S(1)} collective-permute-done((f32[40,128]{1,0:T(8,128)S(1)}, f32[40,128]{1,0:T(8,128)S(1)}, u32[]{:S(2)}, u32[]{:S(2)}) %collective-permute-start.19) | collective-permute-done | bytes 20512 | tf_op jit(solution)/shard_map/ppermute | solution.py:466
  18.1 1.2 %krylov.1 = (f32[3,64,128]{2,1,0:T(8,128)S(1)}, f32[32,128]{1,0:T(8,128)}) custom-call(s32[8,128]{1,0:T(8,128)S(1)} %place.1.meta, s32[1,128]{1,0:T(1,128)S(1)} %bitcast.16, f32[6,80,128]{2,1,0:T(8,128)S(1)} %get-tuple-element.93.ext, f32[24,128]{1,0:T(8,128)S(1)} %get-tuple-element.94.facing_rows, f32[40,128]{1,0:T(8,128)S(1)} %collective-permute-done.18.from_far, ...), custom_call_target="tpu_custom_call" | custom-call | flops 2048000 | bytes 491520 | tf_op jit(solution)/shard_map/krylov/pallas_call | solution.py:379
  19.3 4.8 %all-to-all-start = ((f32[32,1,128]{2,1,0:T(1,128)}), f32[32,1,128]{2,1,0:T(1,128)S(1)}, u32[]{:S(2)}, u32[]{:S(2)}) async-start(f32[32,1,128]{2,1,0:T(1,128)} %bitcast.8), calls=%async_computation | async-start | bytes 32768 | tf_op jit(solution)/shard_map/all_to_all | solution.py:496
  24.2 0.0 collective-permute-done.16.from_far
  24.2 0.0 collective-permute-done.17.from_near
  24.2 3.8 %levels_step.1 = (f32[10,64,128]{2,1,0:T(8,128)}, f32[10,64,128]{2,1,0:T(8,128)}, f32[10,64,128]{2,1,0:T(8,128)}, f32[10,64,128]{2,1,0:T(8,128)}) custom-call(s32[8,128]{1,0:T(8,128)S(1)} %place.1.meta, f32[1,10]{1,0:T(1,128)S(1)} %bitcast.19, s32[1,128]{1,0:T(1,128)S(1)} %bitcast.17, f32[10,64,128]{2,1,0:T(8,128)S(1)} %copy-done, ...), custom_call_target="tpu_custom_call" | custom-call | flops 9830400 | bytes 2621440 | tf_op jit(solution)/shard_map/levels_step/pallas_call | solution.py:379
  28.0 3.3 %all-to-all-done = f32[32,1,128]{2,1,0:T(1,128)S(1)} async-done(((f32[32,1,128]{2,1,0:T(1,128)}), f32[32,1,128]{2,1,0:T(1,128)S(1)}, u32[]{:S(2)}, u32[]{:S(2)}) %all-to-all-start) | async-done | bytes 16416 | tf_op jit(solution)/shard_map/all_to_all | solution.py:496
  31.3 0.8 %surface.1 = f32[64,128]{1,0:T(8,128)} custom-call(f32[32,128]{1,0:T(8,128)S(1)} %bitcast.13, f32[3,64,128]{2,1,0:T(8,128)S(1)} %get-tuple-element.98.base), custom_call_target="tpu_custom_call" | custom-call | flops 49152 | bytes 131072 | tf_op jit(solution)/shard_map/surface/pallas_call | solution.py:379
  (8 shorter events, 0.0 us)
Async XLA Ops:
  0.7 1.0 %copy-start = (f32[10,64,128]{2,1,0:T(8,128)S(1)}, f32[10,64,128]{2,1,0:T(8,128)}, u32[]{:S(2)}) copy-start(f32[10,64,128]{2,1,0:T(8,128)} %heat.3) | copy-start | bytes 983044
  0.7 1.1 %copy-start.1 = (f32[10,64,128]{2,1,0:T(8,128)S(1)}, f32[10,64,128]{2,1,0:T(8,128)}, u32[]{:S(2)}) copy-start(f32[10,64,128]{2,1,0:T(8,128)} %salt.3) | copy-start | bytes 983044
  0.7 1.2 %copy-start.2 = (f32[10,64,128]{2,1,0:T(8,128)S(1)}, f32[10,64,128]{2,1,0:T(8,128)}, u32[]{:S(2)}) copy-start(f32[10,64,128]{2,1,0:T(8,128)} %zonal.3) | copy-start | bytes 983044
  0.7 1.3 %copy-start.3 = (f32[10,64,128]{2,1,0:T(8,128)S(1)}, f32[10,64,128]{2,1,0:T(8,128)}, u32[]{:S(2)}) copy-start(f32[10,64,128]{2,1,0:T(8,128)} %merid.3) | copy-start | bytes 983044
  0.7 1.3 %copy-start.4 = (s32[64,128]{1,0:T(8,128)S(1)}, s32[64,128]{1,0:T(8,128)}, u32[]{:S(2)}) copy-start(s32[64,128]{1,0:T(8,128)} %water.5) | copy-start | bytes 98308
  0.7 1.3 %copy-start.5 = (f32[64,128]{1,0:T(8,128)S(1)}, f32[64,128]{1,0:T(8,128)}, u32[]{:S(2)}) copy-start(f32[64,128]{1,0:T(8,128)} %weights.3) | copy-start | bytes 98308
  0.8 1.2 %copy-start.6 = (f32[64,128]{1,0:T(8,128)S(1)}, f32[64,128]{1,0:T(8,128)}, u32[]{:S(2)}) copy-start(f32[64,128]{1,0:T(8,128)} %anomaly.3) | copy-start | bytes 98308
  0.8 1.2 %copy-start.7 = (s32[128]{0:T(128)S(1)}, s32[128]{0:T(128)}, u32[]{:S(2)}) copy-start(s32[128]{0:T(128)} %param.23) | copy-start | bytes 1540
  0.8 1.2 %copy-start.8 = (f32[10]{0:T(128)S(1)}, f32[10]{0:T(128)}, u32[]{:S(2)}) copy-start(f32[10]{0:T(128)} %param.21) | copy-start | bytes 124
  2.7 5.1 %collective-permute-start.12 = (f32[64,128]{1,0:T(8,128)S(1)}, f32[64,128]{1,0:T(8,128)}, u32[]{:S(2)}, u32[]{:S(2)}) collective-permute-start(f32[64,128]{1,0:T(8,128)S(1)} %get-tuple-element.44), channel_id=1, source_target_pairs={{1,2},{2,1},{5,6},{6,5},{9,10},{10,9},{13,14},{14,13},{17,18},{18,... | collective-permute-start | bytes 98312 | tf_op jit(solution)/shard_map/cond/branch_6_fun/ppermute | solution.py:446
  3.9 4.8 %collective-permute-start.13 = (f32[64,128]{1,0:T(8,128)S(1)}, f32[64,128]{1,0:T(8,128)}, u32[]{:S(2)}, u32[]{:S(2)}) collective-permute-start(f32[64,128]{1,0:T(8,128)S(1)} %get-tuple-element.45), channel_id=1, source_target_pairs={{0,1},{1,0},{2,3},{3,2},{4,5},{5,4},{6,7},{7,6},{8,9},{9,8},{10,11... | collective-permute-start | bytes 98312 | tf_op jit(solution)/shard_map/cond/branch_6_fun/ppermute | solution.py:447
  9.7 6.6 %collective-permute-start.18 = (f32[40,128]{1,0:T(8,128)S(1)}, f32[40,128]{1,0:T(8,128)S(1)}, u32[]{:S(2)}, u32[]{:S(2)}) collective-permute-start(f32[40,128]{1,0:T(8,128)S(1)} %get-tuple-element.95), channel_id=1, source_target_pairs={{0,28},{4,8},{8,4},{12,16},{16,12},{20,24},{24,20},{28,0},{1,29},{... | collective-permute-start | bytes 61448 | tf_op jit(solution)/shard_map/ppermute | solution.py:467
  14.3 3.8 %collective-permute-start.19 = (f32[40,128]{1,0:T(8,128)S(1)}, f32[40,128]{1,0:T(8,128)S(1)}, u32[]{:S(2)}, u32[]{:S(2)}) collective-permute-start(f32[40,128]{1,0:T(8,128)S(1)} %get-tuple-element.96), channel_id=1, source_target_pairs={{0,4},{4,0},{8,12},{12,8},{16,20},{20,16},{24,28},{28,24},{1,5},{5... | collective-permute-start | bytes 61448 | tf_op jit(solution)/shard_map/ppermute | solution.py:466
  14.3 9.9 %collective-permute-start.16 = (f32[64,128]{1,0:T(8,128)S(1)}, f32[64,128]{1,0:T(8,128)S(1)}, u32[]{:S(2)}, u32[]{:S(2)}) collective-permute-start(f32[64,128]{1,0:T(8,128)S(1)} %get-tuple-element.87), channel_id=1, source_target_pairs={{0,28},{4,8},{8,4},{12,16},{16,12},{20,24},{24,20},{28,0},{1,29},{... | collective-permute-start | bytes 98312 | tf_op jit(solution)/shard_map/ppermute | solution.py:467
  16.2 8.0 %collective-permute-start.17 = (f32[64,128]{1,0:T(8,128)S(1)}, f32[64,128]{1,0:T(8,128)S(1)}, u32[]{:S(2)}, u32[]{:S(2)}) collective-permute-start(f32[64,128]{1,0:T(8,128)S(1)} %get-tuple-element.88), channel_id=1, source_target_pairs={{0,4},{4,0},{8,12},{12,8},{16,20},{20,16},{24,28},{28,24},{1,5},{5... | collective-permute-start | bytes 98312 | tf_op jit(solution)/shard_map/ppermute | solution.py:466
  19.3 11.9 %all-to-all-start = ((f32[32,1,128]{2,1,0:T(1,128)}), f32[32,1,128]{2,1,0:T(1,128)S(1)}, u32[]{:S(2)}, u32[]{:S(2)}) async-start(f32[32,1,128]{2,1,0:T(1,128)} %bitcast.8), calls=%async_computation | async-start | bytes 32768 | tf_op jit(solution)/shard_map/all_to_all | solution.py:496

commit v5 on v4

--- a/solution.py
+++ b/solution.py
@@ -34,13 +34,13 @@
 
 
 def flags(meta):
-    return meta[0:1, :] == 1, meta[1:2, :] == 1, meta[2:3, :] == 1
+    return tuple(meta[i : i + 1, :] == 1 for i in range(4))
 
 
 def place_kernel(meta, placed):
-    for i in range(3):
+    for i in range(4):
         placed[i : i + 1, :] = jnp.broadcast_to(meta[0:1, i : i + 1], (1, placed.shape[1]))
-    placed[3:, :] = jnp.zeros((placed.shape[0] - 3, placed.shape[1]), jnp.int32)
+    placed[4:, :] = jnp.zeros((placed.shape[0] - 4, placed.shape[1]), jnp.int32)
 
 
 def pack_kernel(
@@ -89,7 +89,7 @@
     if used < high:
         for packet in (top, bottom, back):
             packet[used:, :] = jnp.zeros((high - used, cols), jnp.float32)
-    odd, last, _ = flags(meta)
+    odd, last, _, _ = flags(meta)
     first[...] = jnp.where(odd, bottom[...], top[...])
     second[...] = jnp.where(last, back[...], jnp.where(odd, top[...], bottom[...]))
 
@@ -101,11 +101,11 @@
     rows, cols = sums.shape[1], sums.shape[2]
     tall = ext.shape[1]
     deep = north_rows.shape[0]
-    odd, _, lon_odd = flags(meta)
+    odd, _, lon_odd, bottom = flags(meta)
     from_first = first[...]
     from_second = second[...]
     north = jnp.where(odd, from_second, from_first)
-    south = jnp.where(odd, from_first, from_second)
+    south = jnp.where(bottom, 0.0, jnp.where(odd, from_first, from_second))
     fields = (sums.at[0], sums.at[1], sums.at[2], water, weights, anomaly)
     for f in range(FIELDS):
         at = deep + ROW[f]
@@ -166,7 +166,7 @@
     rows = base.shape[1]
     size = facing_rows.shape[0]
     middle = tall // 2
-    _, top, lon_odd = flags(meta)
+    _, top, lon_odd, _ = flags(meta)
     west = jnp.where(lon_odd, from_near[...], from_far[...])
     east = jnp.where(lon_odd, from_far[...], from_near[...])
     shift = fold_shift(facing)
@@ -268,7 +268,7 @@
 ):
     levels, rows, cols = heat.shape
     deep = 4 * levels
-    _, top, lon_odd = flags(meta)
+    _, top, lon_odd, _ = flags(meta)
     wet = water[...].astype(jnp.float32)
     lane = iota((rows, cols), 1)
     row = iota((rows, cols), 0)
@@ -410,8 +410,8 @@
     width = cols * lons
     flat = lambda i, j: (i % lons) * lats + j
 
-    place = (lax.rem(lat, 2), (lat == lats - 1).astype(jnp.int32), lax.rem(lon, 2))
-    meta = jnp.stack(place).astype(jnp.int32).reshape(1, 3)
+    place = (lax.rem(lat, 2), lat == lats - 1, lax.rem(lon, 2), lat == 0)
+    meta = jnp.stack([value.astype(jnp.int32) for value in place]).reshape(1, 4)
     (meta,) = call(place_kernel, [(8, cols)], LOAD_FLOPS, 16, "place", types=jnp.int32)(meta)
 
     spans = stratum_spans.reshape(1, levels)
@@ -435,7 +435,7 @@
         for i in range(lons)
         for j in range(1, lats - 1, 2)
         for a, b in ((j, j + 1), (j + 1, j))
-    ]
+    ] + [(flat(i, 0), flat(i, 0)) for i in range(lons)]
 
     counterpart, first = lax.optimization_barrier((opposite_counterpart, first))
     hinge = lax.rem(counterpart[0] + 1 + cols * lon, width)

time: 32.3 us -> 32.2 us (level)
  no operation moved by 1% of the time
where the time goes in v5:
time: 32.2 us; the launch traced here: 32.1 us
  starting transfers between devices  16.6 us (52%)
  Pallas kernels  7.35 us (23%)
  waiting for transfers between devices  6.04 us (19%)
  local copies, waits for them, and re-layouts  1.18 us (4%)
  between operations  0.82 us (3%)
    pallas_call x6, Pallas kernels, run(): pl.pallas_call(kernel, out_shape=[jax.ShapeDtypeStruct(shape, types) for...  7.35 us
    ppermute x2, starting transfers between devices, body(): lax.ppermute(cells, 'lon', [(i, (i + 1 if i % 2 else i - 1) % lons) for i...  6.52 us
    all_to_all x1, starting transfers between devices, body(): shares = lax.all_to_all(moments, axes, 0, 0, tiled=True)  4.87 us
    ppermute x1, starting transfers between devices, exchange(): return (second, lax.ppermute(first, axes, pairs_first))  3.79 us
    all_to_all x1, waiting for transfers between devices, body(): shares = lax.all_to_all(moments, axes, 0, 0, tiled=True)  3.29 us
    ppermute x2, waiting for transfers between devices, body(): lax.ppermute(cells, 'lon', [(i, i ^ 1) for i in range(lons)])  1.75 us
    ppermute x1, starting transfers between devices, exchange(): second = lax.ppermute(second, axes, pairs_inner + pairs_fold)  1.27 us
    unnamed x18, local copies, waits for them, and re-layouts  1.18 us
  transfers between devices with their start and end apart: 7, of which 3 were waited for; matrix products, arithmetic and copies ran while one was open for 0% of the time, Pallas kernels for 16%

profile of v5, /device:TPU:0, one launch (start us, length us, event | category | flops | bytes accessed | tf_op | source)
XLA Modules:
  0.0 32.1 jit_solution(8890281611384412496)
XLA Ops:
  0.6 0.1 add_bitcast_fusion.meta
  0.7 0.0 copy-start.4
  0.7 0.0 copy-start.5
  0.8 0.0 copy-start.6
  0.8 0.1 place.1.meta
  0.8 0.8 %copy-done = f32[10,64,128]{2,1,0:T(8,128)S(1)} copy-done((f32[10,64,128]{2,1,0:T(8,128)S(1)}, f32[10,64,128]{2,1,0:T(8,128)}, u32[]{:S(2)}) %copy-start) | copy-done | bytes 327704
  1.7 0.1 copy-done.1
  1.8 0.1 copy-done.2
  1.9 0.1 copy-done.3
  2.0 0.0 copy-done.4
  2.0 0.0 copy-done.5
  2.0 0.0 copy-done.6
  2.0 0.5 %level_sums.1 = (f32[3,64,128]{2,1,0:T(8,128)S(1)}, f32[64,128]{1,0:T(8,128)S(1)}, f32[64,128]{1,0:T(8,128)S(1)}, f32[64,128]{1,0:T(8,128)S(1)}, f32[64,128]{1,0:T(8,128)S(1)}) custom-call(s32[8,128]{1,0:T(8,128)S(1)} %place.1.meta, f32[1,10]{1,0:T(1,128)S(1)} %bitcast.19, s32[1,128]{1,0:T(1,128)S(1)} %bitcast.15, f32[10,64,128]{2,1,0:T(8,128)S(1)} %copy-done, ...), custom_call_target="tpu_custom_call" | custom-call | flops 983040 | bytes 1310720 | tf_op jit(solution)/shard_map/level_sums/pallas_call | solution.py:379
  2.6 6.1 %conditional.1 = (f32[64,128]{1,0:T(8,128)}, f32[64,128]{1,0:T(8,128)}) conditional(s32[]{:T(128)} %clamp.3, (f32[64,128]{1,0:T(8,128)S(1)}, f32[64,128]{1,0:T(8,128)S(1)}) %tuple.42, (f32[64,128]{1,0:T(8,128)S(1)}, f32[64,128]{1,0:T(8,128)S(1)}) %tuple.42, (f32[64,128]{1,0:T(8,128)S(1)}, ...), branch_computations={%region_0.1_spmd, %region_1.2_spmd, %region_2.3_spmd, %region_3.4_... | conditional | bytes 262240 | solution.py:449
  2.7 1.3 %collective-permute-start.2 = (f32[64,128]{1,0:T(8,128)S(1)}, f32[64,128]{1,0:T(8,128)}, u32[]{:S(2)}, u32[]{:S(2)}) collective-permute-start(f32[64,128]{1,0:T(8,128)S(1)} %get-tuple-element.34), channel_id=1, source_target_pairs={{1,2},{2,1},{5,6},{6,5},{9,10},{10,9},{13,14},{14,13},{17,18},{18,... | collective-permute-start | bytes 98312 | tf_op jit(solution)/shard_map/cond/branch_1_fun/ppermute | solution.py:446
  3.9 3.8 %collective-permute-start.3 = (f32[64,128]{1,0:T(8,128)S(1)}, f32[64,128]{1,0:T(8,128)}, u32[]{:S(2)}, u32[]{:S(2)}) collective-permute-start(f32[64,128]{1,0:T(8,128)S(1)} %get-tuple-element.35), channel_id=1, source_target_pairs={{0,1},{1,0},{2,3},{3,2},{4,5},{5,4},{6,7},{7,6},{8,9},{9,8},{10,11... | collective-permute-start | bytes 98312 | tf_op jit(solution)/shard_map/cond/branch_1_fun/ppermute | solution.py:447
  7.7 0.0 collective-permute-done.2
  7.7 1.0 %collective-permute-done.3 = f32[64,128]{1,0:T(8,128)} collective-permute-done((f32[64,128]{1,0:T(8,128)S(1)}, f32[64,128]{1,0:T(8,128)}, u32[]{:S(2)}, u32[]{:S(2)}) %collective-permute-start.3) | collective-permute-done | bytes 32800 | tf_op jit(solution)/shard_map/cond/branch_1_fun/ppermute | solution.py:447
  8.7 1.0 %row_halos.1 = (f32[6,80,128]{2,1,0:T(8,128)S(1)}, f32[40,128]{1,0:T(8,128)S(1)}, f32[40,128]{1,0:T(8,128)S(1)}, f32[64,128]{1,0:T(8,128)S(1)}, f32[64,128]{1,0:...) custom-call(s32[8,128]{1,0:T(8,128)S(1)} %place.1.meta, ...), custom_call_target="tpu_custom_call" | custom-call | flops 61440 | bytes 983040 | tf_op jit(solution)/shard_map/row_halos/pallas_call | solution.py:379
  9.7 4.6 %collective-permute-start.18 = (f32[40,128]{1,0:T(8,128)S(1)}, f32[40,128]{1,0:T(8,128)S(1)}, u32[]{:S(2)}, u32[]{:S(2)}) collective-permute-start(f32[40,128]{1,0:T(8,128)S(1)} %get-tuple-element.95), channel_id=1, source_target_pairs={{0,28},{4,8},{8,4},{12,16},{16,12},{20,24},{24,20},{28,0},{1,29},{... | collective-permute-start | bytes 61448 | tf_op jit(solution)/shard_map/ppermute | solution.py:467
  14.3 0.0 collective-permute-start.19
  14.3 1.9 %collective-permute-start.16 = (f32[64,128]{1,0:T(8,128)S(1)}, f32[64,128]{1,0:T(8,128)S(1)}, u32[]{:S(2)}, u32[]{:S(2)}) collective-permute-start(f32[64,128]{1,0:T(8,128)S(1)} %get-tuple-element.87), channel_id=1, source_target_pairs={{0,28},{4,8},{8,4},{12,16},{16,12},{20,24},{24,20},{28,0},{1,29},{... | collective-permute-start | bytes 98312 | tf_op jit(solution)/shard_map/ppermute | solution.py:467
  16.2 0.1 collective-permute-start.17
  16.3 0.0 collective-permute-done.18.from_far
  16.3 1.7 %collective-permute-done.19.from_near = f32[40,128]{1,0:T(8,128)S(1)} collective-permute-done((f32[40,128]{1,0:T(8,128)S(1)}, f32[40,128]{1,0:T(8,128)S(1)}, u32[]{:S(2)}, u32[]{:S(2)}) %collective-permute-start.19) | collective-permute-done | bytes 20512 | tf_op jit(solution)/shard_map/ppermute | solution.py:466
  18.1 1.2 %krylov.1 = (f32[3,64,128]{2,1,0:T(8,128)S(1)}, f32[32,128]{1,0:T(8,128)}) custom-call(s32[8,128]{1,0:T(8,128)S(1)} %place.1.meta, s32[1,128]{1,0:T(1,128)S(1)} %bitcast.17, f32[6,80,128]{2,1,0:T(8,128)S(1)} %get-tuple-element.93.ext, f32[24,128]{1,0:T(8,128)S(1)} %get-tuple-element.94.facing_rows, f32[40,128]{1,0:T(8,128)S(1)} %collective-permute-done.18.from_far, ...), custom_call_target="tpu_custom_call" | custom-call | flops 2048000 | bytes 491520 | tf_op jit(solution)/shard_map/krylov/pallas_call | solution.py:379
  19.3 4.9 %all-to-all-start = ((f32[32,1,128]{2,1,0:T(1,128)}), f32[32,1,128]{2,1,0:T(1,128)S(1)}, u32[]{:S(2)}, u32[]{:S(2)}) async-start(f32[32,1,128]{2,1,0:T(1,128)} %bitcast.9), calls=%async_computation | async-start | bytes 32768 | tf_op jit(solution)/shard_map/all_to_all | solution.py:496
  24.2 0.0 collective-permute-done.16.from_far
  24.2 0.0 collective-permute-done.17.from_near
  24.2 3.8 %levels_step.1 = (f32[10,64,128]{2,1,0:T(8,128)}, f32[10,64,128]{2,1,0:T(8,128)}, f32[10,64,128]{2,1,0:T(8,128)}, f32[10,64,128]{2,1,0:T(8,128)}) custom-call(s32[8,128]{1,0:T(8,128)S(1)} %place.1.meta, f32[1,10]{1,0:T(1,128)S(1)} %bitcast.20, s32[1,128]{1,0:T(1,128)S(1)} %bitcast.18, f32[10,64,128]{2,1,0:T(8,128)S(1)} %copy-done, ...), custom_call_target="tpu_custom_call" | custom-call | flops 9830400 | bytes 2621440 | tf_op jit(solution)/shard_map/levels_step/pallas_call | solution.py:379
  28.0 3.3 %all-to-all-done = f32[32,1,128]{2,1,0:T(1,128)S(1)} async-done(((f32[32,1,128]{2,1,0:T(1,128)}), f32[32,1,128]{2,1,0:T(1,128)S(1)}, u32[]{:S(2)}, u32[]{:S(2)}) %all-to-all-start) | async-done | bytes 16416 | tf_op jit(solution)/shard_map/all_to_all | solution.py:496
  31.3 0.8 %surface.1 = f32[64,128]{1,0:T(8,128)} custom-call(f32[32,128]{1,0:T(8,128)S(1)} %bitcast.14, f32[3,64,128]{2,1,0:T(8,128)S(1)} %get-tuple-element.98.base), custom_call_target="tpu_custom_call" | custom-call | flops 49152 | bytes 131072 | tf_op jit(solution)/shard_map/surface/pallas_call | solution.py:379
  (8 shorter events, 0.0 us)
Async XLA Ops:
  0.7 1.0 %copy-start = (f32[10,64,128]{2,1,0:T(8,128)S(1)}, f32[10,64,128]{2,1,0:T(8,128)}, u32[]{:S(2)}) copy-start(f32[10,64,128]{2,1,0:T(8,128)} %heat.3) | copy-start | bytes 983044
  0.7 1.1 %copy-start.1 = (f32[10,64,128]{2,1,0:T(8,128)S(1)}, f32[10,64,128]{2,1,0:T(8,128)}, u32[]{:S(2)}) copy-start(f32[10,64,128]{2,1,0:T(8,128)} %salt.3) | copy-start | bytes 983044
  0.7 1.2 %copy-start.2 = (f32[10,64,128]{2,1,0:T(8,128)S(1)}, f32[10,64,128]{2,1,0:T(8,128)}, u32[]{:S(2)}) copy-start(f32[10,64,128]{2,1,0:T(8,128)} %zonal.3) | copy-start | bytes 983044
  0.7 1.3 %copy-start.3 = (f32[10,64,128]{2,1,0:T(8,128)S(1)}, f32[10,64,128]{2,1,0:T(8,128)}, u32[]{:S(2)}) copy-start(f32[10,64,128]{2,1,0:T(8,128)} %merid.3) | copy-start | bytes 983044
  0.7 1.3 %copy-start.4 = (s32[64,128]{1,0:T(8,128)S(1)}, s32[64,128]{1,0:T(8,128)}, u32[]{:S(2)}) copy-start(s32[64,128]{1,0:T(8,128)} %water.5) | copy-start | bytes 98308
  0.7 1.3 %copy-start.5 = (f32[64,128]{1,0:T(8,128)S(1)}, f32[64,128]{1,0:T(8,128)}, u32[]{:S(2)}) copy-start(f32[64,128]{1,0:T(8,128)} %weights.3) | copy-start | bytes 98308
  0.8 1.2 %copy-start.6 = (f32[64,128]{1,0:T(8,128)S(1)}, f32[64,128]{1,0:T(8,128)}, u32[]{:S(2)}) copy-start(f32[64,128]{1,0:T(8,128)} %anomaly.3) | copy-start | bytes 98308
  0.8 1.2 %copy-start.7 = (s32[128]{0:T(128)S(1)}, s32[128]{0:T(128)}, u32[]{:S(2)}) copy-start(s32[128]{0:T(128)} %param.23) | copy-start | bytes 1540
  0.8 1.2 %copy-start.8 = (f32[10]{0:T(128)S(1)}, f32[10]{0:T(128)}, u32[]{:S(2)}) copy-start(f32[10]{0:T(128)} %param.21) | copy-start | bytes 124
  2.7 5.1 %collective-permute-start.2 = (f32[64,128]{1,0:T(8,128)S(1)}, f32[64,128]{1,0:T(8,128)}, u32[]{:S(2)}, u32[]{:S(2)}) collective-permute-start(f32[64,128]{1,0:T(8,128)S(1)} %get-tuple-element.34), channel_id=1, source_target_pairs={{1,2},{2,1},{5,6},{6,5},{9,10},{10,9},{13,14},{14,13},{17,18},{18,... | collective-permute-start | bytes 98312 | tf_op jit(solution)/shard_map/cond/branch_1_fun/ppermute | solution.py:446
  3.9 4.8 %collective-permute-start.3 = (f32[64,128]{1,0:T(8,128)S(1)}, f32[64,128]{1,0:T(8,128)}, u32[]{:S(2)}, u32[]{:S(2)}) collective-permute-start(f32[64,128]{1,0:T(8,128)S(1)} %get-tuple-element.35), channel_id=1, source_target_pairs={{0,1},{1,0},{2,3},{3,2},{4,5},{5,4},{6,7},{7,6},{8,9},{9,8},{10,11... | collective-permute-start | bytes 98312 | tf_op jit(solution)/shard_map/cond/branch_1_fun/ppermute | solution.py:447
  9.7 6.6 %collective-permute-start.18 = (f32[40,128]{1,0:T(8,128)S(1)}, f32[40,128]{1,0:T(8,128)S(1)}, u32[]{:S(2)}, u32[]{:S(2)}) collective-permute-start(f32[40,128]{1,0:T(8,128)S(1)} %get-tuple-element.95), channel_id=1, source_target_pairs={{0,28},{4,8},{8,4},{12,16},{16,12},{20,24},{24,20},{28,0},{1,29},{... | collective-permute-start | bytes 61448 | tf_op jit(solution)/shard_map/ppermute | solution.py:467
  14.3 3.8 %collective-permute-start.19 = (f32[40,128]{1,0:T(8,128)S(1)}, f32[40,128]{1,0:T(8,128)S(1)}, u32[]{:S(2)}, u32[]{:S(2)}) collective-permute-start(f32[40,128]{1,0:T(8,128)S(1)} %get-tuple-element.96), channel_id=1, source_target_pairs={{0,4},{4,0},{8,12},{12,8},{16,20},{20,16},{24,28},{28,24},{1,5},{5... | collective-permute-start | bytes 61448 | tf_op jit(solution)/shard_map/ppermute | solution.py:466
  14.3 9.9 %collective-permute-start.16 = (f32[64,128]{1,0:T(8,128)S(1)}, f32[64,128]{1,0:T(8,128)S(1)}, u32[]{:S(2)}, u32[]{:S(2)}) collective-permute-start(f32[64,128]{1,0:T(8,128)S(1)} %get-tuple-element.87), channel_id=1, source_target_pairs={{0,28},{4,8},{8,4},{12,16},{16,12},{20,24},{24,20},{28,0},{1,29},{... | collective-permute-start | bytes 98312 | tf_op jit(solution)/shard_map/ppermute | solution.py:467
  16.2 8.0 %collective-permute-start.17 = (f32[64,128]{1,0:T(8,128)S(1)}, f32[64,128]{1,0:T(8,128)S(1)}, u32[]{:S(2)}, u32[]{:S(2)}) collective-permute-start(f32[64,128]{1,0:T(8,128)S(1)} %get-tuple-element.88), channel_id=1, source_target_pairs={{0,4},{4,0},{8,12},{12,8},{16,20},{20,16},{24,28},{28,24},{1,5},{5... | collective-permute-start | bytes 98312 | tf_op jit(solution)/shard_map/ppermute | solution.py:466
  19.3 11.9 %all-to-all-start = ((f32[32,1,128]{2,1,0:T(1,128)}), f32[32,1,128]{2,1,0:T(1,128)S(1)}, u32[]{:S(2)}, u32[]{:S(2)}) async-start(f32[32,1,128]{2,1,0:T(1,128)} %bitcast.9), calls=%async_computation | async-start | bytes 32768 | tf_op jit(solution)/shard_map/all_to_all | solution.py:496

commit v6 on v5

--- a/solution.py
+++ b/solution.py
@@ -38,9 +38,9 @@
 
 
 def place_kernel(meta, placed):
-    for i in range(4):
+    for i in range(5):
         placed[i : i + 1, :] = jnp.broadcast_to(meta[0:1, i : i + 1], (1, placed.shape[1]))
-    placed[4:, :] = jnp.zeros((placed.shape[0] - 4, placed.shape[1]), jnp.int32)
+    placed[5:, :] = jnp.zeros((placed.shape[0] - 5, placed.shape[1]), jnp.int32)
 
 
 def pack_kernel(
@@ -95,15 +95,18 @@
 
 
 def turn_kernel(
-    meta, sums, water, weights, anomaly, second, first, east_columns, west_columns,
+    lons, meta, facing, mine, sums, water, weights, anomaly, second, first, east_columns, west_columns,
     ext, to_far, to_near, state_far, state_near, facing_rows, north_rows, south_rows,
 ):
     rows, cols = sums.shape[1], sums.shape[2]
     tall = ext.shape[1]
     deep = north_rows.shape[0]
-    odd, _, lon_odd, bottom = flags(meta)
+    odd, top, lon_odd, bottom = flags(meta)
     from_first = first[...]
-    from_second = second[...]
+    hinge = facing[0:1, 0:1] + 1 + cols * meta[4:5, 0:1] + cols // 2
+    block = lax.shift_right_logical(hinge & (lons * cols - 1), cols.bit_length() - 1)
+    alone = ((block - 1 - 2 * meta[4:5, 0:1]) & (lons - 1)) == 0
+    from_second = jnp.where(top & alone, mine[...], second[...])
     north = jnp.where(odd, from_second, from_first)
     south = jnp.where(bottom, 0.0, jnp.where(odd, from_first, from_second))
     fields = (sums.at[0], sums.at[1], sums.at[2], water, weights, anomaly)
@@ -410,8 +413,8 @@
     width = cols * lons
     flat = lambda i, j: (i % lons) * lats + j
 
-    place = (lax.rem(lat, 2), lat == lats - 1, lax.rem(lon, 2), lat == 0)
-    meta = jnp.stack([value.astype(jnp.int32) for value in place]).reshape(1, 4)
+    place = (lax.rem(lat, 2), lat == lats - 1, lax.rem(lon, 2), lat == 0, lon)
+    meta = jnp.stack([value.astype(jnp.int32) for value in place]).reshape(1, 5)
     (meta,) = call(place_kernel, [(8, cols)], LOAD_FLOPS, 16, "place", types=jnp.int32)(meta)
 
     spans = stratum_spans.reshape(1, levels)
@@ -435,22 +438,25 @@
         for i in range(lons)
         for j in range(1, lats - 1, 2)
         for a, b in ((j, j + 1), (j + 1, j))
-    ] + [(flat(i, 0), flat(i, 0)) for i in range(lons)]
+    ] + [(flat(i, 0), flat(i ^ 1, 0)) for i in range(lons)]
 
     counterpart, first = lax.optimization_barrier((opposite_counterpart, first))
     hinge = lax.rem(counterpart[0] + 1 + cols * lon, width)
     block = lax.rem((hinge + cols // 2) // cols, lons)
 
     def exchange(shift, first, second):
-        pairs_fold = [(flat(shift - 1 - i, lats - 1), flat(i, lats - 1)) for i in range(lons)]
+        partner = [(shift - 1 - i) % lons for i in range(lons)]
+        partner = [i + lons // 2 if i == p else p for i, p in enumerate(partner)]
+        pairs_fold = [(flat(p, lats - 1), flat(i, lats - 1)) for i, p in enumerate(partner)]
         second = lax.ppermute(second, axes, pairs_inner + pairs_fold)
         return second, lax.ppermute(first, axes, pairs_first)
 
+    mine = second
     second, first = lax.switch(block, [functools.partial(exchange, s) for s in range(lons)], first, second)
 
     deep = 4 * levels
     ext, to_far, to_near, state_far, state_near, facing_rows, north_rows, south_rows = call(
-        turn_kernel,
+        functools.partial(turn_kernel, lons),
         [
             (FIELDS, tall, cols),
             *[(tall // 2, cols)] * 2,
@@ -461,7 +467,7 @@
         FIELDS * tall * cols,
         4 * 4 * FIELDS * tall * cols,
         "row_halos",
-    )(meta, sums, *flat_state, second, first, east_columns, west_columns)
+    )(meta, facing, mine, sums, *flat_state, second, first, east_columns, west_columns)
 
     near = lambda cells: lax.ppermute(cells, "lon", [(i, i ^ 1) for i in range(lons)])
     far = lambda cells: lax.ppermute(cells, "lon", [(i, (i + 1 if i % 2 else i - 1) % lons) for i in range(lons)])

time: 32.2 us -> 30.5 us (0.947)
  starting transfers between devices: 16.6 us -> 13.9 us
  waiting for transfers between devices: 6.04 us -> 6.9 us
    ppermute x1, starting transfers between devices: 3.79 us -> 0.14 us  [exchange(): return (second, lax.ppermute(first, axes, pairs_first))]
    ppermute x1, waiting for transfers between devices: 0.01 us -> 1.86 us  [exchange(): second = lax.ppermute(second, axes, pairs_inner + pairs_fold)]
    ppermute x1, starting transfers between devices: 1.27 us -> 3 us  [exchange(): second = lax.ppermute(second, axes, pairs_inner + pairs_fold)]
    all_to_all x1, starting transfers between devices: 4.87 us -> 3.54 us  [body(): shares = lax.all_to_all(moments, axes, 0, 0, tiled=True)]
    ppermute x1, waiting for transfers between devices: 0.99 us -> 0.01 us  [exchange(): return (second, lax.ppermute(first, axes, pairs_first))]
    ppermute x2, starting transfers between devices: 6.52 us -> 7.06 us  [body(): lax.ppermute(cells, 'lon', [(i, (i + 1 if i % 2 else i - 1) % lons) for i...]
  transfers between devices with their start and end apart: 7 -> 7, of which waited for: 3 -> 3; matrix products, arithmetic and copies ran while one was open for 0% -> 0% of each run, Pallas kernels for 16% -> 17%
where the time goes in v6:
time: 30.5 us; the launch traced here: 30.2 us
  starting transfers between devices  13.9 us (46%)
  Pallas kernels  7.37 us (24%)
  waiting for transfers between devices  6.9 us (23%)
  local copies, waits for them, and re-layouts  1.26 us (4%)
  between operations  0.82 us (3%)
    pallas_call x6, Pallas kernels, run(): pl.pallas_call(kernel, out_shape=[jax.ShapeDtypeStruct(shape, types) for...  7.37 us
    ppermute x2, starting transfers between devices, body(): lax.ppermute(cells, 'lon', [(i, (i + 1 if i % 2 else i - 1) % lons) for i...  7.06 us
    all_to_all x1, starting transfers between devices, body(): shares = lax.all_to_all(moments, axes, 0, 0, tiled=True)  3.54 us
    all_to_all x1, waiting for transfers between devices, body(): shares = lax.all_to_all(moments, axes, 0, 0, tiled=True)  3.29 us
    ppermute x1, starting transfers between devices, exchange(): second = lax.ppermute(second, axes, pairs_inner + pairs_fold)  3 us
    ppermute x1, waiting for transfers between devices, exchange(): second = lax.ppermute(second, axes, pairs_inner + pairs_fold)  1.86 us
    ppermute x2, waiting for transfers between devices, body(): lax.ppermute(cells, 'lon', [(i, i ^ 1) for i in range(lons)])  1.75 us
    unnamed x18, local copies, waits for them, and re-layouts  1.17 us
  transfers between devices with their start and end apart: 7, of which 3 were waited for; matrix products, arithmetic and copies ran while one was open for 0% of the time, Pallas kernels for 17%

profile of v6, /device:TPU:0, one launch (start us, length us, event | category | flops | bytes accessed | tf_op | source)
XLA Modules:
  0.0 30.2 jit_solution(1701806984578350212)
XLA Ops:
  0.6 0.1 stack.31
  0.7 0.0 copy-start.3
  0.7 0.0 copy-start.4
  0.8 0.0 copy-start.5
  0.8 0.0 copy-start.6
  0.8 0.1 place.1.meta
  0.9 0.8 %copy-done = f32[10,64,128]{2,1,0:T(8,128)S(1)} copy-done((f32[10,64,128]{2,1,0:T(8,128)S(1)}, f32[10,64,128]{2,1,0:T(8,128)}, u32[]{:S(2)}) %copy-start) | copy-done | bytes 327704
  1.7 0.1 copy-done.1
  1.8 0.1 copy-done.2
  1.9 0.1 copy-done.3
  2.0 0.0 copy-done.4
  2.0 0.0 copy-done.7
  2.0 0.5 %level_sums.1 = (f32[3,64,128]{2,1,0:T(8,128)S(1)}, f32[64,128]{1,0:T(8,128)S(1)}, f32[64,128]{1,0:T(8,128)S(1)}, f32[64,128]{1,0:T(8,128)S(1)}, f32[64,128]{1,0:T(8,128)S(1)}) custom-call(s32[8,128]{1,0:T(8,128)S(1)} %place.1.meta, f32[1,10]{1,0:T(1,128)S(1)} %bitcast.20, s32[1,128]{1,0:T(1,128)S(1)} %bitcast.15, f32[10,64,128]{2,1,0:T(8,128)S(1)} %copy-done, ...), custom_call_target="tpu_custom_call" | custom-call | flops 983040 | bytes 1310720 | tf_op jit(solution)/shard_map/level_sums/pallas_call | solution.py:382
  2.6 5.0 %conditional.1 = (f32[64,128]{1,0:T(8,128)}, f32[64,128]{1,0:T(8,128)}) conditional(s32[]{:T(128)} %clamp.3, (f32[64,128]{1,0:T(8,128)S(1)}, f32[64,128]{1,0:T(8,128)S(1)}) %tuple.42, (f32[64,128]{1,0:T(8,128)S(1)}, f32[64,128]{1,0:T(8,128)S(1)}) %tuple.42, (f32[64,128]{1,0:T(8,128)S(1)}, ...), branch_computations={%region_0.1_spmd, %region_1.2_spmd, %region_2.3_spmd, %region_3.4_... | conditional | bytes 262240 | solution.py:455
  2.7 3.0 %collective-permute-start.4 = (f32[64,128]{1,0:T(8,128)S(1)}, f32[64,128]{1,0:T(8,128)}, u32[]{:S(2)}, u32[]{:S(2)}) collective-permute-start(f32[64,128]{1,0:T(8,128)S(1)} %get-tuple-element.36), channel_id=1, source_target_pairs={{1,2},{2,1},{5,6},{6,5},{9,10},{10,9},{13,14},{14,13},{17,18},{18,... | collective-permute-start | bytes 98312 | tf_op jit(solution)/shard_map/cond/branch_2_fun/ppermute | solution.py:451
  5.7 0.1 collective-permute-start.5
  5.8 1.9 %collective-permute-done.4 = f32[64,128]{1,0:T(8,128)} collective-permute-done((f32[64,128]{1,0:T(8,128)S(1)}, f32[64,128]{1,0:T(8,128)}, u32[]{:S(2)}, u32[]{:S(2)}) %collective-permute-start.4) | collective-permute-done | bytes 32800 | tf_op jit(solution)/shard_map/cond/branch_2_fun/ppermute | solution.py:451
  7.7 0.0 collective-permute-done.5
  7.7 1.0 %row_halos.1 = (f32[6,80,128]{2,1,0:T(8,128)S(1)}, f32[40,128]{1,0:T(8,128)S(1)}, f32[40,128]{1,0:T(8,128)S(1)}, f32[64,128]{1,0:T(8,128)S(1)}, f32[64,128]{1,0:...) custom-call(s32[8,128]{1,0:T(8,128)S(1)} %place.1.meta, s32[1,128]{1,0:T(1,128)S(1)} %bitcast.17, ...), custom_call_target="tpu_custom_call" | custom-call | flops 61440 | bytes 983040 | tf_op jit(solution)/shard_map/row_halos/pallas_call | solution.py:382
  8.7 5.1 %collective-permute-start.18 = (f32[40,128]{1,0:T(8,128)S(1)}, f32[40,128]{1,0:T(8,128)S(1)}, u32[]{:S(2)}, u32[]{:S(2)}) collective-permute-start(f32[40,128]{1,0:T(8,128)S(1)} %get-tuple-element.95), channel_id=1, source_target_pairs={{0,28},{4,8},{8,4},{12,16},{16,12},{20,24},{24,20},{28,0},{1,29},{... | collective-permute-start | bytes 61448 | tf_op jit(solution)/shard_map/ppermute | solution.py:473
  13.8 0.0 collective-permute-start.19
  13.8 1.9 %collective-permute-start.16 = (f32[64,128]{1,0:T(8,128)S(1)}, f32[64,128]{1,0:T(8,128)S(1)}, u32[]{:S(2)}, u32[]{:S(2)}) collective-permute-start(f32[64,128]{1,0:T(8,128)S(1)} %get-tuple-element.87), channel_id=1, source_target_pairs={{0,28},{4,8},{8,4},{12,16},{16,12},{20,24},{24,20},{28,0},{1,29},{... | collective-permute-start | bytes 98312 | tf_op jit(solution)/shard_map/ppermute | solution.py:473
  15.7 0.1 collective-permute-start.17
  15.8 0.0 collective-permute-done.18.from_far
  15.9 1.7 %collective-permute-done.19.from_near = f32[40,128]{1,0:T(8,128)S(1)} collective-permute-done((f32[40,128]{1,0:T(8,128)S(1)}, f32[40,128]{1,0:T(8,128)S(1)}, u32[]{:S(2)}, u32[]{:S(2)}) %collective-permute-start.19) | collective-permute-done | bytes 20512 | tf_op jit(solution)/shard_map/ppermute | solution.py:472
  17.6 1.3 %krylov.1 = (f32[3,64,128]{2,1,0:T(8,128)S(1)}, f32[32,128]{1,0:T(8,128)}) custom-call(s32[8,128]{1,0:T(8,128)S(1)} %place.1.meta, s32[1,128]{1,0:T(1,128)S(1)} %bitcast.18, f32[6,80,128]{2,1,0:T(8,128)S(1)} %get-tuple-element.93.ext, f32[24,128]{1,0:T(8,128)S(1)} %get-tuple-element.94.facing_rows, f32[40,128]{1,0:T(8,128)S(1)} %collective-permute-done.18.from_far, ...), custom_call_target="tpu_custom_call" | custom-call | flops 2048000 | bytes 491520 | tf_op jit(solution)/shard_map/krylov/pallas_call | solution.py:382
  18.9 3.5 %all-to-all-start = ((f32[32,1,128]{2,1,0:T(1,128)}), f32[32,1,128]{2,1,0:T(1,128)S(1)}, u32[]{:S(2)}, u32[]{:S(2)}) async-start(f32[32,1,128]{2,1,0:T(1,128)} %bitcast.10), calls=%async_computation | async-start | bytes 32768 | tf_op jit(solution)/shard_map/all_to_all | solution.py:502
  22.4 0.0 collective-permute-done.16.from_far
  22.4 0.0 collective-permute-done.17.from_near
  22.4 3.8 %levels_step.1 = (f32[10,64,128]{2,1,0:T(8,128)}, f32[10,64,128]{2,1,0:T(8,128)}, f32[10,64,128]{2,1,0:T(8,128)}, f32[10,64,128]{2,1,0:T(8,128)}) custom-call(s32[8,128]{1,0:T(8,128)S(1)} %place.1.meta, f32[1,10]{1,0:T(1,128)S(1)} %bitcast.21, s32[1,128]{1,0:T(1,128)S(1)} %bitcast.19, f32[10,64,128]{2,1,0:T(8,128)S(1)} %copy-done, ...), custom_call_target="tpu_custom_call" | custom-call | flops 9830400 | bytes 2621440 | tf_op jit(solution)/shard_map/levels_step/pallas_call | solution.py:382
  26.2 3.3 %all-to-all-done = f32[32,1,128]{2,1,0:T(1,128)S(1)} async-done(((f32[32,1,128]{2,1,0:T(1,128)}), f32[32,1,128]{2,1,0:T(1,128)S(1)}, u32[]{:S(2)}, u32[]{:S(2)}) %all-to-all-start) | async-done | bytes 16416 | tf_op jit(solution)/shard_map/all_to_all | solution.py:502
  29.5 0.8 %surface.1 = f32[64,128]{1,0:T(8,128)} custom-call(f32[32,128]{1,0:T(8,128)S(1)} %bitcast.14, f32[3,64,128]{2,1,0:T(8,128)S(1)} %get-tuple-element.98.base), custom_call_target="tpu_custom_call" | custom-call | flops 49152 | bytes 131072 | tf_op jit(solution)/shard_map/surface/pallas_call | solution.py:382
  (8 shorter events, 0.0 us)
Async XLA Ops:
  0.7 1.0 %copy-start = (f32[10,64,128]{2,1,0:T(8,128)S(1)}, f32[10,64,128]{2,1,0:T(8,128)}, u32[]{:S(2)}) copy-start(f32[10,64,128]{2,1,0:T(8,128)} %heat.3) | copy-start | bytes 983044
  0.7 1.1 %copy-start.1 = (f32[10,64,128]{2,1,0:T(8,128)S(1)}, f32[10,64,128]{2,1,0:T(8,128)}, u32[]{:S(2)}) copy-start(f32[10,64,128]{2,1,0:T(8,128)} %salt.3) | copy-start | bytes 983044
  0.7 1.2 %copy-start.2 = (f32[10,64,128]{2,1,0:T(8,128)S(1)}, f32[10,64,128]{2,1,0:T(8,128)}, u32[]{:S(2)}) copy-start(f32[10,64,128]{2,1,0:T(8,128)} %zonal.3) | copy-start | bytes 983044
  0.7 1.3 %copy-start.3 = (f32[10,64,128]{2,1,0:T(8,128)S(1)}, f32[10,64,128]{2,1,0:T(8,128)}, u32[]{:S(2)}) copy-start(f32[10,64,128]{2,1,0:T(8,128)} %merid.3) | copy-start | bytes 983044
  0.7 1.3 %copy-start.4 = (s32[64,128]{1,0:T(8,128)S(1)}, s32[64,128]{1,0:T(8,128)}, u32[]{:S(2)}) copy-start(s32[64,128]{1,0:T(8,128)} %water.5) | copy-start | bytes 98308
  0.8 1.2 %copy-start.5 = (f32[64,128]{1,0:T(8,128)S(1)}, f32[64,128]{1,0:T(8,128)}, u32[]{:S(2)}) copy-start(f32[64,128]{1,0:T(8,128)} %weights.3) | copy-start | bytes 98308
  0.8 1.2 %copy-start.6 = (f32[64,128]{1,0:T(8,128)S(1)}, f32[64,128]{1,0:T(8,128)}, u32[]{:S(2)}) copy-start(f32[64,128]{1,0:T(8,128)} %anomaly.3) | copy-start | bytes 98308
  0.9 1.2 %copy-start.7 = (s32[128]{0:T(128)S(1)}, s32[128]{0:T(128)}, u32[]{:S(2)}) copy-start(s32[128]{0:T(128)} %param.23) | copy-start | bytes 1540
  0.9 1.2 %copy-start.8 = (f32[10]{0:T(128)S(1)}, f32[10]{0:T(128)}, u32[]{:S(2)}) copy-start(f32[10]{0:T(128)} %param.21) | copy-start | bytes 124
  2.7 5.0 %collective-permute-start.4 = (f32[64,128]{1,0:T(8,128)S(1)}, f32[64,128]{1,0:T(8,128)}, u32[]{:S(2)}, u32[]{:S(2)}) collective-permute-start(f32[64,128]{1,0:T(8,128)S(1)} %get-tuple-element.36), channel_id=1, source_target_pairs={{1,2},{2,1},{5,6},{6,5},{9,10},{10,9},{13,14},{14,13},{17,18},{18,... | collective-permute-start | bytes 98312 | tf_op jit(solution)/shard_map/cond/branch_2_fun/ppermute | solution.py:451
  5.7 2.0 %collective-permute-start.5 = (f32[64,128]{1,0:T(8,128)S(1)}, f32[64,128]{1,0:T(8,128)}, u32[]{:S(2)}, u32[]{:S(2)}) collective-permute-start(f32[64,128]{1,0:T(8,128)S(1)} %get-tuple-element.37), channel_id=1, source_target_pairs={{0,1},{1,0},{2,3},{3,2},{4,5},{5,4},{6,7},{7,6},{8,9},{9,8},{10,11... | collective-permute-start | bytes 98312 | tf_op jit(solution)/shard_map/cond/branch_2_fun/ppermute | solution.py:452
  8.7 7.2 %collective-permute-start.18 = (f32[40,128]{1,0:T(8,128)S(1)}, f32[40,128]{1,0:T(8,128)S(1)}, u32[]{:S(2)}, u32[]{:S(2)}) collective-permute-start(f32[40,128]{1,0:T(8,128)S(1)} %get-tuple-element.95), channel_id=1, source_target_pairs={{0,28},{4,8},{8,4},{12,16},{16,12},{20,24},{24,20},{28,0},{1,29},{... | collective-permute-start | bytes 61448 | tf_op jit(solution)/shard_map/ppermute | solution.py:473
  13.8 3.8 %collective-permute-start.19 = (f32[40,128]{1,0:T(8,128)S(1)}, f32[40,128]{1,0:T(8,128)S(1)}, u32[]{:S(2)}, u32[]{:S(2)}) collective-permute-start(f32[40,128]{1,0:T(8,128)S(1)} %get-tuple-element.96), channel_id=1, source_target_pairs={{0,4},{4,0},{8,12},{12,8},{16,20},{20,16},{24,28},{28,24},{1,5},{5... | collective-permute-start | bytes 61448 | tf_op jit(solution)/shard_map/ppermute | solution.py:472
  13.8 8.6 %collective-permute-start.16 = (f32[64,128]{1,0:T(8,128)S(1)}, f32[64,128]{1,0:T(8,128)S(1)}, u32[]{:S(2)}, u32[]{:S(2)}) collective-permute-start(f32[64,128]{1,0:T(8,128)S(1)} %get-tuple-element.87), channel_id=1, source_target_pairs={{0,28},{4,8},{8,4},{12,16},{16,12},{20,24},{24,20},{28,0},{1,29},{... | collective-permute-start | bytes 98312 | tf_op jit(solution)/shard_map/ppermute | solution.py:473
  15.7 6.7 %collective-permute-start.17 = (f32[64,128]{1,0:T(8,128)S(1)}, f32[64,128]{1,0:T(8,128)S(1)}, u32[]{:S(2)}, u32[]{:S(2)}) collective-permute-start(f32[64,128]{1,0:T(8,128)S(1)} %get-tuple-element.88), channel_id=1, source_target_pairs={{0,4},{4,0},{8,12},{12,8},{16,20},{20,16},{24,28},{28,24},{1,5},{5... | collective-permute-start | bytes 98312 | tf_op jit(solution)/shard_map/ppermute | solution.py:472
  18.9 10.6 %all-to-all-start = ((f32[32,1,128]{2,1,0:T(1,128)}), f32[32,1,128]{2,1,0:T(1,128)S(1)}, u32[]{:S(2)}, u32[]{:S(2)}) async-start(f32[32,1,128]{2,1,0:T(1,128)} %bitcast.10), calls=%async_computation | async-start | bytes 32768 | tf_op jit(solution)/shard_map/all_to_all | solution.py:502

commit v7 on v6

--- a/solution.py
+++ b/solution.py
@@ -264,8 +264,44 @@
     moments[...] = jnp.broadcast_to(sums, moments.shape)
 
 
-def step_kernel(
-    meta, spans, facing, heat, salt, zonal, merid, water, north_came, south_rows, from_far, from_near,
+def lat_parts(cells, north_one, south_one, north_two, south_two, speed):
+    grad = 8.0 * (north_one - south_one) - (north_two - south_two)
+    return (-TIME_STEP / 12.0) * (speed * grad) + MIXING * ((north_one + south_one) - 4.0 * cells)
+
+
+def lat_kernel(meta, spans, heat, salt, merid, water, north_rows, south_rows, part_heat, part_salt, new_merid):
+    levels, rows, cols = heat.shape
+    wet = water[...].astype(jnp.float32)
+    row = iota((rows, cols), 0)
+
+    def around(cells, q):
+        n0 = north_rows[2 * q : 2 * q + 1, :]
+        n1 = north_rows[2 * q + 1 : 2 * q + 2, :]
+        s0 = south_rows[2 * q + 1 : 2 * q + 2, :]
+        s1 = south_rows[2 * q : 2 * q + 1, :]
+        north_one = jnp.where(row == rows - 1, n0, pltpu.roll(cells, rows - 1, 0))
+        north_two = jnp.where(row == rows - 1, n1, jnp.where(row == rows - 2, n0, pltpu.roll(cells, rows - 2, 0)))
+        south_one = jnp.where(row == 0, s0, pltpu.roll(cells, 1, 0))
+        south_two = jnp.where(row == 0, s1, jnp.where(row == 1, s0, pltpu.roll(cells, 2, 0)))
+        return north_one, south_one, north_two, south_two
+
+    half = 0.5 * TIME_STEP
+    above = jnp.zeros((rows, cols), jnp.float32)
+    for k in range(levels):
+        t, s, v = heat[k], salt[k], merid[k]
+        around_t = around(t, k)
+        around_s = around(s, levels + k)
+        part_heat[k] = lat_parts(t, *around_t, v)
+        part_salt[k] = lat_parts(s, *around_s, v)
+        layer = density(around_t[0], around_s[0]) - density(around_t[1], around_s[1])
+        layer = spans[0:1, k : k + 1] * layer
+        new_merid[k] = wet * (v - half * (above + 0.5 * layer))
+        above = above + layer
+
+
+def lon_kernel(
+    meta, spans, facing, heat, salt, zonal, merid, water, part_heat, part_salt, part_merid,
+    north_came, from_far, from_near,
     heat_out, salt_out, zonal_out, merid_out,
     new_heat, new_salt, new_zonal, new_merid, north_rows, sems,
 ):
@@ -274,12 +310,13 @@
     _, top, lon_odd, _ = flags(meta)
     wet = water[...].astype(jnp.float32)
     lane = iota((rows, cols), 1)
-    row = iota((rows, cols), 0)
     east = jnp.where(lon_odd, from_far[...], from_near[...])
     west = jnp.where(lon_odd, from_near[...], from_far[...])
     came = north_came[...]
     across = fold(fold_shift(facing), pltpu.roll(west[:deep], cols // 2, 1), came, east[:deep], False)
     north_rows[...] = jnp.where(top, across, came)
+    tail = rows - 8
+    row = iota((16, cols), 0)
 
     def around(cells, q):
         a = pltpu.roll(east, (cols - 2 * q) % cols, 1)
@@ -292,41 +329,44 @@
             own = lane >= by if by > 0 else lane < cols + by
             return jnp.where(own, a, b)
 
+        return shift_x(-1), shift_x(1), shift_x(-2), shift_x(2)
+
+    def around_tail(cells, q):
         n0 = north_rows[2 * q : 2 * q + 1, :]
         n1 = north_rows[2 * q + 1 : 2 * q + 2, :]
-        s0 = south_rows[2 * q + 1 : 2 * q + 2, :]
-        s1 = south_rows[2 * q : 2 * q + 1, :]
-        north_one = jnp.where(row == rows - 1, n0, pltpu.roll(cells, rows - 1, 0))
-        north_two = jnp.where(row == rows - 1, n1, jnp.where(row == rows - 2, n0, pltpu.roll(cells, rows - 2, 0)))
-        south_one = jnp.where(row == 0, s0, pltpu.roll(cells, 1, 0))
-        south_two = jnp.where(row == 0, s1, jnp.where(row == 1, s0, pltpu.roll(cells, 2, 0)))
-        return (shift_x(-1), shift_x(1), shift_x(-2), shift_x(2), north_one, south_one, north_two, south_two)
-
-    def advance(cells, parts, speed_x, speed_y):
-        e1, w1, e2, w2, n1, s1, n2, s2 = parts
-        grad_east = 8.0 * (e1 - w1) - (e2 - w2)
-        grad_north = 8.0 * (n1 - s1) - (n2 - s2)
-        laplace = (e1 + w1) + (n1 + s1) - 4.0 * cells
-        tendency = (-TIME_STEP / 12.0) * (speed_x * grad_east + speed_y * grad_north) + MIXING * laplace
-        return cells + wet * tendency
+        last = cells[rows - 16 :]
+        north_one = jnp.where(row == 15, n0, pltpu.roll(last, 15, 0))
+        north_two = jnp.where(row == 15, n1, jnp.where(row == 14, n0, pltpu.roll(last, 14, 0)))
+        south_one = pltpu.roll(last, 1, 0)
+        south_two = pltpu.roll(last, 2, 0)
+        return tuple(part[8:] for part in (north_one, south_one, north_two, south_two))
+
+    def advance(cells, parts, part, again, speed):
+        e1, w1, e2, w2 = parts
+        grad = 8.0 * (e1 - w1) - (e2 - w2)
+        change = (-TIME_STEP / 12.0) * (speed * grad) + MIXING * (e1 + w1)
+        return cells + wet * (change + jnp.concatenate([part[:tail], again], axis=0))
 
     stores = ((new_heat, heat_out), (new_salt, salt_out), (new_zonal, zonal_out), (new_merid, merid_out))
     size = levels // sems.shape[1]
     copies = []
     half = 0.5 * TIME_STEP
     above_x = jnp.zeros((rows, cols), jnp.float32)
-    above_y = jnp.zeros((rows, cols), jnp.float32)
+    above_y = jnp.zeros((8, cols), jnp.float32)
     for k in range(levels):
-        t, s, u, v = heat[k], salt[k], zonal[k], merid[k]
+        t, s, u, v = heat[k], salt[k], zonal[k], merid[k][tail:]
         around_t = around(t, k)
         around_s = around(s, levels + k)
-        new_heat[k] = advance(t, around_t, u, v)
-        new_salt[k] = advance(s, around_s, u, v)
+        tail_t = around_tail(t, k)
+        tail_s = around_tail(s, levels + k)
+        new_heat[k] = advance(t, around_t, part_heat[k], lat_parts(t[tail:], *tail_t, v), u)
+        new_salt[k] = advance(s, around_s, part_salt[k], lat_parts(s[tail:], *tail_s, v), u)
         span = spans[0:1, k : k + 1]
         layer_x = span * (density(around_t[0], around_s[0]) - density(around_t[1], around_s[1]))
-        layer_y = span * (density(around_t[4], around_s[4]) - density(around_t[5], around_s[5]))
+        layer_y = span * (density(tail_t[0], tail_s[0]) - density(tail_t[1], tail_s[1]))
         new_zonal[k] = wet * (u - half * (above_x + 0.5 * layer_x))
-        new_merid[k] = wet * (v - half * (above_y + 0.5 * layer_y))
+        new_merid[k, :tail, :] = part_merid[k, :tail, :]
+        new_merid[k, tail:, :] = wet[tail:] * (v - half * (above_y + 0.5 * layer_y))
         above_x = above_x + layer_x
         above_y = above_y + layer_y
         if (k + 1) % size == 0:
@@ -407,7 +447,7 @@
     lons, lats = lax.axis_size("lon"), lax.axis_size("lat")
     lon, lat = lax.axis_index("lon"), lax.axis_index("lat")
     levels, rows, cols = warmth_deviation.shape
-    assert cols & (cols - 1) == 0 and 4 * levels <= cols // 2 and 2 * START[-1] <= RELAY and cols == 128
+    assert cols & (cols - 1) == 0 and 4 * levels <= cols // 2 and 2 * START[-1] <= RELAY and cols == 128 and rows >= 16
     high = packet_rows(levels)
     tall = rows + 16
     width = cols * lons
@@ -472,7 +512,6 @@
     near = lambda cells: lax.ppermute(cells, "lon", [(i, i ^ 1) for i in range(lons)])
     far = lambda cells: lax.ppermute(cells, "lon", [(i, (i + 1 if i % 2 else i - 1) % lons) for i in range(lons)])
     from_far, from_near = far(to_far), near(to_near)
-    state_far, state_near = far(state_far), near(state_near)
 
     count = lons * lats
     base, moments = call(
@@ -484,20 +523,31 @@
         scratch=[pltpu.VMEM((2, high - deep + 8, cols), jnp.float32)],
     )(meta, facing, ext, facing_rows, from_far, from_near)
 
+    (moments, state_far, state_near, north_rows, south_rows) = lax.optimization_barrier(
+        (moments, state_far, state_near, north_rows, south_rows)
+    )
+    state_far, state_near = far(state_far), near(state_near)
+    part_heat, part_salt, part_merid = call(
+        lat_kernel,
+        [(levels, rows, cols)] * 3,
+        60 * cells,
+        24 * cells,
+        "latitude_step",
+    )(meta, spans, *state[:2], state[3], water_indicator, north_rows, south_rows)
     chunks = 5 if levels % 5 == 0 else 1
     new_heat, new_salt, new_zonal, new_merid = call(
-        step_kernel,
+        lon_kernel,
         [(levels, rows, cols)] * 4,
-        120 * cells,
+        80 * cells,
         32 * cells,
-        "levels_step",
+        "longitude_step",
         out_space=pltpu.HBM,
         scratch=[
             *[pltpu.VMEM((levels, rows, cols), jnp.float32)] * 4,
             pltpu.VMEM((deep, cols), jnp.float32),
             pltpu.SemaphoreType.DMA((4, chunks)),
         ],
-    )(meta, spans, facing, *state, water_indicator, north_rows, south_rows, state_far, state_near)
+    )(meta, spans, facing, *state, water_indicator, part_heat, part_salt, part_merid, north_rows, state_far, state_near)
 
     shares = lax.all_to_all(moments, axes, 0, 0, tiled=True)
     (surface,) = call(surface_kernel, [(rows, cols)], 6 * rows * cols, 16 * rows * cols, "surface")(shares, base)

time: 30.5 us -> 36.6 us (1.20)
  waiting for transfers between devices: 6.9 us -> 12 us
  Pallas kernels: 7.37 us -> 7.96 us
  starting transfers between devices: 13.9 us -> 14.3 us
    all_to_all x1, waiting for transfers between devices: 3.29 us -> 6.39 us  [body(): shares = lax.all_to_all(moments, axes, 0, 0, tiled=True)]
    ppermute x2, waiting for transfers between devices: 0.01 us -> 1.77 us  [body(): lax.ppermute(cells, 'lon', [(i, (i + 1 if i % 2 else i - 1) % lons) for i...]
    ppermute x2, starting transfers between devices: 7.06 us -> 7.82 us  [body(): lax.ppermute(cells, 'lon', [(i, (i + 1 if i % 2 else i - 1) % lons) for i...]
    pallas_call x6 -> x7, Pallas kernels: 7.37 us -> 7.96 us  [run(): pl.pallas_call(kernel, out_shape=[jax.ShapeDtypeStruct(shape, types) for...]
  transfers between devices with their start and end apart: 7 -> 7, of which waited for: 3 -> 4; matrix products, arithmetic and copies ran while one was open for 0% -> 0% of each run, Pallas kernels for 17% -> 4%
where the time goes in v7:
time: 36.6 us; the launch traced here: 36.4 us
  starting transfers between devices  14.3 us (39%)
  waiting for transfers between devices  12 us (33%)
  Pallas kernels  7.96 us (22%)
  local copies, waits for them, and re-layouts  1.26 us (3%)
  between operations  0.81 us (2%)
    pallas_call x7, Pallas kernels, run(): pl.pallas_call(kernel, out_shape=[jax.ShapeDtypeStruct(shape, types) for...  7.96 us
    ppermute x2, starting transfers between devices, body(): lax.ppermute(cells, 'lon', [(i, (i + 1 if i % 2 else i - 1) % lons) for i...  7.82 us
    all_to_all x1, waiting for transfers between devices, body(): shares = lax.all_to_all(moments, axes, 0, 0, tiled=True)  6.39 us
    all_to_all x1, starting transfers between devices, body(): shares = lax.all_to_all(moments, axes, 0, 0, tiled=True)  3.33 us
    ppermute x1, starting transfers between devices, exchange(): second = lax.ppermute(second, axes, pairs_inner + pairs_fold)  3 us
    ppermute x2, waiting for transfers between devices, body(): lax.ppermute(cells, 'lon', [(i, i ^ 1) for i in range(lons)])  2.01 us
    ppermute x1, waiting for transfers between devices, exchange(): second = lax.ppermute(second, axes, pairs_inner + pairs_fold)  1.86 us
    ppermute x2, waiting for transfers between devices, body(): lax.ppermute(cells, 'lon', [(i, (i + 1 if i % 2 else i - 1) % lons) for i...  1.77 us
  transfers between devices with their start and end apart: 7, of which 4 were waited for; matrix products, arithmetic and copies ran while one was open for 0% of the time, Pallas kernels for 4%

profile of v7, /device:TPU:0, one launch (start us, length us, event | category | flops | bytes accessed | tf_op | source)
XLA Modules:
  0.0 36.4 jit_solution(17155617609632671329)
XLA Ops:
  0.6 0.1 stack.31
  0.7 0.0 copy-start.3
  0.7 0.0 copy-start.4
  0.8 0.0 copy-start.5
  0.8 0.0 copy-start.6
  0.8 0.1 place.1.meta
  0.9 0.8 %copy-done = f32[10,64,128]{2,1,0:T(8,128)S(1)} copy-done((f32[10,64,128]{2,1,0:T(8,128)S(1)}, f32[10,64,128]{2,1,0:T(8,128)}, u32[]{:S(2)}) %copy-start) | copy-done | bytes 327704
  1.7 0.1 copy-done.1
  1.8 0.1 copy-done.2
  1.9 0.1 copy-done.3
  2.0 0.0 copy-done.4
  2.0 0.5 %level_sums.1 = (f32[3,64,128]{2,1,0:T(8,128)S(1)}, f32[64,128]{1,0:T(8,128)S(1)}, f32[64,128]{1,0:T(8,128)S(1)}, f32[64,128]{1,0:T(8,128)S(1)}, f32[64,128]{1,0:T(8,128)S(1)}) custom-call(s32[8,128]{1,0:T(8,128)S(1)} %place.1.meta, f32[1,10]{1,0:T(1,128)S(1)} %bitcast.20, s32[1,128]{1,0:T(1,128)S(1)} %bitcast.15, f32[10,64,128]{2,1,0:T(8,128)S(1)} %copy-done, ...), custom_call_target="tpu_custom_call" | custom-call | flops 983040 | bytes 1310720 | tf_op jit(solution)/shard_map/level_sums/pallas_call | solution.py:422
  2.6 5.0 %conditional.1 = (f32[64,128]{1,0:T(8,128)}, f32[64,128]{1,0:T(8,128)}) conditional(s32[]{:T(128)} %clamp.3, (f32[64,128]{1,0:T(8,128)S(1)}, f32[64,128]{1,0:T(8,128)S(1)}) %tuple.43, (f32[64,128]{1,0:T(8,128)S(1)}, f32[64,128]{1,0:T(8,128)S(1)}) %tuple.43, (f32[64,128]{1,0:T(8,128)S(1)}, ...), branch_computations={%region_0.1_spmd, %region_1.2_spmd, %region_2.3_spmd, %region_3.4_... | conditional | bytes 262240 | solution.py:495
  2.7 3.0 %collective-permute-start.6 = (f32[64,128]{1,0:T(8,128)S(1)}, f32[64,128]{1,0:T(8,128)}, u32[]{:S(2)}, u32[]{:S(2)}) collective-permute-start(f32[64,128]{1,0:T(8,128)S(1)} %get-tuple-element.38), channel_id=1, source_target_pairs={{1,2},{2,1},{5,6},{6,5},{9,10},{10,9},{13,14},{14,13},{17,18},{18,... | collective-permute-start | bytes 98312 | tf_op jit(solution)/shard_map/cond/branch_3_fun/ppermute | solution.py:491
  5.7 0.1 collective-permute-start.7
  5.8 1.9 %collective-permute-done.6 = f32[64,128]{1,0:T(8,128)} collective-permute-done((f32[64,128]{1,0:T(8,128)S(1)}, f32[64,128]{1,0:T(8,128)}, u32[]{:S(2)}, u32[]{:S(2)}) %collective-permute-start.6) | collective-permute-done | bytes 32800 | tf_op jit(solution)/shard_map/cond/branch_3_fun/ppermute | solution.py:491
  7.7 0.0 collective-permute-done.7
  7.7 1.0 %row_halos.1 = (f32[6,80,128]{2,1,0:T(8,128)S(1)}, f32[40,128]{1,0:T(8,128)S(1)}, f32[40,128]{1,0:T(8,128)S(1)}, f32[64,128]{1,0:T(8,128)S(1)}, f32[64,128]{1,0:...) custom-call(s32[8,128]{1,0:T(8,128)S(1)} %place.1.meta, s32[1,128]{1,0:T(1,128)S(1)} %bitcast.17, ...), custom_call_target="tpu_custom_call" | custom-call | flops 61440 | bytes 983040 | tf_op jit(solution)/shard_map/row_halos/pallas_call | solution.py:422
  8.7 5.1 %collective-permute-start.16 = (f32[40,128]{1,0:T(8,128)S(1)}, f32[40,128]{1,0:T(8,128)S(1)}, u32[]{:S(2)}, u32[]{:S(2)}) collective-permute-start(f32[40,128]{1,0:T(8,128)S(1)} %get-tuple-element.95), channel_id=1, source_target_pairs={{0,28},{4,8},{8,4},{12,16},{16,12},{20,24},{24,20},{28,0},{1,29},{... | collective-permute-start | bytes 61448 | tf_op jit(solution)/shard_map/ppermute | solution.py:513
  13.8 0.0 collective-permute-start.17
  13.8 1.8 %collective-permute-done.16.from_far = f32[40,128]{1,0:T(8,128)S(1)} collective-permute-done((f32[40,128]{1,0:T(8,128)S(1)}, f32[40,128]{1,0:T(8,128)S(1)}, u32[]{:S(2)}, u32[]{:S(2)}) %collective-permute-start.16) | collective-permute-done | bytes 20512 | tf_op jit(solution)/shard_map/ppermute | solution.py:513
  15.6 2.0 %collective-permute-done.17.from_near = f32[40,128]{1,0:T(8,128)S(1)} collective-permute-done((f32[40,128]{1,0:T(8,128)S(1)}, f32[40,128]{1,0:T(8,128)S(1)}, u32[]{:S(2)}, u32[]{:S(2)}) %collective-permute-start.17) | collective-permute-done | bytes 20512 | tf_op jit(solution)/shard_map/ppermute | solution.py:512
  17.6 1.3 %krylov.1 = (f32[3,64,128]{2,1,0:T(8,128)S(1)}, f32[32,128]{1,0:T(8,128)}) custom-call(s32[8,128]{1,0:T(8,128)S(1)} %place.1.meta, s32[1,128]{1,0:T(1,128)S(1)} %bitcast.18, f32[6,80,128]{2,1,0:T(8,128)S(1)} %get-tuple-element.93.ext, f32[24,128]{1,0:T(8,128)S(1)} %get-tuple-element.94.facing_rows, f32[40,128]{1,0:T(8,128)S(1)} %collective-permute-done.16.from_far, ...), custom_call_target="tpu_custom_call" | custom-call | flops 2048000 | bytes 491520 | tf_op jit(solution)/shard_map/krylov/pallas_call | solution.py:422
  18.8 2.7 %collective-permute-start.18 = (f32[64,128]{1,0:T(8,128)S(1)}, f32[64,128]{1,0:T(8,128)S(1)}, u32[]{:S(2)}, u32[]{:S(2)}) collective-permute-start(f32[64,128]{1,0:T(8,128)S(1)} %get-tuple-element.107), channel_id=1, source_target_pairs={{0,28},{4,8},{8,4},{12,16},{16,12},{20,24},{24,20},{28,0},{1,29},{... | collective-permute-start | bytes 98312 | tf_op jit(solution)/shard_map/ppermute | solution.py:513
  21.5 0.0 collective-permute-start.19
  21.5 3.3 %all-to-all-start = ((f32[32,1,128]{2,1,0:T(1,128)}), f32[32,1,128]{2,1,0:T(1,128)S(1)}, u32[]{:S(2)}, u32[]{:S(2)}) async-start(f32[32,1,128]{2,1,0:T(1,128)} %bitcast.10), calls=%async_computation | async-start | bytes 32768 | tf_op jit(solution)/shard_map/all_to_all | solution.py:552
  24.9 0.7 %latitude_step.1 = (f32[10,64,128]{2,1,0:T(8,128)S(1)}, f32[10,64,128]{2,1,0:T(8,128)S(1)}, f32[10,64,128]{2,1,0:T(8,128)S(1)}) custom-call(s32[8,128]{1,0:T(8,128)S(1)} %place.1.meta, f32[1,10]{1,0:T(1,128)S(1)} %bitcast.21, f32[10,64,128]{2,1,0:T(8,128)S(1)} %copy-done, f32[10,64,128]{2,1,0:T(8,128)S(1)} %copy-done.1, f32[10,64,128]{2,1,0:T(8,128)S(1)} %copy-done.2, ...), custom_call_target="tpu_custom_call" | custom-call | flops 4915200 | bytes 1966080 | tf_op jit(solution)/shard_map/latitude_step/pallas_call | solution.py:422
  25.6 6.4 %all-to-all-done = f32[32,1,128]{2,1,0:T(1,128)S(1)} async-done(((f32[32,1,128]{2,1,0:T(1,128)}), f32[32,1,128]{2,1,0:T(1,128)S(1)}, u32[]{:S(2)}, u32[]{:S(2)}) %all-to-all-start) | async-done | bytes 16416 | tf_op jit(solution)/shard_map/all_to_all | solution.py:552
  31.9 0.8 %surface.1 = f32[64,128]{1,0:T(8,128)} custom-call(f32[32,128]{1,0:T(8,128)S(1)} %bitcast.14, f32[3,64,128]{2,1,0:T(8,128)S(1)} %get-tuple-element.114.base), custom_call_target="tpu_custom_call" | custom-call | flops 49152 | bytes 131072 | tf_op jit(solution)/shard_map/surface/pallas_call | solution.py:422
  32.7 0.0 collective-permute-done.18.from_far
  32.7 0.0 collective-permute-done.19.from_near
  32.7 3.7 %longitude_step.1 = (f32[10,64,128]{2,1,0:T(8,128)}, f32[10,64,128]{2,1,0:T(8,128)}, f32[10,64,128]{2,1,0:T(8,128)}, f32[10,64,128]{2,1,0:T(8,128)}) custom-call(s32[8,128]{1,0:T(8,128)S(1)} %place.1.meta, f32[1,10]{1,0:T(1,128)S(1)} %bitcast.22, s32[1,128]{1,0:T(1,128)S(1)} %bitcast.19, f32[10,64,128]{2,1,0:T(8,128)S(1)} %copy-done, ...), custom_call_target="tpu_custom_call" | custom-call | flops 6553600 | bytes 2621440 | tf_op jit(solution)/shard_map/longitude_step/pallas_call | solution.py:422
  (9 shorter events, 0.0 us)
Async XLA Ops:
  0.7 1.0 %copy-start = (f32[10,64,128]{2,1,0:T(8,128)S(1)}, f32[10,64,128]{2,1,0:T(8,128)}, u32[]{:S(2)}) copy-start(f32[10,64,128]{2,1,0:T(8,128)} %heat.5) | copy-start | bytes 983044
  0.7 1.1 %copy-start.1 = (f32[10,64,128]{2,1,0:T(8,128)S(1)}, f32[10,64,128]{2,1,0:T(8,128)}, u32[]{:S(2)}) copy-start(f32[10,64,128]{2,1,0:T(8,128)} %salt.5) | copy-start | bytes 983044
  0.7 1.2 %copy-start.2 = (f32[10,64,128]{2,1,0:T(8,128)S(1)}, f32[10,64,128]{2,1,0:T(8,128)}, u32[]{:S(2)}) copy-start(f32[10,64,128]{2,1,0:T(8,128)} %merid.5) | copy-start | bytes 983044
  0.7 1.3 %copy-start.3 = (f32[10,64,128]{2,1,0:T(8,128)S(1)}, f32[10,64,128]{2,1,0:T(8,128)}, u32[]{:S(2)}) copy-start(f32[10,64,128]{2,1,0:T(8,128)} %zonal.3) | copy-start | bytes 983044
  0.7 1.3 %copy-start.4 = (s32[64,128]{1,0:T(8,128)S(1)}, s32[64,128]{1,0:T(8,128)}, u32[]{:S(2)}) copy-start(s32[64,128]{1,0:T(8,128)} %water.7) | copy-start | bytes 98308
  0.8 1.2 %copy-start.5 = (f32[64,128]{1,0:T(8,128)S(1)}, f32[64,128]{1,0:T(8,128)}, u32[]{:S(2)}) copy-start(f32[64,128]{1,0:T(8,128)} %weights.3) | copy-start | bytes 98308
  0.8 1.2 %copy-start.6 = (f32[64,128]{1,0:T(8,128)S(1)}, f32[64,128]{1,0:T(8,128)}, u32[]{:S(2)}) copy-start(f32[64,128]{1,0:T(8,128)} %anomaly.3) | copy-start | bytes 98308
  0.9 1.2 %copy-start.7 = (s32[128]{0:T(128)S(1)}, s32[128]{0:T(128)}, u32[]{:S(2)}) copy-start(s32[128]{0:T(128)} %param.23) | copy-start | bytes 1540
  0.9 1.2 %copy-start.8 = (f32[10]{0:T(128)S(1)}, f32[10]{0:T(128)}, u32[]{:S(2)}) copy-start(f32[10]{0:T(128)} %param.21) | copy-start | bytes 124
  2.7 5.0 %collective-permute-start.6 = (f32[64,128]{1,0:T(8,128)S(1)}, f32[64,128]{1,0:T(8,128)}, u32[]{:S(2)}, u32[]{:S(2)}) collective-permute-start(f32[64,128]{1,0:T(8,128)S(1)} %get-tuple-element.38), channel_id=1, source_target_pairs={{1,2},{2,1},{5,6},{6,5},{9,10},{10,9},{13,14},{14,13},{17,18},{18,... | collective-permute-start | bytes 98312 | tf_op jit(solution)/shard_map/cond/branch_3_fun/ppermute | solution.py:491
  5.7 2.0 %collective-permute-start.7 = (f32[64,128]{1,0:T(8,128)S(1)}, f32[64,128]{1,0:T(8,128)}, u32[]{:S(2)}, u32[]{:S(2)}) collective-permute-start(f32[64,128]{1,0:T(8,128)S(1)} %get-tuple-element.39), channel_id=1, source_target_pairs={{0,1},{1,0},{2,3},{3,2},{4,5},{5,4},{6,7},{7,6},{8,9},{9,8},{10,11... | collective-permute-start | bytes 98312 | tf_op jit(solution)/shard_map/cond/branch_3_fun/ppermute | solution.py:492
  8.7 6.9 %collective-permute-start.16 = (f32[40,128]{1,0:T(8,128)S(1)}, f32[40,128]{1,0:T(8,128)S(1)}, u32[]{:S(2)}, u32[]{:S(2)}) collective-permute-start(f32[40,128]{1,0:T(8,128)S(1)} %get-tuple-element.95), channel_id=1, source_target_pairs={{0,28},{4,8},{8,4},{12,16},{16,12},{20,24},{24,20},{28,0},{1,29},{... | collective-permute-start | bytes 61448 | tf_op jit(solution)/shard_map/ppermute | solution.py:513
  13.8 3.8 %collective-permute-start.17 = (f32[40,128]{1,0:T(8,128)S(1)}, f32[40,128]{1,0:T(8,128)S(1)}, u32[]{:S(2)}, u32[]{:S(2)}) collective-permute-start(f32[40,128]{1,0:T(8,128)S(1)} %get-tuple-element.96), channel_id=1, source_target_pairs={{0,4},{4,0},{8,12},{12,8},{16,20},{20,16},{24,28},{28,24},{1,5},{5... | collective-permute-start | bytes 61448 | tf_op jit(solution)/shard_map/ppermute | solution.py:512
  18.8 13.9 %collective-permute-start.18 = (f32[64,128]{1,0:T(8,128)S(1)}, f32[64,128]{1,0:T(8,128)S(1)}, u32[]{:S(2)}, u32[]{:S(2)}) collective-permute-start(f32[64,128]{1,0:T(8,128)S(1)} %get-tuple-element.107), channel_id=1, source_target_pairs={{0,28},{4,8},{8,4},{12,16},{16,12},{20,24},{24,20},{28,0},{1,29},{... | collective-permute-start | bytes 98312 | tf_op jit(solution)/shard_map/ppermute | solution.py:513
  21.5 11.2 %collective-permute-start.19 = (f32[64,128]{1,0:T(8,128)S(1)}, f32[64,128]{1,0:T(8,128)S(1)}, u32[]{:S(2)}, u32[]{:S(2)}) collective-permute-start(f32[64,128]{1,0:T(8,128)S(1)} %get-tuple-element.108), channel_id=1, source_target_pairs={{0,4},{4,0},{8,12},{12,8},{16,20},{20,16},{24,28},{28,24},{1,5},{5... | collective-permute-start | bytes 98312 | tf_op jit(solution)/shard_map/ppermute | solution.py:512
  21.5 10.4 %all-to-all-start = ((f32[32,1,128]{2,1,0:T(1,128)}), f32[32,1,128]{2,1,0:T(1,128)S(1)}, u32[]{:S(2)}, u32[]{:S(2)}) async-start(f32[32,1,128]{2,1,0:T(1,128)} %bitcast.10), calls=%async_computation | async-start | bytes 32768 | tf_op jit(solution)/shard_map/all_to_all | solution.py:552

commit v8 on v6

--- a/solution.py
+++ b/solution.py
@@ -164,7 +164,32 @@
     return jnp.take_along_axis(merged, cols - 1 - ((lane - shift) & (cols - 1)), axis=1)
 
 
-def krylov_kernel(meta, facing, ext, facing_rows, from_far, from_near, base, moments, folded):
+def shift_kernel(ext, shift):
+    rows, cols = ext.shape[1] - 16, ext.shape[2]
+    press, zonal, merid, wet, weights, anomaly = (ext[f, :rows, :] for f in range(FIELDS))
+    plus_x = lambda cells: pltpu.roll(cells, cols - 1, 1)
+    minus_x = lambda cells: pltpu.roll(cells, 1, 1)
+    plus_y = lambda cells: pltpu.roll(cells, rows - 1, 0)
+    minus_y = lambda cells: pltpu.roll(cells, 1, 0)
+    half = 0.5 * TIME_STEP
+    east_flow = wet * (zonal - half * (plus_x(press) - minus_x(press)))
+    north_flow = wet * (merid - half * (plus_y(press) - minus_y(press)))
+    spread = plus_x(east_flow) - minus_x(east_flow) + plus_y(north_flow) - minus_y(north_flow)
+    right = wet * (weights * anomaly - 0.5 * spread)
+    inverse = 1.0 / (4.0 + weights)
+    zero = right * inverse
+    one = wet * inverse * (plus_x(zero) + minus_x(zero) + plus_y(zero) + minus_y(zero))
+    lane = iota((rows, cols), 1)
+    row = iota((rows, cols), 0)
+    inside = (lane >= 8) & (lane < cols - 8) & (row >= 8) & (row < rows - 8)
+    total = lambda cells: jnp.sum(jnp.sum(jnp.where(inside, cells, 0.0), axis=0, keepdims=True), axis=1, keepdims=True)
+    below = total(right * zero)
+    good = below > 0.0
+    quotient = jnp.where(good, total(right * one) / jnp.where(good, below, 1.0), 0.0)
+    shift[...] = jnp.broadcast_to(quotient, shift.shape)
+
+
+def krylov_kernel(meta, facing, shift, ext, facing_rows, from_far, from_near, base, moments, folded):
     tall, cols = ext.shape[1], ext.shape[2]
     rows = base.shape[1]
     size = facing_rows.shape[0]
@@ -172,11 +197,12 @@
     _, top, lon_odd, _ = flags(meta)
     west = jnp.where(lon_odd, from_near[...], from_far[...])
     east = jnp.where(lon_odd, from_far[...], from_near[...])
-    shift = fold_shift(facing)
+    theta = shift[0:1, 0:1]
+    across = fold_shift(facing)
     row = iota((size, cols), 0)
     flips = (row >= ROW[FLIPPED[0]]) & (row < ROW[FLIPPED[-1] + 1])
     for side in range(2):
-        cells = fold(shift, pltpu.roll(west[:size], cols - RELAY, 1), facing_rows[...], east[:size], side == 1)
+        cells = fold(across, pltpu.roll(west[:size], cols - RELAY, 1), facing_rows[...], east[:size], side == 1)
         folded[side, :size, :] = jnp.where(flips, -cells, cells)
     folded[:, size:, :] = jnp.zeros((2, folded.shape[1] - size, cols), jnp.float32)
     lane = iota((tall, cols), 1)
@@ -238,29 +264,34 @@
     inverse = each(lambda m: 1.0 / m, diagonal)
     scale = each(lambda w, i: w * i, wet, inverse)
     zero = each(lambda r, i: r * i, right, inverse)
-    one = each(lambda a, n: a * n, scale, neighbours(zero))
-    two = each(lambda a, n: a * n, scale, neighbours(one))
-    last_sum = neighbours(two)[0][:rows]
+    one = each(lambda a, n, z: a * n - theta * z, scale, neighbours(zero), zero)
+    two = each(lambda a, n, z: a * n - theta * z, scale, neighbours(one), one)
+    three = scale[0][:rows] * neighbours(two)[0][:rows] - theta * two[0][:rows]
     right, middle = right[0][:rows], diagonal[0][:rows]
     zero, one, two = zero[0][:rows], one[0][:rows], two[0][:rows]
     base[0] = zero
     base[1] = one
     base[2] = two
-    weighted = middle * one
+    weighted_one = middle * one
+    weighted_two = middle * two
     products = (
         right * zero,
         right * one,
-        weighted * one,
-        weighted * two,
-        middle * two * two,
-        last_sum * two,
+        right * two,
+        right * three,
+        weighted_one * one,
+        weighted_one * two,
+        weighted_one * three,
+        weighted_two * two,
+        weighted_two * three,
     )
-    which = iota((8, cols), 0)
-    sums = jnp.zeros((8, cols), jnp.float32)
+    which = iota((16, cols), 0)
+    place = iota((16, cols), 1)
+    sums = jnp.where((which == len(products)) & (place == 0), theta, 0.0)
     for k, product in enumerate(products):
         sums = jnp.where(which == k, jnp.sum(product, axis=0, keepdims=True), sums)
     sums = jnp.sum(sums, axis=1, keepdims=True)
-    sums = jnp.sum(jnp.where(which == iota((8, cols), 1), sums, 0.0), axis=0, keepdims=True)
+    sums = jnp.sum(jnp.where(which == place, sums, 0.0), axis=0, keepdims=True)
     moments[...] = jnp.broadcast_to(sums, moments.shape)
 
 
@@ -338,10 +369,12 @@
         copy.wait()
 
 
-def surface_kernel(shares, base, surface):
-    sums = jnp.sum(shares[...], axis=0, keepdims=True)
-    lane = iota(sums.shape, 1)
-    nu = [jnp.sum(jnp.where(lane == k, sums, 0.0), axis=1, keepdims=True) for k in range(6)]
+def surface_kernel(shares, shift, base, surface):
+    lanes = shares.shape[1]
+    g00, g01, g02, g03, g11, g12, g13, g22, g23, theta = (
+        shares[...] if k == 0 else pltpu.roll(shares[...], lanes - k, 1) for k in range(10)
+    )
+    add = lambda terms: jnp.sum(terms, axis=0, keepdims=True)
 
     def ratio(a, b):
         good = b > 0.0
@@ -355,25 +388,38 @@
                 total = total + (term if i == j else 2.0 * term)
         return total
 
-    gap = [nu[k] - nu[k + 1] for k in range(5)]
-    rz = nu[0]
-    alpha = ratio(rz, gap[0])
-    one = jnp.ones_like(rz)
-    y = [one - alpha, alpha]
+    whole = add(g00)
+    common = ratio(add(theta * g00 + g01), whole)
+    d = theta - common
+    mu = [
+        whole,
+        add(g01 + d * g00),
+        add(g11 + d * (2.0 * g01 + d * g00)),
+        add(g12 + d * (2.0 * g11 + g02 + d * (3.0 * g01 + d * g00))),
+        add(g22 + d * (4.0 * g12 + d * (2.0 * g02 + 4.0 * g11 + d * (4.0 * g01 + d * g00)))),
+        add(
+            g23
+            + d * (3.0 * g22 + 2.0 * g13 + d * (9.0 * g12 + g03 + d * (4.0 * g02 + 6.0 * g11 + d * (5.0 * g01 + d * g00))))
+        ),
+    ]
+    scale = 1.0 - common
+    gap = [scale * mu[k] - mu[k + 1] for k in range(5)]
+    alpha = ratio(mu[0], gap[0])
+    y = [-alpha * ratio(mu[1], mu[0]), alpha]
     x = [alpha, 0.0, 0.0]
-    new = form(y, nu)
-    beta = ratio(new, rz)
-    rz = new
-    p = [y[0] + beta, y[1]]
+    rz = form(y, mu)
+    p = [y[0] + ratio(rz, mu[0]), y[1]]
     alpha = ratio(rz, form(p, gap))
     x = [x[0] + alpha * p[0], alpha * p[1], 0.0]
-    y = [y[0] - alpha * p[0], y[1] - alpha * (p[1] - p[0]), alpha * p[1]]
-    new = form(y, nu)
+    y = [y[0] - alpha * scale * p[0], y[1] - alpha * (scale * p[1] - p[0]), alpha * p[1]]
+    new = form(y, mu)
     beta = ratio(new, rz)
-    rz = new
     p = [y[0] + beta * p[0], y[1] + beta * p[1], y[2]]
-    alpha = ratio(rz, form(p, gap))
+    alpha = ratio(new, form(p, gap))
     x = [x[0] + alpha * p[0], x[1] + alpha * p[1], alpha * p[2]]
+    d = shift[0:1, :] - common
+    x = [x[0] + d * (x[1] + d * x[2]), x[1] + 2.0 * d * x[2], x[2]]
+    x = [value[0:1, 0:1] for value in x]
     surface[...] = x[0] * base[0] + x[1] * base[1] + x[2] * base[2]
 
 
@@ -407,7 +453,7 @@
     lons, lats = lax.axis_size("lon"), lax.axis_size("lat")
     lon, lat = lax.axis_index("lon"), lax.axis_index("lat")
     levels, rows, cols = warmth_deviation.shape
-    assert cols & (cols - 1) == 0 and 4 * levels <= cols // 2 and 2 * START[-1] <= RELAY and cols == 128
+    assert cols & (cols - 1) == 0 and rows >= 24 and 4 * levels <= cols // 2 and 2 * START[-1] <= RELAY and cols == 128
     high = packet_rows(levels)
     tall = rows + 16
     width = cols * lons
@@ -474,6 +520,8 @@
     from_far, from_near = far(to_far), near(to_near)
     state_far, state_near = far(state_far), near(state_near)
 
+    (shift,) = call(shift_kernel, [(8, cols)], 60 * rows * cols, 24 * rows * cols, "basis_shift")(ext)
+
     count = lons * lats
     base, moments = call(
         krylov_kernel,
@@ -482,7 +530,7 @@
         4 * 12 * tall * cols,
         "krylov",
         scratch=[pltpu.VMEM((2, high - deep + 8, cols), jnp.float32)],
-    )(meta, facing, ext, facing_rows, from_far, from_near)
+    )(meta, facing, shift, ext, facing_rows, from_far, from_near)
 
     chunks = 5 if levels % 5 == 0 else 1
     new_heat, new_salt, new_zonal, new_merid = call(
@@ -500,7 +548,7 @@
     )(meta, spans, facing, *state, water_indicator, north_rows, south_rows, state_far, state_near)
 
     shares = lax.all_to_all(moments, axes, 0, 0, tiled=True)
-    (surface,) = call(surface_kernel, [(rows, cols)], 6 * rows * cols, 16 * rows * cols, "surface")(shares, base)
+    (surface,) = call(surface_kernel, [(rows, cols)], 6 * rows * cols, 16 * rows * cols, "surface")(shares, shift, base)
     return (new_heat, new_salt, new_zonal, new_merid, surface)
 
 

time: 30.5 us -> 30.8 us (level)
  Pallas kernels: 7.37 us -> 7.76 us
    pallas_call x6 -> x7, Pallas kernels: 7.37 us -> 7.76 us  [run(): pl.pallas_call(kernel, out_shape=[jax.ShapeDtypeStruct(shape, types) for...]
where the time goes in v8:
time: 30.8 us; the launch traced here: 30.4 us
  starting transfers between devices  14 us (45%)
  Pallas kernels  7.76 us (25%)
  waiting for transfers between devices  6.6 us (21%)
  local copies, waits for them, and re-layouts  1.26 us (4%)
  between operations  0.82 us (3%)
    pallas_call x7, Pallas kernels, run(): pl.pallas_call(kernel, out_shape=[jax.ShapeDtypeStruct(shape, types) for...  7.76 us
    ppermute x2, starting transfers between devices, body(): lax.ppermute(cells, 'lon', [(i, (i + 1 if i % 2 else i - 1) % lons) for i...  7.06 us
    all_to_all x1, starting transfers between devices, body(): shares = lax.all_to_all(moments, axes, 0, 0, tiled=True)  3.64 us
    all_to_all x1, waiting for transfers between devices, body(): shares = lax.all_to_all(moments, axes, 0, 0, tiled=True)  3.29 us
    ppermute x1, starting transfers between devices, exchange(): second = lax.ppermute(second, axes, pairs_inner + pairs_fold)  3 us
    ppermute x1, waiting for transfers between devices, exchange(): second = lax.ppermute(second, axes, pairs_inner + pairs_fold)  1.86 us
    ppermute x2, waiting for transfers between devices, body(): lax.ppermute(cells, 'lon', [(i, i ^ 1) for i in range(lons)])  1.44 us
    unnamed x18, local copies, waits for them, and re-layouts  1.17 us
  transfers between devices with their start and end apart: 7, of which 3 were waited for; matrix products, arithmetic and copies ran while one was open for 0% of the time, Pallas kernels for 17%

profile of v8, /device:TPU:0, one launch (start us, length us, event | category | flops | bytes accessed | tf_op | source)
XLA Modules:
  0.0 30.4 jit_solution(16990095534878816486)
XLA Ops:
  0.6 0.1 stack.31
  0.7 0.0 copy-start.3
  0.7 0.0 copy-start.4
  0.8 0.0 copy-start.5
  0.8 0.0 copy-start.6
  0.8 0.1 place.1.meta
  0.9 0.8 %copy-done = f32[10,64,128]{2,1,0:T(8,128)S(1)} copy-done((f32[10,64,128]{2,1,0:T(8,128)S(1)}, f32[10,64,128]{2,1,0:T(8,128)}, u32[]{:S(2)}) %copy-start) | copy-done | bytes 327704
  1.7 0.1 copy-done.1
  1.8 0.1 copy-done.2
  1.9 0.1 copy-done.3
  2.0 0.0 copy-done.7
  2.0 0.5 %level_sums.1 = (f32[3,64,128]{2,1,0:T(8,128)S(1)}, f32[64,128]{1,0:T(8,128)S(1)}, f32[64,128]{1,0:T(8,128)S(1)}, f32[64,128]{1,0:T(8,128)S(1)}, f32[64,128]{1,0:T(8,128)S(1)}) custom-call(s32[8,128]{1,0:T(8,128)S(1)} %place.1.meta, f32[1,10]{1,0:T(1,128)S(1)} %bitcast.20, s32[1,128]{1,0:T(1,128)S(1)} %bitcast.15, f32[10,64,128]{2,1,0:T(8,128)S(1)} %copy-done, ...), custom_call_target="tpu_custom_call" | custom-call | flops 983040 | bytes 1310720 | tf_op jit(solution)/shard_map/level_sums/pallas_call | solution.py:428
  2.6 5.0 %conditional.1 = (f32[64,128]{1,0:T(8,128)}, f32[64,128]{1,0:T(8,128)}) conditional(s32[]{:T(128)} %clamp.3, (f32[64,128]{1,0:T(8,128)S(1)}, f32[64,128]{1,0:T(8,128)S(1)}) %tuple.42, (f32[64,128]{1,0:T(8,128)S(1)}, f32[64,128]{1,0:T(8,128)S(1)}) %tuple.42, (f32[64,128]{1,0:T(8,128)S(1)}, ...), branch_computations={%region_0.1_spmd, %region_1.2_spmd, %region_2.3_spmd, %region_3.4_... | conditional | bytes 262240 | solution.py:501
  2.7 3.0 %collective-permute-start.10 = (f32[64,128]{1,0:T(8,128)S(1)}, f32[64,128]{1,0:T(8,128)}, u32[]{:S(2)}, u32[]{:S(2)}) collective-permute-start(f32[64,128]{1,0:T(8,128)S(1)} %get-tuple-element.42), channel_id=1, source_target_pairs={{1,2},{2,1},{5,6},{6,5},{9,10},{10,9},{13,14},{14,13},{17,18},{18,... | collective-permute-start | bytes 98312 | tf_op jit(solution)/shard_map/cond/branch_5_fun/ppermute | solution.py:497
  5.7 0.1 collective-permute-start.11
  5.8 1.9 %collective-permute-done.10 = f32[64,128]{1,0:T(8,128)} collective-permute-done((f32[64,128]{1,0:T(8,128)S(1)}, f32[64,128]{1,0:T(8,128)}, u32[]{:S(2)}, u32[]{:S(2)}) %collective-permute-start.10) | collective-permute-done | bytes 32800 | tf_op jit(solution)/shard_map/cond/branch_5_fun/ppermute | solution.py:497
  7.7 0.0 collective-permute-done.11
  7.7 1.0 %row_halos.1 = (f32[6,80,128]{2,1,0:T(8,128)S(1)}, f32[40,128]{1,0:T(8,128)S(1)}, f32[40,128]{1,0:T(8,128)S(1)}, f32[64,128]{1,0:T(8,128)S(1)}, f32[64,128]{1,0:...) custom-call(s32[8,128]{1,0:T(8,128)S(1)} %place.1.meta, s32[1,128]{1,0:T(1,128)S(1)} %bitcast.17, ...), custom_call_target="tpu_custom_call" | custom-call | flops 61440 | bytes 983040 | tf_op jit(solution)/shard_map/row_halos/pallas_call | solution.py:428
  8.7 5.1 %collective-permute-start.18 = (f32[40,128]{1,0:T(8,128)S(1)}, f32[40,128]{1,0:T(8,128)S(1)}, u32[]{:S(2)}, u32[]{:S(2)}) collective-permute-start(f32[40,128]{1,0:T(8,128)S(1)} %get-tuple-element.95), channel_id=1, source_target_pairs={{0,28},{4,8},{8,4},{12,16},{16,12},{20,24},{24,20},{28,0},{1,29},{... | collective-permute-start | bytes 61448 | tf_op jit(solution)/shard_map/ppermute | solution.py:519
  13.8 0.0 collective-permute-start.19
  13.8 1.9 %collective-permute-start.16 = (f32[64,128]{1,0:T(8,128)S(1)}, f32[64,128]{1,0:T(8,128)S(1)}, u32[]{:S(2)}, u32[]{:S(2)}) collective-permute-start(f32[64,128]{1,0:T(8,128)S(1)} %get-tuple-element.87), channel_id=1, source_target_pairs={{0,28},{4,8},{8,4},{12,16},{16,12},{20,24},{24,20},{28,0},{1,29},{... | collective-permute-start | bytes 98312 | tf_op jit(solution)/shard_map/ppermute | solution.py:519
  15.7 0.1 collective-permute-start.17
  15.9 0.3 %basis_shift.1.shift = f32[8,128]{1,0:T(8,128)S(1)} custom-call(f32[6,80,128]{2,1,0:T(8,128)S(1)} %get-tuple-element.93.ext), custom_call_target="tpu_custom_call" | custom-call | flops 491520 | bytes 196608 | tf_op jit(solution)/shard_map/basis_shift/pallas_call | solution.py:428
  16.2 0.0 collective-permute-done.18.from_far
  16.2 1.4 %collective-permute-done.19.from_near = f32[40,128]{1,0:T(8,128)S(1)} collective-permute-done((f32[40,128]{1,0:T(8,128)S(1)}, f32[40,128]{1,0:T(8,128)S(1)}, u32[]{:S(2)}, u32[]{:S(2)}) %collective-permute-start.19) | collective-permute-done | bytes 20512 | tf_op jit(solution)/shard_map/ppermute | solution.py:518
  17.6 1.3 %krylov.1 = (f32[3,64,128]{2,1,0:T(8,128)S(1)}, f32[32,128]{1,0:T(8,128)}) custom-call(s32[8,128]{1,0:T(8,128)S(1)} %place.1.meta, s32[1,128]{1,0:T(1,128)S(1)} %bitcast.18, f32[8,128]{1,0:T(8,128)S(1)} %basis_shift.1.shift, f32[6,80,128]{2,1,0:T(8,128)S(1)} %get-tuple-element.93.ext, f32[24,128]{1,0:T(8,128)S(1)} %get-tuple-element.94.facing_rows, ...), custom_call_target="tpu_custom_call" | custom-call | flops 2048000 | bytes 491520 | tf_op jit(solution)/shard_map/krylov/pallas_call | solution.py:428
  18.9 3.6 %all-to-all-start = ((f32[32,1,128]{2,1,0:T(1,128)}), f32[32,1,128]{2,1,0:T(1,128)S(1)}, u32[]{:S(2)}, u32[]{:S(2)}) async-start(f32[32,1,128]{2,1,0:T(1,128)} %bitcast.10), calls=%async_computation | async-start | bytes 32768 | tf_op jit(solution)/shard_map/all_to_all | solution.py:550
  22.5 0.0 collective-permute-done.16.from_far
  22.5 0.0 collective-permute-done.17.from_near
  22.5 3.8 %levels_step.1 = (f32[10,64,128]{2,1,0:T(8,128)}, f32[10,64,128]{2,1,0:T(8,128)}, f32[10,64,128]{2,1,0:T(8,128)}, f32[10,64,128]{2,1,0:T(8,128)}) custom-call(s32[8,128]{1,0:T(8,128)S(1)} %place.1.meta, f32[1,10]{1,0:T(1,128)S(1)} %bitcast.21, s32[1,128]{1,0:T(1,128)S(1)} %bitcast.19, f32[10,64,128]{2,1,0:T(8,128)S(1)} %copy-done, ...), custom_call_target="tpu_custom_call" | custom-call | flops 9830400 | bytes 2621440 | tf_op jit(solution)/shard_map/levels_step/pallas_call | solution.py:428
  26.3 3.3 %all-to-all-done = f32[32,1,128]{2,1,0:T(1,128)S(1)} async-done(((f32[32,1,128]{2,1,0:T(1,128)}), f32[32,1,128]{2,1,0:T(1,128)S(1)}, u32[]{:S(2)}, u32[]{:S(2)}) %all-to-all-start) | async-done | bytes 16416 | tf_op jit(solution)/shard_map/all_to_all | solution.py:550
  29.6 0.9 %surface.1 = f32[64,128]{1,0:T(8,128)} custom-call(f32[32,128]{1,0:T(8,128)S(1)} %bitcast.14, f32[8,128]{1,0:T(8,128)S(1)} %basis_shift.1.shift, f32[3,64,128]{2,1,0:T(8,128)S(1)} %get-tuple-element.98.base), custom_call_target="tpu_custom_call" | custom-call | flops 49152 | bytes 131072 | tf_op jit(solution)/shard_map/surface/pallas_call | solution.py:428
  (9 shorter events, 0.0 us)
Async XLA Ops:
  0.7 1.0 %copy-start = (f32[10,64,128]{2,1,0:T(8,128)S(1)}, f32[10,64,128]{2,1,0:T(8,128)}, u32[]{:S(2)}) copy-start(f32[10,64,128]{2,1,0:T(8,128)} %heat.3) | copy-start | bytes 983044
  0.7 1.1 %copy-start.1 = (f32[10,64,128]{2,1,0:T(8,128)S(1)}, f32[10,64,128]{2,1,0:T(8,128)}, u32[]{:S(2)}) copy-start(f32[10,64,128]{2,1,0:T(8,128)} %salt.3) | copy-start | bytes 983044
  0.7 1.2 %copy-start.2 = (f32[10,64,128]{2,1,0:T(8,128)S(1)}, f32[10,64,128]{2,1,0:T(8,128)}, u32[]{:S(2)}) copy-start(f32[10,64,128]{2,1,0:T(8,128)} %zonal.3) | copy-start | bytes 983044
  0.7 1.3 %copy-start.3 = (f32[10,64,128]{2,1,0:T(8,128)S(1)}, f32[10,64,128]{2,1,0:T(8,128)}, u32[]{:S(2)}) copy-start(f32[10,64,128]{2,1,0:T(8,128)} %merid.3) | copy-start | bytes 983044
  0.7 1.3 %copy-start.4 = (s32[64,128]{1,0:T(8,128)S(1)}, s32[64,128]{1,0:T(8,128)}, u32[]{:S(2)}) copy-start(s32[64,128]{1,0:T(8,128)} %water.5) | copy-start | bytes 98308
  0.8 1.2 %copy-start.5 = (f32[64,128]{1,0:T(8,128)S(1)}, f32[64,128]{1,0:T(8,128)}, u32[]{:S(2)}) copy-start(f32[64,128]{1,0:T(8,128)} %weights.3) | copy-start | bytes 98308
  0.8 1.2 %copy-start.6 = (f32[64,128]{1,0:T(8,128)S(1)}, f32[64,128]{1,0:T(8,128)}, u32[]{:S(2)}) copy-start(f32[64,128]{1,0:T(8,128)} %anomaly.3) | copy-start | bytes 98308
  0.9 1.2 %copy-start.7 = (s32[128]{0:T(128)S(1)}, s32[128]{0:T(128)}, u32[]{:S(2)}) copy-start(s32[128]{0:T(128)} %param.23) | copy-start | bytes 1540
  0.9 1.2 %copy-start.8 = (f32[10]{0:T(128)S(1)}, f32[10]{0:T(128)}, u32[]{:S(2)}) copy-start(f32[10]{0:T(128)} %param.21) | copy-start | bytes 124
  2.7 5.0 %collective-permute-start.10 = (f32[64,128]{1,0:T(8,128)S(1)}, f32[64,128]{1,0:T(8,128)}, u32[]{:S(2)}, u32[]{:S(2)}) collective-permute-start(f32[64,128]{1,0:T(8,128)S(1)} %get-tuple-element.42), channel_id=1, source_target_pairs={{1,2},{2,1},{5,6},{6,5},{9,10},{10,9},{13,14},{14,13},{17,18},{18,... | collective-permute-start | bytes 98312 | tf_op jit(solution)/shard_map/cond/branch_5_fun/ppermute | solution.py:497
  5.7 2.0 %collective-permute-start.11 = (f32[64,128]{1,0:T(8,128)S(1)}, f32[64,128]{1,0:T(8,128)}, u32[]{:S(2)}, u32[]{:S(2)}) collective-permute-start(f32[64,128]{1,0:T(8,128)S(1)} %get-tuple-element.43), channel_id=1, source_target_pairs={{0,1},{1,0},{2,3},{3,2},{4,5},{5,4},{6,7},{7,6},{8,9},{9,8},{10,11... | collective-permute-start | bytes 98312 | tf_op jit(solution)/shard_map/cond/branch_5_fun/ppermute | solution.py:498
  8.7 7.5 %collective-permute-start.18 = (f32[40,128]{1,0:T(8,128)S(1)}, f32[40,128]{1,0:T(8,128)S(1)}, u32[]{:S(2)}, u32[]{:S(2)}) collective-permute-start(f32[40,128]{1,0:T(8,128)S(1)} %get-tuple-element.95), channel_id=1, source_target_pairs={{0,28},{4,8},{8,4},{12,16},{16,12},{20,24},{24,20},{28,0},{1,29},{... | collective-permute-start | bytes 61448 | tf_op jit(solution)/shard_map/ppermute | solution.py:519
  13.8 3.8 %collective-permute-start.19 = (f32[40,128]{1,0:T(8,128)S(1)}, f32[40,128]{1,0:T(8,128)S(1)}, u32[]{:S(2)}, u32[]{:S(2)}) collective-permute-start(f32[40,128]{1,0:T(8,128)S(1)} %get-tuple-element.96), channel_id=1, source_target_pairs={{0,4},{4,0},{8,12},{12,8},{16,20},{20,16},{24,28},{28,24},{1,5},{5... | collective-permute-start | bytes 61448 | tf_op jit(solution)/shard_map/ppermute | solution.py:518
  13.8 8.7 %collective-permute-start.16 = (f32[64,128]{1,0:T(8,128)S(1)}, f32[64,128]{1,0:T(8,128)S(1)}, u32[]{:S(2)}, u32[]{:S(2)}) collective-permute-start(f32[64,128]{1,0:T(8,128)S(1)} %get-tuple-element.87), channel_id=1, source_target_pairs={{0,28},{4,8},{8,4},{12,16},{16,12},{20,24},{24,20},{28,0},{1,29},{... | collective-permute-start | bytes 98312 | tf_op jit(solution)/shard_map/ppermute | solution.py:519
  15.7 6.8 %collective-permute-start.17 = (f32[64,128]{1,0:T(8,128)S(1)}, f32[64,128]{1,0:T(8,128)S(1)}, u32[]{:S(2)}, u32[]{:S(2)}) collective-permute-start(f32[64,128]{1,0:T(8,128)S(1)} %get-tuple-element.88), channel_id=1, source_target_pairs={{0,4},{4,0},{8,12},{12,8},{16,20},{20,16},{24,28},{28,24},{1,5},{5... | collective-permute-start | bytes 98312 | tf_op jit(solution)/shard_map/ppermute | solution.py:518
  18.9 10.7 %all-to-all-start = ((f32[32,1,128]{2,1,0:T(1,128)}), f32[32,1,128]{2,1,0:T(1,128)S(1)}, u32[]{:S(2)}, u32[]{:S(2)}) async-start(f32[32,1,128]{2,1,0:T(1,128)} %bitcast.10), calls=%async_computation | async-start | bytes 32768 | tf_op jit(solution)/shard_map/all_to_all | solution.py:550

commit v9 on v8

--- a/solution.py
+++ b/solution.py
@@ -96,7 +96,7 @@
 
 def turn_kernel(
     lons, meta, facing, mine, sums, water, weights, anomaly, second, first, east_columns, west_columns,
-    ext, to_far, to_near, state_far, state_near, facing_rows, north_rows, south_rows,
+    ext, to_near, to_far, state_near, state_far, facing_rows, north_rows, south_rows,
 ):
     rows, cols = sums.shape[1], sums.shape[2]
     tall = ext.shape[1]
@@ -189,7 +189,7 @@
     shift[...] = jnp.broadcast_to(quotient, shift.shape)
 
 
-def krylov_kernel(meta, facing, shift, ext, facing_rows, from_far, from_near, base, moments, folded):
+def krylov_kernel(meta, facing, shift, ext, facing_rows, from_near, from_far, base, moments, folded):
     tall, cols = ext.shape[1], ext.shape[2]
     rows = base.shape[1]
     size = facing_rows.shape[0]
@@ -296,7 +296,7 @@
 
 
 def step_kernel(
-    meta, spans, facing, heat, salt, zonal, merid, water, north_came, south_rows, from_far, from_near,
+    meta, spans, facing, heat, salt, zonal, merid, water, north_came, south_rows, from_near, from_far,
     heat_out, salt_out, zonal_out, merid_out,
     new_heat, new_salt, new_zonal, new_merid, north_rows, sems,
 ):
@@ -501,7 +501,7 @@
     second, first = lax.switch(block, [functools.partial(exchange, s) for s in range(lons)], first, second)
 
     deep = 4 * levels
-    ext, to_far, to_near, state_far, state_near, facing_rows, north_rows, south_rows = call(
+    ext, to_near, to_far, state_near, state_far, facing_rows, north_rows, south_rows = call(
         functools.partial(turn_kernel, lons),
         [
             (FIELDS, tall, cols),
@@ -517,8 +517,8 @@
 
     near = lambda cells: lax.ppermute(cells, "lon", [(i, i ^ 1) for i in range(lons)])
     far = lambda cells: lax.ppermute(cells, "lon", [(i, (i + 1 if i % 2 else i - 1) % lons) for i in range(lons)])
-    from_far, from_near = far(to_far), near(to_near)
-    state_far, state_near = far(state_far), near(state_near)
+    from_near, from_far = near(to_near), far(to_far)
+    state_near, state_far = near(state_near), far(state_far)
 
     (shift,) = call(shift_kernel, [(8, cols)], 60 * rows * cols, 24 * rows * cols, "basis_shift")(ext)
 
@@ -530,7 +530,7 @@
         4 * 12 * tall * cols,
         "krylov",
         scratch=[pltpu.VMEM((2, high - deep + 8, cols), jnp.float32)],
-    )(meta, facing, shift, ext, facing_rows, from_far, from_near)
+    )(meta, facing, shift, ext, facing_rows, from_near, from_far)
 
     chunks = 5 if levels % 5 == 0 else 1
     new_heat, new_salt, new_zonal, new_merid = call(
@@ -545,7 +545,7 @@
             pltpu.VMEM((deep, cols), jnp.float32),
             pltpu.SemaphoreType.DMA((4, chunks)),
         ],
-    )(meta, spans, facing, *state, water_indicator, north_rows, south_rows, state_far, state_near)
+    )(meta, spans, facing, *state, water_indicator, north_rows, south_rows, state_near, state_far)
 
     shares = lax.all_to_all(moments, axes, 0, 0, tiled=True)
     (surface,) = call(surface_kernel, [(rows, cols)], 6 * rows * cols, 16 * rows * cols, "surface")(shares, shift, base)

time: 30.8 us -> 31 us (level)
  starting transfers between devices: 14 us -> 15 us
  waiting for transfers between devices: 6.6 us -> 5.84 us
    ppermute x2, starting transfers between devices: 0.12 us -> 2.09 us  [body(): lax.ppermute(cells, 'lon', [(i, i ^ 1) for i in range(lons)])]
    ppermute x2, starting transfers between devices: 7.06 us -> 5.48 us  [body(): lax.ppermute(cells, 'lon', [(i, (i + 1 if i % 2 else i - 1) % lons) for i...]
    ppermute x2, waiting for transfers between devices: 1.44 us -> 0.01 us  [body(): lax.ppermute(cells, 'lon', [(i, i ^ 1) for i in range(lons)])]
    all_to_all x1, starting transfers between devices: 3.64 us -> 4.32 us  [body(): shares = lax.all_to_all(moments, axes, 0, 0, tiled=True)]
    ppermute x2, waiting for transfers between devices: 0.01 us -> 0.69 us  [body(): lax.ppermute(cells, 'lon', [(i, (i + 1 if i % 2 else i - 1) % lons) for i...]
where the time goes in v9:
time: 31 us; the launch traced here: 30.7 us
  starting transfers between devices  15 us (48%)
  Pallas kernels  7.76 us (25%)
  waiting for transfers between devices  5.84 us (19%)
  local copies, waits for them, and re-layouts  1.26 us (4%)
  between operations  0.82 us (3%)
    pallas_call x7, Pallas kernels, run(): pl.pallas_call(kernel, out_shape=[jax.ShapeDtypeStruct(shape, types) for...  7.76 us
    ppermute x2, starting transfers between devices, body(): lax.ppermute(cells, 'lon', [(i, (i + 1 if i % 2 else i - 1) % lons) for i...  5.48 us
    all_to_all x1, starting transfers between devices, body(): shares = lax.all_to_all(moments, axes, 0, 0, tiled=True)  4.32 us
    all_to_all x1, waiting for transfers between devices, body(): shares = lax.all_to_all(moments, axes, 0, 0, tiled=True)  3.29 us
    ppermute x1, starting transfers between devices, exchange(): second = lax.ppermute(second, axes, pairs_inner + pairs_fold)  3 us
    ppermute x2, starting transfers between devices, body(): lax.ppermute(cells, 'lon', [(i, i ^ 1) for i in range(lons)])  2.09 us
    ppermute x1, waiting for transfers between devices, exchange(): second = lax.ppermute(second, axes, pairs_inner + pairs_fold)  1.86 us
    unnamed x18, local copies, waits for them, and re-layouts  1.17 us
  transfers between devices with their start and end apart: 7, of which 3 were waited for; matrix products, arithmetic and copies ran while one was open for 0% of the time, Pallas kernels for 17%

profile of v9, /device:TPU:0, one launch (start us, length us, event | category | flops | bytes accessed | tf_op | source)
XLA Modules:
  0.0 30.7 jit_solution(13413787976712097213)
XLA Ops:
  0.6 0.1 stack.31
  0.7 0.0 copy-start.3
  0.7 0.0 copy-start.4
  0.8 0.0 copy-start.5
  0.8 0.0 copy-start.6
  0.8 0.1 place.1.meta
  0.9 0.8 %copy-done = f32[10,64,128]{2,1,0:T(8,128)S(1)} copy-done((f32[10,64,128]{2,1,0:T(8,128)S(1)}, f32[10,64,128]{2,1,0:T(8,128)}, u32[]{:S(2)}) %copy-start) | copy-done | bytes 327704
  1.7 0.1 copy-done.1
  1.8 0.1 copy-done.2
  1.9 0.1 copy-done.3
  2.0 0.0 copy-done.7
  2.0 0.5 %level_sums.1 = (f32[3,64,128]{2,1,0:T(8,128)S(1)}, f32[64,128]{1,0:T(8,128)S(1)}, f32[64,128]{1,0:T(8,128)S(1)}, f32[64,128]{1,0:T(8,128)S(1)}, f32[64,128]{1,0:T(8,128)S(1)}) custom-call(s32[8,128]{1,0:T(8,128)S(1)} %place.1.meta, f32[1,10]{1,0:T(1,128)S(1)} %bitcast.20, s32[1,128]{1,0:T(1,128)S(1)} %bitcast.15, f32[10,64,128]{2,1,0:T(8,128)S(1)} %copy-done, ...), custom_call_target="tpu_custom_call" | custom-call | flops 983040 | bytes 1310720 | tf_op jit(solution)/shard_map/level_sums/pallas_call | solution.py:428
  2.6 5.0 %conditional.1 = (f32[64,128]{1,0:T(8,128)}, f32[64,128]{1,0:T(8,128)}) conditional(s32[]{:T(128)} %clamp.3, (f32[64,128]{1,0:T(8,128)S(1)}, f32[64,128]{1,0:T(8,128)S(1)}) %tuple.42, (f32[64,128]{1,0:T(8,128)S(1)}, f32[64,128]{1,0:T(8,128)S(1)}) %tuple.42, (f32[64,128]{1,0:T(8,128)S(1)}, ...), branch_computations={%region_0.1_spmd, %region_1.2_spmd, %region_2.3_spmd, %region_3.4_... | conditional | bytes 262240 | solution.py:501
  2.7 3.0 %collective-permute-start.6 = (f32[64,128]{1,0:T(8,128)S(1)}, f32[64,128]{1,0:T(8,128)}, u32[]{:S(2)}, u32[]{:S(2)}) collective-permute-start(f32[64,128]{1,0:T(8,128)S(1)} %get-tuple-element.38), channel_id=1, source_target_pairs={{1,2},{2,1},{5,6},{6,5},{9,10},{10,9},{13,14},{14,13},{17,18},{18,... | collective-permute-start | bytes 98312 | tf_op jit(solution)/shard_map/cond/branch_3_fun/ppermute | solution.py:497
  5.7 0.1 collective-permute-start.7
  5.8 1.9 %collective-permute-done.6 = f32[64,128]{1,0:T(8,128)} collective-permute-done((f32[64,128]{1,0:T(8,128)S(1)}, f32[64,128]{1,0:T(8,128)}, u32[]{:S(2)}, u32[]{:S(2)}) %collective-permute-start.6) | collective-permute-done | bytes 32800 | tf_op jit(solution)/shard_map/cond/branch_3_fun/ppermute | solution.py:497
  7.7 0.0 collective-permute-done.7
  7.7 1.0 %row_halos.1 = (f32[6,80,128]{2,1,0:T(8,128)S(1)}, f32[40,128]{1,0:T(8,128)S(1)}, f32[40,128]{1,0:T(8,128)S(1)}, f32[64,128]{1,0:T(8,128)S(1)}, f32[64,128]{1,0:...) custom-call(s32[8,128]{1,0:T(8,128)S(1)} %place.1.meta, s32[1,128]{1,0:T(1,128)S(1)} %bitcast.17, ...), custom_call_target="tpu_custom_call" | custom-call | flops 61440 | bytes 983040 | tf_op jit(solution)/shard_map/row_halos/pallas_call | solution.py:428
  8.7 2.1 %collective-permute-start.18 = (f32[40,128]{1,0:T(8,128)S(1)}, f32[40,128]{1,0:T(8,128)S(1)}, u32[]{:S(2)}, u32[]{:S(2)}) collective-permute-start(f32[40,128]{1,0:T(8,128)S(1)} %get-tuple-element.95), channel_id=1, source_target_pairs={{0,4},{4,0},{8,12},{12,8},{16,20},{20,16},{24,28},{28,24},{1,5},{5... | collective-permute-start | bytes 61448 | tf_op jit(solution)/shard_map/ppermute | solution.py:518
  10.8 3.6 %collective-permute-start.19 = (f32[40,128]{1,0:T(8,128)S(1)}, f32[40,128]{1,0:T(8,128)S(1)}, u32[]{:S(2)}, u32[]{:S(2)}) collective-permute-start(f32[40,128]{1,0:T(8,128)S(1)} %get-tuple-element.96), channel_id=1, source_target_pairs={{0,28},{4,8},{8,4},{12,16},{16,12},{20,24},{24,20},{28,0},{1,29},{... | collective-permute-start | bytes 61448 | tf_op jit(solution)/shard_map/ppermute | solution.py:519
  14.4 0.0 collective-permute-start.16
  14.4 1.9 %collective-permute-start.17 = (f32[64,128]{1,0:T(8,128)S(1)}, f32[64,128]{1,0:T(8,128)S(1)}, u32[]{:S(2)}, u32[]{:S(2)}) collective-permute-start(f32[64,128]{1,0:T(8,128)S(1)} %get-tuple-element.88), channel_id=1, source_target_pairs={{0,28},{4,8},{8,4},{12,16},{16,12},{20,24},{24,20},{28,0},{1,29},{... | collective-permute-start | bytes 98312 | tf_op jit(solution)/shard_map/ppermute | solution.py:519
  16.2 0.3 basis_shift.1.shift
  16.5 0.0 collective-permute-done.18.from_near
  16.5 0.7 %collective-permute-done.19.from_far = f32[40,128]{1,0:T(8,128)S(1)} collective-permute-done((f32[40,128]{1,0:T(8,128)S(1)}, f32[40,128]{1,0:T(8,128)S(1)}, u32[]{:S(2)}, u32[]{:S(2)}) %collective-permute-start.19) | collective-permute-done | bytes 20512 | tf_op jit(solution)/shard_map/ppermute | solution.py:519
  17.2 1.3 %krylov.1 = (f32[3,64,128]{2,1,0:T(8,128)S(1)}, f32[32,128]{1,0:T(8,128)}) custom-call(s32[8,128]{1,0:T(8,128)S(1)} %place.1.meta, s32[1,128]{1,0:T(1,128)S(1)} %bitcast.18, f32[8,128]{1,0:T(8,128)S(1)} %basis_shift.1.shift, f32[6,80,128]{2,1,0:T(8,128)S(1)} %get-tuple-element.93.ext, f32[24,128]{1,0:T(8,128)S(1)} %get-tuple-element.94.facing_rows, ...), custom_call_target="tpu_custom_call" | custom-call | flops 2048000 | bytes 491520 | tf_op jit(solution)/shard_map/krylov/pallas_call | solution.py:428
  18.5 4.3 %all-to-all-start = ((f32[32,1,128]{2,1,0:T(1,128)}), f32[32,1,128]{2,1,0:T(1,128)S(1)}, u32[]{:S(2)}, u32[]{:S(2)}) async-start(f32[32,1,128]{2,1,0:T(1,128)} %bitcast.10), calls=%async_computation | async-start | bytes 32768 | tf_op jit(solution)/shard_map/all_to_all | solution.py:550
  22.8 0.0 collective-permute-done.16.from_near
  22.8 0.0 collective-permute-done.17.from_far
  22.8 3.8 %levels_step.1 = (f32[10,64,128]{2,1,0:T(8,128)}, f32[10,64,128]{2,1,0:T(8,128)}, f32[10,64,128]{2,1,0:T(8,128)}, f32[10,64,128]{2,1,0:T(8,128)}) custom-call(s32[8,128]{1,0:T(8,128)S(1)} %place.1.meta, f32[1,10]{1,0:T(1,128)S(1)} %bitcast.21, s32[1,128]{1,0:T(1,128)S(1)} %bitcast.19, f32[10,64,128]{2,1,0:T(8,128)S(1)} %copy-done, ...), custom_call_target="tpu_custom_call" | custom-call | flops 9830400 | bytes 2621440 | tf_op jit(solution)/shard_map/levels_step/pallas_call | solution.py:428
  26.6 3.3 %all-to-all-done = f32[32,1,128]{2,1,0:T(1,128)S(1)} async-done(((f32[32,1,128]{2,1,0:T(1,128)}), f32[32,1,128]{2,1,0:T(1,128)S(1)}, u32[]{:S(2)}, u32[]{:S(2)}) %all-to-all-start) | async-done | bytes 16416 | tf_op jit(solution)/shard_map/all_to_all | solution.py:550
  29.9 0.9 %surface.1 = f32[64,128]{1,0:T(8,128)} custom-call(f32[32,128]{1,0:T(8,128)S(1)} %bitcast.14, f32[8,128]{1,0:T(8,128)S(1)} %basis_shift.1.shift, f32[3,64,128]{2,1,0:T(8,128)S(1)} %get-tuple-element.98.base), custom_call_target="tpu_custom_call" | custom-call | flops 49152 | bytes 131072 | tf_op jit(solution)/shard_map/surface/pallas_call | solution.py:428
  (9 shorter events, 0.0 us)
Async XLA Ops:
  0.7 1.0 %copy-start = (f32[10,64,128]{2,1,0:T(8,128)S(1)}, f32[10,64,128]{2,1,0:T(8,128)}, u32[]{:S(2)}) copy-start(f32[10,64,128]{2,1,0:T(8,128)} %heat.3) | copy-start | bytes 983044
  0.7 1.1 %copy-start.1 = (f32[10,64,128]{2,1,0:T(8,128)S(1)}, f32[10,64,128]{2,1,0:T(8,128)}, u32[]{:S(2)}) copy-start(f32[10,64,128]{2,1,0:T(8,128)} %salt.3) | copy-start | bytes 983044
  0.7 1.2 %copy-start.2 = (f32[10,64,128]{2,1,0:T(8,128)S(1)}, f32[10,64,128]{2,1,0:T(8,128)}, u32[]{:S(2)}) copy-start(f32[10,64,128]{2,1,0:T(8,128)} %zonal.3) | copy-start | bytes 983044
  0.7 1.3 %copy-start.3 = (f32[10,64,128]{2,1,0:T(8,128)S(1)}, f32[10,64,128]{2,1,0:T(8,128)}, u32[]{:S(2)}) copy-start(f32[10,64,128]{2,1,0:T(8,128)} %merid.3) | copy-start | bytes 983044
  0.7 1.3 %copy-start.4 = (s32[64,128]{1,0:T(8,128)S(1)}, s32[64,128]{1,0:T(8,128)}, u32[]{:S(2)}) copy-start(s32[64,128]{1,0:T(8,128)} %water.5) | copy-start | bytes 98308
  0.8 1.2 %copy-start.5 = (f32[64,128]{1,0:T(8,128)S(1)}, f32[64,128]{1,0:T(8,128)}, u32[]{:S(2)}) copy-start(f32[64,128]{1,0:T(8,128)} %weights.3) | copy-start | bytes 98308
  0.8 1.2 %copy-start.6 = (f32[64,128]{1,0:T(8,128)S(1)}, f32[64,128]{1,0:T(8,128)}, u32[]{:S(2)}) copy-start(f32[64,128]{1,0:T(8,128)} %anomaly.3) | copy-start | bytes 98308
  0.9 1.2 %copy-start.7 = (s32[128]{0:T(128)S(1)}, s32[128]{0:T(128)}, u32[]{:S(2)}) copy-start(s32[128]{0:T(128)} %param.23) | copy-start | bytes 1540
  0.9 1.2 %copy-start.8 = (f32[10]{0:T(128)S(1)}, f32[10]{0:T(128)}, u32[]{:S(2)}) copy-start(f32[10]{0:T(128)} %param.21) | copy-start | bytes 124
  2.7 5.0 %collective-permute-start.6 = (f32[64,128]{1,0:T(8,128)S(1)}, f32[64,128]{1,0:T(8,128)}, u32[]{:S(2)}, u32[]{:S(2)}) collective-permute-start(f32[64,128]{1,0:T(8,128)S(1)} %get-tuple-element.38), channel_id=1, source_target_pairs={{1,2},{2,1},{5,6},{6,5},{9,10},{10,9},{13,14},{14,13},{17,18},{18,... | collective-permute-start | bytes 98312 | tf_op jit(solution)/shard_map/cond/branch_3_fun/ppermute | solution.py:497
  5.7 2.0 %collective-permute-start.7 = (f32[64,128]{1,0:T(8,128)S(1)}, f32[64,128]{1,0:T(8,128)}, u32[]{:S(2)}, u32[]{:S(2)}) collective-permute-start(f32[64,128]{1,0:T(8,128)S(1)} %get-tuple-element.39), channel_id=1, source_target_pairs={{0,1},{1,0},{2,3},{3,2},{4,5},{5,4},{6,7},{7,6},{8,9},{9,8},{10,11... | collective-permute-start | bytes 98312 | tf_op jit(solution)/shard_map/cond/branch_3_fun/ppermute | solution.py:498
  8.7 7.9 %collective-permute-start.18 = (f32[40,128]{1,0:T(8,128)S(1)}, f32[40,128]{1,0:T(8,128)S(1)}, u32[]{:S(2)}, u32[]{:S(2)}) collective-permute-start(f32[40,128]{1,0:T(8,128)S(1)} %get-tuple-element.95), channel_id=1, source_target_pairs={{0,4},{4,0},{8,12},{12,8},{16,20},{20,16},{24,28},{28,24},{1,5},{5... | collective-permute-start | bytes 61448 | tf_op jit(solution)/shard_map/ppermute | solution.py:518
  10.8 6.5 %collective-permute-start.19 = (f32[40,128]{1,0:T(8,128)S(1)}, f32[40,128]{1,0:T(8,128)S(1)}, u32[]{:S(2)}, u32[]{:S(2)}) collective-permute-start(f32[40,128]{1,0:T(8,128)S(1)} %get-tuple-element.96), channel_id=1, source_target_pairs={{0,28},{4,8},{8,4},{12,16},{16,12},{20,24},{24,20},{28,0},{1,29},{... | collective-permute-start | bytes 61448 | tf_op jit(solution)/shard_map/ppermute | solution.py:519
  14.4 8.5 %collective-permute-start.16 = (f32[64,128]{1,0:T(8,128)S(1)}, f32[64,128]{1,0:T(8,128)S(1)}, u32[]{:S(2)}, u32[]{:S(2)}) collective-permute-start(f32[64,128]{1,0:T(8,128)S(1)} %get-tuple-element.87), channel_id=1, source_target_pairs={{0,4},{4,0},{8,12},{12,8},{16,20},{20,16},{24,28},{28,24},{1,5},{5... | collective-permute-start | bytes 98312 | tf_op jit(solution)/shard_map/ppermute | solution.py:518
  14.4 8.5 %collective-permute-start.17 = (f32[64,128]{1,0:T(8,128)S(1)}, f32[64,128]{1,0:T(8,128)S(1)}, u32[]{:S(2)}, u32[]{:S(2)}) collective-permute-start(f32[64,128]{1,0:T(8,128)S(1)} %get-tuple-element.88), channel_id=1, source_target_pairs={{0,28},{4,8},{8,4},{12,16},{16,12},{20,24},{24,20},{28,0},{1,29},{... | collective-permute-start | bytes 98312 | tf_op jit(solution)/shard_map/ppermute | solution.py:519
  18.5 11.4 %all-to-all-start = ((f32[32,1,128]{2,1,0:T(1,128)}), f32[32,1,128]{2,1,0:T(1,128)S(1)}, u32[]{:S(2)}, u32[]{:S(2)}) async-start(f32[32,1,128]{2,1,0:T(1,128)} %bitcast.10), calls=%async_computation | async-start | bytes 32768 | tf_op jit(solution)/shard_map/all_to_all | solution.py:550

commit v10 on v8

--- a/solution.py
+++ b/solution.py
@@ -35,6 +35,11 @@
 
 def flags(meta):
     return tuple(meta[i : i + 1, :] == 1 for i in range(4))
+
+
+def segments(rows):
+    size = START[-1]
+    return (0, rows // 2, 0), (rows // 2, rows, size), (rows, rows + 8, RELAY), (rows + 8, rows + 16, RELAY + size)
 
 
 def place_kernel(meta, placed):
@@ -117,27 +122,36 @@
         ext[f, rows : rows + size, :] = north[at : at + size]
         ext[f, rows + size : tall - size, :] = jnp.zeros((tall - rows - 2 * size, cols), jnp.float32)
         ext[f, tall - size :, :] = south[at : at + size]
-    middle = tall // 2
     passed = from_second[deep:]
-    spare = jnp.zeros((middle - passed.shape[0], cols), jnp.float32)
-    lane = iota((middle, cols), 1)
+    size = passed.shape[0]
+    half = rows // 2
+    lane = iota((half, cols), 1)
+    lower = iota((half, cols), 0) >= size
+    empty = jnp.zeros((size, cols), jnp.float32)
+    spare = jnp.zeros((half - size, cols), jnp.float32)
     relay = lane >= RELAY
     east = jnp.where(relay, jnp.concatenate([pltpu.roll(passed, RELAY, 1), spare], axis=0), 0.0)
     west = jnp.where(relay, jnp.concatenate([passed, spare], axis=0), 0.0)
     for f in range(FIELDS):
-        for part in range(2):
-            at = START[f] + part * START[-1]
+        for start, stop, first_lane in segments(rows):
+            at = START[f] + first_lane
             here = (lane >= at) & (lane < at + SIDE[f])
-            layer = ext[f, part * middle : (part + 1) * middle, :]
-            east = jnp.where(here, pltpu.roll(layer, (at + SIDE[f]) % cols, 1), east)
-            west = jnp.where(here, pltpu.roll(layer, at, 1), west)
+            layer = ext[f, start:stop, :]
+            to_east = pltpu.roll(layer, (at + SIDE[f]) % cols, 1)
+            to_west = pltpu.roll(layer, at, 1)
+            if stop - start < half:
+                here = here & lower
+                to_east = jnp.concatenate([empty, to_east], axis=0)
+                to_west = jnp.concatenate([empty, to_west], axis=0)
+            east = jnp.where(here, to_east, east)
+            west = jnp.where(here, to_west, west)
     to_far[...] = jnp.where(lon_odd, east, west)
     to_near[...] = jnp.where(lon_odd, west, east)
     passed = from_second[:deep]
     spare = jnp.zeros((rows - deep, cols), jnp.float32)
-    half = iota((rows, cols), 1) >= cols // 2
-    east = jnp.where(half, jnp.concatenate([pltpu.roll(passed, cols // 2, 1), spare], axis=0), east_columns[...])
-    west = jnp.where(half, jnp.concatenate([passed, spare], axis=0), west_columns[...])
+    right_half = iota((rows, cols), 1) >= cols // 2
+    east = jnp.where(right_half, jnp.concatenate([pltpu.roll(passed, cols // 2, 1), spare], axis=0), east_columns[...])
+    west = jnp.where(right_half, jnp.concatenate([passed, spare], axis=0), west_columns[...])
     state_far[...] = jnp.where(lon_odd, east, west)
     state_near[...] = jnp.where(lon_odd, west, east)
     facing_rows[...] = from_second[deep:]
@@ -186,14 +200,13 @@
     below = total(right * zero)
     good = below > 0.0
     quotient = jnp.where(good, total(right * one) / jnp.where(good, below, 1.0), 0.0)
-    shift[...] = jnp.broadcast_to(quotient, shift.shape)
+    shift[...] = jnp.broadcast_to(jnp.clip(quotient, -1.0, 1.0), shift.shape)
 
 
 def krylov_kernel(meta, facing, shift, ext, facing_rows, from_far, from_near, base, moments, folded):
     tall, cols = ext.shape[1], ext.shape[2]
     rows = base.shape[1]
     size = facing_rows.shape[0]
-    middle = tall // 2
     _, top, lon_odd, _ = flags(meta)
     west = jnp.where(lon_odd, from_near[...], from_far[...])
     east = jnp.where(lon_odd, from_far[...], from_near[...])
@@ -211,9 +224,14 @@
     eighth = iota((8, cols), 0)
 
     def load(f):
-        both = [START[f], START[f] + START[-1]]
-        a = jnp.concatenate([pltpu.roll(west, (2 * cols - SIDE[f] - at) % cols, 1) for at in both], axis=0)
-        b = jnp.concatenate([pltpu.roll(east, (cols - at) % cols, 1) for at in both], axis=0)
+        parts = []
+        for packet, shift_of in ((west, 2 * cols - SIDE[f]), (east, cols)):
+            pieces = []
+            for start, stop, first_lane in segments(rows):
+                layer = packet[packet.shape[0] - (stop - start) :]
+                pieces.append(pltpu.roll(layer, (shift_of - START[f] - first_lane) % cols, 1))
+            parts.append(jnp.concatenate(pieces, axis=0))
+        a, b = parts
         beside = jnp.where(lane >= cols - SIDE[f], a, jnp.where(lane < SIDE[f], b, 0.0))
 
         def put(cells, side):
@@ -453,8 +471,8 @@
     lons, lats = lax.axis_size("lon"), lax.axis_size("lat")
     lon, lat = lax.axis_index("lon"), lax.axis_index("lat")
     levels, rows, cols = warmth_deviation.shape
-    assert cols & (cols - 1) == 0 and rows >= 24 and 4 * levels <= cols // 2 and 2 * START[-1] <= RELAY and cols == 128
     high = packet_rows(levels)
+    assert cols & (cols - 1) == 0 and rows >= 24 and rows // 2 == high - 4 * levels + 8 and 4 * levels <= cols // 2 and 2 * START[-1] <= min(RELAY, cols - RELAY) and cols == 128
     tall = rows + 16
     width = cols * lons
     flat = lambda i, j: (i % lons) * lats + j
@@ -505,7 +523,7 @@
         functools.partial(turn_kernel, lons),
         [
             (FIELDS, tall, cols),
-            *[(tall // 2, cols)] * 2,
+            *[(rows // 2, cols)] * 2,
             *[(rows, cols)] * 2,
             (high - deep, cols),
             *[(deep, cols)] * 2,

time: 30.8 us -> 30.6 us (level)
  transfers between devices with their start and end apart: 7 -> 7, of which waited for: 3 -> 3; matrix products, arithmetic and copies ran while one was open for 0% -> 0% of each run, Pallas kernels for 17% -> 18%
where the time goes in v10:
time: 30.6 us; the launch traced here: 30.2 us
  starting transfers between devices  13.8 us (45%)
  Pallas kernels  7.76 us (25%)
  waiting for transfers between devices  6.55 us (21%)
  local copies, waits for them, and re-layouts  1.26 us (4%)
  between operations  0.82 us (3%)
    pallas_call x7, Pallas kernels, run(): pl.pallas_call(kernel, out_shape=[jax.ShapeDtypeStruct(shape, types) for...  7.76 us
    ppermute x2, starting transfers between devices, body(): lax.ppermute(cells, 'lon', [(i, (i + 1 if i % 2 else i - 1) % lons) for i...  7.06 us
    all_to_all x1, starting transfers between devices, body(): shares = lax.all_to_all(moments, axes, 0, 0, tiled=True)  3.5 us
    all_to_all x1, waiting for transfers between devices, body(): shares = lax.all_to_all(moments, axes, 0, 0, tiled=True)  3.29 us
    ppermute x1, starting transfers between devices, exchange(): second = lax.ppermute(second, axes, pairs_inner + pairs_fold)  3 us
    ppermute x1, waiting for transfers between devices, exchange(): second = lax.ppermute(second, axes, pairs_inner + pairs_fold)  1.86 us
    ppermute x2, waiting for transfers between devices, body(): lax.ppermute(cells, 'lon', [(i, i ^ 1) for i in range(lons)])  1.4 us
    unnamed x18, local copies, waits for them, and re-layouts  1.17 us
  transfers between devices with their start and end apart: 7, of which 3 were waited for; matrix products, arithmetic and copies ran while one was open for 0% of the time, Pallas kernels for 18%

profile of v10, /device:TPU:0, one launch (start us, length us, event | category | flops | bytes accessed | tf_op | source)
XLA Modules:
  0.0 30.2 jit_solution(5796787147082213810)
XLA Ops:
  0.6 0.1 stack.31
  0.7 0.0 copy-start.3
  0.7 0.0 copy-start.4
  0.8 0.0 copy-start.5
  0.8 0.0 copy-start.6
  0.8 0.1 place.1.meta
  0.9 0.8 %copy-done = f32[10,64,128]{2,1,0:T(8,128)S(1)} copy-done((f32[10,64,128]{2,1,0:T(8,128)S(1)}, f32[10,64,128]{2,1,0:T(8,128)}, u32[]{:S(2)}) %copy-start) | copy-done | bytes 327704
  1.7 0.1 copy-done.1
  1.8 0.1 copy-done.2
  1.9 0.1 copy-done.3
  2.0 0.0 copy-done.7
  2.0 0.5 %level_sums.1 = (f32[3,64,128]{2,1,0:T(8,128)S(1)}, f32[64,128]{1,0:T(8,128)S(1)}, f32[64,128]{1,0:T(8,128)S(1)}, f32[64,128]{1,0:T(8,128)S(1)}, f32[64,128]{1,0:T(8,128)S(1)}) custom-call(s32[8,128]{1,0:T(8,128)S(1)} %place.1.meta, f32[1,10]{1,0:T(1,128)S(1)} %bitcast.20, s32[1,128]{1,0:T(1,128)S(1)} %bitcast.15, f32[10,64,128]{2,1,0:T(8,128)S(1)} %copy-done, ...), custom_call_target="tpu_custom_call" | custom-call | flops 983040 | bytes 1310720 | tf_op jit(solution)/shard_map/level_sums/pallas_call | solution.py:446
  2.6 5.0 %conditional.1 = (f32[64,128]{1,0:T(8,128)}, f32[64,128]{1,0:T(8,128)}) conditional(s32[]{:T(128)} %clamp.3, (f32[64,128]{1,0:T(8,128)S(1)}, f32[64,128]{1,0:T(8,128)S(1)}) %tuple.42, (f32[64,128]{1,0:T(8,128)S(1)}, f32[64,128]{1,0:T(8,128)S(1)}) %tuple.42, (f32[64,128]{1,0:T(8,128)S(1)}, ...), branch_computations={%region_0.1_spmd, %region_1.2_spmd, %region_2.3_spmd, %region_3.4_... | conditional | bytes 262240 | solution.py:519
  2.7 3.0 %collective-permute-start.4 = (f32[64,128]{1,0:T(8,128)S(1)}, f32[64,128]{1,0:T(8,128)}, u32[]{:S(2)}, u32[]{:S(2)}) collective-permute-start(f32[64,128]{1,0:T(8,128)S(1)} %get-tuple-element.36), channel_id=1, source_target_pairs={{1,2},{2,1},{5,6},{6,5},{9,10},{10,9},{13,14},{14,13},{17,18},{18,... | collective-permute-start | bytes 98312 | tf_op jit(solution)/shard_map/cond/branch_2_fun/ppermute | solution.py:515
  5.7 0.1 collective-permute-start.5
  5.8 1.9 %collective-permute-done.4 = f32[64,128]{1,0:T(8,128)} collective-permute-done((f32[64,128]{1,0:T(8,128)S(1)}, f32[64,128]{1,0:T(8,128)}, u32[]{:S(2)}, u32[]{:S(2)}) %collective-permute-start.4) | collective-permute-done | bytes 32800 | tf_op jit(solution)/shard_map/cond/branch_2_fun/ppermute | solution.py:515
  7.7 0.0 collective-permute-done.5
  7.7 1.0 %row_halos.1 = (f32[6,80,128]{2,1,0:T(8,128)S(1)}, f32[32,128]{1,0:T(8,128)S(1)}, f32[32,128]{1,0:T(8,128)S(1)}, f32[64,128]{1,0:T(8,128)S(1)}, f32[64,128]{1,0:...) custom-call(s32[8,128]{1,0:T(8,128)S(1)} %place.1.meta, s32[1,128]{1,0:T(1,128)S(1)} %bitcast.17, ...), custom_call_target="tpu_custom_call" | custom-call | flops 61440 | bytes 983040 | tf_op jit(solution)/shard_map/row_halos/pallas_call | solution.py:446
  8.7 5.1 %collective-permute-start.18 = (f32[32,128]{1,0:T(8,128)S(1)}, f32[32,128]{1,0:T(8,128)S(1)}, u32[]{:S(2)}, u32[]{:S(2)}) collective-permute-start(f32[32,128]{1,0:T(8,128)S(1)} %get-tuple-element.95), channel_id=1, source_target_pairs={{0,28},{4,8},{8,4},{12,16},{16,12},{20,24},{24,20},{28,0},{1,29},{... | collective-permute-start | bytes 49160 | tf_op jit(solution)/shard_map/ppermute | solution.py:537
  13.8 0.0 collective-permute-start.19
  13.8 1.9 %collective-permute-start.16 = (f32[64,128]{1,0:T(8,128)S(1)}, f32[64,128]{1,0:T(8,128)S(1)}, u32[]{:S(2)}, u32[]{:S(2)}) collective-permute-start(f32[64,128]{1,0:T(8,128)S(1)} %get-tuple-element.87), channel_id=1, source_target_pairs={{0,28},{4,8},{8,4},{12,16},{16,12},{20,24},{24,20},{28,0},{1,29},{... | collective-permute-start | bytes 98312 | tf_op jit(solution)/shard_map/ppermute | solution.py:537
  15.7 0.1 collective-permute-start.17
  15.9 0.3 %basis_shift.1.shift = f32[8,128]{1,0:T(8,128)S(1)} custom-call(f32[6,80,128]{2,1,0:T(8,128)S(1)} %get-tuple-element.93.ext), custom_call_target="tpu_custom_call" | custom-call | flops 491520 | bytes 196608 | tf_op jit(solution)/shard_map/basis_shift/pallas_call | solution.py:446
  16.2 0.0 collective-permute-done.18.from_far
  16.2 1.4 %collective-permute-done.19.from_near = f32[32,128]{1,0:T(8,128)S(1)} collective-permute-done((f32[32,128]{1,0:T(8,128)S(1)}, f32[32,128]{1,0:T(8,128)S(1)}, u32[]{:S(2)}, u32[]{:S(2)}) %collective-permute-start.19) | collective-permute-done | bytes 16416 | tf_op jit(solution)/shard_map/ppermute | solution.py:536
  17.6 1.3 %krylov.1 = (f32[3,64,128]{2,1,0:T(8,128)S(1)}, f32[32,128]{1,0:T(8,128)}) custom-call(s32[8,128]{1,0:T(8,128)S(1)} %place.1.meta, s32[1,128]{1,0:T(1,128)S(1)} %bitcast.18, f32[8,128]{1,0:T(8,128)S(1)} %basis_shift.1.shift, f32[6,80,128]{2,1,0:T(8,128)S(1)} %get-tuple-element.93.ext, f32[24,128]{1,0:T(8,128)S(1)} %get-tuple-element.94.facing_rows, ...), custom_call_target="tpu_custom_call" | custom-call | flops 2048000 | bytes 491520 | tf_op jit(solution)/shard_map/krylov/pallas_call | solution.py:446
  18.8 3.5 %all-to-all-start = ((f32[32,1,128]{2,1,0:T(1,128)}), f32[32,1,128]{2,1,0:T(1,128)S(1)}, u32[]{:S(2)}, u32[]{:S(2)}) async-start(f32[32,1,128]{2,1,0:T(1,128)} %bitcast.10), calls=%async_computation | async-start | bytes 32768 | tf_op jit(solution)/shard_map/all_to_all | solution.py:568
  22.3 0.0 collective-permute-done.16.from_far
  22.3 0.0 collective-permute-done.17.from_near
  22.3 3.8 %levels_step.1 = (f32[10,64,128]{2,1,0:T(8,128)}, f32[10,64,128]{2,1,0:T(8,128)}, f32[10,64,128]{2,1,0:T(8,128)}, f32[10,64,128]{2,1,0:T(8,128)}) custom-call(s32[8,128]{1,0:T(8,128)S(1)} %place.1.meta, f32[1,10]{1,0:T(1,128)S(1)} %bitcast.21, s32[1,128]{1,0:T(1,128)S(1)} %bitcast.19, f32[10,64,128]{2,1,0:T(8,128)S(1)} %copy-done, ...), custom_call_target="tpu_custom_call" | custom-call | flops 9830400 | bytes 2621440 | tf_op jit(solution)/shard_map/levels_step/pallas_call | solution.py:446
  26.1 3.3 %all-to-all-done = f32[32,1,128]{2,1,0:T(1,128)S(1)} async-done(((f32[32,1,128]{2,1,0:T(1,128)}), f32[32,1,128]{2,1,0:T(1,128)S(1)}, u32[]{:S(2)}, u32[]{:S(2)}) %all-to-all-start) | async-done | bytes 16416 | tf_op jit(solution)/shard_map/all_to_all | solution.py:568
  29.4 0.9 %surface.1 = f32[64,128]{1,0:T(8,128)} custom-call(f32[32,128]{1,0:T(8,128)S(1)} %bitcast.14, f32[8,128]{1,0:T(8,128)S(1)} %basis_shift.1.shift, f32[3,64,128]{2,1,0:T(8,128)S(1)} %get-tuple-element.98.base), custom_call_target="tpu_custom_call" | custom-call | flops 49152 | bytes 131072 | tf_op jit(solution)/shard_map/surface/pallas_call | solution.py:446
  (9 shorter events, 0.0 us)
Async XLA Ops:
  0.7 1.0 %copy-start = (f32[10,64,128]{2,1,0:T(8,128)S(1)}, f32[10,64,128]{2,1,0:T(8,128)}, u32[]{:S(2)}) copy-start(f32[10,64,128]{2,1,0:T(8,128)} %heat.3) | copy-start | bytes 983044
  0.7 1.1 %copy-start.1 = (f32[10,64,128]{2,1,0:T(8,128)S(1)}, f32[10,64,128]{2,1,0:T(8,128)}, u32[]{:S(2)}) copy-start(f32[10,64,128]{2,1,0:T(8,128)} %salt.3) | copy-start | bytes 983044
  0.7 1.2 %copy-start.2 = (f32[10,64,128]{2,1,0:T(8,128)S(1)}, f32[10,64,128]{2,1,0:T(8,128)}, u32[]{:S(2)}) copy-start(f32[10,64,128]{2,1,0:T(8,128)} %zonal.3) | copy-start | bytes 983044
  0.7 1.3 %copy-start.3 = (f32[10,64,128]{2,1,0:T(8,128)S(1)}, f32[10,64,128]{2,1,0:T(8,128)}, u32[]{:S(2)}) copy-start(f32[10,64,128]{2,1,0:T(8,128)} %merid.3) | copy-start | bytes 983044
  0.7 1.3 %copy-start.4 = (s32[64,128]{1,0:T(8,128)S(1)}, s32[64,128]{1,0:T(8,128)}, u32[]{:S(2)}) copy-start(s32[64,128]{1,0:T(8,128)} %water.5) | copy-start | bytes 98308
  0.8 1.2 %copy-start.5 = (f32[64,128]{1,0:T(8,128)S(1)}, f32[64,128]{1,0:T(8,128)}, u32[]{:S(2)}) copy-start(f32[64,128]{1,0:T(8,128)} %weights.3) | copy-start | bytes 98308
  0.8 1.2 %copy-start.6 = (f32[64,128]{1,0:T(8,128)S(1)}, f32[64,128]{1,0:T(8,128)}, u32[]{:S(2)}) copy-start(f32[64,128]{1,0:T(8,128)} %anomaly.3) | copy-start | bytes 98308
  0.9 1.2 %copy-start.7 = (s32[128]{0:T(128)S(1)}, s32[128]{0:T(128)}, u32[]{:S(2)}) copy-start(s32[128]{0:T(128)} %param.23) | copy-start | bytes 1540
  0.9 1.2 %copy-start.8 = (f32[10]{0:T(128)S(1)}, f32[10]{0:T(128)}, u32[]{:S(2)}) copy-start(f32[10]{0:T(128)} %param.21) | copy-start | bytes 124
  2.7 5.0 %collective-permute-start.4 = (f32[64,128]{1,0:T(8,128)S(1)}, f32[64,128]{1,0:T(8,128)}, u32[]{:S(2)}, u32[]{:S(2)}) collective-permute-start(f32[64,128]{1,0:T(8,128)S(1)} %get-tuple-element.36), channel_id=1, source_target_pairs={{1,2},{2,1},{5,6},{6,5},{9,10},{10,9},{13,14},{14,13},{17,18},{18,... | collective-permute-start | bytes 98312 | tf_op jit(solution)/shard_map/cond/branch_2_fun/ppermute | solution.py:515
  5.7 2.0 %collective-permute-start.5 = (f32[64,128]{1,0:T(8,128)S(1)}, f32[64,128]{1,0:T(8,128)}, u32[]{:S(2)}, u32[]{:S(2)}) collective-permute-start(f32[64,128]{1,0:T(8,128)S(1)} %get-tuple-element.37), channel_id=1, source_target_pairs={{0,1},{1,0},{2,3},{3,2},{4,5},{5,4},{6,7},{7,6},{8,9},{9,8},{10,11... | collective-permute-start | bytes 98312 | tf_op jit(solution)/shard_map/cond/branch_2_fun/ppermute | solution.py:516
  8.7 7.5 %collective-permute-start.18 = (f32[32,128]{1,0:T(8,128)S(1)}, f32[32,128]{1,0:T(8,128)S(1)}, u32[]{:S(2)}, u32[]{:S(2)}) collective-permute-start(f32[32,128]{1,0:T(8,128)S(1)} %get-tuple-element.95), channel_id=1, source_target_pairs={{0,28},{4,8},{8,4},{12,16},{16,12},{20,24},{24,20},{28,0},{1,29},{... | collective-permute-start | bytes 49160 | tf_op jit(solution)/shard_map/ppermute | solution.py:537
  13.8 3.8 %collective-permute-start.19 = (f32[32,128]{1,0:T(8,128)S(1)}, f32[32,128]{1,0:T(8,128)S(1)}, u32[]{:S(2)}, u32[]{:S(2)}) collective-permute-start(f32[32,128]{1,0:T(8,128)S(1)} %get-tuple-element.96), channel_id=1, source_target_pairs={{0,4},{4,0},{8,12},{12,8},{16,20},{20,16},{24,28},{28,24},{1,5},{5... | collective-permute-start | bytes 49160 | tf_op jit(solution)/shard_map/ppermute | solution.py:536
  13.8 8.5 %collective-permute-start.16 = (f32[64,128]{1,0:T(8,128)S(1)}, f32[64,128]{1,0:T(8,128)S(1)}, u32[]{:S(2)}, u32[]{:S(2)}) collective-permute-start(f32[64,128]{1,0:T(8,128)S(1)} %get-tuple-element.87), channel_id=1, source_target_pairs={{0,28},{4,8},{8,4},{12,16},{16,12},{20,24},{24,20},{28,0},{1,29},{... | collective-permute-start | bytes 98312 | tf_op jit(solution)/shard_map/ppermute | solution.py:537
  15.7 6.6 %collective-permute-start.17 = (f32[64,128]{1,0:T(8,128)S(1)}, f32[64,128]{1,0:T(8,128)S(1)}, u32[]{:S(2)}, u32[]{:S(2)}) collective-permute-start(f32[64,128]{1,0:T(8,128)S(1)} %get-tuple-element.88), channel_id=1, source_target_pairs={{0,4},{4,0},{8,12},{12,8},{16,20},{20,16},{24,28},{28,24},{1,5},{5... | collective-permute-start | bytes 98312 | tf_op jit(solution)/shard_map/ppermute | solution.py:536
  18.8 10.6 %all-to-all-start = ((f32[32,1,128]{2,1,0:T(1,128)}), f32[32,1,128]{2,1,0:T(1,128)S(1)}, u32[]{:S(2)}, u32[]{:S(2)}) async-start(f32[32,1,128]{2,1,0:T(1,128)} %bitcast.10), calls=%async_computation | async-start | bytes 32768 | tf_op jit(solution)/shard_map/all_to_all | solution.py:568

commit v11 on v10

--- a/solution.py
+++ b/solution.py
@@ -12,11 +12,15 @@
 
 DEEP = (5, 3, 4, 4, 3, 3)
 SIDE = (5, 4, 3, 4, 3, 3)
+RING = (10, 9, 8, 9, 8, 8)
 FIELDS = len(SIDE)
 ROW = tuple(sum(DEEP[:f]) for f in range(FIELDS + 1))
 START = tuple(sum(SIDE[:f]) for f in range(FIELDS + 1))
+RING_START = tuple(sum(RING[:f]) for f in range(FIELDS + 1))
 RELAY = 56
 FLIPPED = (1, 2)
+SHIFTED = 5
+WEST_ONLY = 120
 VMEM_LIMIT = 32 * 1024 * 1024
 LOAD_FLOPS = 10**10
 
@@ -99,16 +103,15 @@
     second[...] = jnp.where(last, back[...], jnp.where(odd, top[...], bottom[...]))
 
 
-def turn_kernel(
-    lons, meta, facing, mine, sums, water, weights, anomaly, second, first, east_columns, west_columns,
-    ext, to_far, to_near, state_far, state_near, facing_rows, north_rows, south_rows,
+def extend(
+    lons, nearest, meta, facing, mine, sums, water, weights, anomaly, second, first, ext, facing_rows, north_rows, south_rows
 ):
     rows, cols = sums.shape[1], sums.shape[2]
     tall = ext.shape[1]
     deep = north_rows.shape[0]
     odd, top, lon_odd, bottom = flags(meta)
     from_first = first[...]
-    hinge = facing[0:1, 0:1] + 1 + cols * meta[4:5, 0:1] + cols // 2
+    hinge = facing[0:1, 0:1] + 1 + cols * meta[4:5, 0:1] + (cols // 2 if nearest else 0)
     block = lax.shift_right_logical(hinge & (lons * cols - 1), cols.bit_length() - 1)
     alone = ((block - 1 - 2 * meta[4:5, 0:1]) & (lons - 1)) == 0
     from_second = jnp.where(top & alone, mine[...], second[...])
@@ -122,6 +125,22 @@
         ext[f, rows : rows + size, :] = north[at : at + size]
         ext[f, rows + size : tall - size, :] = jnp.zeros((tall - rows - 2 * size, cols), jnp.float32)
         ext[f, tall - size :, :] = south[at : at + size]
+    facing_rows[...] = from_second[deep:]
+    north_rows[...] = north[:deep]
+    south_rows[...] = south[:deep]
+    return from_second, lon_odd
+
+
+def turn_kernel(
+    lons, meta, facing, mine, sums, water, weights, anomaly, second, first, east_columns, west_columns,
+    ext, to_far, to_near, state_far, state_near, facing_rows, north_rows, south_rows,
+):
+    from_second, lon_odd = extend(
+        lons, True, meta, facing, mine, sums, water, weights, anomaly, second, first,
+        ext, facing_rows, north_rows, south_rows,
+    )
+    rows, cols = sums.shape[1], sums.shape[2]
+    deep = north_rows.shape[0]
     passed = from_second[deep:]
     size = passed.shape[0]
     half = rows // 2
@@ -154,15 +173,50 @@
     west = jnp.where(right_half, jnp.concatenate([passed, spare], axis=0), west_columns[...])
     state_far[...] = jnp.where(lon_odd, east, west)
     state_near[...] = jnp.where(lon_odd, west, east)
-    facing_rows[...] = from_second[deep:]
-    north_rows[...] = north[:deep]
-    south_rows[...] = south[:deep]
-
-
-def fold_shift(facing):
+
+
+def ring_turn_kernel(
+    lons, meta, facing, mine, sums, water, weights, anomaly, second, first, east_columns, west_columns,
+    ext, to_ring, to_far, to_near, facing_rows, north_rows, south_rows,
+):
+    from_second, lon_odd = extend(
+        lons, False, meta, facing, mine, sums, water, weights, anomaly, second, first,
+        ext, facing_rows, north_rows, south_rows,
+    )
+    rows, cols = sums.shape[1], sums.shape[2]
+    tall = ext.shape[1]
+    deep = north_rows.shape[0]
+    middle = tall // 2
+    lane = iota((middle, cols), 1)
+    ring = jnp.zeros((middle, cols), jnp.float32)
+    for f in range(FIELDS):
+        for part in range(2):
+            at = RING_START[f] + part * RING_START[-1]
+            layer = ext[f, part * middle : (part + 1) * middle, :]
+            here = (lane >= at) & (lane < at + RING[f])
+            ring = jnp.where(here, pltpu.roll(layer, (at + RING[f]) % cols, 1), ring)
+    to_ring[:middle, :] = ring
+    to_ring[middle:, :] = from_second[deep:]
+    lane = iota((tall, cols), 1)
+    spare = jnp.zeros((tall - rows, cols), jnp.float32)
+    east = jnp.concatenate([east_columns[...], spare], axis=0)
+    west = jnp.concatenate([west_columns[...], spare], axis=0)
+    for f in range(FIELDS):
+        at = deep + START[f]
+        here = (lane >= at) & (lane < at + SIDE[f])
+        layer = ext[f]
+        east = jnp.where(here, pltpu.roll(layer, (at + SIDE[f]) % cols, 1), east)
+        west = jnp.where(here, pltpu.roll(layer, at, 1), west)
+    to_far[:tall, :] = jnp.where(lon_odd, east, west)
+    to_near[:tall, :] = jnp.where(lon_odd, west, east)
+    to_far[tall:, :] = from_second
+    to_near[tall:, :] = from_second
+
+
+def fold_shift(facing, nearest):
     cols = facing.shape[1]
     offset = (facing[0:1, 0:1] + 1) & (cols - 1)
-    return jnp.where(offset >= cols // 2, offset - cols, offset)
+    return jnp.where(offset >= cols // 2, offset - cols, offset) if nearest else offset
 
 
 def fold(shift, west, own, east, beside):
@@ -203,43 +257,11 @@
     shift[...] = jnp.broadcast_to(jnp.clip(quotient, -1.0, 1.0), shift.shape)
 
 
-def krylov_kernel(meta, facing, shift, ext, facing_rows, from_far, from_near, base, moments, folded):
-    tall, cols = ext.shape[1], ext.shape[2]
-    rows = base.shape[1]
-    size = facing_rows.shape[0]
-    _, top, lon_odd, _ = flags(meta)
-    west = jnp.where(lon_odd, from_near[...], from_far[...])
-    east = jnp.where(lon_odd, from_far[...], from_near[...])
-    theta = shift[0:1, 0:1]
-    across = fold_shift(facing)
-    row = iota((size, cols), 0)
-    flips = (row >= ROW[FLIPPED[0]]) & (row < ROW[FLIPPED[-1] + 1])
-    for side in range(2):
-        cells = fold(across, pltpu.roll(west[:size], cols - RELAY, 1), facing_rows[...], east[:size], side == 1)
-        folded[side, :size, :] = jnp.where(flips, -cells, cells)
-    folded[:, size:, :] = jnp.zeros((2, folded.shape[1] - size, cols), jnp.float32)
+def krylov(fields, theta):
+    tall, cols = fields[0][0].shape
     lane = iota((tall, cols), 1)
     first = lane == 0
     last = lane == cols - 1
-    eighth = iota((8, cols), 0)
-
-    def load(f):
-        parts = []
-        for packet, shift_of in ((west, 2 * cols - SIDE[f]), (east, cols)):
-            pieces = []
-            for start, stop, first_lane in segments(rows):
-                layer = packet[packet.shape[0] - (stop - start) :]
-                pieces.append(pltpu.roll(layer, (shift_of - START[f] - first_lane) % cols, 1))
-            parts.append(jnp.concatenate(pieces, axis=0))
-        a, b = parts
-        beside = jnp.where(lane >= cols - SIDE[f], a, jnp.where(lane < SIDE[f], b, 0.0))
-
-        def put(cells, side):
-            new = folded[side, ROW[f] : ROW[f] + 8, :]
-            new = jnp.where(eighth < DEEP[f], jnp.where(top, new, cells[rows : rows + 8]), 0.0)
-            return jnp.concatenate([cells[:rows], new, cells[rows + 8 :]], axis=0)
-
-        return put(ext[f], 0), put(beside, 1)
 
     def plus_x(pair):
         a, b = (pltpu.roll(part, cols - 1, 1) for part in pair)
@@ -263,7 +285,7 @@
             lambda a, b, c, d: (a + b) + (c + d), plus_x(pair), minus_x(pair), plus_y(pair), minus_y(pair)
         )
 
-    press, zonal, merid, wet, weights, anomaly = (load(f) for f in range(FIELDS))
+    press, zonal, merid, wet, weights, anomaly = fields
     half = 0.5 * TIME_STEP
     flow = lambda w, speed, a, b: w * (speed - half * (a - b))
     east_flow = each(flow, wet, zonal, plus_x(press), minus_x(press))
@@ -284,12 +306,34 @@
     zero = each(lambda r, i: r * i, right, inverse)
     one = each(lambda a, n, z: a * n - theta * z, scale, neighbours(zero), zero)
     two = each(lambda a, n, z: a * n - theta * z, scale, neighbours(one), one)
-    three = scale[0][:rows] * neighbours(two)[0][:rows] - theta * two[0][:rows]
-    right, middle = right[0][:rows], diagonal[0][:rows]
-    zero, one, two = zero[0][:rows], one[0][:rows], two[0][:rows]
-    base[0] = zero
-    base[1] = one
-    base[2] = two
+    three = each(lambda a, n, z: a * n - theta * z, scale, neighbours(two), two)
+    return right, diagonal, zero, one, two, three
+
+
+def put_fold(f, pair, folded, top):
+    rows = pair[0].shape[0] - 16
+    eighth = iota((8, pair[0].shape[1]), 0)
+
+    def put(cells, side):
+        new = folded[side, ROW[f] : ROW[f] + 8, :]
+        new = jnp.where(eighth < DEEP[f], jnp.where(top, new, cells[rows : rows + 8]), 0.0)
+        return jnp.concatenate([cells[:rows], new, cells[rows + 8 :]], axis=0)
+
+    return put(pair[0], 0), put(pair[1], 1)
+
+
+def fill_fold(folded, across, west, own, east):
+    size, cols = own.shape
+    row = iota((size, cols), 0)
+    flips = (row >= ROW[FLIPPED[0]]) & (row < ROW[FLIPPED[-1] + 1])
+    for side in range(2):
+        cells = fold(across, west, own, east, side == 1)
+        folded[side, :size, :] = jnp.where(flips, -cells, cells)
+    folded[:, size:, :] = jnp.zeros((2, folded.shape[1] - size, cols), jnp.float32)
+
+
+def put_moments(right, middle, zero, one, two, three, theta, moments):
+    cols = moments.shape[1]
     weighted_one = middle * one
     weighted_two = middle * two
     products = (
@@ -313,8 +357,84 @@
     moments[...] = jnp.broadcast_to(sums, moments.shape)
 
 
+def krylov_kernel(meta, facing, shift, ext, facing_rows, from_far, from_near, base, moments, folded):
+    tall, cols = ext.shape[1], ext.shape[2]
+    rows = base.shape[1]
+    size = facing_rows.shape[0]
+    _, top, lon_odd, _ = flags(meta)
+    west = jnp.where(lon_odd, from_near[...], from_far[...])
+    east = jnp.where(lon_odd, from_far[...], from_near[...])
+    theta = shift[0:1, 0:1]
+    relay = pltpu.roll(west[:size], cols - RELAY, 1)
+    fill_fold(folded, fold_shift(facing, True), relay, facing_rows[...], east[:size])
+    lane = iota((tall, cols), 1)
+
+    def load(f):
+        parts = []
+        for packet, shift_of in ((west, 2 * cols - SIDE[f]), (east, cols)):
+            pieces = []
+            for start, stop, first_lane in segments(rows):
+                layer = packet[packet.shape[0] - (stop - start) :]
+                pieces.append(pltpu.roll(layer, (shift_of - START[f] - first_lane) % cols, 1))
+            parts.append(jnp.concatenate(pieces, axis=0))
+        a, b = parts
+        beside = jnp.where(lane >= cols - SIDE[f], a, jnp.where(lane < SIDE[f], b, 0.0))
+        return put_fold(f, (ext[f], beside), folded, top)
+
+    vectors = krylov([load(f) for f in range(FIELDS)], theta)
+    right, middle, zero, one, two, three = (pair[0][:rows] for pair in vectors)
+    base[0] = zero
+    base[1] = one
+    base[2] = two
+    put_moments(right, middle, zero, one, two, three, theta, moments)
+
+
+def ring_kernel(meta, facing, shift, ext, facing_rows, from_ring, moments, folded):
+    tall, cols = ext.shape[1], ext.shape[2]
+    rows, middle = tall - 16, tall // 2
+    top = flags(meta)[1]
+    theta = shift[0:1, 0:1]
+    own = facing_rows[...]
+    fill_fold(folded, fold_shift(facing, False), from_ring[middle:, :], own, own)
+    lane = iota((tall, cols), 1)
+    packet = from_ring[:middle, :]
+
+    def load(f):
+        both = [RING_START[f], RING_START[f] + RING_START[-1]]
+        a = jnp.concatenate([pltpu.roll(packet, (2 * cols - RING[f] - at) % cols, 1) for at in both], axis=0)
+        return put_fold(f, (ext[f], jnp.where(lane >= cols - RING[f], a, 0.0)), folded, top)
+
+    vectors = krylov([load(f) for f in range(FIELDS)], theta)
+    here = lane[:rows] < cols - SHIFTED
+    put_moments(*(jnp.where(here, a[:rows], b[:rows]) for a, b in vectors), theta, moments)
+
+
+def base_kernel(used, meta, facing, shift, ext, facing_rows, from_far, from_near, base, folded):
+    tall, cols = ext.shape[1], ext.shape[2]
+    rows = base.shape[1]
+    size = facing_rows.shape[0]
+    _, top, lon_odd, _ = flags(meta)
+    west = jnp.where(lon_odd, from_near[...], from_far[...])
+    east = jnp.where(lon_odd, from_far[...], from_near[...])
+    at = tall + used
+    fill_fold(folded, fold_shift(facing, False), west[at : at + size], facing_rows[...], east[at : at + size])
+    lane = iota((tall, cols), 1)
+
+    def load(f):
+        at = used + START[f]
+        a = pltpu.roll(west[:tall], (2 * cols - SIDE[f] - at) % cols, 1)
+        b = pltpu.roll(east[:tall], (cols - at) % cols, 1)
+        beside = jnp.where(lane >= cols - SIDE[f], a, jnp.where(lane < SIDE[f], b, 0.0))
+        return put_fold(f, (ext[f], beside), folded, top)
+
+    _, _, zero, one, two, _ = krylov([load(f) for f in range(FIELDS)], shift[0:1, 0:1])
+    base[0] = zero[0][:rows]
+    base[1] = one[0][:rows]
+    base[2] = two[0][:rows]
+
+
 def step_kernel(
-    meta, spans, facing, heat, salt, zonal, merid, water, north_came, south_rows, from_far, from_near,
+    nearest, meta, spans, facing, heat, salt, zonal, merid, water, north_came, south_rows, from_far, from_near,
     heat_out, salt_out, zonal_out, merid_out,
     new_heat, new_salt, new_zonal, new_merid, north_rows, sems,
 ):
@@ -327,7 +447,12 @@
     east = jnp.where(lon_odd, from_far[...], from_near[...])
     west = jnp.where(lon_odd, from_near[...], from_far[...])
     came = north_came[...]
-    across = fold(fold_shift(facing), pltpu.roll(west[:deep], cols // 2, 1), came, east[:deep], False)
+    if nearest:
+        relays = pltpu.roll(west[:deep], cols // 2, 1), east[:deep]
+    else:
+        relays = west[rows + 16 : rows + 16 + deep], east[rows + 16 : rows + 16 + deep]
+    across = fold(fold_shift(facing, nearest), relays[0], came, relays[1], False)
+    east, west = east[:rows], west[:rows]
     north_rows[...] = jnp.where(top, across, came)
 
     def around(cells, q):
@@ -472,7 +597,7 @@
     lon, lat = lax.axis_index("lon"), lax.axis_index("lat")
     levels, rows, cols = warmth_deviation.shape
     high = packet_rows(levels)
-    assert cols & (cols - 1) == 0 and rows >= 24 and rows // 2 == high - 4 * levels + 8 and 4 * levels <= cols // 2 and 2 * START[-1] <= min(RELAY, cols - RELAY) and cols == 128
+    assert cols & (cols - 1) == 0 and rows >= 24 and rows // 2 == high - 4 * levels + 8 and 4 * levels <= cols // 2 and 2 * RING_START[-1] <= cols and 2 * START[-1] <= min(RELAY, cols - RELAY) and cols == 128
     tall = rows + 16
     width = cols * lons
     flat = lambda i, j: (i % lons) * lats + j
@@ -504,70 +629,92 @@
         for a, b in ((j, j + 1), (j + 1, j))
     ] + [(flat(i, 0), flat(i ^ 1, 0)) for i in range(lons)]
 
+    near = lambda cells: lax.ppermute(cells, "lon", [(i, i ^ 1) for i in range(lons)])
+    far = lambda cells: lax.ppermute(cells, "lon", [(i, (i + 1 if i % 2 else i - 1) % lons) for i in range(lons)])
+    deep = 4 * levels
+    count = lons * lats
+    folds = [pltpu.VMEM((2, high - deep + 8, cols), jnp.float32)]
+    work = (200 * tall * cols, 48 * tall * cols)
+
+    def exchange(block, first, second):
+        def swap(shift, first, second):
+            partner = [(shift - 1 - i) % lons for i in range(lons)]
+            partner = [i + lons // 2 if i == p else p for i, p in enumerate(partner)]
+            pairs_fold = [(flat(p, lats - 1), flat(i, lats - 1)) for i, p in enumerate(partner)]
+            second = lax.ppermute(second, axes, pairs_inner + pairs_fold)
+            return second, lax.ppermute(first, axes, pairs_first)
+
+        return lax.switch(block, [functools.partial(swap, s) for s in range(lons)], first, second)
+
+    def turn(kernel, packets, first, second, mine):
+        return call(
+            kernel,
+            [(FIELDS, tall, cols), *packets, (high - deep, cols), *[(deep, cols)] * 2],
+            FIELDS * tall * cols,
+            16 * FIELDS * tall * cols,
+            "row_halos",
+        )(meta, facing, mine, sums, *flat_state, second, first, east_columns, west_columns)
+
+    def basis_shift(ext):
+        return call(shift_kernel, [(8, cols)], 60 * rows * cols, 24 * rows * cols, "basis_shift")(ext)[0]
+
+    def step(nearest, north_rows, south_rows, from_far, from_near):
+        chunks = 5 if levels % 5 == 0 else 1
+        return call(
+            functools.partial(step_kernel, nearest),
+            [(levels, rows, cols)] * 4,
+            120 * cells,
+            32 * cells,
+            "levels_step",
+            out_space=pltpu.HBM,
+            scratch=[*[pltpu.VMEM((levels, rows, cols), jnp.float32)] * 4, pltpu.VMEM((deep, cols), jnp.float32), pltpu.SemaphoreType.DMA((4, chunks))],
+        )(meta, spans, facing, *state, water_indicator, north_rows, south_rows, from_far, from_near)
+
+    def finish(shares, shift, base):
+        return call(surface_kernel, [(rows, cols)], 6 * rows * cols, 16 * rows * cols, "surface")(shares, shift, base)[0]
+
+    def by_swaps(hinge, first, second):
+        block = lax.rem((hinge + cols // 2) // cols, lons)
+        got_second, got_first = exchange(block, first, second)
+        ext, to_far, to_near, state_far, state_near, facing_rows, north_rows, south_rows = turn(
+            functools.partial(turn_kernel, lons),
+            [*[(rows // 2, cols)] * 2, *[(rows, cols)] * 2],
+            got_first, got_second, second,
+        )
+        from_far, from_near = far(to_far), near(to_near)
+        state_far, state_near = far(state_far), near(state_near)
+        shift = basis_shift(ext)
+        base, moments = call(krylov_kernel, [(3, rows, cols), (count, cols)], *work, "krylov", scratch=folds)(
+            meta, facing, shift, ext, facing_rows, from_far, from_near
+        )
+        results = step(True, north_rows, south_rows, state_far, state_near)
+        shares = lax.all_to_all(moments, axes, 0, 0, tiled=True)
+        return (*results, finish(shares, shift, base))
+
+    def by_ring(hinge, first, second):
+        got_second, got_first = exchange(hinge // cols, first, second)
+        ext, to_ring, to_far, to_near, facing_rows, north_rows, south_rows = turn(
+            functools.partial(ring_turn_kernel, lons),
+            [(tall // 2 + high - deep, cols), *[(tall + high, cols)] * 2],
+            got_first, got_second, second,
+        )
+        from_ring = lax.ppermute(to_ring, "lon", [(i, (i + 1) % lons) for i in range(lons)])
+        from_far, from_near = far(to_far), near(to_near)
+        shift = basis_shift(ext)
+        (moments,) = call(ring_kernel, [(count, cols)], *work, "moments", scratch=folds)(
+            meta, facing, shift, ext, facing_rows, from_ring
+        )
+        shares = lax.all_to_all(moments, axes, 0, 0, tiled=True)
+        _, from_far, from_near = lax.optimization_barrier((moments, from_far, from_near))
+        results = step(False, north_rows, south_rows, from_far, from_near)
+        (base,) = call(functools.partial(base_kernel, deep), [(3, rows, cols)], *work, "krylov", scratch=folds)(
+            meta, facing, shift, ext, facing_rows, from_far, from_near
+        )
+        return (*results, finish(shares, shift, base))
+
     counterpart, first = lax.optimization_barrier((opposite_counterpart, first))
     hinge = lax.rem(counterpart[0] + 1 + cols * lon, width)
-    block = lax.rem((hinge + cols // 2) // cols, lons)
-
-    def exchange(shift, first, second):
-        partner = [(shift - 1 - i) % lons for i in range(lons)]
-        partner = [i + lons // 2 if i == p else p for i, p in enumerate(partner)]
-        pairs_fold = [(flat(p, lats - 1), flat(i, lats - 1)) for i, p in enumerate(partner)]
-        second = lax.ppermute(second, axes, pairs_inner + pairs_fold)
-        return second, lax.ppermute(first, axes, pairs_first)
-
-    mine = second
-    second, first = lax.switch(block, [functools.partial(exchange, s) for s in range(lons)], first, second)
-
-    deep = 4 * levels
-    ext, to_far, to_near, state_far, state_near, facing_rows, north_rows, south_rows = call(
-        functools.partial(turn_kernel, lons),
-        [
-            (FIELDS, tall, cols),
-            *[(rows // 2, cols)] * 2,
-            *[(rows, cols)] * 2,
-            (high - deep, cols),
-            *[(deep, cols)] * 2,
-        ],
-        FIELDS * tall * cols,
-        4 * 4 * FIELDS * tall * cols,
-        "row_halos",
-    )(meta, facing, mine, sums, *flat_state, second, first, east_columns, west_columns)
-
-    near = lambda cells: lax.ppermute(cells, "lon", [(i, i ^ 1) for i in range(lons)])
-    far = lambda cells: lax.ppermute(cells, "lon", [(i, (i + 1 if i % 2 else i - 1) % lons) for i in range(lons)])
-    from_far, from_near = far(to_far), near(to_near)
-    state_far, state_near = far(state_far), near(state_near)
-
-    (shift,) = call(shift_kernel, [(8, cols)], 60 * rows * cols, 24 * rows * cols, "basis_shift")(ext)
-
-    count = lons * lats
-    base, moments = call(
-        krylov_kernel,
-        [(3, rows, cols), (count, cols)],
-        200 * tall * cols,
-        4 * 12 * tall * cols,
-        "krylov",
-        scratch=[pltpu.VMEM((2, high - deep + 8, cols), jnp.float32)],
-    )(meta, facing, shift, ext, facing_rows, from_far, from_near)
-
-    chunks = 5 if levels % 5 == 0 else 1
-    new_heat, new_salt, new_zonal, new_merid = call(
-        step_kernel,
-        [(levels, rows, cols)] * 4,
-        120 * cells,
-        32 * cells,
-        "levels_step",
-        out_space=pltpu.HBM,
-        scratch=[
-            *[pltpu.VMEM((levels, rows, cols), jnp.float32)] * 4,
-            pltpu.VMEM((deep, cols), jnp.float32),
-            pltpu.SemaphoreType.DMA((4, chunks)),
-        ],
-    )(meta, spans, facing, *state, water_indicator, north_rows, south_rows, state_far, state_near)
-
-    shares = lax.all_to_all(moments, axes, 0, 0, tiled=True)
-    (surface,) = call(surface_kernel, [(rows, cols)], 6 * rows * cols, 16 * rows * cols, "surface")(shares, shift, base)
-    return (new_heat, new_salt, new_zonal, new_merid, surface)
+    return lax.cond(lax.rem(hinge, cols) < WEST_ONLY, by_ring, by_swaps, hinge, first, second)
 
 
 def solution(mesh):

time: 30.6 us -> 36.3 us (1.19)
  waiting for transfers between devices: 6.55 us -> 12.6 us
  starting transfers between devices: 13.8 us -> 12.8 us
  Pallas kernels: 7.76 us -> 8.42 us
    ppermute x2 -> x3, waiting for transfers between devices: 1.86 us -> 6.14 us  [the longest x1 4.28 us: by_ring(): lax.ppermute(to_ring, 'lon', [(i, (i + 1) % lons) for i in range(lons)])]
    all_to_all x1, waiting for transfers between devices: 3.29 us -> 6.48 us  [by_ring(): shares = lax.all_to_all(moments, axes, 0, 0, tiled=True)]
    ppermute x2 -> x3, starting transfers between devices: 3.15 us -> 5.17 us  [the longest x1 3 us: swap(): second = lax.ppermute(second, axes, pairs_inner + pairs_fold)]
    ppermute x2 -> x1, starting transfers between devices: 7.06 us -> 5.12 us  [body(): lax.ppermute(cells, 'lon', [(i, (i + 1 if i % 2 else i - 1) % lons) for i...]
    ppermute x2 -> x1, waiting for transfers between devices: 1.4 us -> 0.01 us  [body(): lax.ppermute(cells, 'lon', [(i, i ^ 1) for i in range(lons)])]
    all_to_all x1, starting transfers between devices: 3.5 us -> 2.54 us  [by_ring(): shares = lax.all_to_all(moments, axes, 0, 0, tiled=True)]
    pallas_call x7 -> x8, Pallas kernels: 7.76 us -> 8.42 us  [run(): pl.pallas_call(kernel, out_shape=[jax.ShapeDtypeStruct(shape, types) for...]
  transfers between devices with their start and end apart: 7 -> 6, of which waited for: 3 -> 3; matrix products, arithmetic and copies ran while one was open for 0% -> 0% of each run, Pallas kernels for 18% -> 6%
where the time goes in v11:
time: 36.3 us; the launch traced here: 36 us
  starting transfers between devices  12.8 us (35%)
  waiting for transfers between devices  12.6 us (35%)
  Pallas kernels  8.42 us (23%)
  local copies, waits for them, and re-layouts  1.24 us (3%)
  between operations  0.78 us (2%)
    pallas_call x8, Pallas kernels, run(): pl.pallas_call(kernel, out_shape=[jax.ShapeDtypeStruct(shape, types) for...  8.42 us
    all_to_all x1, waiting for transfers between devices, by_ring(): shares = lax.all_to_all(moments, axes, 0, 0, tiled=True)  6.48 us
    ppermute x1, starting transfers between devices, body(): lax.ppermute(cells, 'lon', [(i, (i + 1 if i % 2 else i - 1) % lons) for i...  5.12 us
    ppermute x1, waiting for transfers between devices, by_ring(): lax.ppermute(to_ring, 'lon', [(i, (i + 1) % lons) for i in range(lons)])  4.28 us
    ppermute x1, starting transfers between devices, swap(): second = lax.ppermute(second, axes, pairs_inner + pairs_fold)  3 us
    all_to_all x1, starting transfers between devices, by_ring(): shares = lax.all_to_all(moments, axes, 0, 0, tiled=True)  2.54 us
    ppermute x1, starting transfers between devices, by_ring(): lax.ppermute(to_ring, 'lon', [(i, (i + 1) % lons) for i in range(lons)])  2.02 us
    ppermute x1, waiting for transfers between devices, swap(): second = lax.ppermute(second, axes, pairs_inner + pairs_fold)  1.86 us
  transfers between devices with their start and end apart: 6, of which 3 were waited for; matrix products, arithmetic and copies ran while one was open for 0% of the time, Pallas kernels for 6%

profile of v11, /device:TPU:0, one launch (start us, length us, event | category | flops | bytes accessed | tf_op | source)
XLA Modules:
  0.0 36.0 jit_solution(5707955890353590112)
XLA Ops:
  0.6 0.1 stack.31
  0.7 0.0 copy-start.4
  0.8 0.0 copy-start.5
  0.8 0.0 copy-start.6
  0.8 0.0 copy-start.7
  0.8 0.0 copy-start.8
  0.8 0.1 place.1.meta
  0.9 0.8 %copy-done = f32[10,64,128]{2,1,0:T(8,128)S(1)} copy-done((f32[10,64,128]{2,1,0:T(8,128)S(1)}, f32[10,64,128]{2,1,0:T(8,128)}, u32[]{:S(2)}) %copy-start) | copy-done | bytes 327704
  1.7 0.1 copy-done.1
  1.8 0.1 copy-done.2
  1.9 0.1 copy-done.3
  2.0 0.6 %level_sums.1 = (f32[3,64,128]{2,1,0:T(8,128)S(1)}, f32[64,128]{1,0:T(8,128)S(1)}, f32[64,128]{1,0:T(8,128)S(1)}, f32[64,128]{1,0:T(8,128)S(1)}, f32[64,128]{1,0:T(8,128)S(1)}) custom-call(s32[8,128]{1,0:T(8,128)S(1)} %place.1.meta, f32[1,10]{1,0:T(1,128)S(1)} %bitcast.25, s32[1,128]{1,0:T(1,128)S(1)} %bitcast.21, f32[10,64,128]{2,1,0:T(8,128)S(1)} %copy-done, ...), custom_call_target="tpu_custom_call" | custom-call | flops 983040 | bytes 1310720 | tf_op jit(solution)/shard_map/level_sums/pallas_call | solution.py:571
  2.7 33.4 %conditional.3 = (f32[10,64,128]{2,1,0:T(8,128)}, f32[10,64,128]{2,1,0:T(8,128)}, f32[10,64,128]{2,1,0:T(8,128)}, f32[10,64,128]{2,1,0:T(8,128)}, f32[64,128]{1,0:T(8,128)}) conditional(s32[]{:T(128)} %convert_element_type.2, (s32[]{:T(128)}, f32[64,128]{1,0:T(8,128)S(1)}, f32[64,128]{1,0:T(8,128)S(1)}, s32[8,128]{1,0:T(8,128)S(1)}, ...), branch_computations={%region_0.9_spmd, %region_9.18_spmd} | conditional | flops 14528528 | bytes 5947862 | solution.py:717
  2.7 5.0 %conditional.1 = (f32[64,128]{1,0:T(8,128)}, f32[64,128]{1,0:T(8,128)}) conditional(s32[]{:T(128)} %clamp.5, (f32[64,128]{1,0:T(8,128)S(1)}, f32[64,128]{1,0:T(8,128)S(1)}) %tuple.67, (f32[64,128]{1,0:T(8,128)S(1)}, f32[64,128]{1,0:T(8,128)S(1)}) %tuple.67, (f32[64,128]{1,0:T(8,128)S(1)}, ...), branch_computations={%region_10.10_spmd, %region_11.11_spmd, %region_12.12_spmd, %regio... | conditional | bytes 262240 | solution.py:647
  2.7 3.0 %collective-permute-start.34 = (f32[64,128]{1,0:T(8,128)S(1)}, f32[64,128]{1,0:T(8,128)}, u32[]{:S(2)}, u32[]{:S(2)}) collective-permute-start(f32[64,128]{1,0:T(8,128)S(1)} %get-tuple-element.190), channel_id=1, source_target_pairs={{1,2},{2,1},{5,6},{6,5},{9,10},{10,9},{13,14},{14,13},{17,18},{18,... | collective-permute-start | bytes 98312 | tf_op jit(solution)/shard_map/cond/branch_1_fun/cond/branch_7_fun/ppermute | solution.py:644
  5.7 0.1 collective-permute-start.35
  5.9 1.9 %collective-permute-done.34 = f32[64,128]{1,0:T(8,128)} collective-permute-done((f32[64,128]{1,0:T(8,128)S(1)}, f32[64,128]{1,0:T(8,128)}, u32[]{:S(2)}, u32[]{:S(2)}) %collective-permute-start.34) | collective-permute-done | bytes 32800 | tf_op jit(solution)/shard_map/cond/branch_1_fun/cond/branch_7_fun/ppermute | solution.py:644
  7.7 0.0 collective-permute-done.35
  7.7 1.1 %row_halos.3 = (f32[6,80,128]{2,1,0:T(8,128)S(1)}, f32[64,128]{1,0:T(8,128)S(1)}, f32[144,128]{1,0:T(8,128)S(1)}, f32[144,128]{1,0:T(8,128)S(1)}, f32[24,128]{1,...) custom-call(s32[8,128]{1,0:T(8,128)S(1)} %get-tuple-element.192.meta, ...), custom_call_target="tpu_custom_call" | custom-call | flops 61440 | bytes 983040 | tf_op jit(solution)/shard_map/cond/branch_1_fun/row_halos/pallas_call | solution.py:571
  8.8 5.1 %collective-permute-start.37 = (f32[144,128]{1,0:T(8,128)S(1)}, f32[144,128]{1,0:T(8,128)S(1)}, u32[]{:S(2)}, u32[]{:S(2)}) collective-permute-start(f32[144,128]{1,0:T(8,128)S(1)} %get-tuple-element.215), channel_id=1, source_target_pairs={{0,28},{4,8},{8,4},{12,16},{16,12},{20,24},{24,20},{28,0},{1,29},{... | collective-permute-start | bytes 221192 | tf_op jit(solution)/shard_map/cond/branch_1_fun/ppermute | solution.py:633
  13.9 0.0 collective-permute-start.38
  13.9 2.0 %collective-permute-start.36 = (f32[64,128]{1,0:T(8,128)S(1)}, f32[64,128]{1,0:T(8,128)S(1)}, u32[]{:S(2)}, u32[]{:S(2)}) collective-permute-start(f32[64,128]{1,0:T(8,128)S(1)} %get-tuple-element.214), channel_id=1, source_target_pairs={{0,4},{4,8},{8,12},{12,16},{16,20},{20,24},{24,28},{28,0},{1,5},{5... | collective-permute-start | bytes 98312 | tf_op jit(solution)/shard_map/cond/branch_1_fun/ppermute | solution.py:701
  16.0 0.3 basis_shift.3.shift
  16.3 4.3 %collective-permute-done.36.from_ring = f32[64,128]{1,0:T(8,128)S(1)} collective-permute-done((f32[64,128]{1,0:T(8,128)S(1)}, f32[64,128]{1,0:T(8,128)S(1)}, u32[]{:S(2)}, u32[]{:S(2)}) %collective-permute-start.36) | collective-permute-done | bytes 32800 | tf_op jit(solution)/shard_map/cond/branch_1_fun/ppermute | solution.py:701
  20.5 1.2 %moments.1 = f32[32,128]{1,0:T(8,128)} custom-call(s32[8,128]{1,0:T(8,128)S(1)} %get-tuple-element.192.meta, s32[1,128]{1,0:T(1,128)S(1)} %get-tuple-element.194.facing, f32[8,128]{1,0:T(8,128)S(1)} %basis_shift.3.shift, f32[6,80,128]{2,1,0:T(8,128)S(1)} %get-tuple-element.212.ext, f32[24,128]{1,0:T(8,128)S(1)} %get-tuple-element.213.facing_rows, ...), custom_call_target="tpu_custom_call" | custom-call | flops 2048000 | bytes 491520 | tf_op jit(solution)/shard_map/cond/branch_1_fun/moments/pallas_call | solution.py:571
  21.7 2.5 %all-to-all-start.1 = ((f32[32,1,128]{2,1,0:T(1,128)}), f32[32,1,128]{2,1,0:T(1,128)S(1)}, u32[]{:S(2)}, u32[]{:S(2)}) async-start(f32[32,1,128]{2,1,0:T(1,128)} %bitcast.5), calls=%async_computation.1 | async-start | bytes 32768 | tf_op jit(solution)/shard_map/cond/branch_1_fun/all_to_all | solution.py:707
  24.3 0.0 collective-permute-done.37.from_far
  24.3 0.0 collective-permute-done.38.from_near
  24.3 0.6 %krylov.3.base = f32[3,64,128]{2,1,0:T(8,128)S(1)} custom-call(s32[8,128]{1,0:T(8,128)S(1)} %get-tuple-element.192.meta, s32[1,128]{1,0:T(1,128)S(1)} %get-tuple-element.194.facing, f32[8,128]{1,0:T(8,128)S(1)} %basis_shift.3.shift, f32[6,80,128]{2,1,0:T(8,128)S(1)} %get-tuple-element.212.ext, f32[24,128]{1,0:T(8,128)S(1)} %get-tuple-element.213.facing_rows, ...), custom_call_target="tpu_custom_call" | custom-call | flops 2048000 | bytes 491520 | tf_op jit(solution)/shard_map/cond/branch_1_fun/krylov/pallas_call | solution.py:571
  24.9 6.5 %all-to-all-done.1 = f32[32,1,128]{2,1,0:T(1,128)S(1)} async-done(((f32[32,1,128]{2,1,0:T(1,128)}), f32[32,1,128]{2,1,0:T(1,128)S(1)}, u32[]{:S(2)}, u32[]{:S(2)}) %all-to-all-start.1) | async-done | bytes 16416 | tf_op jit(solution)/shard_map/cond/branch_1_fun/all_to_all | solution.py:707
  31.4 0.9 %surface.3 = f32[64,128]{1,0:T(8,128)} custom-call(f32[32,128]{1,0:T(8,128)S(1)} %bitcast.19, f32[8,128]{1,0:T(8,128)S(1)} %basis_shift.3.shift, f32[3,64,128]{2,1,0:T(8,128)S(1)} %krylov.3.base), custom_call_target="tpu_custom_call" | custom-call | flops 49152 | bytes 131072 | tf_op jit(solution)/shard_map/cond/branch_1_fun/surface/pallas_call | solution.py:571
  32.2 3.8 %levels_step.3 = (f32[10,64,128]{2,1,0:T(8,128)}, f32[10,64,128]{2,1,0:T(8,128)}, f32[10,64,128]{2,1,0:T(8,128)}, f32[10,64,128]{2,1,0:T(8,128)}) custom-call(s32[8,128]{1,0:T(8,128)S(1)} %get-tuple-element.192.meta, f32[1,10]{1,0:T(1,128)S(1)} %get-tuple-element.193.spans, s32[1,128]{1,0:T(1,128)S(1)} %get-tuple-element.194.facing, ...), custom_call_target="tpu_custom_call" | custom-call | flops 9830400 | bytes 2621440 | tf_op jit(solution)/shard_map/cond/branch_1_fun/levels_step/pallas_call | solution.py:571
  (9 shorter events, 0.0 us)
Async XLA Ops:
  0.7 1.0 %copy-start = (f32[10,64,128]{2,1,0:T(8,128)S(1)}, f32[10,64,128]{2,1,0:T(8,128)}, u32[]{:S(2)}) copy-start(f32[10,64,128]{2,1,0:T(8,128)} %heat.1) | copy-start | bytes 983044
  0.7 1.1 %copy-start.1 = (f32[10,64,128]{2,1,0:T(8,128)S(1)}, f32[10,64,128]{2,1,0:T(8,128)}, u32[]{:S(2)}) copy-start(f32[10,64,128]{2,1,0:T(8,128)} %salt.1) | copy-start | bytes 983044
  0.7 1.2 %copy-start.2 = (f32[10,64,128]{2,1,0:T(8,128)S(1)}, f32[10,64,128]{2,1,0:T(8,128)}, u32[]{:S(2)}) copy-start(f32[10,64,128]{2,1,0:T(8,128)} %zonal.1) | copy-start | bytes 983044
  0.7 1.3 %copy-start.3 = (f32[10,64,128]{2,1,0:T(8,128)S(1)}, f32[10,64,128]{2,1,0:T(8,128)}, u32[]{:S(2)}) copy-start(f32[10,64,128]{2,1,0:T(8,128)} %merid.1) | copy-start | bytes 983044
  0.7 1.3 %copy-start.4 = (s32[64,128]{1,0:T(8,128)S(1)}, s32[64,128]{1,0:T(8,128)}, u32[]{:S(2)}) copy-start(s32[64,128]{1,0:T(8,128)} %water.1) | copy-start | bytes 98308
  0.8 1.2 %copy-start.5 = (f32[64,128]{1,0:T(8,128)S(1)}, f32[64,128]{1,0:T(8,128)}, u32[]{:S(2)}) copy-start(f32[64,128]{1,0:T(8,128)} %weights.1) | copy-start | bytes 98308
  0.8 1.2 %copy-start.6 = (f32[64,128]{1,0:T(8,128)S(1)}, f32[64,128]{1,0:T(8,128)}, u32[]{:S(2)}) copy-start(f32[64,128]{1,0:T(8,128)} %anomaly.1) | copy-start | bytes 98308
  0.8 1.2 %copy-start.7 = (s32[128]{0:T(128)S(1)}, s32[128]{0:T(128)}, u32[]{:S(2)}) copy-start(s32[128]{0:T(128)} %param.33) | copy-start | bytes 1540
  0.8 1.2 %copy-start.8 = (f32[10]{0:T(128)S(1)}, f32[10]{0:T(128)}, u32[]{:S(2)}) copy-start(f32[10]{0:T(128)} %param.31) | copy-start | bytes 124
  2.7 5.0 %collective-permute-start.34 = (f32[64,128]{1,0:T(8,128)S(1)}, f32[64,128]{1,0:T(8,128)}, u32[]{:S(2)}, u32[]{:S(2)}) collective-permute-start(f32[64,128]{1,0:T(8,128)S(1)} %get-tuple-element.190), channel_id=1, source_target_pairs={{1,2},{2,1},{5,6},{6,5},{9,10},{10,9},{13,14},{14,13},{17,18},{18,... | collective-permute-start | bytes 98312 | tf_op jit(solution)/shard_map/cond/branch_1_fun/cond/branch_7_fun/ppermute | solution.py:644
  5.7 2.0 %collective-permute-start.35 = (f32[64,128]{1,0:T(8,128)S(1)}, f32[64,128]{1,0:T(8,128)}, u32[]{:S(2)}, u32[]{:S(2)}) collective-permute-start(f32[64,128]{1,0:T(8,128)S(1)} %get-tuple-element.191), channel_id=1, source_target_pairs={{0,1},{1,0},{2,3},{3,2},{4,5},{5,4},{6,7},{7,6},{8,9},{9,8},{10,11... | collective-permute-start | bytes 98312 | tf_op jit(solution)/shard_map/cond/branch_1_fun/cond/branch_7_fun/ppermute | solution.py:645
  8.8 15.5 %collective-permute-start.37 = (f32[144,128]{1,0:T(8,128)S(1)}, f32[144,128]{1,0:T(8,128)S(1)}, u32[]{:S(2)}, u32[]{:S(2)}) collective-permute-start(f32[144,128]{1,0:T(8,128)S(1)} %get-tuple-element.215), channel_id=1, source_target_pairs={{0,28},{4,8},{8,4},{12,16},{16,12},{20,24},{24,20},{28,0},{1,29},{... | collective-permute-start | bytes 221192 | tf_op jit(solution)/shard_map/cond/branch_1_fun/ppermute | solution.py:633
  13.9 10.4 %collective-permute-start.38 = (f32[144,128]{1,0:T(8,128)S(1)}, f32[144,128]{1,0:T(8,128)S(1)}, u32[]{:S(2)}, u32[]{:S(2)}) collective-permute-start(f32[144,128]{1,0:T(8,128)S(1)} %get-tuple-element.216), channel_id=1, source_target_pairs={{0,4},{4,0},{8,12},{12,8},{16,20},{20,16},{24,28},{28,24},{1,5},{5... | collective-permute-start | bytes 221192 | tf_op jit(solution)/shard_map/cond/branch_1_fun/ppermute | solution.py:632
  13.9 6.6 %collective-permute-start.36 = (f32[64,128]{1,0:T(8,128)S(1)}, f32[64,128]{1,0:T(8,128)S(1)}, u32[]{:S(2)}, u32[]{:S(2)}) collective-permute-start(f32[64,128]{1,0:T(8,128)S(1)} %get-tuple-element.214), channel_id=1, source_target_pairs={{0,4},{4,8},{8,12},{12,16},{16,20},{20,24},{24,28},{28,0},{1,5},{5... | collective-permute-start | bytes 98312 | tf_op jit(solution)/shard_map/cond/branch_1_fun/ppermute | solution.py:701
  21.7 9.6 %all-to-all-start.1 = ((f32[32,1,128]{2,1,0:T(1,128)}), f32[32,1,128]{2,1,0:T(1,128)S(1)}, u32[]{:S(2)}, u32[]{:S(2)}) async-start(f32[32,1,128]{2,1,0:T(1,128)} %bitcast.5), calls=%async_computation.1 | async-start | bytes 32768 | tf_op jit(solution)/shard_map/cond/branch_1_fun/all_to_all | solution.py:707

commit v12 on v10

--- a/solution.py
+++ b/solution.py
@@ -508,30 +508,31 @@
     hinge = lax.rem(counterpart[0] + 1 + cols * lon, width)
     block = lax.rem((hinge + cols // 2) // cols, lons)
 
-    def exchange(shift, first, second):
-        partner = [(shift - 1 - i) % lons for i in range(lons)]
+    deep = 4 * levels
+
+    def exchange(block, first, mine):
+        partner = [(block - 1 - i) % lons for i in range(lons)]
         partner = [i + lons // 2 if i == p else p for i, p in enumerate(partner)]
         pairs_fold = [(flat(p, lats - 1), flat(i, lats - 1)) for i, p in enumerate(partner)]
-        second = lax.ppermute(second, axes, pairs_inner + pairs_fold)
-        return second, lax.ppermute(first, axes, pairs_first)
-
-    mine = second
-    second, first = lax.switch(block, [functools.partial(exchange, s) for s in range(lons)], first, second)
-
-    deep = 4 * levels
-    ext, to_far, to_near, state_far, state_near, facing_rows, north_rows, south_rows = call(
-        functools.partial(turn_kernel, lons),
-        [
-            (FIELDS, tall, cols),
-            *[(rows // 2, cols)] * 2,
-            *[(rows, cols)] * 2,
-            (high - deep, cols),
-            *[(deep, cols)] * 2,
-        ],
-        FIELDS * tall * cols,
-        4 * 4 * FIELDS * tall * cols,
-        "row_halos",
-    )(meta, facing, mine, sums, *flat_state, second, first, east_columns, west_columns)
+        second = lax.ppermute(mine, axes, pairs_inner + pairs_fold)
+        first = lax.ppermute(first, axes, pairs_first)
+        return call(
+            functools.partial(turn_kernel, lons),
+            [
+                (FIELDS, tall, cols),
+                *[(rows // 2, cols)] * 2,
+                *[(rows, cols)] * 2,
+                (high - deep, cols),
+                *[(deep, cols)] * 2,
+            ],
+            FIELDS * tall * cols,
+            4 * 4 * FIELDS * tall * cols,
+            "row_halos",
+        )(meta, facing, mine, sums, *flat_state, second, first, east_columns, west_columns)
+
+    ext, to_far, to_near, state_far, state_near, facing_rows, north_rows, south_rows = lax.switch(
+        block, [functools.partial(exchange, s) for s in range(lons)], first, second
+    )
 
     near = lambda cells: lax.ppermute(cells, "lon", [(i, i ^ 1) for i in range(lons)])
     far = lambda cells: lax.ppermute(cells, "lon", [(i, (i + 1 if i % 2 else i - 1) % lons) for i in range(lons)])

time: 30.6 us -> 29.6 us (0.967)
  Pallas kernels: 7.76 us -> 7 us
    pallas_call x7, Pallas kernels: 7.76 us -> 7 us  [run(): pl.pallas_call(kernel, out_shape=[jax.ShapeDtypeStruct(shape, types) for...]
where the time goes in v12:
time: 29.6 us; the launch traced here: 29.4 us
  starting transfers between devices  13.7 us (46%)
  Pallas kernels  7 us (24%)
  waiting for transfers between devices  6.59 us (22%)
  local copies, waits for them, and re-layouts  1.26 us (4%)
  between operations  0.82 us (3%)
    ppermute x2, starting transfers between devices, body(): lax.ppermute(cells, 'lon', [(i, (i + 1 if i % 2 else i - 1) % lons) for i...  7.03 us
    pallas_call x7, Pallas kernels, run(): pl.pallas_call(kernel, out_shape=[jax.ShapeDtypeStruct(shape, types) for...  7 us
    all_to_all x1, starting transfers between devices, body(): shares = lax.all_to_all(moments, axes, 0, 0, tiled=True)  3.45 us
    all_to_all x1, waiting for transfers between devices, body(): shares = lax.all_to_all(moments, axes, 0, 0, tiled=True)  3.29 us
    ppermute x1, starting transfers between devices, exchange(): second = lax.ppermute(mine, axes, pairs_inner + pairs_fold)  2.56 us
    ppermute x1, waiting for transfers between devices, exchange(): second = lax.ppermute(mine, axes, pairs_inner + pairs_fold)  1.89 us
    ppermute x2, waiting for transfers between devices, body(): lax.ppermute(cells, 'lon', [(i, i ^ 1) for i in range(lons)])  1.4 us
    unnamed x18, local copies, waits for them, and re-layouts  1.17 us
  transfers between devices with their start and end apart: 7, of which 3 were waited for; matrix products, arithmetic and copies ran while one was open for 0% of the time, Pallas kernels for 18%

profile of v12, /device:TPU:0, one launch (start us, length us, event | category | flops | bytes accessed | tf_op | source)
XLA Modules:
  0.0 29.4 jit_solution(12493632515567611727)
XLA Ops:
  0.6 0.1 stack.31
  0.7 0.0 copy-start.3
  0.7 0.0 copy-start.5
  0.8 0.0 copy-start.6
  0.8 0.0 copy-start.7
  0.8 0.1 place.1.meta
  0.9 0.8 %copy-done = f32[10,64,128]{2,1,0:T(8,128)S(1)} copy-done((f32[10,64,128]{2,1,0:T(8,128)S(1)}, f32[10,64,128]{2,1,0:T(8,128)}, u32[]{:S(2)}) %copy-start) | copy-done | bytes 327704
  1.7 0.1 copy-done.1
  1.8 0.1 copy-done.2
  1.9 0.1 copy-done.3
  2.0 0.0 copy-done.4
  2.0 0.5 %level_sums.1 = (f32[3,64,128]{2,1,0:T(8,128)S(1)}, f32[64,128]{1,0:T(8,128)S(1)}, f32[64,128]{1,0:T(8,128)S(1)}, f32[64,128]{1,0:T(8,128)S(1)}, f32[64,128]{1,0:T(8,128)S(1)}) custom-call(s32[8,128]{1,0:T(8,128)S(1)} %place.1.meta, f32[1,10]{1,0:T(1,128)S(1)} %bitcast.15, s32[1,128]{1,0:T(1,128)S(1)} %bitcast.18, f32[10,64,128]{2,1,0:T(8,128)S(1)} %copy-done, ...), custom_call_target="tpu_custom_call" | custom-call | flops 983040 | bytes 1310720 | tf_op jit(solution)/shard_map/level_sums/pallas_call | solution.py:446
  2.6 5.2 %conditional.1 = ((f32[6,80,128]{2,1,0:T(8,128)S(1)}, f32[32,128]{1,0:T(8,128)S(1)}, f32[32,128]{1,0:T(8,128)S(1)}, f32[64,128]{1,0:T(8,128)S(1)}, f32[64,128]{1...) conditional(s32[]{:T(128)} %clamp.3, ...), branch_computations={%region_0.1_spmd, %region_1.2_spmd, %region_2.3_spmd, %region_3.4_... | conditional | flops 61440 | bytes 1245272 | solution.py:533
  2.7 0.5 %collective-permute-start.11 = (f32[64,128]{1,0:T(8,128)S(1)}, f32[64,128]{1,0:T(8,128)S(1)}, u32[]{:S(2)}, u32[]{:S(2)}) collective-permute-start(f32[64,128]{1,0:T(8,128)S(1)} %get-tuple-element.217), channel_id=1, source_target_pairs={{0,1},{1,0},{2,3},{3,2},{4,5},{5,4},{6,7},{7,6},{8,9},{9,8},{10,11... | collective-permute-start | bytes 98312 | tf_op jit(solution)/shard_map/cond/branch_5_fun/ppermute | solution.py:518
  3.2 2.6 %collective-permute-start.10 = (f32[64,128]{1,0:T(8,128)S(1)}, f32[64,128]{1,0:T(8,128)S(1)}, u32[]{:S(2)}, u32[]{:S(2)}) collective-permute-start(f32[64,128]{1,0:T(8,128)S(1)} %get-tuple-element.212.mine), channel_id=1, source_target_pairs={{1,2},{2,1},{5,6},{6,5},{9,10},{10,9},{13,14},{14,13},{17,18},{18,... | collective-permute-start | bytes 98312 | tf_op jit(solution)/shard_map/cond/branch_5_fun/ppermute | solution.py:517
  5.8 0.0 collective-permute-done.11.first
  5.8 1.9 %collective-permute-done.10.second = f32[64,128]{1,0:T(8,128)S(1)} collective-permute-done((f32[64,128]{1,0:T(8,128)S(1)}, f32[64,128]{1,0:T(8,128)S(1)}, u32[]{:S(2)}, u32[]{:S(2)}) %collective-permute-start.10) | collective-permute-done | bytes 32800 | tf_op jit(solution)/shard_map/cond/branch_5_fun/ppermute | solution.py:517
  7.7 0.2 row_halos.13
  7.9 5.1 %collective-permute-start.18 = (f32[32,128]{1,0:T(8,128)S(1)}, f32[32,128]{1,0:T(8,128)S(1)}, u32[]{:S(2)}, u32[]{:S(2)}) collective-permute-start(f32[32,128]{1,0:T(8,128)S(1)} %get-tuple-element.283), channel_id=1, source_target_pairs={{0,28},{4,8},{8,4},{12,16},{16,12},{20,24},{24,20},{28,0},{1,29},{... | collective-permute-start | bytes 49160 | tf_op jit(solution)/shard_map/ppermute | solution.py:538
  13.0 0.0 collective-permute-start.19
  13.0 1.9 %collective-permute-start.16 = (f32[64,128]{1,0:T(8,128)S(1)}, f32[64,128]{1,0:T(8,128)S(1)}, u32[]{:S(2)}, u32[]{:S(2)}) collective-permute-start(f32[64,128]{1,0:T(8,128)S(1)} %get-tuple-element.275), channel_id=1, source_target_pairs={{0,28},{4,8},{8,4},{12,16},{16,12},{20,24},{24,20},{28,0},{1,29},{... | collective-permute-start | bytes 98312 | tf_op jit(solution)/shard_map/ppermute | solution.py:538
  14.9 0.1 collective-permute-start.17
  15.0 0.3 %basis_shift.1.shift = f32[8,128]{1,0:T(8,128)S(1)} custom-call(f32[6,80,128]{2,1,0:T(8,128)S(1)} %get-tuple-element.281.ext), custom_call_target="tpu_custom_call" | custom-call | flops 491520 | bytes 196608 | tf_op jit(solution)/shard_map/basis_shift/pallas_call | solution.py:446
  15.4 0.0 collective-permute-done.18.from_far
  15.4 1.4 %collective-permute-done.19.from_near = f32[32,128]{1,0:T(8,128)S(1)} collective-permute-done((f32[32,128]{1,0:T(8,128)S(1)}, f32[32,128]{1,0:T(8,128)S(1)}, u32[]{:S(2)}, u32[]{:S(2)}) %collective-permute-start.19) | collective-permute-done | bytes 16416 | tf_op jit(solution)/shard_map/ppermute | solution.py:537
  16.8 1.3 %krylov.1 = (f32[3,64,128]{2,1,0:T(8,128)S(1)}, f32[32,128]{1,0:T(8,128)}) custom-call(s32[8,128]{1,0:T(8,128)S(1)} %place.1.meta, s32[1,128]{1,0:T(1,128)S(1)} %bitcast.28, f32[8,128]{1,0:T(8,128)S(1)} %basis_shift.1.shift, f32[6,80,128]{2,1,0:T(8,128)S(1)} %get-tuple-element.281.ext, f32[24,128]{1,0:T(8,128)S(1)} %get-tuple-element.282.facing_rows, ...), custom_call_target="tpu_custom_call" | custom-call | flops 2048000 | bytes 491520 | tf_op jit(solution)/shard_map/krylov/pallas_call | solution.py:446
  18.0 3.4 %all-to-all-start = ((f32[32,1,128]{2,1,0:T(1,128)}), f32[32,1,128]{2,1,0:T(1,128)S(1)}, u32[]{:S(2)}, u32[]{:S(2)}) async-start(f32[32,1,128]{2,1,0:T(1,128)} %bitcast.10), calls=%async_computation | async-start | bytes 32768 | tf_op jit(solution)/shard_map/all_to_all | solution.py:569
  21.5 0.0 collective-permute-done.16.from_far
  21.5 0.0 collective-permute-done.17.from_near
  21.5 3.8 %levels_step.1 = (f32[10,64,128]{2,1,0:T(8,128)}, f32[10,64,128]{2,1,0:T(8,128)}, f32[10,64,128]{2,1,0:T(8,128)}, f32[10,64,128]{2,1,0:T(8,128)}) custom-call(s32[8,128]{1,0:T(8,128)S(1)} %place.1.meta, f32[1,10]{1,0:T(1,128)S(1)} %bitcast.16, s32[1,128]{1,0:T(1,128)S(1)} %bitcast.29, f32[10,64,128]{2,1,0:T(8,128)S(1)} %copy-done, ...), custom_call_target="tpu_custom_call" | custom-call | flops 9830400 | bytes 2621440 | tf_op jit(solution)/shard_map/levels_step/pallas_call | solution.py:446
  25.3 3.3 %all-to-all-done = f32[32,1,128]{2,1,0:T(1,128)S(1)} async-done(((f32[32,1,128]{2,1,0:T(1,128)}), f32[32,1,128]{2,1,0:T(1,128)S(1)}, u32[]{:S(2)}, u32[]{:S(2)}) %all-to-all-start) | async-done | bytes 16416 | tf_op jit(solution)/shard_map/all_to_all | solution.py:569
  28.5 0.9 %surface.1 = f32[64,128]{1,0:T(8,128)} custom-call(f32[32,128]{1,0:T(8,128)S(1)} %bitcast.14, f32[8,128]{1,0:T(8,128)S(1)} %basis_shift.1.shift, f32[3,64,128]{2,1,0:T(8,128)S(1)} %get-tuple-element.286.base), custom_call_target="tpu_custom_call" | custom-call | flops 49152 | bytes 131072 | tf_op jit(solution)/shard_map/surface/pallas_call | solution.py:446
  (9 shorter events, 0.0 us)
Async XLA Ops:
  0.7 1.0 %copy-start = (f32[10,64,128]{2,1,0:T(8,128)S(1)}, f32[10,64,128]{2,1,0:T(8,128)}, u32[]{:S(2)}) copy-start(f32[10,64,128]{2,1,0:T(8,128)} %heat.3) | copy-start | bytes 983044
  0.7 1.1 %copy-start.1 = (f32[10,64,128]{2,1,0:T(8,128)S(1)}, f32[10,64,128]{2,1,0:T(8,128)}, u32[]{:S(2)}) copy-start(f32[10,64,128]{2,1,0:T(8,128)} %salt.3) | copy-start | bytes 983044
  0.7 1.2 %copy-start.2 = (f32[10,64,128]{2,1,0:T(8,128)S(1)}, f32[10,64,128]{2,1,0:T(8,128)}, u32[]{:S(2)}) copy-start(f32[10,64,128]{2,1,0:T(8,128)} %zonal.3) | copy-start | bytes 983044
  0.7 1.3 %copy-start.3 = (f32[10,64,128]{2,1,0:T(8,128)S(1)}, f32[10,64,128]{2,1,0:T(8,128)}, u32[]{:S(2)}) copy-start(f32[10,64,128]{2,1,0:T(8,128)} %merid.3) | copy-start | bytes 983044
  0.7 1.3 %copy-start.5 = (s32[64,128]{1,0:T(8,128)S(1)}, s32[64,128]{1,0:T(8,128)}, u32[]{:S(2)}) copy-start(s32[64,128]{1,0:T(8,128)} %water.3) | copy-start | bytes 98308
  0.8 1.2 %copy-start.6 = (f32[64,128]{1,0:T(8,128)S(1)}, f32[64,128]{1,0:T(8,128)}, u32[]{:S(2)}) copy-start(f32[64,128]{1,0:T(8,128)} %weights.1) | copy-start | bytes 98308
  0.8 1.2 %copy-start.7 = (f32[64,128]{1,0:T(8,128)S(1)}, f32[64,128]{1,0:T(8,128)}, u32[]{:S(2)}) copy-start(f32[64,128]{1,0:T(8,128)} %anomaly.1) | copy-start | bytes 98308
  0.9 1.2 %copy-start.4 = (f32[10]{0:T(128)S(1)}, f32[10]{0:T(128)}, u32[]{:S(2)}) copy-start(f32[10]{0:T(128)} %param.21) | copy-start | bytes 124
  0.9 1.2 %copy-start.8 = (s32[128]{0:T(128)S(1)}, s32[128]{0:T(128)}, u32[]{:S(2)}) copy-start(s32[128]{0:T(128)} %param.23) | copy-start | bytes 1540
  2.7 3.1 %collective-permute-start.11 = (f32[64,128]{1,0:T(8,128)S(1)}, f32[64,128]{1,0:T(8,128)S(1)}, u32[]{:S(2)}, u32[]{:S(2)}) collective-permute-start(f32[64,128]{1,0:T(8,128)S(1)} %get-tuple-element.217), channel_id=1, source_target_pairs={{0,1},{1,0},{2,3},{3,2},{4,5},{5,4},{6,7},{7,6},{8,9},{9,8},{10,11... | collective-permute-start | bytes 98312 | tf_op jit(solution)/shard_map/cond/branch_5_fun/ppermute | solution.py:518
  3.2 4.5 %collective-permute-start.10 = (f32[64,128]{1,0:T(8,128)S(1)}, f32[64,128]{1,0:T(8,128)S(1)}, u32[]{:S(2)}, u32[]{:S(2)}) collective-permute-start(f32[64,128]{1,0:T(8,128)S(1)} %get-tuple-element.212.mine), channel_id=1, source_target_pairs={{1,2},{2,1},{5,6},{6,5},{9,10},{10,9},{13,14},{14,13},{17,18},{18,... | collective-permute-start | bytes 98312 | tf_op jit(solution)/shard_map/cond/branch_5_fun/ppermute | solution.py:517
  7.9 7.5 %collective-permute-start.18 = (f32[32,128]{1,0:T(8,128)S(1)}, f32[32,128]{1,0:T(8,128)S(1)}, u32[]{:S(2)}, u32[]{:S(2)}) collective-permute-start(f32[32,128]{1,0:T(8,128)S(1)} %get-tuple-element.283), channel_id=1, source_target_pairs={{0,28},{4,8},{8,4},{12,16},{16,12},{20,24},{24,20},{28,0},{1,29},{... | collective-permute-start | bytes 49160 | tf_op jit(solution)/shard_map/ppermute | solution.py:538
  13.0 3.7 %collective-permute-start.19 = (f32[32,128]{1,0:T(8,128)S(1)}, f32[32,128]{1,0:T(8,128)S(1)}, u32[]{:S(2)}, u32[]{:S(2)}) collective-permute-start(f32[32,128]{1,0:T(8,128)S(1)} %get-tuple-element.284), channel_id=1, source_target_pairs={{0,4},{4,0},{8,12},{12,8},{16,20},{20,16},{24,28},{28,24},{1,5},{5... | collective-permute-start | bytes 49160 | tf_op jit(solution)/shard_map/ppermute | solution.py:537
  13.0 8.4 %collective-permute-start.16 = (f32[64,128]{1,0:T(8,128)S(1)}, f32[64,128]{1,0:T(8,128)S(1)}, u32[]{:S(2)}, u32[]{:S(2)}) collective-permute-start(f32[64,128]{1,0:T(8,128)S(1)} %get-tuple-element.275), channel_id=1, source_target_pairs={{0,28},{4,8},{8,4},{12,16},{16,12},{20,24},{24,20},{28,0},{1,29},{... | collective-permute-start | bytes 98312 | tf_op jit(solution)/shard_map/ppermute | solution.py:538
  14.9 6.5 %collective-permute-start.17 = (f32[64,128]{1,0:T(8,128)S(1)}, f32[64,128]{1,0:T(8,128)S(1)}, u32[]{:S(2)}, u32[]{:S(2)}) collective-permute-start(f32[64,128]{1,0:T(8,128)S(1)} %get-tuple-element.276), channel_id=1, source_target_pairs={{0,4},{4,0},{8,12},{12,8},{16,20},{20,16},{24,28},{28,24},{1,5},{5... | collective-permute-start | bytes 98312 | tf_op jit(solution)/shard_map/ppermute | solution.py:537
  18.0 10.5 %all-to-all-start = ((f32[32,1,128]{2,1,0:T(1,128)}), f32[32,1,128]{2,1,0:T(1,128)S(1)}, u32[]{:S(2)}, u32[]{:S(2)}) async-start(f32[32,1,128]{2,1,0:T(1,128)} %bitcast.10), calls=%async_computation | async-start | bytes 32768 | tf_op jit(solution)/shard_map/all_to_all | solution.py:569

commit v13 on v12

--- a/solution.py
+++ b/solution.py
@@ -50,7 +50,7 @@
 
 def pack_kernel(
     meta, spans, facing, heat, salt, zonal, merid, water, weights, anomaly,
-    sums, first, second, east_columns, west_columns,
+    sums, first, second, kept, east_columns, west_columns,
     top, bottom, back,
 ):
     levels, rows, cols = heat.shape
@@ -96,7 +96,9 @@
             packet[used:, :] = jnp.zeros((high - used, cols), jnp.float32)
     odd, last, _, _ = flags(meta)
     first[...] = jnp.where(odd, bottom[...], top[...])
-    second[...] = jnp.where(last, back[...], jnp.where(odd, top[...], bottom[...]))
+    packet = jnp.where(last, back[...], jnp.where(odd, top[...], bottom[...]))
+    second[...] = packet
+    kept[...] = packet
 
 
 def turn_kernel(
@@ -486,9 +488,9 @@
     state = (warmth_deviation, saltiness_deviation, easterly_speed, poleward_speed)
     flat_state = (water_indicator, elevation_weights, elevation_anomaly)
     cells = levels * rows * cols
-    sums, first, second, east_columns, west_columns = call(
+    sums, first, second, kept, east_columns, west_columns = call(
         pack_kernel,
-        [(3, rows, cols), (high, cols), (high, cols), (rows, cols), (rows, cols)],
+        [(3, rows, cols), *[(high, cols)] * 3, (rows, cols), (rows, cols)],
         12 * cells,
         16 * cells,
         "level_sums",
@@ -510,11 +512,11 @@
 
     deep = 4 * levels
 
-    def exchange(block, first, mine):
+    def exchange(block, first, second):
         partner = [(block - 1 - i) % lons for i in range(lons)]
         partner = [i + lons // 2 if i == p else p for i, p in enumerate(partner)]
         pairs_fold = [(flat(p, lats - 1), flat(i, lats - 1)) for i, p in enumerate(partner)]
-        second = lax.ppermute(mine, axes, pairs_inner + pairs_fold)
+        second = lax.ppermute(second, axes, pairs_inner + pairs_fold)
         first = lax.ppermute(first, axes, pairs_first)
         return call(
             functools.partial(turn_kernel, lons),
@@ -528,7 +530,7 @@
             FIELDS * tall * cols,
             4 * 4 * FIELDS * tall * cols,
             "row_halos",
-        )(meta, facing, mine, sums, *flat_state, second, first, east_columns, west_columns)
+        )(meta, facing, kept, sums, *flat_state, second, first, east_columns, west_columns)
 
     ext, to_far, to_near, state_far, state_near, facing_rows, north_rows, south_rows = lax.switch(
         block, [functools.partial(exchange, s) for s in range(lons)], first, second

time: 29.6 us -> 29.5 us (level)
    ppermute x1, starting transfers between devices: 2.56 us -> 3 us  [exchange(): second = lax.ppermute(second, axes, pairs_inner + pairs_fold)]
    ppermute x1, starting transfers between devices: 0.52 us -> 0.14 us  [exchange(): first = lax.ppermute(first, axes, pairs_first)]
where the time goes in v13:
time: 29.5 us; the launch traced here: 29.3 us
  starting transfers between devices  13.7 us (46%)
  Pallas kernels  7 us (24%)
  waiting for transfers between devices  6.45 us (22%)
  local copies, waits for them, and re-layouts  1.26 us (4%)
  between operations  0.82 us (3%)
    ppermute x2, starting transfers between devices, body(): lax.ppermute(cells, 'lon', [(i, (i + 1 if i % 2 else i - 1) % lons) for i...  7.06 us
    pallas_call x7, Pallas kernels, run(): pl.pallas_call(kernel, out_shape=[jax.ShapeDtypeStruct(shape, types) for...  7 us
    all_to_all x1, starting transfers between devices, body(): shares = lax.all_to_all(moments, axes, 0, 0, tiled=True)  3.42 us
    all_to_all x1, waiting for transfers between devices, body(): shares = lax.all_to_all(moments, axes, 0, 0, tiled=True)  3.29 us
    ppermute x1, starting transfers between devices, exchange(): second = lax.ppermute(second, axes, pairs_inner + pairs_fold)  3 us
    ppermute x1, waiting for transfers between devices, exchange(): second = lax.ppermute(second, axes, pairs_inner + pairs_fold)  1.75 us
    ppermute x2, waiting for transfers between devices, body(): lax.ppermute(cells, 'lon', [(i, i ^ 1) for i in range(lons)])  1.4 us
    unnamed x18, local copies, waits for them, and re-layouts  1.17 us
  transfers between devices with their start and end apart: 7, of which 3 were waited for; matrix products, arithmetic and copies ran while one was open for 0% of the time, Pallas kernels for 18%

profile of v13, /device:TPU:0, one launch (start us, length us, event | category | flops | bytes accessed | tf_op | source)
XLA Modules:
  0.0 29.3 jit_solution(5245588268309910992)
XLA Ops:
  0.6 0.1 stack.31
  0.7 0.0 copy-start.3
  0.7 0.0 copy-start.5
  0.8 0.0 copy-start.6
  0.8 0.0 copy-start.7
  0.8 0.1 place.1.meta
  0.9 0.8 %copy-done = f32[10,64,128]{2,1,0:T(8,128)S(1)} copy-done((f32[10,64,128]{2,1,0:T(8,128)S(1)}, f32[10,64,128]{2,1,0:T(8,128)}, u32[]{:S(2)}) %copy-start) | copy-done | bytes 327704
  1.7 0.1 copy-done.1
  1.8 0.1 copy-done.2
  1.9 0.1 copy-done.3
  2.0 0.0 copy-done.4
  2.0 0.5 %level_sums.1 = (f32[3,64,128]{2,1,0:T(8,128)S(1)}, f32[64,128]{1,0:T(8,128)S(1)}, f32[64,128]{1,0:T(8,128)S(1)}, f32[64,128]{1,0:T(8,128)S(1)}, f32[64,128]{1,0:T(8,128)S(1)}, /*index=5*/f32[64,128]{1,0:T(8,128)S(1)}) custom-call(s32[8,128]{1,0:T(8,128)S(1)} %place.1.meta, f32[1,10]{1,0:T(1,128)S(1)} %bitcast.15, s32[1,128]{1,0:T(1,128)S(1)} %bitcast.18, ...), custom_call_target="tpu_custom_call" | custom-call | flops 983040 | bytes 1310720 | tf_op jit(solution)/shard_map/level_sums/pallas_call | solution.py:448
  2.6 5.2 %conditional.1 = ((f32[6,80,128]{2,1,0:T(8,128)S(1)}, f32[32,128]{1,0:T(8,128)S(1)}, f32[32,128]{1,0:T(8,128)S(1)}, f32[64,128]{1,0:T(8,128)S(1)}, f32[64,128]{1...) conditional(s32[]{:T(128)} %clamp.3, ...), branch_computations={%region_0.1_spmd, %region_1.2_spmd, %region_2.3_spmd, %region_3.4_... | conditional | flops 61440 | bytes 1245272 | solution.py:535
  2.7 3.0 %collective-permute-start.6 = (f32[64,128]{1,0:T(8,128)S(1)}, f32[64,128]{1,0:T(8,128)S(1)}, u32[]{:S(2)}, u32[]{:S(2)}) collective-permute-start(f32[64,128]{1,0:T(8,128)S(1)} %get-tuple-element.216), channel_id=1, source_target_pairs={{1,2},{2,1},{5,6},{6,5},{9,10},{10,9},{13,14},{14,13},{17,18},{18,... | collective-permute-start | bytes 98312 | tf_op jit(solution)/shard_map/cond/branch_3_fun/ppermute | solution.py:519
  5.7 0.1 collective-permute-start.7
  5.8 1.8 %collective-permute-done.6.second = f32[64,128]{1,0:T(8,128)S(1)} collective-permute-done((f32[64,128]{1,0:T(8,128)S(1)}, f32[64,128]{1,0:T(8,128)S(1)}, u32[]{:S(2)}, u32[]{:S(2)}) %collective-permute-start.6) | collective-permute-done | bytes 32800 | tf_op jit(solution)/shard_map/cond/branch_3_fun/ppermute | solution.py:519
  7.6 0.0 collective-permute-done.7.first
  7.6 0.2 row_halos.11
  7.8 5.1 %collective-permute-start.18 = (f32[32,128]{1,0:T(8,128)S(1)}, f32[32,128]{1,0:T(8,128)S(1)}, u32[]{:S(2)}, u32[]{:S(2)}) collective-permute-start(f32[32,128]{1,0:T(8,128)S(1)} %get-tuple-element.309), channel_id=1, source_target_pairs={{0,28},{4,8},{8,4},{12,16},{16,12},{20,24},{24,20},{28,0},{1,29},{... | collective-permute-start | bytes 49160 | tf_op jit(solution)/shard_map/ppermute | solution.py:540
  12.9 0.0 collective-permute-start.19
  12.9 1.9 %collective-permute-start.16 = (f32[64,128]{1,0:T(8,128)S(1)}, f32[64,128]{1,0:T(8,128)S(1)}, u32[]{:S(2)}, u32[]{:S(2)}) collective-permute-start(f32[64,128]{1,0:T(8,128)S(1)} %get-tuple-element.301), channel_id=1, source_target_pairs={{0,28},{4,8},{8,4},{12,16},{16,12},{20,24},{24,20},{28,0},{1,29},{... | collective-permute-start | bytes 98312 | tf_op jit(solution)/shard_map/ppermute | solution.py:540
  14.9 0.1 collective-permute-start.17
  15.0 0.3 %basis_shift.1.shift = f32[8,128]{1,0:T(8,128)S(1)} custom-call(f32[6,80,128]{2,1,0:T(8,128)S(1)} %get-tuple-element.307.ext), custom_call_target="tpu_custom_call" | custom-call | flops 491520 | bytes 196608 | tf_op jit(solution)/shard_map/basis_shift/pallas_call | solution.py:448
  15.3 0.0 collective-permute-done.18.from_far
  15.3 1.4 %collective-permute-done.19.from_near = f32[32,128]{1,0:T(8,128)S(1)} collective-permute-done((f32[32,128]{1,0:T(8,128)S(1)}, f32[32,128]{1,0:T(8,128)S(1)}, u32[]{:S(2)}, u32[]{:S(2)}) %collective-permute-start.19) | collective-permute-done | bytes 16416 | tf_op jit(solution)/shard_map/ppermute | solution.py:539
  16.7 1.3 %krylov.1 = (f32[3,64,128]{2,1,0:T(8,128)S(1)}, f32[32,128]{1,0:T(8,128)}) custom-call(s32[8,128]{1,0:T(8,128)S(1)} %place.1.meta, s32[1,128]{1,0:T(1,128)S(1)} %bitcast.28, f32[8,128]{1,0:T(8,128)S(1)} %basis_shift.1.shift, f32[6,80,128]{2,1,0:T(8,128)S(1)} %get-tuple-element.307.ext, f32[24,128]{1,0:T(8,128)S(1)} %get-tuple-element.308.facing_rows, ...), custom_call_target="tpu_custom_call" | custom-call | flops 2048000 | bytes 491520 | tf_op jit(solution)/shard_map/krylov/pallas_call | solution.py:448
  18.0 3.4 %all-to-all-start = ((f32[32,1,128]{2,1,0:T(1,128)}), f32[32,1,128]{2,1,0:T(1,128)S(1)}, u32[]{:S(2)}, u32[]{:S(2)}) async-start(f32[32,1,128]{2,1,0:T(1,128)} %bitcast.10), calls=%async_computation | async-start | bytes 32768 | tf_op jit(solution)/shard_map/all_to_all | solution.py:571
  21.4 0.0 collective-permute-done.16.from_far
  21.4 0.0 collective-permute-done.17.from_near
  21.4 3.8 %levels_step.1 = (f32[10,64,128]{2,1,0:T(8,128)}, f32[10,64,128]{2,1,0:T(8,128)}, f32[10,64,128]{2,1,0:T(8,128)}, f32[10,64,128]{2,1,0:T(8,128)}) custom-call(s32[8,128]{1,0:T(8,128)S(1)} %place.1.meta, f32[1,10]{1,0:T(1,128)S(1)} %bitcast.16, s32[1,128]{1,0:T(1,128)S(1)} %bitcast.29, f32[10,64,128]{2,1,0:T(8,128)S(1)} %copy-done, ...), custom_call_target="tpu_custom_call" | custom-call | flops 9830400 | bytes 2621440 | tf_op jit(solution)/shard_map/levels_step/pallas_call | solution.py:448
  25.2 3.3 %all-to-all-done = f32[32,1,128]{2,1,0:T(1,128)S(1)} async-done(((f32[32,1,128]{2,1,0:T(1,128)}), f32[32,1,128]{2,1,0:T(1,128)S(1)}, u32[]{:S(2)}, u32[]{:S(2)}) %all-to-all-start) | async-done | bytes 16416 | tf_op jit(solution)/shard_map/all_to_all | solution.py:571
  28.5 0.9 %surface.1 = f32[64,128]{1,0:T(8,128)} custom-call(f32[32,128]{1,0:T(8,128)S(1)} %bitcast.14, f32[8,128]{1,0:T(8,128)S(1)} %basis_shift.1.shift, f32[3,64,128]{2,1,0:T(8,128)S(1)} %get-tuple-element.312.base), custom_call_target="tpu_custom_call" | custom-call | flops 49152 | bytes 131072 | tf_op jit(solution)/shard_map/surface/pallas_call | solution.py:448
  (9 shorter events, 0.0 us)
Async XLA Ops:
  0.7 1.0 %copy-start = (f32[10,64,128]{2,1,0:T(8,128)S(1)}, f32[10,64,128]{2,1,0:T(8,128)}, u32[]{:S(2)}) copy-start(f32[10,64,128]{2,1,0:T(8,128)} %heat.3) | copy-start | bytes 983044
  0.7 1.1 %copy-start.1 = (f32[10,64,128]{2,1,0:T(8,128)S(1)}, f32[10,64,128]{2,1,0:T(8,128)}, u32[]{:S(2)}) copy-start(f32[10,64,128]{2,1,0:T(8,128)} %salt.3) | copy-start | bytes 983044
  0.7 1.2 %copy-start.2 = (f32[10,64,128]{2,1,0:T(8,128)S(1)}, f32[10,64,128]{2,1,0:T(8,128)}, u32[]{:S(2)}) copy-start(f32[10,64,128]{2,1,0:T(8,128)} %zonal.3) | copy-start | bytes 983044
  0.7 1.3 %copy-start.3 = (f32[10,64,128]{2,1,0:T(8,128)S(1)}, f32[10,64,128]{2,1,0:T(8,128)}, u32[]{:S(2)}) copy-start(f32[10,64,128]{2,1,0:T(8,128)} %merid.3) | copy-start | bytes 983044
  0.7 1.3 %copy-start.5 = (s32[64,128]{1,0:T(8,128)S(1)}, s32[64,128]{1,0:T(8,128)}, u32[]{:S(2)}) copy-start(s32[64,128]{1,0:T(8,128)} %water.3) | copy-start | bytes 98308
  0.8 1.2 %copy-start.6 = (f32[64,128]{1,0:T(8,128)S(1)}, f32[64,128]{1,0:T(8,128)}, u32[]{:S(2)}) copy-start(f32[64,128]{1,0:T(8,128)} %weights.1) | copy-start | bytes 98308
  0.8 1.2 %copy-start.7 = (f32[64,128]{1,0:T(8,128)S(1)}, f32[64,128]{1,0:T(8,128)}, u32[]{:S(2)}) copy-start(f32[64,128]{1,0:T(8,128)} %anomaly.1) | copy-start | bytes 98308
  0.9 1.2 %copy-start.4 = (f32[10]{0:T(128)S(1)}, f32[10]{0:T(128)}, u32[]{:S(2)}) copy-start(f32[10]{0:T(128)} %param.21) | copy-start | bytes 124
  0.9 1.2 %copy-start.8 = (s32[128]{0:T(128)S(1)}, s32[128]{0:T(128)}, u32[]{:S(2)}) copy-start(s32[128]{0:T(128)} %param.23) | copy-start | bytes 1540
  2.7 4.9 %collective-permute-start.6 = (f32[64,128]{1,0:T(8,128)S(1)}, f32[64,128]{1,0:T(8,128)S(1)}, u32[]{:S(2)}, u32[]{:S(2)}) collective-permute-start(f32[64,128]{1,0:T(8,128)S(1)} %get-tuple-element.216), channel_id=1, source_target_pairs={{1,2},{2,1},{5,6},{6,5},{9,10},{10,9},{13,14},{14,13},{17,18},{18,... | collective-permute-start | bytes 98312 | tf_op jit(solution)/shard_map/cond/branch_3_fun/ppermute | solution.py:519
  5.7 1.9 %collective-permute-start.7 = (f32[64,128]{1,0:T(8,128)S(1)}, f32[64,128]{1,0:T(8,128)S(1)}, u32[]{:S(2)}, u32[]{:S(2)}) collective-permute-start(f32[64,128]{1,0:T(8,128)S(1)} %get-tuple-element.217), channel_id=1, source_target_pairs={{0,1},{1,0},{2,3},{3,2},{4,5},{5,4},{6,7},{7,6},{8,9},{9,8},{10,11... | collective-permute-start | bytes 98312 | tf_op jit(solution)/shard_map/cond/branch_3_fun/ppermute | solution.py:520
  7.8 7.5 %collective-permute-start.18 = (f32[32,128]{1,0:T(8,128)S(1)}, f32[32,128]{1,0:T(8,128)S(1)}, u32[]{:S(2)}, u32[]{:S(2)}) collective-permute-start(f32[32,128]{1,0:T(8,128)S(1)} %get-tuple-element.309), channel_id=1, source_target_pairs={{0,28},{4,8},{8,4},{12,16},{16,12},{20,24},{24,20},{28,0},{1,29},{... | collective-permute-start | bytes 49160 | tf_op jit(solution)/shard_map/ppermute | solution.py:540
  12.9 3.8 %collective-permute-start.19 = (f32[32,128]{1,0:T(8,128)S(1)}, f32[32,128]{1,0:T(8,128)S(1)}, u32[]{:S(2)}, u32[]{:S(2)}) collective-permute-start(f32[32,128]{1,0:T(8,128)S(1)} %get-tuple-element.310), channel_id=1, source_target_pairs={{0,4},{4,0},{8,12},{12,8},{16,20},{20,16},{24,28},{28,24},{1,5},{5... | collective-permute-start | bytes 49160 | tf_op jit(solution)/shard_map/ppermute | solution.py:539
  12.9 8.4 %collective-permute-start.16 = (f32[64,128]{1,0:T(8,128)S(1)}, f32[64,128]{1,0:T(8,128)S(1)}, u32[]{:S(2)}, u32[]{:S(2)}) collective-permute-start(f32[64,128]{1,0:T(8,128)S(1)} %get-tuple-element.301), channel_id=1, source_target_pairs={{0,28},{4,8},{8,4},{12,16},{16,12},{20,24},{24,20},{28,0},{1,29},{... | collective-permute-start | bytes 98312 | tf_op jit(solution)/shard_map/ppermute | solution.py:540
  14.9 6.5 %collective-permute-start.17 = (f32[64,128]{1,0:T(8,128)S(1)}, f32[64,128]{1,0:T(8,128)S(1)}, u32[]{:S(2)}, u32[]{:S(2)}) collective-permute-start(f32[64,128]{1,0:T(8,128)S(1)} %get-tuple-element.302), channel_id=1, source_target_pairs={{0,4},{4,0},{8,12},{12,8},{16,20},{20,16},{24,28},{28,24},{1,5},{5... | collective-permute-start | bytes 98312 | tf_op jit(solution)/shard_map/ppermute | solution.py:539
  18.0 10.5 %all-to-all-start = ((f32[32,1,128]{2,1,0:T(1,128)}), f32[32,1,128]{2,1,0:T(1,128)S(1)}, u32[]{:S(2)}, u32[]{:S(2)}) async-start(f32[32,1,128]{2,1,0:T(1,128)} %bitcast.10), calls=%async_computation | async-start | bytes 32768 | tf_op jit(solution)/shard_map/all_to_all | solution.py:571

commit v14 on v13

--- a/solution.py
+++ b/solution.py
@@ -568,7 +568,7 @@
         ],
     )(meta, spans, facing, *state, water_indicator, north_rows, south_rows, state_far, state_near)
 
-    shares = lax.all_to_all(moments, axes, 0, 0, tiled=True)
+    shares = lax.all_to_all(moments, ("lat", "lon"), 0, 0, tiled=True)
     (surface,) = call(surface_kernel, [(rows, cols)], 6 * rows * cols, 16 * rows * cols, "surface")(shares, shift, base)
     return (new_heat, new_salt, new_zonal, new_merid, surface)
 

time: 29.5 us -> 29.6 us (level)
  no operation moved by 1% of the time
where the time goes in v14:
time: 29.6 us; the launch traced here: 29.3 us
  starting transfers between devices  13.7 us (46%)
  Pallas kernels  7 us (24%)
  waiting for transfers between devices  6.41 us (22%)
  local copies, waits for them, and re-layouts  1.26 us (4%)
  between operations  0.82 us (3%)
    ppermute x2, starting transfers between devices, body(): lax.ppermute(cells, 'lon', [(i, (i + 1 if i % 2 else i - 1) % lons) for i...  7.06 us
    pallas_call x7, Pallas kernels, run(): pl.pallas_call(kernel, out_shape=[jax.ShapeDtypeStruct(shape, types) for...  7 us
    all_to_all x1, starting transfers between devices, body(): shares = lax.all_to_all(moments, ('lat', 'lon'), 0, 0, tiled=True)  3.42 us
    all_to_all x1, waiting for transfers between devices, body(): shares = lax.all_to_all(moments, ('lat', 'lon'), 0, 0, tiled=True)  3.25 us
    ppermute x1, starting transfers between devices, exchange(): second = lax.ppermute(second, axes, pairs_inner + pairs_fold)  3 us
    ppermute x1, waiting for transfers between devices, exchange(): second = lax.ppermute(second, axes, pairs_inner + pairs_fold)  1.75 us
    ppermute x2, waiting for transfers between devices, body(): lax.ppermute(cells, 'lon', [(i, i ^ 1) for i in range(lons)])  1.4 us
    unnamed x18, local copies, waits for them, and re-layouts  1.17 us
  transfers between devices with their start and end apart: 7, of which 3 were waited for; matrix products, arithmetic and copies ran while one was open for 0% of the time, Pallas kernels for 18%

profile of v14, /device:TPU:0, one launch (start us, length us, event | category | flops | bytes accessed | tf_op | source)
XLA Modules:
  0.0 29.3 jit_solution(12376574437139586015)
XLA Ops:
  0.6 0.1 stack.31
  0.7 0.0 copy-start.3
  0.7 0.0 copy-start.5
  0.8 0.0 copy-start.6
  0.8 0.0 copy-start.7
  0.8 0.1 place.1.meta
  0.9 0.8 %copy-done = f32[10,64,128]{2,1,0:T(8,128)S(1)} copy-done((f32[10,64,128]{2,1,0:T(8,128)S(1)}, f32[10,64,128]{2,1,0:T(8,128)}, u32[]{:S(2)}) %copy-start) | copy-done | bytes 327704
  1.7 0.1 copy-done.1
  1.8 0.1 copy-done.2
  1.9 0.1 copy-done.3
  2.0 0.0 copy-done.4
  2.0 0.5 %level_sums.1 = (f32[3,64,128]{2,1,0:T(8,128)S(1)}, f32[64,128]{1,0:T(8,128)S(1)}, f32[64,128]{1,0:T(8,128)S(1)}, f32[64,128]{1,0:T(8,128)S(1)}, f32[64,128]{1,0:T(8,128)S(1)}, /*index=5*/f32[64,128]{1,0:T(8,128)S(1)}) custom-call(s32[8,128]{1,0:T(8,128)S(1)} %place.1.meta, f32[1,10]{1,0:T(1,128)S(1)} %bitcast.15, s32[1,128]{1,0:T(1,128)S(1)} %bitcast.18, ...), custom_call_target="tpu_custom_call" | custom-call | flops 983040 | bytes 1310720 | tf_op jit(solution)/shard_map/level_sums/pallas_call | solution.py:448
  2.6 5.2 %conditional.1 = ((f32[6,80,128]{2,1,0:T(8,128)S(1)}, f32[32,128]{1,0:T(8,128)S(1)}, f32[32,128]{1,0:T(8,128)S(1)}, f32[64,128]{1,0:T(8,128)S(1)}, f32[64,128]{1...) conditional(s32[]{:T(128)} %clamp.3, ...), branch_computations={%region_0.1_spmd, %region_1.2_spmd, %region_2.3_spmd, %region_3.4_... | conditional | flops 61440 | bytes 1245272 | solution.py:535
  2.7 3.0 %collective-permute-start.6 = (f32[64,128]{1,0:T(8,128)S(1)}, f32[64,128]{1,0:T(8,128)S(1)}, u32[]{:S(2)}, u32[]{:S(2)}) collective-permute-start(f32[64,128]{1,0:T(8,128)S(1)} %get-tuple-element.216), channel_id=1, source_target_pairs={{1,2},{2,1},{5,6},{6,5},{9,10},{10,9},{13,14},{14,13},{17,18},{18,... | collective-permute-start | bytes 98312 | tf_op jit(solution)/shard_map/cond/branch_3_fun/ppermute | solution.py:519
  5.7 0.1 collective-permute-start.7
  5.8 1.8 %collective-permute-done.6.second = f32[64,128]{1,0:T(8,128)S(1)} collective-permute-done((f32[64,128]{1,0:T(8,128)S(1)}, f32[64,128]{1,0:T(8,128)S(1)}, u32[]{:S(2)}, u32[]{:S(2)}) %collective-permute-start.6) | collective-permute-done | bytes 32800 | tf_op jit(solution)/shard_map/cond/branch_3_fun/ppermute | solution.py:519
  7.6 0.0 collective-permute-done.7.first
  7.6 0.2 row_halos.11
  7.8 5.1 %collective-permute-start.18 = (f32[32,128]{1,0:T(8,128)S(1)}, f32[32,128]{1,0:T(8,128)S(1)}, u32[]{:S(2)}, u32[]{:S(2)}) collective-permute-start(f32[32,128]{1,0:T(8,128)S(1)} %get-tuple-element.309), channel_id=1, source_target_pairs={{0,28},{4,8},{8,4},{12,16},{16,12},{20,24},{24,20},{28,0},{1,29},{... | collective-permute-start | bytes 49160 | tf_op jit(solution)/shard_map/ppermute | solution.py:540
  12.9 0.0 collective-permute-start.19
  12.9 1.9 %collective-permute-start.16 = (f32[64,128]{1,0:T(8,128)S(1)}, f32[64,128]{1,0:T(8,128)S(1)}, u32[]{:S(2)}, u32[]{:S(2)}) collective-permute-start(f32[64,128]{1,0:T(8,128)S(1)} %get-tuple-element.301), channel_id=1, source_target_pairs={{0,28},{4,8},{8,4},{12,16},{16,12},{20,24},{24,20},{28,0},{1,29},{... | collective-permute-start | bytes 98312 | tf_op jit(solution)/shard_map/ppermute | solution.py:540
  14.9 0.1 collective-permute-start.17
  15.0 0.3 %basis_shift.1.shift = f32[8,128]{1,0:T(8,128)S(1)} custom-call(f32[6,80,128]{2,1,0:T(8,128)S(1)} %get-tuple-element.307.ext), custom_call_target="tpu_custom_call" | custom-call | flops 491520 | bytes 196608 | tf_op jit(solution)/shard_map/basis_shift/pallas_call | solution.py:448
  15.3 0.0 collective-permute-done.18.from_far
  15.3 1.4 %collective-permute-done.19.from_near = f32[32,128]{1,0:T(8,128)S(1)} collective-permute-done((f32[32,128]{1,0:T(8,128)S(1)}, f32[32,128]{1,0:T(8,128)S(1)}, u32[]{:S(2)}, u32[]{:S(2)}) %collective-permute-start.19) | collective-permute-done | bytes 16416 | tf_op jit(solution)/shard_map/ppermute | solution.py:539
  16.7 1.3 %krylov.1 = (f32[3,64,128]{2,1,0:T(8,128)S(1)}, f32[32,128]{1,0:T(8,128)}) custom-call(s32[8,128]{1,0:T(8,128)S(1)} %place.1.meta, s32[1,128]{1,0:T(1,128)S(1)} %bitcast.28, f32[8,128]{1,0:T(8,128)S(1)} %basis_shift.1.shift, f32[6,80,128]{2,1,0:T(8,128)S(1)} %get-tuple-element.307.ext, f32[24,128]{1,0:T(8,128)S(1)} %get-tuple-element.308.facing_rows, ...), custom_call_target="tpu_custom_call" | custom-call | flops 2048000 | bytes 491520 | tf_op jit(solution)/shard_map/krylov/pallas_call | solution.py:448
  18.0 3.4 %all-to-all-start = ((f32[32,1,128]{2,1,0:T(1,128)}), f32[32,1,128]{2,1,0:T(1,128)S(1)}, u32[]{:S(2)}, u32[]{:S(2)}) async-start(f32[32,1,128]{2,1,0:T(1,128)} %bitcast.10), calls=%async_computation | async-start | bytes 32768 | tf_op jit(solution)/shard_map/all_to_all | solution.py:571
  21.4 0.0 collective-permute-done.16.from_far
  21.4 0.0 collective-permute-done.17.from_near
  21.4 3.8 %levels_step.1 = (f32[10,64,128]{2,1,0:T(8,128)}, f32[10,64,128]{2,1,0:T(8,128)}, f32[10,64,128]{2,1,0:T(8,128)}, f32[10,64,128]{2,1,0:T(8,128)}) custom-call(s32[8,128]{1,0:T(8,128)S(1)} %place.1.meta, f32[1,10]{1,0:T(1,128)S(1)} %bitcast.16, s32[1,128]{1,0:T(1,128)S(1)} %bitcast.29, f32[10,64,128]{2,1,0:T(8,128)S(1)} %copy-done, ...), custom_call_target="tpu_custom_call" | custom-call | flops 9830400 | bytes 2621440 | tf_op jit(solution)/shard_map/levels_step/pallas_call | solution.py:448
  25.2 3.3 %all-to-all-done = f32[32,1,128]{2,1,0:T(1,128)S(1)} async-done(((f32[32,1,128]{2,1,0:T(1,128)}), f32[32,1,128]{2,1,0:T(1,128)S(1)}, u32[]{:S(2)}, u32[]{:S(2)}) %all-to-all-start) | async-done | bytes 16416 | tf_op jit(solution)/shard_map/all_to_all | solution.py:571
  28.4 0.9 %surface.1 = f32[64,128]{1,0:T(8,128)} custom-call(f32[32,128]{1,0:T(8,128)S(1)} %bitcast.14, f32[8,128]{1,0:T(8,128)S(1)} %basis_shift.1.shift, f32[3,64,128]{2,1,0:T(8,128)S(1)} %get-tuple-element.312.base), custom_call_target="tpu_custom_call" | custom-call | flops 49152 | bytes 131072 | tf_op jit(solution)/shard_map/surface/pallas_call | solution.py:448
  (9 shorter events, 0.0 us)
Async XLA Ops:
  0.7 1.0 %copy-start = (f32[10,64,128]{2,1,0:T(8,128)S(1)}, f32[10,64,128]{2,1,0:T(8,128)}, u32[]{:S(2)}) copy-start(f32[10,64,128]{2,1,0:T(8,128)} %heat.3) | copy-start | bytes 983044
  0.7 1.1 %copy-start.1 = (f32[10,64,128]{2,1,0:T(8,128)S(1)}, f32[10,64,128]{2,1,0:T(8,128)}, u32[]{:S(2)}) copy-start(f32[10,64,128]{2,1,0:T(8,128)} %salt.3) | copy-start | bytes 983044
  0.7 1.2 %copy-start.2 = (f32[10,64,128]{2,1,0:T(8,128)S(1)}, f32[10,64,128]{2,1,0:T(8,128)}, u32[]{:S(2)}) copy-start(f32[10,64,128]{2,1,0:T(8,128)} %zonal.3) | copy-start | bytes 983044
  0.7 1.3 %copy-start.3 = (f32[10,64,128]{2,1,0:T(8,128)S(1)}, f32[10,64,128]{2,1,0:T(8,128)}, u32[]{:S(2)}) copy-start(f32[10,64,128]{2,1,0:T(8,128)} %merid.3) | copy-start | bytes 983044
  0.7 1.3 %copy-start.5 = (s32[64,128]{1,0:T(8,128)S(1)}, s32[64,128]{1,0:T(8,128)}, u32[]{:S(2)}) copy-start(s32[64,128]{1,0:T(8,128)} %water.3) | copy-start | bytes 98308
  0.8 1.2 %copy-start.6 = (f32[64,128]{1,0:T(8,128)S(1)}, f32[64,128]{1,0:T(8,128)}, u32[]{:S(2)}) copy-start(f32[64,128]{1,0:T(8,128)} %weights.1) | copy-start | bytes 98308
  0.8 1.2 %copy-start.7 = (f32[64,128]{1,0:T(8,128)S(1)}, f32[64,128]{1,0:T(8,128)}, u32[]{:S(2)}) copy-start(f32[64,128]{1,0:T(8,128)} %anomaly.1) | copy-start | bytes 98308
  0.9 1.2 %copy-start.4 = (f32[10]{0:T(128)S(1)}, f32[10]{0:T(128)}, u32[]{:S(2)}) copy-start(f32[10]{0:T(128)} %param.21) | copy-start | bytes 124
  0.9 1.2 %copy-start.8 = (s32[128]{0:T(128)S(1)}, s32[128]{0:T(128)}, u32[]{:S(2)}) copy-start(s32[128]{0:T(128)} %param.23) | copy-start | bytes 1540
  2.7 4.9 %collective-permute-start.6 = (f32[64,128]{1,0:T(8,128)S(1)}, f32[64,128]{1,0:T(8,128)S(1)}, u32[]{:S(2)}, u32[]{:S(2)}) collective-permute-start(f32[64,128]{1,0:T(8,128)S(1)} %get-tuple-element.216), channel_id=1, source_target_pairs={{1,2},{2,1},{5,6},{6,5},{9,10},{10,9},{13,14},{14,13},{17,18},{18,... | collective-permute-start | bytes 98312 | tf_op jit(solution)/shard_map/cond/branch_3_fun/ppermute | solution.py:519
  5.7 1.9 %collective-permute-start.7 = (f32[64,128]{1,0:T(8,128)S(1)}, f32[64,128]{1,0:T(8,128)S(1)}, u32[]{:S(2)}, u32[]{:S(2)}) collective-permute-start(f32[64,128]{1,0:T(8,128)S(1)} %get-tuple-element.217), channel_id=1, source_target_pairs={{0,1},{1,0},{2,3},{3,2},{4,5},{5,4},{6,7},{7,6},{8,9},{9,8},{10,11... | collective-permute-start | bytes 98312 | tf_op jit(solution)/shard_map/cond/branch_3_fun/ppermute | solution.py:520
  7.8 7.5 %collective-permute-start.18 = (f32[32,128]{1,0:T(8,128)S(1)}, f32[32,128]{1,0:T(8,128)S(1)}, u32[]{:S(2)}, u32[]{:S(2)}) collective-permute-start(f32[32,128]{1,0:T(8,128)S(1)} %get-tuple-element.309), channel_id=1, source_target_pairs={{0,28},{4,8},{8,4},{12,16},{16,12},{20,24},{24,20},{28,0},{1,29},{... | collective-permute-start | bytes 49160 | tf_op jit(solution)/shard_map/ppermute | solution.py:540
  12.9 3.8 %collective-permute-start.19 = (f32[32,128]{1,0:T(8,128)S(1)}, f32[32,128]{1,0:T(8,128)S(1)}, u32[]{:S(2)}, u32[]{:S(2)}) collective-permute-start(f32[32,128]{1,0:T(8,128)S(1)} %get-tuple-element.310), channel_id=1, source_target_pairs={{0,4},{4,0},{8,12},{12,8},{16,20},{20,16},{24,28},{28,24},{1,5},{5... | collective-permute-start | bytes 49160 | tf_op jit(solution)/shard_map/ppermute | solution.py:539
  12.9 8.4 %collective-permute-start.16 = (f32[64,128]{1,0:T(8,128)S(1)}, f32[64,128]{1,0:T(8,128)S(1)}, u32[]{:S(2)}, u32[]{:S(2)}) collective-permute-start(f32[64,128]{1,0:T(8,128)S(1)} %get-tuple-element.301), channel_id=1, source_target_pairs={{0,28},{4,8},{8,4},{12,16},{16,12},{20,24},{24,20},{28,0},{1,29},{... | collective-permute-start | bytes 98312 | tf_op jit(solution)/shard_map/ppermute | solution.py:540
  14.9 6.5 %collective-permute-start.17 = (f32[64,128]{1,0:T(8,128)S(1)}, f32[64,128]{1,0:T(8,128)S(1)}, u32[]{:S(2)}, u32[]{:S(2)}) collective-permute-start(f32[64,128]{1,0:T(8,128)S(1)} %get-tuple-element.302), channel_id=1, source_target_pairs={{0,4},{4,0},{8,12},{12,8},{16,20},{20,16},{24,28},{28,24},{1,5},{5... | collective-permute-start | bytes 98312 | tf_op jit(solution)/shard_map/ppermute | solution.py:539
  18.0 10.5 %all-to-all-start = ((f32[32,1,128]{2,1,0:T(1,128)}), f32[32,1,128]{2,1,0:T(1,128)S(1)}, u32[]{:S(2)}, u32[]{:S(2)}) async-start(f32[32,1,128]{2,1,0:T(1,128)} %bitcast.10), calls=%async_computation | async-start | bytes 32768 | tf_op jit(solution)/shard_map/all_to_all | solution.py:571

commit v15 on v13

--- a/solution.py
+++ b/solution.py
@@ -504,7 +504,7 @@
         for i in range(lons)
         for j in range(1, lats - 1, 2)
         for a, b in ((j, j + 1), (j + 1, j))
-    ] + [(flat(i, 0), flat(i ^ 1, 0)) for i in range(lons)]
+    ] + [(flat(i, 0), flat(i ^ 2, 0)) for i in range(lons)]
 
     counterpart, first = lax.optimization_barrier((opposite_counterpart, first))
     hinge = lax.rem(counterpart[0] + 1 + cols * lon, width)
@@ -574,6 +574,7 @@
 
 
 def solution(mesh):
+    assert mesh.shape["lon"] > 2
     for axis in mesh.shape.values():
         assert axis > 1 and axis & (axis - 1) == 0
     levels = P(None, "lat", "lon")

time: 29.5 us -> 29.7 us (level)
  no operation moved by 1% of the time
where the time goes in v15:
time: 29.7 us; the launch traced here: 29.3 us
  starting transfers between devices  13.7 us (46%)
  Pallas kernels  7 us (24%)
  waiting for transfers between devices  6.53 us (22%)
  local copies, waits for them, and re-layouts  1.26 us (4%)
  between operations  0.82 us (3%)
    pallas_call x7, Pallas kernels, run(): pl.pallas_call(kernel, out_shape=[jax.ShapeDtypeStruct(shape, types) for...  7 us
    ppermute x2, starting transfers between devices, body(): lax.ppermute(cells, 'lon', [(i, (i + 1 if i % 2 else i - 1) % lons) for i...  6.98 us
    all_to_all x1, starting transfers between devices, body(): shares = lax.all_to_all(moments, axes, 0, 0, tiled=True)  3.42 us
    all_to_all x1, waiting for transfers between devices, body(): shares = lax.all_to_all(moments, axes, 0, 0, tiled=True)  3.29 us
    ppermute x1, starting transfers between devices, exchange(): second = lax.ppermute(second, axes, pairs_inner + pairs_fold)  3.09 us
    ppermute x1, waiting for transfers between devices, exchange(): second = lax.ppermute(second, axes, pairs_inner + pairs_fold)  1.84 us
    ppermute x2, waiting for transfers between devices, body(): lax.ppermute(cells, 'lon', [(i, i ^ 1) for i in range(lons)])  1.4 us
    unnamed x18, local copies, waits for them, and re-layouts  1.17 us
  transfers between devices with their start and end apart: 7, of which 3 were waited for; matrix products, arithmetic and copies ran while one was open for 0% of the time, Pallas kernels for 18%

profile of v15, /device:TPU:0, one launch (start us, length us, event | category | flops | bytes accessed | tf_op | source)
XLA Modules:
  0.0 29.3 jit_solution(9473742298534593876)
XLA Ops:
  0.6 0.1 stack.31
  0.7 0.0 copy-start.3
  0.7 0.0 copy-start.5
  0.8 0.0 copy-start.6
  0.8 0.0 copy-start.7
  0.8 0.1 place.1.meta
  0.9 0.8 %copy-done = f32[10,64,128]{2,1,0:T(8,128)S(1)} copy-done((f32[10,64,128]{2,1,0:T(8,128)S(1)}, f32[10,64,128]{2,1,0:T(8,128)}, u32[]{:S(2)}) %copy-start) | copy-done | bytes 327704
  1.7 0.1 copy-done.1
  1.8 0.1 copy-done.2
  1.9 0.1 copy-done.3
  2.0 0.0 copy-done.4
  2.0 0.5 %level_sums.1 = (f32[3,64,128]{2,1,0:T(8,128)S(1)}, f32[64,128]{1,0:T(8,128)S(1)}, f32[64,128]{1,0:T(8,128)S(1)}, f32[64,128]{1,0:T(8,128)S(1)}, f32[64,128]{1,0:T(8,128)S(1)}, /*index=5*/f32[64,128]{1,0:T(8,128)S(1)}) custom-call(s32[8,128]{1,0:T(8,128)S(1)} %place.1.meta, f32[1,10]{1,0:T(1,128)S(1)} %bitcast.15, s32[1,128]{1,0:T(1,128)S(1)} %bitcast.18, ...), custom_call_target="tpu_custom_call" | custom-call | flops 983040 | bytes 1310720 | tf_op jit(solution)/shard_map/level_sums/pallas_call | solution.py:448
  2.6 5.3 %conditional.1 = ((f32[6,80,128]{2,1,0:T(8,128)S(1)}, f32[32,128]{1,0:T(8,128)S(1)}, f32[32,128]{1,0:T(8,128)S(1)}, f32[64,128]{1,0:T(8,128)S(1)}, f32[64,128]{1...) conditional(s32[]{:T(128)} %clamp.3, ...), branch_computations={%region_0.1_spmd, %region_1.2_spmd, %region_2.3_spmd, %region_3.4_... | conditional | flops 61440 | bytes 1245272 | solution.py:535
  2.7 3.1 %collective-permute-start.8 = (f32[64,128]{1,0:T(8,128)S(1)}, f32[64,128]{1,0:T(8,128)S(1)}, u32[]{:S(2)}, u32[]{:S(2)}) collective-permute-start(f32[64,128]{1,0:T(8,128)S(1)} %get-tuple-element.227), channel_id=1, source_target_pairs={{1,2},{2,1},{5,6},{6,5},{9,10},{10,9},{13,14},{14,13},{17,18},{18,... | collective-permute-start | bytes 98312 | tf_op jit(solution)/shard_map/cond/branch_4_fun/ppermute | solution.py:519
  5.8 0.1 collective-permute-start.9
  5.8 1.8 %collective-permute-done.8.second = f32[64,128]{1,0:T(8,128)S(1)} collective-permute-done((f32[64,128]{1,0:T(8,128)S(1)}, f32[64,128]{1,0:T(8,128)S(1)}, u32[]{:S(2)}, u32[]{:S(2)}) %collective-permute-start.8) | collective-permute-done | bytes 32800 | tf_op jit(solution)/shard_map/cond/branch_4_fun/ppermute | solution.py:519
  7.7 0.0 collective-permute-done.9.first
  7.7 0.2 row_halos.12
  7.9 5.0 %collective-permute-start.18 = (f32[32,128]{1,0:T(8,128)S(1)}, f32[32,128]{1,0:T(8,128)S(1)}, u32[]{:S(2)}, u32[]{:S(2)}) collective-permute-start(f32[32,128]{1,0:T(8,128)S(1)} %get-tuple-element.309), channel_id=1, source_target_pairs={{0,28},{4,8},{8,4},{12,16},{16,12},{20,24},{24,20},{28,0},{1,29},{... | collective-permute-start | bytes 49160 | tf_op jit(solution)/shard_map/ppermute | solution.py:540
  12.9 0.0 collective-permute-start.19
  12.9 1.9 %collective-permute-start.16 = (f32[64,128]{1,0:T(8,128)S(1)}, f32[64,128]{1,0:T(8,128)S(1)}, u32[]{:S(2)}, u32[]{:S(2)}) collective-permute-start(f32[64,128]{1,0:T(8,128)S(1)} %get-tuple-element.301), channel_id=1, source_target_pairs={{0,28},{4,8},{8,4},{12,16},{16,12},{20,24},{24,20},{28,0},{1,29},{... | collective-permute-start | bytes 98312 | tf_op jit(solution)/shard_map/ppermute | solution.py:540
  14.9 0.1 collective-permute-start.17
  15.0 0.3 %basis_shift.1.shift = f32[8,128]{1,0:T(8,128)S(1)} custom-call(f32[6,80,128]{2,1,0:T(8,128)S(1)} %get-tuple-element.307.ext), custom_call_target="tpu_custom_call" | custom-call | flops 491520 | bytes 196608 | tf_op jit(solution)/shard_map/basis_shift/pallas_call | solution.py:448
  15.3 0.0 collective-permute-done.18.from_far
  15.3 1.4 %collective-permute-done.19.from_near = f32[32,128]{1,0:T(8,128)S(1)} collective-permute-done((f32[32,128]{1,0:T(8,128)S(1)}, f32[32,128]{1,0:T(8,128)S(1)}, u32[]{:S(2)}, u32[]{:S(2)}) %collective-permute-start.19) | collective-permute-done | bytes 16416 | tf_op jit(solution)/shard_map/ppermute | solution.py:539
  16.7 1.3 %krylov.1 = (f32[3,64,128]{2,1,0:T(8,128)S(1)}, f32[32,128]{1,0:T(8,128)}) custom-call(s32[8,128]{1,0:T(8,128)S(1)} %place.1.meta, s32[1,128]{1,0:T(1,128)S(1)} %bitcast.28, f32[8,128]{1,0:T(8,128)S(1)} %basis_shift.1.shift, f32[6,80,128]{2,1,0:T(8,128)S(1)} %get-tuple-element.307.ext, f32[24,128]{1,0:T(8,128)S(1)} %get-tuple-element.308.facing_rows, ...), custom_call_target="tpu_custom_call" | custom-call | flops 2048000 | bytes 491520 | tf_op jit(solution)/shard_map/krylov/pallas_call | solution.py:448
  18.0 3.4 %all-to-all-start = ((f32[32,1,128]{2,1,0:T(1,128)}), f32[32,1,128]{2,1,0:T(1,128)S(1)}, u32[]{:S(2)}, u32[]{:S(2)}) async-start(f32[32,1,128]{2,1,0:T(1,128)} %bitcast.10), calls=%async_computation | async-start | bytes 32768 | tf_op jit(solution)/shard_map/all_to_all | solution.py:571
  21.4 0.0 collective-permute-done.16.from_far
  21.4 0.0 collective-permute-done.17.from_near
  21.4 3.8 %levels_step.1 = (f32[10,64,128]{2,1,0:T(8,128)}, f32[10,64,128]{2,1,0:T(8,128)}, f32[10,64,128]{2,1,0:T(8,128)}, f32[10,64,128]{2,1,0:T(8,128)}) custom-call(s32[8,128]{1,0:T(8,128)S(1)} %place.1.meta, f32[1,10]{1,0:T(1,128)S(1)} %bitcast.16, s32[1,128]{1,0:T(1,128)S(1)} %bitcast.29, f32[10,64,128]{2,1,0:T(8,128)S(1)} %copy-done, ...), custom_call_target="tpu_custom_call" | custom-call | flops 9830400 | bytes 2621440 | tf_op jit(solution)/shard_map/levels_step/pallas_call | solution.py:448
  25.2 3.3 %all-to-all-done = f32[32,1,128]{2,1,0:T(1,128)S(1)} async-done(((f32[32,1,128]{2,1,0:T(1,128)}), f32[32,1,128]{2,1,0:T(1,128)S(1)}, u32[]{:S(2)}, u32[]{:S(2)}) %all-to-all-start) | async-done | bytes 16416 | tf_op jit(solution)/shard_map/all_to_all | solution.py:571
  28.5 0.9 %surface.1 = f32[64,128]{1,0:T(8,128)} custom-call(f32[32,128]{1,0:T(8,128)S(1)} %bitcast.14, f32[8,128]{1,0:T(8,128)S(1)} %basis_shift.1.shift, f32[3,64,128]{2,1,0:T(8,128)S(1)} %get-tuple-element.312.base), custom_call_target="tpu_custom_call" | custom-call | flops 49152 | bytes 131072 | tf_op jit(solution)/shard_map/surface/pallas_call | solution.py:448
  (9 shorter events, 0.0 us)
Async XLA Ops:
  0.7 1.0 %copy-start = (f32[10,64,128]{2,1,0:T(8,128)S(1)}, f32[10,64,128]{2,1,0:T(8,128)}, u32[]{:S(2)}) copy-start(f32[10,64,128]{2,1,0:T(8,128)} %heat.3) | copy-start | bytes 983044
  0.7 1.1 %copy-start.1 = (f32[10,64,128]{2,1,0:T(8,128)S(1)}, f32[10,64,128]{2,1,0:T(8,128)}, u32[]{:S(2)}) copy-start(f32[10,64,128]{2,1,0:T(8,128)} %salt.3) | copy-start | bytes 983044
  0.7 1.2 %copy-start.2 = (f32[10,64,128]{2,1,0:T(8,128)S(1)}, f32[10,64,128]{2,1,0:T(8,128)}, u32[]{:S(2)}) copy-start(f32[10,64,128]{2,1,0:T(8,128)} %zonal.3) | copy-start | bytes 983044
  0.7 1.3 %copy-start.3 = (f32[10,64,128]{2,1,0:T(8,128)S(1)}, f32[10,64,128]{2,1,0:T(8,128)}, u32[]{:S(2)}) copy-start(f32[10,64,128]{2,1,0:T(8,128)} %merid.3) | copy-start | bytes 983044
  0.7 1.3 %copy-start.5 = (s32[64,128]{1,0:T(8,128)S(1)}, s32[64,128]{1,0:T(8,128)}, u32[]{:S(2)}) copy-start(s32[64,128]{1,0:T(8,128)} %water.3) | copy-start | bytes 98308
  0.8 1.2 %copy-start.6 = (f32[64,128]{1,0:T(8,128)S(1)}, f32[64,128]{1,0:T(8,128)}, u32[]{:S(2)}) copy-start(f32[64,128]{1,0:T(8,128)} %weights.1) | copy-start | bytes 98308
  0.8 1.2 %copy-start.7 = (f32[64,128]{1,0:T(8,128)S(1)}, f32[64,128]{1,0:T(8,128)}, u32[]{:S(2)}) copy-start(f32[64,128]{1,0:T(8,128)} %anomaly.1) | copy-start | bytes 98308
  0.9 1.2 %copy-start.4 = (f32[10]{0:T(128)S(1)}, f32[10]{0:T(128)}, u32[]{:S(2)}) copy-start(f32[10]{0:T(128)} %param.21) | copy-start | bytes 124
  0.9 1.2 %copy-start.8 = (s32[128]{0:T(128)S(1)}, s32[128]{0:T(128)}, u32[]{:S(2)}) copy-start(s32[128]{0:T(128)} %param.23) | copy-start | bytes 1540
  2.7 5.0 %collective-permute-start.8 = (f32[64,128]{1,0:T(8,128)S(1)}, f32[64,128]{1,0:T(8,128)S(1)}, u32[]{:S(2)}, u32[]{:S(2)}) collective-permute-start(f32[64,128]{1,0:T(8,128)S(1)} %get-tuple-element.227), channel_id=1, source_target_pairs={{1,2},{2,1},{5,6},{6,5},{9,10},{10,9},{13,14},{14,13},{17,18},{18,... | collective-permute-start | bytes 98312 | tf_op jit(solution)/shard_map/cond/branch_4_fun/ppermute | solution.py:519
  5.8 1.9 %collective-permute-start.9 = (f32[64,128]{1,0:T(8,128)S(1)}, f32[64,128]{1,0:T(8,128)S(1)}, u32[]{:S(2)}, u32[]{:S(2)}) collective-permute-start(f32[64,128]{1,0:T(8,128)S(1)} %get-tuple-element.228), channel_id=1, source_target_pairs={{0,1},{1,0},{2,3},{3,2},{4,5},{5,4},{6,7},{7,6},{8,9},{9,8},{10,11... | collective-permute-start | bytes 98312 | tf_op jit(solution)/shard_map/cond/branch_4_fun/ppermute | solution.py:520
  7.9 7.4 %collective-permute-start.18 = (f32[32,128]{1,0:T(8,128)S(1)}, f32[32,128]{1,0:T(8,128)S(1)}, u32[]{:S(2)}, u32[]{:S(2)}) collective-permute-start(f32[32,128]{1,0:T(8,128)S(1)} %get-tuple-element.309), channel_id=1, source_target_pairs={{0,28},{4,8},{8,4},{12,16},{16,12},{20,24},{24,20},{28,0},{1,29},{... | collective-permute-start | bytes 49160 | tf_op jit(solution)/shard_map/ppermute | solution.py:540
  12.9 3.8 %collective-permute-start.19 = (f32[32,128]{1,0:T(8,128)S(1)}, f32[32,128]{1,0:T(8,128)S(1)}, u32[]{:S(2)}, u32[]{:S(2)}) collective-permute-start(f32[32,128]{1,0:T(8,128)S(1)} %get-tuple-element.310), channel_id=1, source_target_pairs={{0,4},{4,0},{8,12},{12,8},{16,20},{20,16},{24,28},{28,24},{1,5},{5... | collective-permute-start | bytes 49160 | tf_op jit(solution)/shard_map/ppermute | solution.py:539
  12.9 8.4 %collective-permute-start.16 = (f32[64,128]{1,0:T(8,128)S(1)}, f32[64,128]{1,0:T(8,128)S(1)}, u32[]{:S(2)}, u32[]{:S(2)}) collective-permute-start(f32[64,128]{1,0:T(8,128)S(1)} %get-tuple-element.301), channel_id=1, source_target_pairs={{0,28},{4,8},{8,4},{12,16},{16,12},{20,24},{24,20},{28,0},{1,29},{... | collective-permute-start | bytes 98312 | tf_op jit(solution)/shard_map/ppermute | solution.py:540
  14.9 6.5 %collective-permute-start.17 = (f32[64,128]{1,0:T(8,128)S(1)}, f32[64,128]{1,0:T(8,128)S(1)}, u32[]{:S(2)}, u32[]{:S(2)}) collective-permute-start(f32[64,128]{1,0:T(8,128)S(1)} %get-tuple-element.302), channel_id=1, source_target_pairs={{0,4},{4,0},{8,12},{12,8},{16,20},{20,16},{24,28},{28,24},{1,5},{5... | collective-permute-start | bytes 98312 | tf_op jit(solution)/shard_map/ppermute | solution.py:539
  18.0 10.5 %all-to-all-start = ((f32[32,1,128]{2,1,0:T(1,128)}), f32[32,1,128]{2,1,0:T(1,128)S(1)}, u32[]{:S(2)}, u32[]{:S(2)}) async-start(f32[32,1,128]{2,1,0:T(1,128)} %bitcast.10), calls=%async_computation | async-start | bytes 32768 | tf_op jit(solution)/shard_map/all_to_all | solution.py:571

commit v16 on v13

--- a/solution.py
+++ b/solution.py
@@ -50,7 +50,7 @@
 
 def pack_kernel(
     meta, spans, facing, heat, salt, zonal, merid, water, weights, anomaly,
-    sums, first, second, kept, east_columns, west_columns,
+    sums, first, second, kept,
     top, bottom, back,
 ):
     levels, rows, cols = heat.shape
@@ -60,24 +60,17 @@
     for k in reversed(range(levels)):
         below[k] = span[k] * (0.5 * span[k] + total)
         total = total + span[k]
-    pair = iota((rows, cols), 1) // 2
     zero = jnp.zeros((rows, cols), jnp.float32)
-    press, east, north, east_edge, west_edge = zero, zero, zero, zero, zero
+    press, east, north = zero, zero, zero
     for k in range(levels):
         press = press + below[k] * density(heat[k], salt[k])
         east = east + span[k] * zonal[k]
         north = north + span[k] * merid[k]
         for q, source in ((k, heat), (levels + k, salt)):
-            cells = source[k]
-            here = pair == q
-            east_edge = jnp.where(here, pltpu.roll(cells, (2 * q + 2) % cols, 1), east_edge)
-            west_edge = jnp.where(here, pltpu.roll(cells, 2 * q, 1), west_edge)
             top[2 * q : 2 * q + 2, :] = source[k, rows - 2 :, :]
             bottom[2 * q : 2 * q + 2, :] = source[k, :2, :]
             for i in range(2):
                 back[2 * q + i : 2 * q + i + 1, :] = source[k, rows - 1 - i : rows - i, :]
-    east_columns[...] = east_edge
-    west_columns[...] = west_edge
     sums[0] = press
     sums[1] = east
     sums[2] = north
@@ -99,6 +92,20 @@
     packet = jnp.where(last, back[...], jnp.where(odd, top[...], bottom[...]))
     second[...] = packet
     kept[...] = packet
+
+
+def column_kernel(heat, salt, east_columns, west_columns):
+    levels, rows, cols = heat.shape
+    pair = iota((rows, cols), 1) // 2
+    east = jnp.zeros((rows, cols), jnp.float32)
+    west = jnp.zeros((rows, cols), jnp.float32)
+    for q in range(2 * levels):
+        cells = heat[q] if q < levels else salt[q - levels]
+        here = pair == q
+        east = jnp.where(here, pltpu.roll(cells, (2 * q + 2) % cols, 1), east)
+        west = jnp.where(here, pltpu.roll(cells, 2 * q, 1), west)
+    east_columns[...] = east
+    west_columns[...] = west
 
 
 def turn_kernel(
@@ -488,9 +495,9 @@
     state = (warmth_deviation, saltiness_deviation, easterly_speed, poleward_speed)
     flat_state = (water_indicator, elevation_weights, elevation_anomaly)
     cells = levels * rows * cols
-    sums, first, second, kept, east_columns, west_columns = call(
+    sums, first, second, kept = call(
         pack_kernel,
-        [(3, rows, cols), *[(high, cols)] * 3, (rows, cols), (rows, cols)],
+        [(3, rows, cols), *[(high, cols)] * 3],
         12 * cells,
         16 * cells,
         "level_sums",
@@ -518,6 +525,7 @@
         pairs_fold = [(flat(p, lats - 1), flat(i, lats - 1)) for i, p in enumerate(partner)]
         second = lax.ppermute(second, axes, pairs_inner + pairs_fold)
         first = lax.ppermute(first, axes, pairs_first)
+        columns = call(column_kernel, [(rows, cols)] * 2, 4 * cells, 8 * cells, "columns")(*state[:2])
         return call(
             functools.partial(turn_kernel, lons),
             [
@@ -530,7 +538,7 @@
             FIELDS * tall * cols,
             4 * 4 * FIELDS * tall * cols,
             "row_halos",
-        )(meta, facing, kept, sums, *flat_state, second, first, east_columns, west_columns)
+        )(meta, facing, kept, sums, *flat_state, second, first, *columns)
 
     ext, to_far, to_near, state_far, state_near, facing_rows, north_rows, south_rows = lax.switch(
         block, [functools.partial(exchange, s) for s in range(lons)], first, second

time: 29.5 us -> 29.4 us (level)
  waiting for transfers between devices: 6.45 us -> 6.02 us
    ppermute x1, waiting for transfers between devices: 1.75 us -> 1.34 us  [exchange(): second = lax.ppermute(second, axes, pairs_inner + pairs_fold)]
    pallas_call x7 -> x8, Pallas kernels: 7 us -> 7.21 us  [run(): pl.pallas_call(kernel, out_shape=[jax.ShapeDtypeStruct(shape, types) for...]
  transfers between devices with their start and end apart: 7 -> 7, of which waited for: 3 -> 3; matrix products, arithmetic and copies ran while one was open for 0% -> 0% of each run, Pallas kernels for 18% -> 20%
where the time goes in v16:
time: 29.4 us; the launch traced here: 29.2 us
  starting transfers between devices  13.8 us (47%)
  Pallas kernels  7.21 us (25%)
  waiting for transfers between devices  6.02 us (20%)
  local copies, waits for them, and re-layouts  1.26 us (4%)
  between operations  0.82 us (3%)
    pallas_call x8, Pallas kernels, run(): pl.pallas_call(kernel, out_shape=[jax.ShapeDtypeStruct(shape, types) for...  7.21 us
    ppermute x2, starting transfers between devices, body(): lax.ppermute(cells, 'lon', [(i, (i + 1 if i % 2 else i - 1) % lons) for i...  7.06 us
    all_to_all x1, starting transfers between devices, body(): shares = lax.all_to_all(moments, axes, 0, 0, tiled=True)  3.5 us
    all_to_all x1, waiting for transfers between devices, body(): shares = lax.all_to_all(moments, axes, 0, 0, tiled=True)  3.27 us
    ppermute x1, starting transfers between devices, exchange(): second = lax.ppermute(second, axes, pairs_inner + pairs_fold)  3 us
    ppermute x2, waiting for transfers between devices, body(): lax.ppermute(cells, 'lon', [(i, i ^ 1) for i in range(lons)])  1.4 us
    ppermute x1, waiting for transfers between devices, exchange(): second = lax.ppermute(second, axes, pairs_inner + pairs_fold)  1.34 us
    unnamed x18, local copies, waits for them, and re-layouts  1.17 us
  transfers between devices with their start and end apart: 7, of which 3 were waited for; matrix products, arithmetic and copies ran while one was open for 0% of the time, Pallas kernels for 20%

profile of v16, /device:TPU:0, one launch (start us, length us, event | category | flops | bytes accessed | tf_op | source)
XLA Modules:
  0.0 29.2 jit_solution(15151143655068337710)
XLA Ops:
  0.6 0.1 stack.31
  0.7 0.0 copy-start.5
  0.8 0.0 copy-start.6
  0.8 0.0 copy-start.7
  0.8 0.1 place.1.meta
  0.9 0.8 %copy-done = f32[10,64,128]{2,1,0:T(8,128)S(1)} copy-done((f32[10,64,128]{2,1,0:T(8,128)S(1)}, f32[10,64,128]{2,1,0:T(8,128)}, u32[]{:S(2)}) %copy-start) | copy-done | bytes 327704
  1.7 0.1 copy-done.1
  1.8 0.1 copy-done.3
  1.9 0.1 copy-done.4
  2.0 0.0 copy-done.2
  2.0 0.3 %level_sums.1 = (f32[3,64,128]{2,1,0:T(8,128)S(1)}, f32[64,128]{1,0:T(8,128)S(1)}, f32[64,128]{1,0:T(8,128)S(1)}, f32[64,128]{1,0:T(8,128)S(1)}) custom-call(s32[8,128]{1,0:T(8,128)S(1)} %place.1.meta, f32[1,10]{1,0:T(1,128)S(1)} %bitcast.15, s32[1,128]{1,0:T(1,128)S(1)} %bitcast.18, f32[10,64,128]{2,1,0:T(8,128)S(1)} %copy-done.3, ...), custom_call_target="tpu_custom_call" | custom-call | flops 983040 | bytes 1310720 | tf_op jit(solution)/shard_map/level_sums/pallas_call | solution.py:455
  2.4 5.2 %conditional.1 = ((f32[6,80,128]{2,1,0:T(8,128)S(1)}, f32[32,128]{1,0:T(8,128)S(1)}, f32[32,128]{1,0:T(8,128)S(1)}, f32[64,128]{1,0:T(8,128)S(1)}, f32[64,128]{1...) conditional(s32[]{:T(128)} %clamp.3, ...), branch_computations={%region_0.1_spmd, %region_1.2_spmd, %region_2.3_spmd, %region_3.4_... | conditional | flops 389120 | bytes 1900632 | solution.py:543
  2.5 3.0 %collective-permute-start.4 = (f32[64,128]{1,0:T(8,128)S(1)}, f32[64,128]{1,0:T(8,128)S(1)}, u32[]{:S(2)}, u32[]{:S(2)}) collective-permute-start(f32[64,128]{1,0:T(8,128)S(1)} %get-tuple-element.209), channel_id=1, source_target_pairs={{1,2},{2,1},{5,6},{6,5},{9,10},{10,9},{13,14},{14,13},{17,18},{18,... | collective-permute-start | bytes 98312 | tf_op jit(solution)/shard_map/cond/branch_2_fun/ppermute | solution.py:526
  5.5 0.1 collective-permute-start.5
  5.6 0.4 %columns.10 = (f32[64,128]{1,0:T(8,128)S(1)}, f32[64,128]{1,0:T(8,128)S(1)}) custom-call(f32[10,64,128]{2,1,0:T(8,128)S(1)} %get-tuple-element.211.heat, f32[10,64,128]{2,1,0:T(8,128)S(1)} %get-tuple-element.212.salt), custom_call_target="tpu_custom_call" | custom-call | flops 327680 | bytes 655360 | tf_op jit(solution)/shard_map/cond/branch_2_fun/columns/pallas_call | solution.py:455
  6.0 1.3 %collective-permute-done.4.second = f32[64,128]{1,0:T(8,128)S(1)} collective-permute-done((f32[64,128]{1,0:T(8,128)S(1)}, f32[64,128]{1,0:T(8,128)S(1)}, u32[]{:S(2)}, u32[]{:S(2)}) %collective-permute-start.4) | collective-permute-done | bytes 32800 | tf_op jit(solution)/shard_map/cond/branch_2_fun/ppermute | solution.py:526
  7.4 0.0 collective-permute-done.5.first
  7.4 0.2 row_halos.10
  7.6 5.1 %collective-permute-start.18 = (f32[32,128]{1,0:T(8,128)S(1)}, f32[32,128]{1,0:T(8,128)S(1)}, u32[]{:S(2)}, u32[]{:S(2)}) collective-permute-start(f32[32,128]{1,0:T(8,128)S(1)} %get-tuple-element.321), channel_id=1, source_target_pairs={{0,28},{4,8},{8,4},{12,16},{16,12},{20,24},{24,20},{28,0},{1,29},{... | collective-permute-start | bytes 49160 | tf_op jit(solution)/shard_map/ppermute | solution.py:548
  12.7 0.0 collective-permute-start.19
  12.7 1.9 %collective-permute-start.16 = (f32[64,128]{1,0:T(8,128)S(1)}, f32[64,128]{1,0:T(8,128)S(1)}, u32[]{:S(2)}, u32[]{:S(2)}) collective-permute-start(f32[64,128]{1,0:T(8,128)S(1)} %get-tuple-element.313), channel_id=1, source_target_pairs={{0,28},{4,8},{8,4},{12,16},{16,12},{20,24},{24,20},{28,0},{1,29},{... | collective-permute-start | bytes 98312 | tf_op jit(solution)/shard_map/ppermute | solution.py:548
  14.7 0.1 collective-permute-start.17
  14.8 0.3 %basis_shift.1.shift = f32[8,128]{1,0:T(8,128)S(1)} custom-call(f32[6,80,128]{2,1,0:T(8,128)S(1)} %get-tuple-element.319.ext), custom_call_target="tpu_custom_call" | custom-call | flops 491520 | bytes 196608 | tf_op jit(solution)/shard_map/basis_shift/pallas_call | solution.py:455
  15.1 0.0 collective-permute-done.18.from_far
  15.1 1.4 %collective-permute-done.19.from_near = f32[32,128]{1,0:T(8,128)S(1)} collective-permute-done((f32[32,128]{1,0:T(8,128)S(1)}, f32[32,128]{1,0:T(8,128)S(1)}, u32[]{:S(2)}, u32[]{:S(2)}) %collective-permute-start.19) | collective-permute-done | bytes 16416 | tf_op jit(solution)/shard_map/ppermute | solution.py:547
  16.5 1.3 %krylov.1 = (f32[3,64,128]{2,1,0:T(8,128)S(1)}, f32[32,128]{1,0:T(8,128)}) custom-call(s32[8,128]{1,0:T(8,128)S(1)} %place.1.meta, s32[1,128]{1,0:T(1,128)S(1)} %bitcast.28, f32[8,128]{1,0:T(8,128)S(1)} %basis_shift.1.shift, f32[6,80,128]{2,1,0:T(8,128)S(1)} %get-tuple-element.319.ext, f32[24,128]{1,0:T(8,128)S(1)} %get-tuple-element.320.facing_rows, ...), custom_call_target="tpu_custom_call" | custom-call | flops 2048000 | bytes 491520 | tf_op jit(solution)/shard_map/krylov/pallas_call | solution.py:455
  17.8 3.5 %all-to-all-start = ((f32[32,1,128]{2,1,0:T(1,128)}), f32[32,1,128]{2,1,0:T(1,128)S(1)}, u32[]{:S(2)}, u32[]{:S(2)}) async-start(f32[32,1,128]{2,1,0:T(1,128)} %bitcast.10), calls=%async_computation | async-start | bytes 32768 | tf_op jit(solution)/shard_map/all_to_all | solution.py:579
  21.3 0.0 collective-permute-done.16.from_far
  21.3 0.0 collective-permute-done.17.from_near
  21.3 3.8 %levels_step.1 = (f32[10,64,128]{2,1,0:T(8,128)}, f32[10,64,128]{2,1,0:T(8,128)}, f32[10,64,128]{2,1,0:T(8,128)}, f32[10,64,128]{2,1,0:T(8,128)}) custom-call(s32[8,128]{1,0:T(8,128)S(1)} %place.1.meta, f32[1,10]{1,0:T(1,128)S(1)} %bitcast.16, s32[1,128]{1,0:T(1,128)S(1)} %bitcast.29, f32[10,64,128]{2,1,0:T(8,128)S(1)} %copy-done.3, ...), custom_call_target="tpu_custom_call" | custom-call | flops 9830400 | bytes 2621440 | tf_op jit(solution)/shard_map/levels_step/pallas_call | solution.py:455
  25.1 3.3 %all-to-all-done = f32[32,1,128]{2,1,0:T(1,128)S(1)} async-done(((f32[32,1,128]{2,1,0:T(1,128)}), f32[32,1,128]{2,1,0:T(1,128)S(1)}, u32[]{:S(2)}, u32[]{:S(2)}) %all-to-all-start) | async-done | bytes 16416 | tf_op jit(solution)/shard_map/all_to_all | solution.py:579
  28.3 0.9 %surface.1 = f32[64,128]{1,0:T(8,128)} custom-call(f32[32,128]{1,0:T(8,128)S(1)} %bitcast.14, f32[8,128]{1,0:T(8,128)S(1)} %basis_shift.1.shift, f32[3,64,128]{2,1,0:T(8,128)S(1)} %get-tuple-element.324.base), custom_call_target="tpu_custom_call" | custom-call | flops 49152 | bytes 131072 | tf_op jit(solution)/shard_map/surface/pallas_call | solution.py:455
  (10 shorter events, 0.0 us)
Async XLA Ops:
  0.7 1.0 %copy-start = (f32[10,64,128]{2,1,0:T(8,128)S(1)}, f32[10,64,128]{2,1,0:T(8,128)}, u32[]{:S(2)}) copy-start(f32[10,64,128]{2,1,0:T(8,128)} %zonal.3) | copy-start | bytes 983044
  0.7 1.1 %copy-start.1 = (f32[10,64,128]{2,1,0:T(8,128)S(1)}, f32[10,64,128]{2,1,0:T(8,128)}, u32[]{:S(2)}) copy-start(f32[10,64,128]{2,1,0:T(8,128)} %merid.3) | copy-start | bytes 983044
  0.7 1.2 %copy-start.3 = (f32[10,64,128]{2,1,0:T(8,128)S(1)}, f32[10,64,128]{2,1,0:T(8,128)}, u32[]{:S(2)}) copy-start(f32[10,64,128]{2,1,0:T(8,128)} %heat.3) | copy-start | bytes 983044
  0.7 1.3 %copy-start.4 = (f32[10,64,128]{2,1,0:T(8,128)S(1)}, f32[10,64,128]{2,1,0:T(8,128)}, u32[]{:S(2)}) copy-start(f32[10,64,128]{2,1,0:T(8,128)} %salt.3) | copy-start | bytes 983044
  0.7 1.3 %copy-start.5 = (s32[64,128]{1,0:T(8,128)S(1)}, s32[64,128]{1,0:T(8,128)}, u32[]{:S(2)}) copy-start(s32[64,128]{1,0:T(8,128)} %water.3) | copy-start | bytes 98308
  0.8 1.2 %copy-start.6 = (f32[64,128]{1,0:T(8,128)S(1)}, f32[64,128]{1,0:T(8,128)}, u32[]{:S(2)}) copy-start(f32[64,128]{1,0:T(8,128)} %weights.1) | copy-start | bytes 98308
  0.8 1.2 %copy-start.7 = (f32[64,128]{1,0:T(8,128)S(1)}, f32[64,128]{1,0:T(8,128)}, u32[]{:S(2)}) copy-start(f32[64,128]{1,0:T(8,128)} %anomaly.1) | copy-start | bytes 98308
  0.9 1.2 %copy-start.2 = (f32[10]{0:T(128)S(1)}, f32[10]{0:T(128)}, u32[]{:S(2)}) copy-start(f32[10]{0:T(128)} %param.21) | copy-start | bytes 124
  0.9 1.2 %copy-start.8 = (s32[128]{0:T(128)S(1)}, s32[128]{0:T(128)}, u32[]{:S(2)}) copy-start(s32[128]{0:T(128)} %param.23) | copy-start | bytes 1540
  2.5 4.9 %collective-permute-start.4 = (f32[64,128]{1,0:T(8,128)S(1)}, f32[64,128]{1,0:T(8,128)S(1)}, u32[]{:S(2)}, u32[]{:S(2)}) collective-permute-start(f32[64,128]{1,0:T(8,128)S(1)} %get-tuple-element.209), channel_id=1, source_target_pairs={{1,2},{2,1},{5,6},{6,5},{9,10},{10,9},{13,14},{14,13},{17,18},{18,... | collective-permute-start | bytes 98312 | tf_op jit(solution)/shard_map/cond/branch_2_fun/ppermute | solution.py:526
  5.5 1.9 %collective-permute-start.5 = (f32[64,128]{1,0:T(8,128)S(1)}, f32[64,128]{1,0:T(8,128)S(1)}, u32[]{:S(2)}, u32[]{:S(2)}) collective-permute-start(f32[64,128]{1,0:T(8,128)S(1)} %get-tuple-element.210), channel_id=1, source_target_pairs={{0,1},{1,0},{2,3},{3,2},{4,5},{5,4},{6,7},{7,6},{8,9},{9,8},{10,11... | collective-permute-start | bytes 98312 | tf_op jit(solution)/shard_map/cond/branch_2_fun/ppermute | solution.py:527
  7.6 7.5 %collective-permute-start.18 = (f32[32,128]{1,0:T(8,128)S(1)}, f32[32,128]{1,0:T(8,128)S(1)}, u32[]{:S(2)}, u32[]{:S(2)}) collective-permute-start(f32[32,128]{1,0:T(8,128)S(1)} %get-tuple-element.321), channel_id=1, source_target_pairs={{0,28},{4,8},{8,4},{12,16},{16,12},{20,24},{24,20},{28,0},{1,29},{... | collective-permute-start | bytes 49160 | tf_op jit(solution)/shard_map/ppermute | solution.py:548
  12.7 3.8 %collective-permute-start.19 = (f32[32,128]{1,0:T(8,128)S(1)}, f32[32,128]{1,0:T(8,128)S(1)}, u32[]{:S(2)}, u32[]{:S(2)}) collective-permute-start(f32[32,128]{1,0:T(8,128)S(1)} %get-tuple-element.322), channel_id=1, source_target_pairs={{0,4},{4,0},{8,12},{12,8},{16,20},{20,16},{24,28},{28,24},{1,5},{5... | collective-permute-start | bytes 49160 | tf_op jit(solution)/shard_map/ppermute | solution.py:547
  12.7 8.5 %collective-permute-start.16 = (f32[64,128]{1,0:T(8,128)S(1)}, f32[64,128]{1,0:T(8,128)S(1)}, u32[]{:S(2)}, u32[]{:S(2)}) collective-permute-start(f32[64,128]{1,0:T(8,128)S(1)} %get-tuple-element.313), channel_id=1, source_target_pairs={{0,28},{4,8},{8,4},{12,16},{16,12},{20,24},{24,20},{28,0},{1,29},{... | collective-permute-start | bytes 98312 | tf_op jit(solution)/shard_map/ppermute | solution.py:548
  14.7 6.6 %collective-permute-start.17 = (f32[64,128]{1,0:T(8,128)S(1)}, f32[64,128]{1,0:T(8,128)S(1)}, u32[]{:S(2)}, u32[]{:S(2)}) collective-permute-start(f32[64,128]{1,0:T(8,128)S(1)} %get-tuple-element.314), channel_id=1, source_target_pairs={{0,4},{4,0},{8,12},{12,8},{16,20},{20,16},{24,28},{28,24},{1,5},{5... | collective-permute-start | bytes 98312 | tf_op jit(solution)/shard_map/ppermute | solution.py:547
  17.8 10.6 %all-to-all-start = ((f32[32,1,128]{2,1,0:T(1,128)}), f32[32,1,128]{2,1,0:T(1,128)S(1)}, u32[]{:S(2)}, u32[]{:S(2)}) async-start(f32[32,1,128]{2,1,0:T(1,128)} %bitcast.10), calls=%async_computation | async-start | bytes 32768 | tf_op jit(solution)/shard_map/all_to_all | solution.py:579

commit v17 on v16

--- a/solution.py
+++ b/solution.py
@@ -110,7 +110,7 @@
 
 def turn_kernel(
     lons, meta, facing, mine, sums, water, weights, anomaly, second, first, east_columns, west_columns,
-    ext, to_far, to_near, state_far, state_near, facing_rows, north_rows, south_rows,
+    ext, to_far, to_near, state_near, state_far, facing_rows, north_rows, south_rows,
 ):
     rows, cols = sums.shape[1], sums.shape[2]
     tall = ext.shape[1]
@@ -323,7 +323,7 @@
 
 
 def step_kernel(
-    meta, spans, facing, heat, salt, zonal, merid, water, north_came, south_rows, from_far, from_near,
+    meta, spans, facing, heat, salt, zonal, merid, water, north_came, south_rows, from_near, from_far,
     heat_out, salt_out, zonal_out, merid_out,
     new_heat, new_salt, new_zonal, new_merid, north_rows, sems,
 ):
@@ -540,14 +540,14 @@
             "row_halos",
         )(meta, facing, kept, sums, *flat_state, second, first, *columns)
 
-    ext, to_far, to_near, state_far, state_near, facing_rows, north_rows, south_rows = lax.switch(
+    ext, to_far, to_near, state_near, state_far, facing_rows, north_rows, south_rows = lax.switch(
         block, [functools.partial(exchange, s) for s in range(lons)], first, second
     )
 
     near = lambda cells: lax.ppermute(cells, "lon", [(i, i ^ 1) for i in range(lons)])
     far = lambda cells: lax.ppermute(cells, "lon", [(i, (i + 1 if i % 2 else i - 1) % lons) for i in range(lons)])
     from_far, from_near = far(to_far), near(to_near)
-    state_far, state_near = far(state_far), near(state_near)
+    state_near, state_far = near(state_near), far(state_far)
 
     (shift,) = call(shift_kernel, [(8, cols)], 60 * rows * cols, 24 * rows * cols, "basis_shift")(ext)
 
@@ -574,7 +574,7 @@
             pltpu.VMEM((deep, cols), jnp.float32),
             pltpu.SemaphoreType.DMA((4, chunks)),
         ],
-    )(meta, spans, facing, *state, water_indicator, north_rows, south_rows, state_far, state_near)
+    )(meta, spans, facing, *state, water_indicator, north_rows, south_rows, state_near, state_far)
 
     shares = lax.all_to_all(moments, axes, 0, 0, tiled=True)
     (surface,) = call(surface_kernel, [(rows, cols)], 6 * rows * cols, 16 * rows * cols, "surface")(shares, shift, base)

time: 29.4 us -> 30.2 us (1.027)
  starting transfers between devices: 13.8 us -> 14.5 us
    ppermute x2, starting transfers between devices: 0.12 us -> 2.03 us  [body(): lax.ppermute(cells, 'lon', [(i, i ^ 1) for i in range(lons)])]
    ppermute x2, starting transfers between devices: 7.06 us -> 5.2 us  [body(): lax.ppermute(cells, 'lon', [(i, (i + 1 if i % 2 else i - 1) % lons) for i...]
    all_to_all x1, starting transfers between devices: 3.5 us -> 4.09 us  [body(): shares = lax.all_to_all(moments, axes, 0, 0, tiled=True)]
  transfers between devices with their start and end apart: 7 -> 7, of which waited for: 3 -> 3; matrix products, arithmetic and copies ran while one was open for 0% -> 0% of each run, Pallas kernels for 20% -> 19%
where the time goes in v17:
time: 30.2 us; the launch traced here: 29.7 us
  starting transfers between devices  14.5 us (48%)
  Pallas kernels  7.21 us (24%)
  waiting for transfers between devices  5.94 us (20%)
  local copies, waits for them, and re-layouts  1.26 us (4%)
  between operations  0.82 us (3%)
    pallas_call x8, Pallas kernels, run(): pl.pallas_call(kernel, out_shape=[jax.ShapeDtypeStruct(shape, types) for...  7.21 us
    ppermute x2, starting transfers between devices, body(): lax.ppermute(cells, 'lon', [(i, (i + 1 if i % 2 else i - 1) % lons) for i...  5.2 us
    all_to_all x1, starting transfers between devices, body(): shares = lax.all_to_all(moments, axes, 0, 0, tiled=True)  4.09 us
    all_to_all x1, waiting for transfers between devices, body(): shares = lax.all_to_all(moments, axes, 0, 0, tiled=True)  3.27 us
    ppermute x1, starting transfers between devices, exchange(): second = lax.ppermute(second, axes, pairs_inner + pairs_fold)  3 us
    ppermute x2, starting transfers between devices, body(): lax.ppermute(cells, 'lon', [(i, i ^ 1) for i in range(lons)])  2.03 us
    ppermute x1, waiting for transfers between devices, exchange(): second = lax.ppermute(second, axes, pairs_inner + pairs_fold)  1.34 us
    ppermute x2, waiting for transfers between devices, body(): lax.ppermute(cells, 'lon', [(i, i ^ 1) for i in range(lons)])  1.32 us
  transfers between devices with their start and end apart: 7, of which 3 were waited for; matrix products, arithmetic and copies ran while one was open for 0% of the time, Pallas kernels for 19%

profile of v17, /device:TPU:0, one launch (start us, length us, event | category | flops | bytes accessed | tf_op | source)
XLA Modules:
  0.0 29.7 jit_solution(4195114187917430096)
XLA Ops:
  0.6 0.1 stack.31
  0.7 0.0 copy-start.5
  0.8 0.0 copy-start.6
  0.8 0.0 copy-start.7
  0.8 0.1 place.1.meta
  0.9 0.8 %copy-done = f32[10,64,128]{2,1,0:T(8,128)S(1)} copy-done((f32[10,64,128]{2,1,0:T(8,128)S(1)}, f32[10,64,128]{2,1,0:T(8,128)}, u32[]{:S(2)}) %copy-start) | copy-done | bytes 327704
  1.7 0.1 copy-done.1
  1.8 0.1 copy-done.3
  1.9 0.1 copy-done.4
  2.0 0.0 copy-done.2
  2.0 0.3 %level_sums.1 = (f32[3,64,128]{2,1,0:T(8,128)S(1)}, f32[64,128]{1,0:T(8,128)S(1)}, f32[64,128]{1,0:T(8,128)S(1)}, f32[64,128]{1,0:T(8,128)S(1)}) custom-call(s32[8,128]{1,0:T(8,128)S(1)} %place.1.meta, f32[1,10]{1,0:T(1,128)S(1)} %bitcast.15, s32[1,128]{1,0:T(1,128)S(1)} %bitcast.18, f32[10,64,128]{2,1,0:T(8,128)S(1)} %copy-done.3, ...), custom_call_target="tpu_custom_call" | custom-call | flops 983040 | bytes 1310720 | tf_op jit(solution)/shard_map/level_sums/pallas_call | solution.py:455
  2.4 5.2 %conditional.1 = ((f32[6,80,128]{2,1,0:T(8,128)S(1)}, f32[32,128]{1,0:T(8,128)S(1)}, f32[32,128]{1,0:T(8,128)S(1)}, f32[64,128]{1,0:T(8,128)S(1)}, f32[64,128]{1...) conditional(s32[]{:T(128)} %clamp.3, ...), branch_computations={%region_0.1_spmd, %region_1.2_spmd, %region_2.3_spmd, %region_3.4_... | conditional | flops 389120 | bytes 1900632 | solution.py:543
  2.5 3.0 %collective-permute-start.4 = (f32[64,128]{1,0:T(8,128)S(1)}, f32[64,128]{1,0:T(8,128)S(1)}, u32[]{:S(2)}, u32[]{:S(2)}) collective-permute-start(f32[64,128]{1,0:T(8,128)S(1)} %get-tuple-element.209), channel_id=1, source_target_pairs={{1,2},{2,1},{5,6},{6,5},{9,10},{10,9},{13,14},{14,13},{17,18},{18,... | collective-permute-start | bytes 98312 | tf_op jit(solution)/shard_map/cond/branch_2_fun/ppermute | solution.py:526
  5.5 0.1 collective-permute-start.5
  5.6 0.4 %columns.10 = (f32[64,128]{1,0:T(8,128)S(1)}, f32[64,128]{1,0:T(8,128)S(1)}) custom-call(f32[10,64,128]{2,1,0:T(8,128)S(1)} %get-tuple-element.211.heat, f32[10,64,128]{2,1,0:T(8,128)S(1)} %get-tuple-element.212.salt), custom_call_target="tpu_custom_call" | custom-call | flops 327680 | bytes 655360 | tf_op jit(solution)/shard_map/cond/branch_2_fun/columns/pallas_call | solution.py:455
  6.0 1.3 %collective-permute-done.4.second = f32[64,128]{1,0:T(8,128)S(1)} collective-permute-done((f32[64,128]{1,0:T(8,128)S(1)}, f32[64,128]{1,0:T(8,128)S(1)}, u32[]{:S(2)}, u32[]{:S(2)}) %collective-permute-start.4) | collective-permute-done | bytes 32800 | tf_op jit(solution)/shard_map/cond/branch_2_fun/ppermute | solution.py:526
  7.4 0.0 collective-permute-done.5.first
  7.4 0.2 row_halos.10
  7.6 5.1 %collective-permute-start.18 = (f32[32,128]{1,0:T(8,128)S(1)}, f32[32,128]{1,0:T(8,128)S(1)}, u32[]{:S(2)}, u32[]{:S(2)}) collective-permute-start(f32[32,128]{1,0:T(8,128)S(1)} %get-tuple-element.321), channel_id=1, source_target_pairs={{0,28},{4,8},{8,4},{12,16},{16,12},{20,24},{24,20},{28,0},{1,29},{... | collective-permute-start | bytes 49160 | tf_op jit(solution)/shard_map/ppermute | solution.py:548
  12.7 0.0 collective-permute-start.19
  12.7 2.0 %collective-permute-start.16 = (f32[64,128]{1,0:T(8,128)S(1)}, f32[64,128]{1,0:T(8,128)S(1)}, u32[]{:S(2)}, u32[]{:S(2)}) collective-permute-start(f32[64,128]{1,0:T(8,128)S(1)} %get-tuple-element.313), channel_id=1, source_target_pairs={{0,4},{4,0},{8,12},{12,8},{16,20},{20,16},{24,28},{28,24},{1,5},{5... | collective-permute-start | bytes 98312 | tf_op jit(solution)/shard_map/ppermute | solution.py:547
  14.8 0.1 collective-permute-start.17
  14.8 0.3 %basis_shift.1.shift = f32[8,128]{1,0:T(8,128)S(1)} custom-call(f32[6,80,128]{2,1,0:T(8,128)S(1)} %get-tuple-element.319.ext), custom_call_target="tpu_custom_call" | custom-call | flops 491520 | bytes 196608 | tf_op jit(solution)/shard_map/basis_shift/pallas_call | solution.py:455
  15.2 0.0 collective-permute-done.18.from_far
  15.2 1.3 %collective-permute-done.19.from_near = f32[32,128]{1,0:T(8,128)S(1)} collective-permute-done((f32[32,128]{1,0:T(8,128)S(1)}, f32[32,128]{1,0:T(8,128)S(1)}, u32[]{:S(2)}, u32[]{:S(2)}) %collective-permute-start.19) | collective-permute-done | bytes 16416 | tf_op jit(solution)/shard_map/ppermute | solution.py:547
  16.5 1.3 %krylov.1 = (f32[3,64,128]{2,1,0:T(8,128)S(1)}, f32[32,128]{1,0:T(8,128)}) custom-call(s32[8,128]{1,0:T(8,128)S(1)} %place.1.meta, s32[1,128]{1,0:T(1,128)S(1)} %bitcast.28, f32[8,128]{1,0:T(8,128)S(1)} %basis_shift.1.shift, f32[6,80,128]{2,1,0:T(8,128)S(1)} %get-tuple-element.319.ext, f32[24,128]{1,0:T(8,128)S(1)} %get-tuple-element.320.facing_rows, ...), custom_call_target="tpu_custom_call" | custom-call | flops 2048000 | bytes 491520 | tf_op jit(solution)/shard_map/krylov/pallas_call | solution.py:455
  17.7 4.1 %all-to-all-start = ((f32[32,1,128]{2,1,0:T(1,128)}), f32[32,1,128]{2,1,0:T(1,128)S(1)}, u32[]{:S(2)}, u32[]{:S(2)}) async-start(f32[32,1,128]{2,1,0:T(1,128)} %bitcast.10), calls=%async_computation | async-start | bytes 32768 | tf_op jit(solution)/shard_map/all_to_all | solution.py:579
  21.8 0.0 collective-permute-done.16.from_near
  21.8 0.0 collective-permute-done.17.from_far
  21.8 3.8 %levels_step.1 = (f32[10,64,128]{2,1,0:T(8,128)}, f32[10,64,128]{2,1,0:T(8,128)}, f32[10,64,128]{2,1,0:T(8,128)}, f32[10,64,128]{2,1,0:T(8,128)}) custom-call(s32[8,128]{1,0:T(8,128)S(1)} %place.1.meta, f32[1,10]{1,0:T(1,128)S(1)} %bitcast.16, s32[1,128]{1,0:T(1,128)S(1)} %bitcast.29, f32[10,64,128]{2,1,0:T(8,128)S(1)} %copy-done.3, ...), custom_call_target="tpu_custom_call" | custom-call | flops 9830400 | bytes 2621440 | tf_op jit(solution)/shard_map/levels_step/pallas_call | solution.py:455
  25.6 3.3 %all-to-all-done = f32[32,1,128]{2,1,0:T(1,128)S(1)} async-done(((f32[32,1,128]{2,1,0:T(1,128)}), f32[32,1,128]{2,1,0:T(1,128)S(1)}, u32[]{:S(2)}, u32[]{:S(2)}) %all-to-all-start) | async-done | bytes 16416 | tf_op jit(solution)/shard_map/all_to_all | solution.py:579
  28.9 0.9 %surface.1 = f32[64,128]{1,0:T(8,128)} custom-call(f32[32,128]{1,0:T(8,128)S(1)} %bitcast.14, f32[8,128]{1,0:T(8,128)S(1)} %basis_shift.1.shift, f32[3,64,128]{2,1,0:T(8,128)S(1)} %get-tuple-element.324.base), custom_call_target="tpu_custom_call" | custom-call | flops 49152 | bytes 131072 | tf_op jit(solution)/shard_map/surface/pallas_call | solution.py:455
  (10 shorter events, 0.0 us)
Async XLA Ops:
  0.7 1.0 %copy-start = (f32[10,64,128]{2,1,0:T(8,128)S(1)}, f32[10,64,128]{2,1,0:T(8,128)}, u32[]{:S(2)}) copy-start(f32[10,64,128]{2,1,0:T(8,128)} %zonal.3) | copy-start | bytes 983044
  0.7 1.1 %copy-start.1 = (f32[10,64,128]{2,1,0:T(8,128)S(1)}, f32[10,64,128]{2,1,0:T(8,128)}, u32[]{:S(2)}) copy-start(f32[10,64,128]{2,1,0:T(8,128)} %merid.3) | copy-start | bytes 983044
  0.7 1.2 %copy-start.3 = (f32[10,64,128]{2,1,0:T(8,128)S(1)}, f32[10,64,128]{2,1,0:T(8,128)}, u32[]{:S(2)}) copy-start(f32[10,64,128]{2,1,0:T(8,128)} %heat.3) | copy-start | bytes 983044
  0.7 1.3 %copy-start.4 = (f32[10,64,128]{2,1,0:T(8,128)S(1)}, f32[10,64,128]{2,1,0:T(8,128)}, u32[]{:S(2)}) copy-start(f32[10,64,128]{2,1,0:T(8,128)} %salt.3) | copy-start | bytes 983044
  0.7 1.3 %copy-start.5 = (s32[64,128]{1,0:T(8,128)S(1)}, s32[64,128]{1,0:T(8,128)}, u32[]{:S(2)}) copy-start(s32[64,128]{1,0:T(8,128)} %water.3) | copy-start | bytes 98308
  0.8 1.2 %copy-start.6 = (f32[64,128]{1,0:T(8,128)S(1)}, f32[64,128]{1,0:T(8,128)}, u32[]{:S(2)}) copy-start(f32[64,128]{1,0:T(8,128)} %weights.1) | copy-start | bytes 98308
  0.8 1.2 %copy-start.7 = (f32[64,128]{1,0:T(8,128)S(1)}, f32[64,128]{1,0:T(8,128)}, u32[]{:S(2)}) copy-start(f32[64,128]{1,0:T(8,128)} %anomaly.1) | copy-start | bytes 98308
  0.9 1.2 %copy-start.2 = (f32[10]{0:T(128)S(1)}, f32[10]{0:T(128)}, u32[]{:S(2)}) copy-start(f32[10]{0:T(128)} %param.21) | copy-start | bytes 124
  0.9 1.2 %copy-start.8 = (s32[128]{0:T(128)S(1)}, s32[128]{0:T(128)}, u32[]{:S(2)}) copy-start(s32[128]{0:T(128)} %param.23) | copy-start | bytes 1540
  2.5 4.9 %collective-permute-start.4 = (f32[64,128]{1,0:T(8,128)S(1)}, f32[64,128]{1,0:T(8,128)S(1)}, u32[]{:S(2)}, u32[]{:S(2)}) collective-permute-start(f32[64,128]{1,0:T(8,128)S(1)} %get-tuple-element.209), channel_id=1, source_target_pairs={{1,2},{2,1},{5,6},{6,5},{9,10},{10,9},{13,14},{14,13},{17,18},{18,... | collective-permute-start | bytes 98312 | tf_op jit(solution)/shard_map/cond/branch_2_fun/ppermute | solution.py:526
  5.5 1.9 %collective-permute-start.5 = (f32[64,128]{1,0:T(8,128)S(1)}, f32[64,128]{1,0:T(8,128)S(1)}, u32[]{:S(2)}, u32[]{:S(2)}) collective-permute-start(f32[64,128]{1,0:T(8,128)S(1)} %get-tuple-element.210), channel_id=1, source_target_pairs={{0,1},{1,0},{2,3},{3,2},{4,5},{5,4},{6,7},{7,6},{8,9},{9,8},{10,11... | collective-permute-start | bytes 98312 | tf_op jit(solution)/shard_map/cond/branch_2_fun/ppermute | solution.py:527
  7.6 7.5 %collective-permute-start.18 = (f32[32,128]{1,0:T(8,128)S(1)}, f32[32,128]{1,0:T(8,128)S(1)}, u32[]{:S(2)}, u32[]{:S(2)}) collective-permute-start(f32[32,128]{1,0:T(8,128)S(1)} %get-tuple-element.321), channel_id=1, source_target_pairs={{0,28},{4,8},{8,4},{12,16},{16,12},{20,24},{24,20},{28,0},{1,29},{... | collective-permute-start | bytes 49160 | tf_op jit(solution)/shard_map/ppermute | solution.py:548
  12.7 3.7 %collective-permute-start.19 = (f32[32,128]{1,0:T(8,128)S(1)}, f32[32,128]{1,0:T(8,128)S(1)}, u32[]{:S(2)}, u32[]{:S(2)}) collective-permute-start(f32[32,128]{1,0:T(8,128)S(1)} %get-tuple-element.322), channel_id=1, source_target_pairs={{0,4},{4,0},{8,12},{12,8},{16,20},{20,16},{24,28},{28,24},{1,5},{5... | collective-permute-start | bytes 49160 | tf_op jit(solution)/shard_map/ppermute | solution.py:547
  12.7 9.1 %collective-permute-start.16 = (f32[64,128]{1,0:T(8,128)S(1)}, f32[64,128]{1,0:T(8,128)S(1)}, u32[]{:S(2)}, u32[]{:S(2)}) collective-permute-start(f32[64,128]{1,0:T(8,128)S(1)} %get-tuple-element.313), channel_id=1, source_target_pairs={{0,4},{4,0},{8,12},{12,8},{16,20},{20,16},{24,28},{28,24},{1,5},{5... | collective-permute-start | bytes 98312 | tf_op jit(solution)/shard_map/ppermute | solution.py:547
  14.8 7.1 %collective-permute-start.17 = (f32[64,128]{1,0:T(8,128)S(1)}, f32[64,128]{1,0:T(8,128)S(1)}, u32[]{:S(2)}, u32[]{:S(2)}) collective-permute-start(f32[64,128]{1,0:T(8,128)S(1)} %get-tuple-element.314), channel_id=1, source_target_pairs={{0,28},{4,8},{8,4},{12,16},{16,12},{20,24},{24,20},{28,0},{1,29},{... | collective-permute-start | bytes 98312 | tf_op jit(solution)/shard_map/ppermute | solution.py:548
  17.7 11.2 %all-to-all-start = ((f32[32,1,128]{2,1,0:T(1,128)}), f32[32,1,128]{2,1,0:T(1,128)S(1)}, u32[]{:S(2)}, u32[]{:S(2)}) async-start(f32[32,1,128]{2,1,0:T(1,128)} %bitcast.10), calls=%async_computation | async-start | bytes 32768 | tf_op jit(solution)/shard_map/all_to_all | solution.py:579

commit v18 on v13

--- a/solution.py
+++ b/solution.py
@@ -103,7 +103,7 @@
 
 def turn_kernel(
     lons, meta, facing, mine, sums, water, weights, anomaly, second, first, east_columns, west_columns,
-    ext, to_far, to_near, state_far, state_near, facing_rows, north_rows, south_rows,
+    ext, to_far, to_near, state_far, facing_rows, north_rows, south_rows,
 ):
     rows, cols = sums.shape[1], sums.shape[2]
     tall = ext.shape[1]
@@ -148,14 +148,14 @@
             east = jnp.where(here, to_east, east)
             west = jnp.where(here, to_west, west)
     to_far[...] = jnp.where(lon_odd, east, west)
-    to_near[...] = jnp.where(lon_odd, west, east)
+    to_near[:half, :] = jnp.where(lon_odd, west, east)
     passed = from_second[:deep]
     spare = jnp.zeros((rows - deep, cols), jnp.float32)
     right_half = iota((rows, cols), 1) >= cols // 2
     east = jnp.where(right_half, jnp.concatenate([pltpu.roll(passed, cols // 2, 1), spare], axis=0), east_columns[...])
     west = jnp.where(right_half, jnp.concatenate([passed, spare], axis=0), west_columns[...])
     state_far[...] = jnp.where(lon_odd, east, west)
-    state_near[...] = jnp.where(lon_odd, west, east)
+    to_near[half:, :] = jnp.where(lon_odd, west, east)
     facing_rows[...] = from_second[deep:]
     north_rows[...] = north[:deep]
     south_rows[...] = south[:deep]
@@ -210,8 +210,9 @@
     rows = base.shape[1]
     size = facing_rows.shape[0]
     _, top, lon_odd, _ = flags(meta)
-    west = jnp.where(lon_odd, from_near[...], from_far[...])
-    east = jnp.where(lon_odd, from_far[...], from_near[...])
+    near = from_near[: from_far.shape[0], :]
+    west = jnp.where(lon_odd, near, from_far[...])
+    east = jnp.where(lon_odd, from_far[...], near)
     theta = shift[0:1, 0:1]
     across = fold_shift(facing)
     row = iota((size, cols), 0)
@@ -326,8 +327,9 @@
     wet = water[...].astype(jnp.float32)
     lane = iota((rows, cols), 1)
     row = iota((rows, cols), 0)
-    east = jnp.where(lon_odd, from_far[...], from_near[...])
-    west = jnp.where(lon_odd, from_near[...], from_far[...])
+    near = from_near[from_near.shape[0] - rows :, :]
+    east = jnp.where(lon_odd, from_far[...], near)
+    west = jnp.where(lon_odd, near, from_far[...])
     came = north_came[...]
     across = fold(fold_shift(facing), pltpu.roll(west[:deep], cols // 2, 1), came, east[:deep], False)
     north_rows[...] = jnp.where(top, across, came)
@@ -522,8 +524,9 @@
             functools.partial(turn_kernel, lons),
             [
                 (FIELDS, tall, cols),
-                *[(rows // 2, cols)] * 2,
-                *[(rows, cols)] * 2,
+                (rows // 2, cols),
+                (rows // 2 + rows, cols),
+                (rows, cols),
                 (high - deep, cols),
                 *[(deep, cols)] * 2,
             ],
@@ -532,14 +535,14 @@
             "row_halos",
         )(meta, facing, kept, sums, *flat_state, second, first, east_columns, west_columns)
 
-    ext, to_far, to_near, state_far, state_near, facing_rows, north_rows, south_rows = lax.switch(
+    ext, to_far, to_near, state_far, facing_rows, north_rows, south_rows = lax.switch(
         block, [functools.partial(exchange, s) for s in range(lons)], first, second
     )
 
     near = lambda cells: lax.ppermute(cells, "lon", [(i, i ^ 1) for i in range(lons)])
     far = lambda cells: lax.ppermute(cells, "lon", [(i, (i + 1 if i % 2 else i - 1) % lons) for i in range(lons)])
     from_far, from_near = far(to_far), near(to_near)
-    state_far, state_near = far(state_far), near(state_near)
+    state_far = far(state_far)
 
     (shift,) = call(shift_kernel, [(8, cols)], 60 * rows * cols, 24 * rows * cols, "basis_shift")(ext)
 
@@ -566,7 +569,7 @@
             pltpu.VMEM((deep, cols), jnp.float32),
             pltpu.SemaphoreType.DMA((4, chunks)),
         ],
-    )(meta, spans, facing, *state, water_indicator, north_rows, south_rows, state_far, state_near)
+    )(meta, spans, facing, *state, water_indicator, north_rows, south_rows, state_far, from_near)
 
     shares = lax.all_to_all(moments, axes, 0, 0, tiled=True)
     (surface,) = call(surface_kernel, [(rows, cols)], 6 * rows * cols, 16 * rows * cols, "surface")(shares, shift, base)

time: 29.5 us -> 30 us (1.017)
  starting transfers between devices: 13.7 us -> 14.3 us
    ppermute x2, starting transfers between devices: 7.06 us -> 4.72 us  [body(): lax.ppermute(cells, 'lon', [(i, (i + 1 if i % 2 else i - 1) % lons) for i...]
    ppermute x2 -> x1, starting transfers between devices: 0.12 us -> 2.09 us  [body(): lax.ppermute(cells, 'lon', [(i, i ^ 1) for i in range(lons)])]
    ppermute x2, waiting for transfers between devices: 0.01 us -> 1.41 us  [body(): lax.ppermute(cells, 'lon', [(i, (i + 1 if i % 2 else i - 1) % lons) for i...]
    ppermute x2 -> x1, waiting for transfers between devices: 1.4 us -> 0.01 us  [body(): lax.ppermute(cells, 'lon', [(i, i ^ 1) for i in range(lons)])]
    all_to_all x1, starting transfers between devices: 3.42 us -> 4.32 us  [body(): shares = lax.all_to_all(moments, axes, 0, 0, tiled=True)]
  transfers between devices with their start and end apart: 7 -> 6, of which waited for: 3 -> 3; matrix products, arithmetic and copies ran while one was open for 0% -> 0% of each run, Pallas kernels for 18% -> 18%
where the time goes in v18:
time: 30 us; the launch traced here: 29.8 us
  starting transfers between devices  14.3 us (48%)
  Pallas kernels  7 us (23%)
  waiting for transfers between devices  6.46 us (22%)
  local copies, waits for them, and re-layouts  1.26 us (4%)
  between operations  0.82 us (3%)
    pallas_call x7, Pallas kernels, run(): pl.pallas_call(kernel, out_shape=[jax.ShapeDtypeStruct(shape, types) for...  7 us
    ppermute x2, starting transfers between devices, body(): lax.ppermute(cells, 'lon', [(i, (i + 1 if i % 2 else i - 1) % lons) for i...  4.72 us
    all_to_all x1, starting transfers between devices, body(): shares = lax.all_to_all(moments, axes, 0, 0, tiled=True)  4.32 us
    all_to_all x1, waiting for transfers between devices, body(): shares = lax.all_to_all(moments, axes, 0, 0, tiled=True)  3.3 us
    ppermute x1, starting transfers between devices, exchange(): second = lax.ppermute(second, axes, pairs_inner + pairs_fold)  3 us
    ppermute x1, starting transfers between devices, body(): lax.ppermute(cells, 'lon', [(i, i ^ 1) for i in range(lons)])  2.09 us
    ppermute x1, waiting for transfers between devices, exchange(): second = lax.ppermute(second, axes, pairs_inner + pairs_fold)  1.75 us
    ppermute x2, waiting for transfers between devices, body(): lax.ppermute(cells, 'lon', [(i, (i + 1 if i % 2 else i - 1) % lons) for i...  1.41 us
  transfers between devices with their start and end apart: 6, of which 3 were waited for; matrix products, arithmetic and copies ran while one was open for 0% of the time, Pallas kernels for 18%

profile of v18, /device:TPU:0, one launch (start us, length us, event | category | flops | bytes accessed | tf_op | source)
XLA Modules:
  0.0 29.8 jit_solution(11601859763351964610)
XLA Ops:
  0.6 0.1 stack.31
  0.7 0.0 copy-start.3
  0.7 0.0 copy-start.5
  0.8 0.0 copy-start.6
  0.8 0.0 copy-start.7
  0.8 0.1 place.1.meta
  0.9 0.8 %copy-done = f32[10,64,128]{2,1,0:T(8,128)S(1)} copy-done((f32[10,64,128]{2,1,0:T(8,128)S(1)}, f32[10,64,128]{2,1,0:T(8,128)}, u32[]{:S(2)}) %copy-start) | copy-done | bytes 327704
  1.7 0.1 copy-done.1
  1.8 0.1 copy-done.2
  1.9 0.1 copy-done.3
  2.0 0.0 copy-done.5
  2.0 0.0 copy-done.6
  2.0 0.0 copy-done.4
  2.0 0.5 %level_sums.1 = (f32[3,64,128]{2,1,0:T(8,128)S(1)}, f32[64,128]{1,0:T(8,128)S(1)}, f32[64,128]{1,0:T(8,128)S(1)}, f32[64,128]{1,0:T(8,128)S(1)}, f32[64,128]{1,0:T(8,128)S(1)}, /*index=5*/f32[64,128]{1,0:T(8,128)S(1)}) custom-call(s32[8,128]{1,0:T(8,128)S(1)} %place.1.meta, f32[1,10]{1,0:T(1,128)S(1)} %bitcast.15, s32[1,128]{1,0:T(1,128)S(1)} %bitcast.18, ...), custom_call_target="tpu_custom_call" | custom-call | flops 983040 | bytes 1310720 | tf_op jit(solution)/shard_map/level_sums/pallas_call | solution.py:450
  2.6 5.2 %conditional.1 = ((f32[6,80,128]{2,1,0:T(8,128)S(1)}, f32[32,128]{1,0:T(8,128)S(1)}, f32[96,128]{1,0:T(8,128)S(1)}, f32[64,128]{1,0:T(8,128)S(1)}, f32[24,128]{1...) conditional(s32[]{:T(128)} %clamp.3, (f32[64,128]{1,0:T(8,128)S(1)}, ...), branch_computations={%region_0.1_spmd, %region_1.2_spmd, %region_2.3_spmd, %region_3.4_... | conditional | flops 61440 | bytes 1245272 | solution.py:538
  2.7 3.0 %collective-permute-start.10 = (f32[64,128]{1,0:T(8,128)S(1)}, f32[64,128]{1,0:T(8,128)S(1)}, u32[]{:S(2)}, u32[]{:S(2)}) collective-permute-start(f32[64,128]{1,0:T(8,128)S(1)} %get-tuple-element.238), channel_id=1, source_target_pairs={{1,2},{2,1},{5,6},{6,5},{9,10},{10,9},{13,14},{14,13},{17,18},{18,... | collective-permute-start | bytes 98312 | tf_op jit(solution)/shard_map/cond/branch_5_fun/ppermute | solution.py:521
  5.7 0.1 collective-permute-start.11
  5.8 1.8 %collective-permute-done.10.second = f32[64,128]{1,0:T(8,128)S(1)} collective-permute-done((f32[64,128]{1,0:T(8,128)S(1)}, f32[64,128]{1,0:T(8,128)S(1)}, u32[]{:S(2)}, u32[]{:S(2)}) %collective-permute-start.10) | collective-permute-done | bytes 32800 | tf_op jit(solution)/shard_map/cond/branch_5_fun/ppermute | solution.py:521
  7.6 0.0 collective-permute-done.11.first
  7.6 0.2 row_halos.13
  7.8 2.1 %collective-permute-start.17 = (f32[96,128]{1,0:T(8,128)S(1)}, f32[96,128]{1,0:T(8,128)S(1)}, u32[]{:S(2)}, u32[]{:S(2)}) collective-permute-start(f32[96,128]{1,0:T(8,128)S(1)} %get-tuple-element.301), channel_id=1, source_target_pairs={{0,4},{4,0},{8,12},{12,8},{16,20},{20,16},{24,28},{28,24},{1,5},{5... | collective-permute-start | bytes 147464 | tf_op jit(solution)/shard_map/ppermute | solution.py:542
  9.9 3.6 %collective-permute-start.18 = (f32[32,128]{1,0:T(8,128)S(1)}, f32[32,128]{1,0:T(8,128)S(1)}, u32[]{:S(2)}, u32[]{:S(2)}) collective-permute-start(f32[32,128]{1,0:T(8,128)S(1)} %get-tuple-element.308), channel_id=1, source_target_pairs={{0,28},{4,8},{8,4},{12,16},{16,12},{20,24},{24,20},{28,0},{1,29},{... | collective-permute-start | bytes 49160 | tf_op jit(solution)/shard_map/ppermute | solution.py:543
  13.5 1.1 %collective-permute-start.16 = (f32[64,128]{1,0:T(8,128)S(1)}, f32[64,128]{1,0:T(8,128)S(1)}, u32[]{:S(2)}, u32[]{:S(2)}) collective-permute-start(f32[64,128]{1,0:T(8,128)S(1)} %get-tuple-element.300), channel_id=1, source_target_pairs={{0,28},{4,8},{8,4},{12,16},{16,12},{20,24},{24,20},{28,0},{1,29},{... | collective-permute-start | bytes 98312 | tf_op jit(solution)/shard_map/ppermute | solution.py:543
  14.6 0.3 %basis_shift.1.shift = f32[8,128]{1,0:T(8,128)S(1)} custom-call(f32[6,80,128]{2,1,0:T(8,128)S(1)} %get-tuple-element.306.ext), custom_call_target="tpu_custom_call" | custom-call | flops 491520 | bytes 196608 | tf_op jit(solution)/shard_map/basis_shift/pallas_call | solution.py:450
  14.9 1.4 %collective-permute-done.18.from_far = f32[32,128]{1,0:T(8,128)S(1)} collective-permute-done((f32[32,128]{1,0:T(8,128)S(1)}, f32[32,128]{1,0:T(8,128)S(1)}, u32[]{:S(2)}, u32[]{:S(2)}) %collective-permute-start.18) | collective-permute-done | bytes 16416 | tf_op jit(solution)/shard_map/ppermute | solution.py:543
  16.3 0.0 collective-permute-done.17.from_near
  16.3 1.3 %krylov.1 = (f32[3,64,128]{2,1,0:T(8,128)S(1)}, f32[32,128]{1,0:T(8,128)}) custom-call(s32[8,128]{1,0:T(8,128)S(1)} %place.1.meta, s32[1,128]{1,0:T(1,128)S(1)} %bitcast.28, f32[8,128]{1,0:T(8,128)S(1)} %basis_shift.1.shift, f32[6,80,128]{2,1,0:T(8,128)S(1)} %get-tuple-element.306.ext, f32[24,128]{1,0:T(8,128)S(1)} %get-tuple-element.307.facing_rows, ...), custom_call_target="tpu_custom_call" | custom-call | flops 2048000 | bytes 491520 | tf_op jit(solution)/shard_map/krylov/pallas_call | solution.py:450
  17.6 4.3 %all-to-all-start = ((f32[32,1,128]{2,1,0:T(1,128)}), f32[32,1,128]{2,1,0:T(1,128)S(1)}, u32[]{:S(2)}, u32[]{:S(2)}) async-start(f32[32,1,128]{2,1,0:T(1,128)} %bitcast.10), calls=%async_computation | async-start | bytes 32768 | tf_op jit(solution)/shard_map/all_to_all | solution.py:574
  21.9 0.0 collective-permute-done.16.from_far
  21.9 3.8 %levels_step.1 = (f32[10,64,128]{2,1,0:T(8,128)}, f32[10,64,128]{2,1,0:T(8,128)}, f32[10,64,128]{2,1,0:T(8,128)}, f32[10,64,128]{2,1,0:T(8,128)}) custom-call(s32[8,128]{1,0:T(8,128)S(1)} %place.1.meta, f32[1,10]{1,0:T(1,128)S(1)} %bitcast.16, s32[1,128]{1,0:T(1,128)S(1)} %bitcast.29, f32[10,64,128]{2,1,0:T(8,128)S(1)} %copy-done, ...), custom_call_target="tpu_custom_call" | custom-call | flops 9830400 | bytes 2621440 | tf_op jit(solution)/shard_map/levels_step/pallas_call | solution.py:450
  25.7 3.3 %all-to-all-done = f32[32,1,128]{2,1,0:T(1,128)S(1)} async-done(((f32[32,1,128]{2,1,0:T(1,128)}), f32[32,1,128]{2,1,0:T(1,128)S(1)}, u32[]{:S(2)}, u32[]{:S(2)}) %all-to-all-start) | async-done | bytes 16416 | tf_op jit(solution)/shard_map/all_to_all | solution.py:574
  29.0 0.9 %surface.1 = f32[64,128]{1,0:T(8,128)} custom-call(f32[32,128]{1,0:T(8,128)S(1)} %bitcast.14, f32[8,128]{1,0:T(8,128)S(1)} %basis_shift.1.shift, f32[3,64,128]{2,1,0:T(8,128)S(1)} %get-tuple-element.310.base), custom_call_target="tpu_custom_call" | custom-call | flops 49152 | bytes 131072 | tf_op jit(solution)/shard_map/surface/pallas_call | solution.py:450
  (7 shorter events, 0.0 us)
Async XLA Ops:
  0.7 1.0 %copy-start = (f32[10,64,128]{2,1,0:T(8,128)S(1)}, f32[10,64,128]{2,1,0:T(8,128)}, u32[]{:S(2)}) copy-start(f32[10,64,128]{2,1,0:T(8,128)} %heat.3) | copy-start | bytes 983044
  0.7 1.1 %copy-start.1 = (f32[10,64,128]{2,1,0:T(8,128)S(1)}, f32[10,64,128]{2,1,0:T(8,128)}, u32[]{:S(2)}) copy-start(f32[10,64,128]{2,1,0:T(8,128)} %salt.3) | copy-start | bytes 983044
  0.7 1.2 %copy-start.2 = (f32[10,64,128]{2,1,0:T(8,128)S(1)}, f32[10,64,128]{2,1,0:T(8,128)}, u32[]{:S(2)}) copy-start(f32[10,64,128]{2,1,0:T(8,128)} %zonal.3) | copy-start | bytes 983044
  0.7 1.3 %copy-start.3 = (f32[10,64,128]{2,1,0:T(8,128)S(1)}, f32[10,64,128]{2,1,0:T(8,128)}, u32[]{:S(2)}) copy-start(f32[10,64,128]{2,1,0:T(8,128)} %merid.3) | copy-start | bytes 983044
  0.7 1.3 %copy-start.5 = (s32[64,128]{1,0:T(8,128)S(1)}, s32[64,128]{1,0:T(8,128)}, u32[]{:S(2)}) copy-start(s32[64,128]{1,0:T(8,128)} %water.3) | copy-start | bytes 98308
  0.8 1.2 %copy-start.6 = (f32[64,128]{1,0:T(8,128)S(1)}, f32[64,128]{1,0:T(8,128)}, u32[]{:S(2)}) copy-start(f32[64,128]{1,0:T(8,128)} %weights.1) | copy-start | bytes 98308
  0.8 1.2 %copy-start.7 = (f32[64,128]{1,0:T(8,128)S(1)}, f32[64,128]{1,0:T(8,128)}, u32[]{:S(2)}) copy-start(f32[64,128]{1,0:T(8,128)} %anomaly.1) | copy-start | bytes 98308
  0.9 1.2 %copy-start.4 = (f32[10]{0:T(128)S(1)}, f32[10]{0:T(128)}, u32[]{:S(2)}) copy-start(f32[10]{0:T(128)} %param.21) | copy-start | bytes 124
  0.9 1.2 %copy-start.8 = (s32[128]{0:T(128)S(1)}, s32[128]{0:T(128)}, u32[]{:S(2)}) copy-start(s32[128]{0:T(128)} %param.23) | copy-start | bytes 1540
  2.7 4.9 %collective-permute-start.10 = (f32[64,128]{1,0:T(8,128)S(1)}, f32[64,128]{1,0:T(8,128)S(1)}, u32[]{:S(2)}, u32[]{:S(2)}) collective-permute-start(f32[64,128]{1,0:T(8,128)S(1)} %get-tuple-element.238), channel_id=1, source_target_pairs={{1,2},{2,1},{5,6},{6,5},{9,10},{10,9},{13,14},{14,13},{17,18},{18,... | collective-permute-start | bytes 98312 | tf_op jit(solution)/shard_map/cond/branch_5_fun/ppermute | solution.py:521
  5.7 1.9 %collective-permute-start.11 = (f32[64,128]{1,0:T(8,128)S(1)}, f32[64,128]{1,0:T(8,128)S(1)}, u32[]{:S(2)}, u32[]{:S(2)}) collective-permute-start(f32[64,128]{1,0:T(8,128)S(1)} %get-tuple-element.239), channel_id=1, source_target_pairs={{0,1},{1,0},{2,3},{3,2},{4,5},{5,4},{6,7},{7,6},{8,9},{9,8},{10,11... | collective-permute-start | bytes 98312 | tf_op jit(solution)/shard_map/cond/branch_5_fun/ppermute | solution.py:522
  7.8 8.5 %collective-permute-start.17 = (f32[96,128]{1,0:T(8,128)S(1)}, f32[96,128]{1,0:T(8,128)S(1)}, u32[]{:S(2)}, u32[]{:S(2)}) collective-permute-start(f32[96,128]{1,0:T(8,128)S(1)} %get-tuple-element.301), channel_id=1, source_target_pairs={{0,4},{4,0},{8,12},{12,8},{16,20},{20,16},{24,28},{28,24},{1,5},{5... | collective-permute-start | bytes 147464 | tf_op jit(solution)/shard_map/ppermute | solution.py:542
  9.9 6.4 %collective-permute-start.18 = (f32[32,128]{1,0:T(8,128)S(1)}, f32[32,128]{1,0:T(8,128)S(1)}, u32[]{:S(2)}, u32[]{:S(2)}) collective-permute-start(f32[32,128]{1,0:T(8,128)S(1)} %get-tuple-element.308), channel_id=1, source_target_pairs={{0,28},{4,8},{8,4},{12,16},{16,12},{20,24},{24,20},{28,0},{1,29},{... | collective-permute-start | bytes 49160 | tf_op jit(solution)/shard_map/ppermute | solution.py:543
  13.5 8.4 %collective-permute-start.16 = (f32[64,128]{1,0:T(8,128)S(1)}, f32[64,128]{1,0:T(8,128)S(1)}, u32[]{:S(2)}, u32[]{:S(2)}) collective-permute-start(f32[64,128]{1,0:T(8,128)S(1)} %get-tuple-element.300), channel_id=1, source_target_pairs={{0,28},{4,8},{8,4},{12,16},{16,12},{20,24},{24,20},{28,0},{1,29},{... | collective-permute-start | bytes 98312 | tf_op jit(solution)/shard_map/ppermute | solution.py:543
  17.6 11.4 %all-to-all-start = ((f32[32,1,128]{2,1,0:T(1,128)}), f32[32,1,128]{2,1,0:T(1,128)S(1)}, u32[]{:S(2)}, u32[]{:S(2)}) async-start(f32[32,1,128]{2,1,0:T(1,128)} %bitcast.10), calls=%async_computation | async-start | bytes 32768 | tf_op jit(solution)/shard_map/all_to_all | solution.py:574

commit v19 on v13

--- a/solution.py
+++ b/solution.py
@@ -103,7 +103,7 @@
 
 def turn_kernel(
     lons, meta, facing, mine, sums, water, weights, anomaly, second, first, east_columns, west_columns,
-    ext, to_far, to_near, state_far, state_near, facing_rows, north_rows, south_rows,
+    ext, to_far, to_near, state_near, facing_rows, north_rows, south_rows,
 ):
     rows, cols = sums.shape[1], sums.shape[2]
     tall = ext.shape[1]
@@ -147,14 +147,14 @@
                 to_west = jnp.concatenate([empty, to_west], axis=0)
             east = jnp.where(here, to_east, east)
             west = jnp.where(here, to_west, west)
-    to_far[...] = jnp.where(lon_odd, east, west)
+    to_far[:half, :] = jnp.where(lon_odd, east, west)
     to_near[...] = jnp.where(lon_odd, west, east)
     passed = from_second[:deep]
     spare = jnp.zeros((rows - deep, cols), jnp.float32)
     right_half = iota((rows, cols), 1) >= cols // 2
     east = jnp.where(right_half, jnp.concatenate([pltpu.roll(passed, cols // 2, 1), spare], axis=0), east_columns[...])
     west = jnp.where(right_half, jnp.concatenate([passed, spare], axis=0), west_columns[...])
-    state_far[...] = jnp.where(lon_odd, east, west)
+    to_far[half:, :] = jnp.where(lon_odd, east, west)
     state_near[...] = jnp.where(lon_odd, west, east)
     facing_rows[...] = from_second[deep:]
     north_rows[...] = north[:deep]
@@ -210,8 +210,9 @@
     rows = base.shape[1]
     size = facing_rows.shape[0]
     _, top, lon_odd, _ = flags(meta)
-    west = jnp.where(lon_odd, from_near[...], from_far[...])
-    east = jnp.where(lon_odd, from_far[...], from_near[...])
+    far = from_far[: from_near.shape[0], :]
+    west = jnp.where(lon_odd, from_near[...], far)
+    east = jnp.where(lon_odd, far, from_near[...])
     theta = shift[0:1, 0:1]
     across = fold_shift(facing)
     row = iota((size, cols), 0)
@@ -326,8 +327,9 @@
     wet = water[...].astype(jnp.float32)
     lane = iota((rows, cols), 1)
     row = iota((rows, cols), 0)
-    east = jnp.where(lon_odd, from_far[...], from_near[...])
-    west = jnp.where(lon_odd, from_near[...], from_far[...])
+    far = from_far[from_far.shape[0] - rows :, :]
+    east = jnp.where(lon_odd, far, from_near[...])
+    west = jnp.where(lon_odd, from_near[...], far)
     came = north_came[...]
     across = fold(fold_shift(facing), pltpu.roll(west[:deep], cols // 2, 1), came, east[:deep], False)
     north_rows[...] = jnp.where(top, across, came)
@@ -522,8 +524,9 @@
             functools.partial(turn_kernel, lons),
             [
                 (FIELDS, tall, cols),
-                *[(rows // 2, cols)] * 2,
-                *[(rows, cols)] * 2,
+                (rows // 2 + rows, cols),
+                (rows // 2, cols),
+                (rows, cols),
                 (high - deep, cols),
                 *[(deep, cols)] * 2,
             ],
@@ -532,14 +535,14 @@
             "row_halos",
         )(meta, facing, kept, sums, *flat_state, second, first, east_columns, west_columns)
 
-    ext, to_far, to_near, state_far, state_near, facing_rows, north_rows, south_rows = lax.switch(
+    ext, to_far, to_near, state_near, facing_rows, north_rows, south_rows = lax.switch(
         block, [functools.partial(exchange, s) for s in range(lons)], first, second
     )
 
     near = lambda cells: lax.ppermute(cells, "lon", [(i, i ^ 1) for i in range(lons)])
     far = lambda cells: lax.ppermute(cells, "lon", [(i, (i + 1 if i % 2 else i - 1) % lons) for i in range(lons)])
     from_far, from_near = far(to_far), near(to_near)
-    state_far, state_near = far(state_far), near(state_near)
+    state_near = near(state_near)
 
     (shift,) = call(shift_kernel, [(8, cols)], 60 * rows * cols, 24 * rows * cols, "basis_shift")(ext)
 
@@ -566,7 +569,7 @@
             pltpu.VMEM((deep, cols), jnp.float32),
             pltpu.SemaphoreType.DMA((4, chunks)),
         ],
-    )(meta, spans, facing, *state, water_indicator, north_rows, south_rows, state_far, state_near)
+    )(meta, spans, facing, *state, water_indicator, north_rows, south_rows, from_far, state_near)
 
     shares = lax.all_to_all(moments, axes, 0, 0, tiled=True)
     (surface,) = call(surface_kernel, [(rows, cols)], 6 * rows * cols, 16 * rows * cols, "surface")(shares, shift, base)

time: 29.5 us -> 29.8 us (1.010)
  starting transfers between devices: 13.7 us -> 14.1 us
    ppermute x2 -> x1, starting transfers between devices: 7.06 us -> 5.12 us  [body(): lax.ppermute(cells, 'lon', [(i, (i + 1 if i % 2 else i - 1) % lons) for i...]
    ppermute x2, starting transfers between devices: 0.12 us -> 2.03 us  [body(): lax.ppermute(cells, 'lon', [(i, i ^ 1) for i in range(lons)])]
    all_to_all x1, starting transfers between devices: 3.42 us -> 3.79 us  [body(): shares = lax.all_to_all(moments, axes, 0, 0, tiled=True)]
  transfers between devices with their start and end apart: 7 -> 6, of which waited for: 3 -> 3; matrix products, arithmetic and copies ran while one was open for 0% -> 0% of each run, Pallas kernels for 18% -> 18%
where the time goes in v19:
time: 29.8 us; the launch traced here: 29.7 us
  starting transfers between devices  14.1 us (47%)
  Pallas kernels  7 us (23%)
  waiting for transfers between devices  6.46 us (22%)
  local copies, waits for them, and re-layouts  1.26 us (4%)
  between operations  0.82 us (3%)
    pallas_call x7, Pallas kernels, run(): pl.pallas_call(kernel, out_shape=[jax.ShapeDtypeStruct(shape, types) for...  7 us
    ppermute x1, starting transfers between devices, body(): lax.ppermute(cells, 'lon', [(i, (i + 1 if i % 2 else i - 1) % lons) for i...  5.12 us
    all_to_all x1, starting transfers between devices, body(): shares = lax.all_to_all(moments, axes, 0, 0, tiled=True)  3.79 us
    all_to_all x1, waiting for transfers between devices, body(): shares = lax.all_to_all(moments, axes, 0, 0, tiled=True)  3.3 us
    ppermute x1, starting transfers between devices, exchange(): second = lax.ppermute(second, axes, pairs_inner + pairs_fold)  3 us
    ppermute x2, starting transfers between devices, body(): lax.ppermute(cells, 'lon', [(i, i ^ 1) for i in range(lons)])  2.03 us
    ppermute x1, waiting for transfers between devices, exchange(): second = lax.ppermute(second, axes, pairs_inner + pairs_fold)  1.75 us
    ppermute x2, waiting for transfers between devices, body(): lax.ppermute(cells, 'lon', [(i, i ^ 1) for i in range(lons)])  1.41 us
  transfers between devices with their start and end apart: 6, of which 3 were waited for; matrix products, arithmetic and copies ran while one was open for 0% of the time, Pallas kernels for 18%

profile of v19, /device:TPU:0, one launch (start us, length us, event | category | flops | bytes accessed | tf_op | source)
XLA Modules:
  0.0 29.7 jit_solution(8062274332144218350)
XLA Ops:
  0.6 0.1 stack.31
  0.7 0.0 copy-start.3
  0.7 0.0 copy-start.5
  0.8 0.0 copy-start.6
  0.8 0.0 copy-start.7
  0.8 0.1 place.1.meta
  0.9 0.8 %copy-done = f32[10,64,128]{2,1,0:T(8,128)S(1)} copy-done((f32[10,64,128]{2,1,0:T(8,128)S(1)}, f32[10,64,128]{2,1,0:T(8,128)}, u32[]{:S(2)}) %copy-start) | copy-done | bytes 327704
  1.7 0.1 copy-done.1
  1.8 0.1 copy-done.2
  1.9 0.1 copy-done.3
  2.0 0.0 copy-done.5
  2.0 0.0 copy-done.6
  2.0 0.0 copy-done.4
  2.0 0.5 %level_sums.1 = (f32[3,64,128]{2,1,0:T(8,128)S(1)}, f32[64,128]{1,0:T(8,128)S(1)}, f32[64,128]{1,0:T(8,128)S(1)}, f32[64,128]{1,0:T(8,128)S(1)}, f32[64,128]{1,0:T(8,128)S(1)}, /*index=5*/f32[64,128]{1,0:T(8,128)S(1)}) custom-call(s32[8,128]{1,0:T(8,128)S(1)} %place.1.meta, f32[1,10]{1,0:T(1,128)S(1)} %bitcast.15, s32[1,128]{1,0:T(1,128)S(1)} %bitcast.18, ...), custom_call_target="tpu_custom_call" | custom-call | flops 983040 | bytes 1310720 | tf_op jit(solution)/shard_map/level_sums/pallas_call | solution.py:450
  2.6 5.2 %conditional.1 = ((f32[6,80,128]{2,1,0:T(8,128)S(1)}, f32[96,128]{1,0:T(8,128)S(1)}, f32[32,128]{1,0:T(8,128)S(1)}, f32[64,128]{1,0:T(8,128)S(1)}, f32[24,128]{1...) conditional(s32[]{:T(128)} %clamp.3, (f32[64,128]{1,0:T(8,128)S(1)}, ...), branch_computations={%region_0.1_spmd, %region_1.2_spmd, %region_2.3_spmd, %region_3.4_... | conditional | flops 61440 | bytes 1245272 | solution.py:538
  2.7 3.0 %collective-permute-start.10 = (f32[64,128]{1,0:T(8,128)S(1)}, f32[64,128]{1,0:T(8,128)S(1)}, u32[]{:S(2)}, u32[]{:S(2)}) collective-permute-start(f32[64,128]{1,0:T(8,128)S(1)} %get-tuple-element.238), channel_id=1, source_target_pairs={{1,2},{2,1},{5,6},{6,5},{9,10},{10,9},{13,14},{14,13},{17,18},{18,... | collective-permute-start | bytes 98312 | tf_op jit(solution)/shard_map/cond/branch_5_fun/ppermute | solution.py:521
  5.7 0.1 collective-permute-start.11
  5.8 1.8 %collective-permute-done.10.second = f32[64,128]{1,0:T(8,128)S(1)} collective-permute-done((f32[64,128]{1,0:T(8,128)S(1)}, f32[64,128]{1,0:T(8,128)S(1)}, u32[]{:S(2)}, u32[]{:S(2)}) %collective-permute-start.10) | collective-permute-done | bytes 32800 | tf_op jit(solution)/shard_map/cond/branch_5_fun/ppermute | solution.py:521
  7.6 0.0 collective-permute-done.11.first
  7.6 0.2 row_halos.13
  7.8 5.1 %collective-permute-start.16 = (f32[96,128]{1,0:T(8,128)S(1)}, f32[96,128]{1,0:T(8,128)S(1)}, u32[]{:S(2)}, u32[]{:S(2)}) collective-permute-start(f32[96,128]{1,0:T(8,128)S(1)} %get-tuple-element.300), channel_id=1, source_target_pairs={{0,28},{4,8},{8,4},{12,16},{16,12},{20,24},{24,20},{28,0},{1,29},{... | collective-permute-start | bytes 147464 | tf_op jit(solution)/shard_map/ppermute | solution.py:543
  12.9 0.0 collective-permute-start.18
  12.9 2.0 %collective-permute-start.17 = (f32[64,128]{1,0:T(8,128)S(1)}, f32[64,128]{1,0:T(8,128)S(1)}, u32[]{:S(2)}, u32[]{:S(2)}) collective-permute-start(f32[64,128]{1,0:T(8,128)S(1)} %get-tuple-element.301), channel_id=1, source_target_pairs={{0,4},{4,0},{8,12},{12,8},{16,20},{20,16},{24,28},{28,24},{1,5},{5... | collective-permute-start | bytes 98312 | tf_op jit(solution)/shard_map/ppermute | solution.py:542
  15.0 0.3 %basis_shift.1.shift = f32[8,128]{1,0:T(8,128)S(1)} custom-call(f32[6,80,128]{2,1,0:T(8,128)S(1)} %get-tuple-element.306.ext), custom_call_target="tpu_custom_call" | custom-call | flops 491520 | bytes 196608 | tf_op jit(solution)/shard_map/basis_shift/pallas_call | solution.py:450
  15.3 1.4 %collective-permute-done.18.from_near = f32[32,128]{1,0:T(8,128)S(1)} collective-permute-done((f32[32,128]{1,0:T(8,128)S(1)}, f32[32,128]{1,0:T(8,128)S(1)}, u32[]{:S(2)}, u32[]{:S(2)}) %collective-permute-start.18) | collective-permute-done | bytes 16416 | tf_op jit(solution)/shard_map/ppermute | solution.py:542
  16.7 0.0 collective-permute-done.16.from_far
  16.7 1.3 %krylov.1 = (f32[3,64,128]{2,1,0:T(8,128)S(1)}, f32[32,128]{1,0:T(8,128)}) custom-call(s32[8,128]{1,0:T(8,128)S(1)} %place.1.meta, s32[1,128]{1,0:T(1,128)S(1)} %bitcast.28, f32[8,128]{1,0:T(8,128)S(1)} %basis_shift.1.shift, f32[6,80,128]{2,1,0:T(8,128)S(1)} %get-tuple-element.306.ext, f32[24,128]{1,0:T(8,128)S(1)} %get-tuple-element.307.facing_rows, ...), custom_call_target="tpu_custom_call" | custom-call | flops 2048000 | bytes 491520 | tf_op jit(solution)/shard_map/krylov/pallas_call | solution.py:450
  17.9 3.8 %all-to-all-start = ((f32[32,1,128]{2,1,0:T(1,128)}), f32[32,1,128]{2,1,0:T(1,128)S(1)}, u32[]{:S(2)}, u32[]{:S(2)}) async-start(f32[32,1,128]{2,1,0:T(1,128)} %bitcast.10), calls=%async_computation | async-start | bytes 32768 | tf_op jit(solution)/shard_map/all_to_all | solution.py:574
  21.7 0.0 collective-permute-done.17.from_near
  21.7 3.8 %levels_step.1 = (f32[10,64,128]{2,1,0:T(8,128)}, f32[10,64,128]{2,1,0:T(8,128)}, f32[10,64,128]{2,1,0:T(8,128)}, f32[10,64,128]{2,1,0:T(8,128)}) custom-call(s32[8,128]{1,0:T(8,128)S(1)} %place.1.meta, f32[1,10]{1,0:T(1,128)S(1)} %bitcast.16, s32[1,128]{1,0:T(1,128)S(1)} %bitcast.29, f32[10,64,128]{2,1,0:T(8,128)S(1)} %copy-done, ...), custom_call_target="tpu_custom_call" | custom-call | flops 9830400 | bytes 2621440 | tf_op jit(solution)/shard_map/levels_step/pallas_call | solution.py:450
  25.5 3.3 %all-to-all-done = f32[32,1,128]{2,1,0:T(1,128)S(1)} async-done(((f32[32,1,128]{2,1,0:T(1,128)}), f32[32,1,128]{2,1,0:T(1,128)S(1)}, u32[]{:S(2)}, u32[]{:S(2)}) %all-to-all-start) | async-done | bytes 16416 | tf_op jit(solution)/shard_map/all_to_all | solution.py:574
  28.8 0.9 %surface.1 = f32[64,128]{1,0:T(8,128)} custom-call(f32[32,128]{1,0:T(8,128)S(1)} %bitcast.14, f32[8,128]{1,0:T(8,128)S(1)} %basis_shift.1.shift, f32[3,64,128]{2,1,0:T(8,128)S(1)} %get-tuple-element.310.base), custom_call_target="tpu_custom_call" | custom-call | flops 49152 | bytes 131072 | tf_op jit(solution)/shard_map/surface/pallas_call | solution.py:450
  (7 shorter events, 0.0 us)
Async XLA Ops:
  0.7 1.0 %copy-start = (f32[10,64,128]{2,1,0:T(8,128)S(1)}, f32[10,64,128]{2,1,0:T(8,128)}, u32[]{:S(2)}) copy-start(f32[10,64,128]{2,1,0:T(8,128)} %heat.3) | copy-start | bytes 983044
  0.7 1.1 %copy-start.1 = (f32[10,64,128]{2,1,0:T(8,128)S(1)}, f32[10,64,128]{2,1,0:T(8,128)}, u32[]{:S(2)}) copy-start(f32[10,64,128]{2,1,0:T(8,128)} %salt.3) | copy-start | bytes 983044
  0.7 1.2 %copy-start.2 = (f32[10,64,128]{2,1,0:T(8,128)S(1)}, f32[10,64,128]{2,1,0:T(8,128)}, u32[]{:S(2)}) copy-start(f32[10,64,128]{2,1,0:T(8,128)} %zonal.3) | copy-start | bytes 983044
  0.7 1.3 %copy-start.3 = (f32[10,64,128]{2,1,0:T(8,128)S(1)}, f32[10,64,128]{2,1,0:T(8,128)}, u32[]{:S(2)}) copy-start(f32[10,64,128]{2,1,0:T(8,128)} %merid.3) | copy-start | bytes 983044
  0.7 1.3 %copy-start.5 = (s32[64,128]{1,0:T(8,128)S(1)}, s32[64,128]{1,0:T(8,128)}, u32[]{:S(2)}) copy-start(s32[64,128]{1,0:T(8,128)} %water.3) | copy-start | bytes 98308
  0.8 1.2 %copy-start.6 = (f32[64,128]{1,0:T(8,128)S(1)}, f32[64,128]{1,0:T(8,128)}, u32[]{:S(2)}) copy-start(f32[64,128]{1,0:T(8,128)} %weights.1) | copy-start | bytes 98308
  0.8 1.2 %copy-start.7 = (f32[64,128]{1,0:T(8,128)S(1)}, f32[64,128]{1,0:T(8,128)}, u32[]{:S(2)}) copy-start(f32[64,128]{1,0:T(8,128)} %anomaly.1) | copy-start | bytes 98308
  0.9 1.2 %copy-start.4 = (f32[10]{0:T(128)S(1)}, f32[10]{0:T(128)}, u32[]{:S(2)}) copy-start(f32[10]{0:T(128)} %param.21) | copy-start | bytes 124
  0.9 1.2 %copy-start.8 = (s32[128]{0:T(128)S(1)}, s32[128]{0:T(128)}, u32[]{:S(2)}) copy-start(s32[128]{0:T(128)} %param.23) | copy-start | bytes 1540
  2.7 4.9 %collective-permute-start.10 = (f32[64,128]{1,0:T(8,128)S(1)}, f32[64,128]{1,0:T(8,128)S(1)}, u32[]{:S(2)}, u32[]{:S(2)}) collective-permute-start(f32[64,128]{1,0:T(8,128)S(1)} %get-tuple-element.238), channel_id=1, source_target_pairs={{1,2},{2,1},{5,6},{6,5},{9,10},{10,9},{13,14},{14,13},{17,18},{18,... | collective-permute-start | bytes 98312 | tf_op jit(solution)/shard_map/cond/branch_5_fun/ppermute | solution.py:521
  5.7 1.9 %collective-permute-start.11 = (f32[64,128]{1,0:T(8,128)S(1)}, f32[64,128]{1,0:T(8,128)S(1)}, u32[]{:S(2)}, u32[]{:S(2)}) collective-permute-start(f32[64,128]{1,0:T(8,128)S(1)} %get-tuple-element.239), channel_id=1, source_target_pairs={{0,1},{1,0},{2,3},{3,2},{4,5},{5,4},{6,7},{7,6},{8,9},{9,8},{10,11... | collective-permute-start | bytes 98312 | tf_op jit(solution)/shard_map/cond/branch_5_fun/ppermute | solution.py:522
  7.8 8.9 %collective-permute-start.16 = (f32[96,128]{1,0:T(8,128)S(1)}, f32[96,128]{1,0:T(8,128)S(1)}, u32[]{:S(2)}, u32[]{:S(2)}) collective-permute-start(f32[96,128]{1,0:T(8,128)S(1)} %get-tuple-element.300), channel_id=1, source_target_pairs={{0,28},{4,8},{8,4},{12,16},{16,12},{20,24},{24,20},{28,0},{1,29},{... | collective-permute-start | bytes 147464 | tf_op jit(solution)/shard_map/ppermute | solution.py:543
  12.9 3.7 %collective-permute-start.18 = (f32[32,128]{1,0:T(8,128)S(1)}, f32[32,128]{1,0:T(8,128)S(1)}, u32[]{:S(2)}, u32[]{:S(2)}) collective-permute-start(f32[32,128]{1,0:T(8,128)S(1)} %get-tuple-element.308), channel_id=1, source_target_pairs={{0,4},{4,0},{8,12},{12,8},{16,20},{20,16},{24,28},{28,24},{1,5},{5... | collective-permute-start | bytes 49160 | tf_op jit(solution)/shard_map/ppermute | solution.py:542
  12.9 8.8 %collective-permute-start.17 = (f32[64,128]{1,0:T(8,128)S(1)}, f32[64,128]{1,0:T(8,128)S(1)}, u32[]{:S(2)}, u32[]{:S(2)}) collective-permute-start(f32[64,128]{1,0:T(8,128)S(1)} %get-tuple-element.301), channel_id=1, source_target_pairs={{0,4},{4,0},{8,12},{12,8},{16,20},{20,16},{24,28},{28,24},{1,5},{5... | collective-permute-start | bytes 98312 | tf_op jit(solution)/shard_map/ppermute | solution.py:542
  17.9 10.9 %all-to-all-start = ((f32[32,1,128]{2,1,0:T(1,128)}), f32[32,1,128]{2,1,0:T(1,128)S(1)}, u32[]{:S(2)}, u32[]{:S(2)}) async-start(f32[32,1,128]{2,1,0:T(1,128)} %bitcast.10), calls=%async_computation | async-start | bytes 32768 | tf_op jit(solution)/shard_map/all_to_all | solution.py:574
